TPU v7x, 32 devices: a whole 2x2x4 slice. The times are simulated.
32 devices in a mesh: row: 4 (over y, x), col: 8 (over z, core).
Axes of the slice: x: 2, y: 2, z: 4, core: 2. Of those that a mesh axis runs over, the one named last changes fastest.
Arguments:
- tokens: bfloat16 [2, 64, 16384], P(None, 'col', 'row'), may hold values from -6 to 6
- gate_weight: bfloat16 [16384, 26624], P(('row', 'col')), may hold values from -0.046875 to 0.046875
- up_weight: bfloat16 [16384, 26624], P(('row', 'col')), may hold values from -0.046875 to 0.046875
- down_weight: bfloat16 [16384, 26624], P(('row', 'col')), may hold values from -0.0390625 to 0.0390625
Outputs:
- block_out: bfloat16 [2, 64, 16384], P(None, 'col', 'row')
All inputs are finite; a program needn't handle non-finite values.
Results may differ from a plain program's by a relative error of at most 0.028.
Values may be sent and summed in bfloat16 or wider, within the bound.
No kernel may reach another device: no remote copies, remote signals or barrier semaphores. Data moves between devices by JAX's collectives and lax.ppermute only.
A program may use at most 320 MiB of HBM per device.

v0:
```python
import jax
import jax.numpy as jnp
from jax import lax
from jax.sharding import PartitionSpec as P


def on_device(tokens, gate_weight, up_weight, down_weight):
    batches = tokens.shape[0]

    def gate_up(batch_index, gate_tile, up_tile):
        gathered = lax.all_gather(tokens[batch_index], "col", axis=0, tiled=True)
        half_width = gate_tile.shape[1]
        summed = lax.psum_scatter(
            jnp.concatenate(
                [
                    jnp.dot(gathered, gate_tile, preferred_element_type=jnp.float32),
                    jnp.dot(gathered, up_tile, preferred_element_type=jnp.float32),
                ],
                1,
            ).astype(jnp.bfloat16),
            "row",
            scatter_dimension=0,
            tiled=True,
        ).astype(jnp.float32)
        hidden_part = (jax.nn.silu(summed[:, :half_width]) * summed[:, half_width:]).astype(
            jnp.bfloat16
        )
        return lax.all_gather(hidden_part, "row", axis=0, tiled=True)

    def project(hidden, down_tile):
        return lax.psum_scatter(
            lax.dot_general(
                hidden, down_tile, (((1,), (1,)), ((), ())), preferred_element_type=jnp.float32
            ).astype(jnp.bfloat16),
            "col",
            scatter_dimension=0,
            tiled=True,
        )

    gate_tile, up_tile, down_tile = (
        lax.all_to_all(gate_weight, "col", split_axis=1, concat_axis=0, tiled=True),
        lax.all_to_all(up_weight, "col", split_axis=1, concat_axis=0, tiled=True),
        lax.all_to_all(down_weight, "col", split_axis=1, concat_axis=0, tiled=True),
    )
    hiddens = [gate_up(batch_index, gate_tile, up_tile) for batch_index in range(batches)]
    outputs = [project(hidden, down_tile) for hidden in hiddens]
    return jnp.stack(outputs, 0)


def solution(mesh):
    in_specs = (
        P(None, "col", "row"),
        P(("row", "col"), None),
        P(("row", "col"), None),
        P(("row", "col"), None),
    )
    out_specs = P(None, "col", "row")
    return jax.shard_map(
        on_device, mesh=mesh, in_specs=in_specs, out_specs=out_specs, check_vma=False
    )
```

profile of v0, /device:TPU:0, one launch (start us, length us, event | category | flops | bytes accessed | tf_op | source)
XLA Modules:
  0.0 2105.3 jit_solution(9905880063742128366)
XLA Ops:
  6.5 36.1 %copy.5 = bf16[512,26624]{0,1:T(8,128)(2,1)} copy(bf16[512,26624]{1,0:T(8,128)(2,1)} %param.5) | data formatting | bytes 54525952 | tf_op args[1]
  42.6 6.6 all-to-all-start
  49.2 36.0 %copy.7 = bf16[512,26624]{0,1:T(8,128)(2,1)} copy(bf16[512,26624]{1,0:T(8,128)(2,1)} %param.6) | data formatting | bytes 54525952 | tf_op args[2]
  85.2 553.2 %all-to-all-done = bf16[512,8,3328]{0,2,1:T(8,128)(2,1)} async-done(((bf16[512,8,3328]{0,2,1:T(8,128)(2,1)}), bf16[512,8,3328]{0,2,1:T(8,128)(2,1)}, u32[]{:S(2)}, u32[]{:S(2)}) %all-to-all-start) | async-done | bytes 27263008 | tf_op jit(solution)/shard_map/all_to_all | solution.py:41
  638.4 6.6 all-to-all-start.1
  645.0 36.1 %copy.9 = bf16[512,26624]{0,1:T(8,128)(2,1)} copy(bf16[512,26624]{1,0:T(8,128)(2,1)} %param.7) | data formatting | bytes 54525952 | tf_op args[3]
  681.1 552.3 %all-to-all-done.1 = bf16[512,8,3328]{0,2,1:T(8,128)(2,1)} async-done(((bf16[512,8,3328]{0,2,1:T(8,128)(2,1)}), bf16[512,8,3328]{0,2,1:T(8,128)(2,1)}, u32[]{:S(2)}, u32[]{:S(2)}) %all-to-all-start.1) | async-done | bytes 27263008 | tf_op jit(solution)/shard_map/all_to_all | solution.py:42
  1233.3 0.0 copy-start
  1233.3 6.7 all-to-all-start.2
  1240.1 0.0 reduce-scatter.5.cloned.1.call-start
  1240.1 0.0 copy-done
  1240.1 596.3 %all-gather = bf16[1,64,4096]{2,1,0:T(8,128)(2,1)S(1)} all-gather(bf16[1,8,4096]{2,1,0:T(8,128)(2,1)S(1)} %get-tuple-element.5), channel_id=2, replica_groups=mesh['row'=4,'col'=8] {'col'}, dimensions={1}, use_global_device_ids=true | all-gather | bytes 589824 | tf_op jit(solution)/shard_map/all_gather | solution.py:11
  1836.5 14.7 all-gather.1
  1851.2 33.1 %copy.6 = bf16[8,512,3328]{2,1,0:T(8,128)(2,1)} copy(bf16[8,512,3328]{1,2,0:T(8,128)(2,1)} %bitcast.2) | data formatting | bytes 54525952 | tf_op jit(solution)/shard_map/all_to_all | solution.py:41
  1884.4 33.2 %copy.8 = bf16[8,512,3328]{2,1,0:T(8,128)(2,1)} copy(bf16[8,512,3328]{1,2,0:T(8,128)(2,1)} %bitcast.5) | data formatting | bytes 54525952 | tf_op jit(solution)/shard_map/all_to_all | solution.py:42
  1917.6 11.3 convolution_convert_fusion.5
  1928.8 11.3 convolution_convert_fusion.4
  1940.1 1.0 pad_maximum_fusion
  1941.1 0.0 reduce-scatter.5.cloned.1.call-update
  1941.1 0.0 reduce-scatter.9.cloned.1.call-start
  1941.1 11.4 convolution_convert_fusion.3
  1952.6 11.5 convolution_convert_fusion.2
  1964.1 1.0 pad_maximum_fusion.1
  1965.1 0.0 reduce-scatter.9.cloned.1.call-update
  1965.1 0.0 reduce-scatter.7.cloned.1.call-start
  1965.1 0.0 all-to-all-done.2
  1965.1 33.5 %copy.10 = bf16[8,512,3328]{2,1,0:T(8,128)(2,1)} copy(bf16[8,512,3328]{1,2,0:T(8,128)(2,1)} %bitcast.8) | data formatting | bytes 54525952 | tf_op jit(solution)/shard_map/all_to_all | solution.py:43
  1998.7 0.0 reduce-scatter.5.cloned.1.call-done
  1998.7 1.0 convert_element_type.20
  1999.6 0.1 fusion.5
  1999.7 0.0 reduce-scatter.9.cloned.1.call-done
  1999.8 1.0 convert_element_type.23
  2000.7 0.1 fusion.4
  2000.8 10.2 all_gather.15
  2011.0 10.0 all_gather.13
  2021.0 14.2 convolution_convert_fusion.1
  2035.2 0.0 reduce-scatter.7.cloned.1.call-update
  2035.3 0.0 reduce-scatter.11.cloned.1.call-start
  2035.3 14.2 convolution_convert_fusion
  2049.6 0.0 reduce-scatter.11.cloned.1.call-update
  2049.6 16.4 reduce-scatter.7.cloned.1.call-done
  2065.9 31.3 %reduce-scatter.11.cloned.1.call-done = bf16[8,4096]{1,0:T(8,128)(2,1)} async-done(((bf16[64,4096]{1,0:T(8,128)(2,1)}), bf16[8,4096]{1,0:T(8,128)(2,1)}) %reduce-scatter.11.cloned.1.call-update) | async-done | bytes 65552 | tf_op jit(solution)/shard_map/reduce_scatter | solution.py:31
  2097.3 1.5 pad_maximum_fusion.2
  (1 shorter events, 0.0 us)
Async XLA Ops:
  42.6 595.7 %all-to-all-start = ((bf16[512,8,3328]{0,2,1:T(8,128)(2,1)}), bf16[512,8,3328]{0,2,1:T(8,128)(2,1)}, u32[]{:S(2)}, u32[]{:S(2)}) async-start(bf16[512,8,3328]{0,2,1:T(8,128)(2,1)} %bitcast.37), calls=%async_computation | async-start | bytes 54525952 | tf_op jit(solution)/shard_map/all_to_all | solution.py:41
  638.4 595.0 %all-to-all-start.1 = ((bf16[512,8,3328]{0,2,1:T(8,128)(2,1)}), bf16[512,8,3328]{0,2,1:T(8,128)(2,1)}, u32[]{:S(2)}, u32[]{:S(2)}) async-start(bf16[512,8,3328]{0,2,1:T(8,128)(2,1)} %bitcast.36), calls=%async_computation.1 | async-start | bytes 54525952 | tf_op jit(solution)/shard_map/all_to_all | solution.py:42
  1233.3 6.8 copy-start
  1233.3 731.8 %all-to-all-start.2 = ((bf16[512,8,3328]{0,2,1:T(8,128)(2,1)}), bf16[512,8,3328]{0,2,1:T(8,128)(2,1)}, u32[]{:S(2)}, u32[]{:S(2)}) async-start(bf16[512,8,3328]{0,2,1:T(8,128)(2,1)} %bitcast.35), calls=%async_computation.3 | async-start | bytes 54525952 | tf_op jit(solution)/shard_map/all_to_all | solution.py:43
  1240.1 758.6 %reduce-scatter.5.cloned.1.call-start = ((), (), s32[]{:S(2)}) async-start(), calls=%async_computation.7 | async-start | bytes 1064960 | tf_op jit(solution)/shard_map/reduce_scatter | solution.py:13
  1941.1 58.6 %reduce-scatter.9.cloned.1.call-start = ((), (), s32[]{:S(2)}) async-start(), calls=%async_computation.9 | async-start | bytes 1064960 | tf_op jit(solution)/shard_map/reduce_scatter | solution.py:13
  1965.1 100.9 %reduce-scatter.7.cloned.1.call-start = ((), (), s32[]{:S(2)}) async-start(), calls=%async_computation.8 | async-start | bytes 589824 | tf_op jit(solution)/shard_map/reduce_scatter | solution.py:31
  2035.3 62.0 %reduce-scatter.11.cloned.1.call-start = ((), (), s32[]{:S(2)}) async-start(), calls=%async_computation.10 | async-start | bytes 589824 | tf_op jit(solution)/shard_map/reduce_scatter | solution.py:31
Sparse Core Ops, SparseCore 0:
  1941.2 27.7 reduce-scatter.4
  1971.9 26.4 reduce-scatter.8
  2035.4 30.5 reduce-scatter.6
  2068.2 29.0 reduce-scatter.10
where the time goes:
time: 2110 us
  waiting for transfers between devices  1150 us (55%)
  blocking collectives  631 us (30%)
  local copies, waits for them, and re-layouts  208 us (10%)
  matrix products  73.9 us (4%)
    all_gather x2, blocking collectives, gate_up(): gathered = lax.all_gather(tokens[batch_index], 'col', axis=0, tiled=True)  611 us
    all_to_all x1, waiting for transfers between devices, on_device(): lax.all_to_all(gate_weight, 'col', split_axis=1, concat_axis=0, tiled=True)  553 us
    all_to_all x1, waiting for transfers between devices, on_device(): lax.all_to_all(up_weight, 'col', split_axis=1, concat_axis=0, tiled=True)  552 us
    unnamed x5, local copies, waits for them, and re-layouts  108 us
    reduce_scatter x2, waiting for transfers between devices, project(): lax.psum_scatter(lax.dot_general(hidden, down_tile, (((1,), (1,)), ((), (...  47.7 us
  transfers between devices with their start and end apart: 7, of which 4 were waited for; matrix products, arithmetic and copies ran while one was open for 11% of the time, Pallas kernels for 0%

commit v1 on v0

v1 whole, which is shorter than its diff:
```python
import functools

import jax
import jax.numpy as jnp
import numpy as np
from jax import lax
from jax.sharding import PartitionSpec as P

SHARES = (2, 2, 2, 2)
ORDER = (2, 0, 2, 3, 0, 1, 2, 0, 2, 1, 0, 2, 3, 0, 1, 2, 0, 3, 2, 1, 0, 3, 2, 1, 0, 3, 1, 2, 3, 1, 0, 3, 1, 2, 3, 1, 0, 3, 2, 1, 0, 3, 1, 3)

def swap(value, axis, size, bit):
    return lax.ppermute(value, axis, [(i, i ^ bit) for i in range(size)])


def gate_up(x, gate_weight, up_weight, start, width):
    half = x.shape[0] // 2
    parts = [
        jnp.dot(
            x, lax.slice_in_dim(weight, start, start + width, axis=1),
            preferred_element_type=jnp.float32,
        ).astype(jnp.bfloat16)
        for weight in (gate_weight, up_weight)
    ]
    return [p[:half] for p in parts], [p[half:] for p in parts]


def down(own, other, down_weight, before, start):
    hidden = jnp.concatenate([own, other], 0)
    weight = lax.slice_in_dim(down_weight, start, start + own.shape[1], axis=1)
    return before + lax.dot_general(
        hidden, weight, (((1,), (1,)), ((), ())), preferred_element_type=jnp.float32
    )


def add_halves(keep, received, axis):
    half = keep.shape[axis] // 2
    sides = []
    for k in range(2):
        kept = lax.slice_in_dim(keep, k * half, (k + 1) * half, axis=axis).astype(jnp.float32)
        came = lax.slice_in_dim(received, k * half, (k + 1) * half, axis=axis).astype(jnp.float32)
        sides.append((kept + came).astype(jnp.bfloat16))
    return sides


def step_order(pairs, steps):
    if len(ORDER) == pairs * steps:
        return ORDER
    return [p for t in range(steps + 2 * pairs) for p in range(pairs) if 0 <= t - 2 * p < steps]


def on_device(n_row, n_col, tokens, gate_weight, up_weight, down_weight):
    batches, local_tokens, local_features = tokens.shape
    own_tokens = batches * local_tokens
    all_tokens = own_tokens * n_col
    features, units = gate_weight.shape
    per_device = own_tokens // n_row
    row, col = lax.axis_index("row"), lax.axis_index("col")
    row_bits = [1 << k for k in range(n_row.bit_length() - 1)]
    col_bits = [1 << k for k in range(1, n_col.bit_length() - 1)]
    core_bit = 1
    orders = (row_bits, row_bits[::-1])

    x = tokens.reshape(own_tokens, local_features)
    for bit in col_bits[::-1] + [core_bit]:
        half = x.shape[1] // 2
        low, high = x[:, :half], x[:, half:]
        mine = (col & bit) != 0
        keep, send = jnp.where(mine, high, low), jnp.where(mine, low, high)
        x = jnp.concatenate([keep, swap(send, "col", n_col, bit)], 0)

    base = np.arange(all_tokens).reshape(
        (2,) + (2,) * len(col_bits) + (2,) * len(row_bits) + (per_device,)
    )
    n_cb, n_rb = len(col_bits), len(row_bits)
    sources = []
    for order in orders:
        row_dims = [1 + n_cb + n_rb - 1 - row_bits.index(bit) for bit in order]
        dims = [0] + row_dims + list(range(1, 1 + n_cb)) + [1 + n_cb + n_rb]
        sources.append(base.transpose(dims).reshape(-1))
    source = jnp.asarray(np.concatenate(sources), jnp.int32) ^ (row * per_device)
    pick = source[:, None] == lax.broadcasted_iota(jnp.int32, (2 * all_tokens, all_tokens), 1)
    ordered = jnp.dot(pick.astype(jnp.bfloat16), x, preferred_element_type=jnp.float32).astype(
        jnp.bfloat16
    )
    x_orders = (ordered[:all_tokens], ordered[all_tokens:])

    totals = [jnp.zeros((all_tokens, features), jnp.float32) for _ in orders]
    last = [x]

    def after(*values):
        return lax.optimization_barrier((values, last[0]))[0]

    def steps(starts, width):
        sums = []
        for k in range(2):
            (x_now,) = after(x_orders[k])
            keep, send = gate_up(x_now, gate_weight, up_weight, starts[k], width)
            last[0] = send
            came = [swap(part, "col", n_col, core_bit) for part in send]
            sums.append((keep, came))
        yield
        for stage in range(n_rb):
            for k in range(2):
                if stage == 0:
                    (kept_gate, kept_up), (came_gate, came_up) = after(*sums[k])
                    halves = add_halves(kept_gate, came_gate, 0), add_halves(kept_up, came_up, 0)
                    keep, send = (jnp.stack(side) for side in zip(*halves))
                else:
                    keep, send = add_halves(*after(*sums[k]), 1)
                last[0] = send
                sums[k] = keep, swap(send, "row", n_row, orders[k][stage])
            yield
        keep, received = (jnp.stack(parts) for parts in zip(*(after(*s) for s in sums)))
        for bit in col_bits:
            keep, send = add_halves(keep, received, 2)
            last[0] = send
            received = swap(send, "col", n_col, bit)
            yield
            keep, received = after(keep, received)
        total = keep.astype(jnp.float32) + received.astype(jnp.float32)
        hidden = (jax.nn.silu(total[:, 0]) * total[:, 1]).astype(jnp.bfloat16)
        for bit in col_bits[::-1]:
            last[0] = hidden
            received = swap(hidden, "col", n_col, bit)
            yield
            hidden = jnp.concatenate(after(hidden, received), 1)
        parts = [hidden[k] for k in range(2)]
        for stage in range(n_rb):
            came = []
            for k in range(2):
                last[0] = parts[k]
                came.append(swap(parts[k], "row", n_row, orders[k][n_rb - 1 - stage]))
            yield
            for k in range(2):
                parts[k] = jnp.concatenate(after(parts[k], came[k]), 0)
        others = []
        for k in range(2):
            last[0] = parts[k]
            others.append(swap(parts[k], "col", n_col, core_bit))
        yield
        for k in range(2):
            own, other = after(parts[k], others[k])
            totals[k] = last[0] = down(own, other, down_weight, totals[k], starts[k])

    share = units // (2 * sum(SHARES))
    ends = np.cumsum(SHARES) * share
    half_units = units // 2
    running = [
        steps([int(end) - n * share, half_units + int(end) - n * share], n * share)
        for n, end in zip(SHARES, ends)
    ]
    for pair in step_order(len(SHARES), 3 + 2 * n_rb + 2 * n_cb):
        next(running[pair], None)

    total = jnp.concatenate(totals, 0)
    out = lax.dot_general(
        pick.astype(jnp.float32), total, (((0,), (0,)), ((), ())),
        precision=lax.Precision.HIGHEST, preferred_element_type=jnp.float32,
    ).astype(jnp.bfloat16)

    for bit in [core_bit] + col_bits:
        half = out.shape[0] // 2
        keep, came = out[:half], swap(out[half:], "col", n_col, bit)
        mine = (col & bit) != 0
        out = jnp.concatenate([jnp.where(mine, came, keep), jnp.where(mine, keep, came)], 1)
    return out.reshape(batches, local_tokens, local_features)


def solution(mesh):
    in_specs = (
        P(None, "col", "row"),
        P(("row", "col"), None),
        P(("row", "col"), None),
        P(("row", "col"), None),
    )
    out_specs = P(None, "col", "row")
    body = functools.partial(on_device, mesh.shape["row"], mesh.shape["col"])
    return jax.shard_map(body, mesh=mesh, in_specs=in_specs, out_specs=out_specs, check_vma=False)
```

time: 2110 us -> 198 us (0.09)
  waiting for transfers between devices: 1150 us -> 74.2 us
  blocking collectives: 631 us -> 0 us
  local copies, waits for them, and re-layouts: 208 us -> 1.51 us
  starting transfers between devices: 20 us -> 69 us
  matrix products: 73.9 us -> 44.4 us
    all_to_all x3 -> x0, waiting for transfers between devices: 1110 us -> none  [the longest x1 553 us: on_device(): lax.all_to_all(gate_weight, 'col', split_axis=1, concat_axis=0, tiled=True)]
    all_gather x4 -> x0, blocking collectives: 631 us -> none  [the longest x2 611 us: gate_up(): gathered = lax.all_gather(tokens[batch_index], 'col', axis=0, tiled=True)]
    unnamed x5 -> x36, local copies, waits for them, and re-layouts: 108 us -> 0.26 us
    all_to_all x3 -> x0, local copies, waits for them, and re-layouts: 99.9 us -> none  [the longest x1 33.5 us: on_device(): lax.all_to_all(down_weight, 'col', split_axis=1, concat_axis=0, tiled=True)]
    ppermute x0 -> x78, waiting for transfers between devices: none -> 74.2 us  [swap(): return lax.ppermute(value, axis, [(i, i ^ bit) for i in range(size)])]
    ppermute x0 -> x78, starting transfers between devices: none -> 69 us  [swap(): return lax.ppermute(value, axis, [(i, i ^ bit) for i in range(size)])]
    reduce_scatter x4 -> x0, waiting for transfers between devices: 47.7 us -> none  [the longest x2 47.7 us: project(): lax.psum_scatter(lax.dot_general(hidden, down_tile, (((1,), (1,)), ((), (...]
    dot_general x6 -> x26, matrix products: 73.9 us -> 44.4 us  [the longest x16 33.4 us: gate_up(): jnp.dot(x, lax.slice_in_dim(weight, start, start + width, axis=1), prefer...]
  transfers between devices with their start and end apart: 7 -> 78, of which waited for: 4 -> 29; matrix products, arithmetic and copies ran while one was open for 11% -> 19% of each run, Pallas kernels for 0% -> 0%
where the time goes in v1:
time: 198 us
  waiting for transfers between devices  74.2 us (37%)
  starting transfers between devices  69 us (35%)
  matrix products  44.4 us (22%)
  other arithmetic  7.1 us (4%)
    ppermute x78, waiting for transfers between devices, swap(): return lax.ppermute(value, axis, [(i, i ^ bit) for i in range(size)])  74.2 us
    ppermute x78, starting transfers between devices, swap(): return lax.ppermute(value, axis, [(i, i ^ bit) for i in range(size)])  69 us
    dot_general x16, matrix products, gate_up(): jnp.dot(x, lax.slice_in_dim(weight, start, start + width, axis=1), prefer...  33.4 us
    dot_general x8, matrix products, down(): lax.dot_general(hidden, weight, (((1,), (1,)), ((), ())), preferred_eleme...  10.3 us
  transfers between devices with their start and end apart: 78, of which 29 were waited for; matrix products, arithmetic and copies ran while one was open for 19% of the time, Pallas kernels for 0%

profile of v1, /device:TPU:0, one launch (start us, length us, event | category | flops | bytes accessed | tf_op | source)
XLA Modules:
  0.0 197.6 jit_solution(17237328805010147389)
XLA Ops:
  0.9 4.1 %collective-permute-start = (bf16[16,2048]{1,0:T(8,128)(2,1)S(1)}, bf16[16,2048]{1,0:T(8,128)(2,1)S(1)}, u32[]{:S(2)}, u32[]{:S(2)}) collective-permute-start(bf16[16,2048]{1,0:T(8,128)(2,1)S(1)} %get-tuple-element.426), channel_id=1, source_target_pairs={{0,4},{1,5},{2,6},{3,7},{4,0},{5,1},{6,2},{7,3},{8,12},{9,13},{10,... | collective-permute-start | bytes 196616 | tf_op jit(solution)/shard_map/ppermute | solution.py:13
  5.0 3.6 %collective-permute-done = bf16[16,2048]{1,0:T(8,128)(2,1)S(1)} collective-permute-done((bf16[16,2048]{1,0:T(8,128)(2,1)S(1)}, bf16[16,2048]{1,0:T(8,128)(2,1)S(1)}, u32[]{:S(2)}, u32[]{:S(2)}) %collective-permute-start) | collective-permute-done | bytes 65568 | tf_op jit(solution)/shard_map/ppermute | solution.py:13
  9.3 3.7 %collective-permute-done.1 = bf16[32,1024]{1,0:T(8,128)(2,1)S(1)} collective-permute-done((bf16[32,1024]{1,0:T(8,128)(2,1)S(1)}, bf16[32,1024]{1,0:T(8,128)(2,1)S(1)}, u32[]{:S(2)}, u32[]{:S(2)}) %collective-permute-start.1) | collective-permute-done | bytes 65568 | tf_op jit(solution)/shard_map/ppermute | solution.py:13
  14.6 2.6 %convolution_convert_fusion.15 = bf16[128,3328]{1,0:T(8,128)(2,1)S(1)} fusion(bf16[128,512]{1,0:T(8,128)(2,1)S(1)} %get-tuple-element.179, bf16[512,26624]{1,0:T(8,128)(2,1)} %param.6), kind=kOutput, calls=%fused_computation.15 | convolution fusion | flops 436633600 | bytes 4390912 | tf_op jit(solution)/shard_map/dot_general | solution.py:19
  17.3 2.6 %convolution_convert_fusion.14 = bf16[128,3328]{1,0:T(8,128)(2,1)S(1)} fusion(bf16[128,512]{1,0:T(8,128)(2,1)S(1)} %get-tuple-element.179, bf16[512,26624]{1,0:T(8,128)(2,1)} %param.7), kind=kOutput, calls=%fused_computation.14 | convolution fusion | flops 436633600 | bytes 4390912 | tf_op jit(solution)/shard_map/dot_general | solution.py:19
  20.0 2.7 %convolution_convert_fusion.13 = bf16[128,3328]{1,0:T(8,128)(2,1)S(1)} fusion(bf16[128,512]{1,0:T(8,128)(2,1)S(1)} %get-tuple-element.180, bf16[512,26624]{1,0:T(8,128)(2,1)} %param.6), kind=kOutput, calls=%fused_computation.13 | convolution fusion | flops 436633600 | bytes 4390912 | tf_op jit(solution)/shard_map/dot_general | solution.py:19
  22.7 3.1 %convolution_convert_fusion.12 = bf16[128,3328]{1,0:T(8,128)(2,1)S(1)} fusion(bf16[128,512]{1,0:T(8,128)(2,1)S(1)} %get-tuple-element.180, bf16[512,26624]{1,0:T(8,128)(2,1)} %param.7), kind=kOutput, calls=%fused_computation.12 | convolution fusion | flops 436633600 | bytes 4390912 | tf_op jit(solution)/shard_map/dot_general | solution.py:19
  27.1 3.3 %convolution_convert_fusion.11 = bf16[128,3328]{1,0:T(8,128)(2,1)S(1)} fusion(bf16[128,512]{1,0:T(8,128)(2,1)S(1)} %get-tuple-element.179, bf16[512,26624]{1,0:T(8,128)(2,1)} %param.6), kind=kOutput, calls=%fused_computation.11 | convolution fusion | flops 436633600 | bytes 4390912 | tf_op jit(solution)/shard_map/dot_general | solution.py:19
  30.5 2.8 %convolution_convert_fusion.10 = bf16[128,3328]{1,0:T(8,128)(2,1)S(1)} fusion(bf16[128,512]{1,0:T(8,128)(2,1)S(1)} %get-tuple-element.179, bf16[512,26624]{1,0:T(8,128)(2,1)} %param.7), kind=kOutput, calls=%fused_computation.10 | convolution fusion | flops 436633600 | bytes 4390912 | tf_op jit(solution)/shard_map/dot_general | solution.py:19
  34.1 2.6 %convolution_convert_fusion.8 = bf16[128,3328]{1,0:T(8,128)(2,1)S(1)} fusion(bf16[128,512]{1,0:T(8,128)(2,1)S(1)} %get-tuple-element.180, bf16[512,26624]{1,0:T(8,128)(2,1)} %param.7), kind=kOutput, calls=%fused_computation.8 | convolution fusion | flops 436633600 | bytes 4390912 | tf_op jit(solution)/shard_map/dot_general | solution.py:19
  38.6 1.8 collective-permute-start.15
  41.0 2.6 %convolution_convert_fusion.6 = bf16[128,3328]{1,0:T(8,128)(2,1)S(1)} fusion(bf16[128,512]{1,0:T(8,128)(2,1)S(1)} %get-tuple-element.179, bf16[512,26624]{1,0:T(8,128)(2,1)} %param.7), kind=kOutput, calls=%fused_computation.6 | convolution fusion | flops 436633600 | bytes 4390912 | tf_op jit(solution)/shard_map/dot_general | solution.py:19
  44.3 2.6 %convolution_convert_fusion.4 = bf16[128,3328]{1,0:T(8,128)(2,1)S(1)} fusion(bf16[128,512]{1,0:T(8,128)(2,1)S(1)} %get-tuple-element.180, bf16[512,26624]{1,0:T(8,128)(2,1)} %param.7), kind=kOutput, calls=%fused_computation.4 | convolution fusion | flops 436633600 | bytes 4390912 | tf_op jit(solution)/shard_map/dot_general | solution.py:19
  47.1 1.6 collective-permute-start.5
  49.8 2.6 %convolution_convert_fusion.2 = bf16[128,3328]{1,0:T(8,128)(2,1)S(1)} fusion(bf16[128,512]{1,0:T(8,128)(2,1)S(1)} %get-tuple-element.179, bf16[512,26624]{1,0:T(8,128)(2,1)} %param.7), kind=kOutput, calls=%fused_computation.2 | convolution fusion | flops 436633600 | bytes 4390912 | tf_op jit(solution)/shard_map/dot_general | solution.py:19
  53.2 2.7 %convolution_convert_fusion = bf16[128,3328]{1,0:T(8,128)(2,1)S(1)} fusion(bf16[128,512]{1,0:T(8,128)(2,1)S(1)} %get-tuple-element.180, bf16[512,26624]{1,0:T(8,128)(2,1)} %param.7), kind=kOutput, calls=%fused_computation | convolution fusion | flops 436633600 | bytes 4390912 | tf_op jit(solution)/shard_map/dot_general | solution.py:19
  57.2 1.8 collective-permute-done.5
  59.8 8.1 %collective-permute-done.14 = bf16[2,32,3328]{2,1,0:T(8,128)(2,1)S(1)} collective-permute-done((bf16[2,32,3328]{2,1,0:T(8,128)(2,1)S(1)}, bf16[2,32,3328]{2,1,0:T(8,128)(2,1)S(1)}, u32[]{:S(2)}, u32[]{:S(2)}) %collective-permute-start.14) | collective-permute-done | bytes 426016 | tf_op jit(solution)/shard_map/ppermute | solution.py:13
  67.9 1.5 collective-permute-start.16
  70.2 3.6 %collective-permute-done.16 = bf16[2,16,3328]{2,1,0:T(8,128)(2,1)S(1)} collective-permute-done((bf16[2,16,3328]{2,1,0:T(8,128)(2,1)S(1)}, bf16[2,16,3328]{2,1,0:T(8,128)(2,1)S(1)}, u32[]{:S(2)}, u32[]{:S(2)}) %collective-permute-start.16) | collective-permute-done | bytes 213024 | tf_op jit(solution)/shard_map/ppermute | solution.py:13
  73.8 1.6 collective-permute-done.12
  76.5 1.3 collective-permute-start.23
  78.5 5.7 %collective-permute-done.23 = bf16[2,16,3328]{2,1,0:T(8,128)(2,1)S(1)} collective-permute-done((bf16[2,16,3328]{2,1,0:T(8,128)(2,1)S(1)}, bf16[2,16,3328]{2,1,0:T(8,128)(2,1)S(1)}, u32[]{:S(2)}, u32[]{:S(2)}) %collective-permute-start.23) | collective-permute-done | bytes 213024 | tf_op jit(solution)/shard_map/ppermute | solution.py:13
  85.6 6.2 %collective-permute-done.17 = bf16[2,2,8,3328]{3,2,1,0:T(8,128)(2,1)S(1)} collective-permute-done((bf16[2,2,8,3328]{3,2,1,0:T(8,128)(2,1)S(1)}, bf16[2,2,8,3328]{3,2,1,0:T(8,128)(2,1)S(1)}, u32[]{:S(2)}, u32[]{:S(2)}) %collective-permute-start.17) | collective-permute-done | bytes 213024 | tf_op jit(solution)/shard_map/ppermute | solution.py:13
  94.4 3.4 %collective-permute-start.24 = (bf16[2,2,4,3328]{3,2,1,0:T(4,128)(2,1)S(1)}, bf16[2,2,4,3328]{3,2,1,0:T(4,128)(2,1)S(1)}, u32[]{:S(2)}, u32[]{:S(2)}) collective-permute-start(bf16[2,2,4,3328]{3,2,1,0:T(4,128)(2,1)S(1)} %get-tuple-element.403), channel_id=1, source_target_pairs={{0,4},{1,5},{2,6},{3,7},{4,0},{5,1},{6,2},{7,3},{8,12},{9,13},{10,... | collective-permute-start | bytes 319496 | tf_op jit(solution)/shard_map/ppermute | solution.py:13
  99.0 2.7 %collective-permute-done.27 = bf16[2,2,8,3328]{3,2,0,1:T(8,128)(2,1)S(1)} collective-permute-done((bf16[2,2,8,3328]{3,2,0,1:T(8,128)(2,1)S(1)}, bf16[2,2,8,3328]{3,2,0,1:T(8,128)(2,1)S(1)}, u32[]{:S(2)}, u32[]{:S(2)}) %collective-permute-start.27) | collective-permute-done | bytes 213024 | tf_op jit(solution)/shard_map/ppermute | solution.py:13
  101.7 1.5 collective-permute-start.33
  103.4 1.9 collective-permute-done.26
  105.3 2.0 %collective-permute-start.35 = (bf16[2,2,4,3328]{3,2,0,1:T(4,128)(2,1)S(1)}, bf16[2,2,4,3328]{3,2,0,1:T(4,128)(2,1)S(1)}, u32[]{:S(2)}, u32[]{:S(2)}) collective-permute-start(bf16[2,2,4,3328]{3,2,0,1:T(4,128)(2,1)S(1)} %get-tuple-element.402), channel_id=1, source_target_pairs={{0,4},{1,5},{2,6},{3,7},{4,0},{5,1},{6,2},{7,3},{8,12},{9,13},{10,... | collective-permute-start | bytes 319496 | tf_op jit(solution)/shard_map/ppermute | solution.py:13
  107.5 1.6 collective-permute-start.39
  110.5 2.3 %collective-permute-done.35 = bf16[2,2,4,3328]{3,2,0,1:T(4,128)(2,1)S(1)} collective-permute-done((bf16[2,2,4,3328]{3,2,0,1:T(4,128)(2,1)S(1)}, bf16[2,2,4,3328]{3,2,0,1:T(4,128)(2,1)S(1)}, u32[]{:S(2)}, u32[]{:S(2)}) %collective-permute-start.35) | collective-permute-done | bytes 106528 | tf_op jit(solution)/shard_map/ppermute | solution.py:13
  114.2 2.3 %collective-permute-start.38 = (bf16[2,4,3328]{2,1,0:T(4,128)(2,1)S(1)}, bf16[2,4,3328]{2,1,0:T(4,128)(2,1)S(1)}, u32[]{:S(2)}, u32[]{:S(2)}) collective-permute-start(bf16[2,4,3328]{2,1,0:T(4,128)(2,1)S(1)} %fusion.123), channel_id=1, source_target_pairs={{0,4},{1,5},{2,6},{3,7},{4,0},{5,1},{6,2},{7,3},{8,12},{9,13},{10,... | collective-permute-start | bytes 159752 | tf_op jit(solution)/shard_map/ppermute | solution.py:13
  116.6 1.6 collective-permute-start.37
  118.3 1.5 collective-permute-start.41
  119.9 1.4 collective-permute-start.36
  122.3 1.4 collective-permute-start.46
  123.7 1.6 collective-permute-done.41
  125.5 1.5 collective-permute-start.45
  127.0 1.5 collective-permute-start.50
  128.5 1.6 collective-permute-done.43
  131.5 1.6 collective-permute-start.53
  133.0 1.5 collective-permute-start.42
  135.3 2.9 %collective-permute-done.44 = bf16[2,2,4,3328]{3,2,0,1:T(4,128)(2,1)S(1)} collective-permute-done((bf16[2,2,4,3328]{3,2,0,1:T(4,128)(2,1)S(1)}, bf16[2,2,4,3328]{3,2,0,1:T(4,128)(2,1)S(1)}, u32[]{:S(2)}, u32[]{:S(2)}) %collective-permute-start.44) | collective-permute-done | bytes 106528 | tf_op jit(solution)/shard_map/ppermute | solution.py:13
  138.3 3.0 %collective-permute-start.48 = (bf16[2,4,3328]{2,1,0:T(4,128)(2,1)S(1)}, bf16[2,4,3328]{2,1,0:T(4,128)(2,1)S(1)}, u32[]{:S(2)}, u32[]{:S(2)}) collective-permute-start(bf16[2,4,3328]{2,1,0:T(4,128)(2,1)S(1)} %fusion.122), channel_id=1, source_target_pairs={{0,4},{1,5},{2,6},{3,7},{4,0},{5,1},{6,2},{7,3},{8,12},{9,13},{10,... | collective-permute-start | bytes 159752 | tf_op jit(solution)/shard_map/ppermute | solution.py:13
  141.4 1.7 collective-permute-start.56
  143.1 3.6 %collective-permute-done.49 = bf16[2,2,4,3328]{3,2,0,1:T(4,128)(2,1)S(1)} collective-permute-done((bf16[2,2,4,3328]{3,2,0,1:T(4,128)(2,1)S(1)}, bf16[2,2,4,3328]{3,2,0,1:T(4,128)(2,1)S(1)}, u32[]{:S(2)}, u32[]{:S(2)}) %collective-permute-start.49) | collective-permute-done | bytes 106528 | tf_op jit(solution)/shard_map/ppermute | solution.py:13
  147.7 2.0 %collective-permute-start.51 = (bf16[2,8,3328]{2,1,0:T(8,128)(2,1)S(1)}, bf16[2,8,3328]{2,1,0:T(8,128)(2,1)S(1)}, u32[]{:S(2)}, u32[]{:S(2)}) collective-permute-start(bf16[2,8,3328]{2,1,0:T(8,128)(2,1)S(1)} %pad_maximum_fusion.27), channel_id=1, source_target_pairs={{0,2},{1,3},{2,0},{3,1},{4,6},{5,7},{6,4},{7,5},{8,10},{9,11},{10,... | collective-permute-start | bytes 319496 | tf_op jit(solution)/shard_map/ppermute | solution.py:13
  150.9 1.8 collective-permute-done.52
  152.7 1.3 collective-permute-start.61
  155.6 3.2 %collective-permute-done.55 = bf16[2,8,3328]{2,1,0:T(8,128)(2,1)S(1)} collective-permute-done((bf16[2,8,3328]{2,1,0:T(8,128)(2,1)S(1)}, bf16[2,8,3328]{2,1,0:T(8,128)(2,1)S(1)}, u32[]{:S(2)}, u32[]{:S(2)}) %collective-permute-start.55) | collective-permute-done | bytes 106528 | tf_op jit(solution)/shard_map/ppermute | solution.py:13
  161.6 1.6 collective-permute-start.70
  163.2 2.3 %collective-permute-done.65 = bf16[16,3328]{1,0:T(8,128)(2,1)S(1)} collective-permute-done((bf16[16,3328]{1,0:T(8,128)(2,1)S(1)}, bf16[16,3328]{1,0:T(8,128)(2,1)S(1)}, u32[]{:S(2)}, u32[]{:S(2)}) %collective-permute-start.65) | collective-permute-done | bytes 106528 | tf_op jit(solution)/shard_map/ppermute | solution.py:13
  165.8 1.8 collective-permute-done.70
  167.6 1.3 collective-permute-start.66
  172.7 1.4 collective-permute-start.71
  174.1 1.3 collective-permute-done.66
  176.0 1.5 fusion.32
  181.4 1.3 fusion.41
  182.6 1.3 fusion.44
  183.9 1.3 fusion.47
  187.1 1.5 collective-permute-start.76
  188.6 2.9 %collective-permute-done.76 = bf16[32,1024]{1,0:T(8,128)(2,1)S(1)} collective-permute-done((bf16[32,1024]{1,0:T(8,128)(2,1)S(1)}, bf16[32,1024]{1,0:T(8,128)(2,1)S(1)}, u32[]{:S(2)}, u32[]{:S(2)}) %collective-permute-start.76) | collective-permute-done | bytes 65568 | tf_op jit(solution)/shard_map/ppermute | solution.py:13
  191.5 1.5 collective-permute-start.77
  193.0 3.9 %collective-permute-done.77 = bf16[16,2048]{1,0:T(8,128)(2,1)S(1)} collective-permute-done((bf16[16,2048]{1,0:T(8,128)(2,1)S(1)}, bf16[16,2048]{1,0:T(8,128)(2,1)S(1)}, u32[]{:S(2)}, u32[]{:S(2)}) %collective-permute-start.77) | collective-permute-done | bytes 65568 | tf_op jit(solution)/shard_map/ppermute | solution.py:13
  (266 shorter events, 43.9 us)
Async XLA Ops:
  0.9 7.8 %collective-permute-start = (bf16[16,2048]{1,0:T(8,128)(2,1)S(1)}, bf16[16,2048]{1,0:T(8,128)(2,1)S(1)}, u32[]{:S(2)}, u32[]{:S(2)}) collective-permute-start(bf16[16,2048]{1,0:T(8,128)(2,1)S(1)} %get-tuple-element.426), channel_id=1, source_target_pairs={{0,4},{1,5},{2,6},{3,7},{4,0},{5,1},{6,2},{7,3},{8,12},{9,13},{10,... | collective-permute-start | bytes 196616 | tf_op jit(solution)/shard_map/ppermute | solution.py:13
  25.9 11.2 %collective-permute-start.3 = (bf16[64,3328]{1,0:T(8,128)(2,1)S(1)}, bf16[64,3328]{1,0:T(8,128)(2,1)S(1)}, u32[]{:S(2)}, u32[]{:S(2)}) collective-permute-start(bf16[64,3328]{1,0:T(8,128)(2,1)S(1)} %get-tuple-element.395), channel_id=1, source_target_pairs={{0,1},{1,0},{2,3},{3,2},{4,5},{5,4},{6,7},{7,6},{8,9},{9,8},{10,11... | collective-permute-start | bytes 1277960 | tf_op jit(solution)/shard_map/ppermute | solution.py:13
  26.1 11.4 %collective-permute-start.4 = (bf16[64,3328]{1,0:T(8,128)(2,1)S(1)}, bf16[64,3328]{1,0:T(8,128)(2,1)S(1)}, u32[]{:S(2)}, u32[]{:S(2)}) collective-permute-start(bf16[64,3328]{1,0:T(8,128)(2,1)S(1)} %get-tuple-element.393), channel_id=1, source_target_pairs={{0,1},{1,0},{2,3},{3,2},{4,5},{5,4},{6,7},{7,6},{8,9},{9,8},{10,11... | collective-permute-start | bytes 1277960 | tf_op jit(solution)/shard_map/ppermute | solution.py:13
  26.6 11.3 %collective-permute-start.10 = (bf16[64,3328]{1,0:T(8,128)(2,1)S(1)}, bf16[64,3328]{1,0:T(8,128)(2,1)S(1)}, u32[]{:S(2)}, u32[]{:S(2)}) collective-permute-start(bf16[64,3328]{1,0:T(8,128)(2,1)S(1)} %get-tuple-element.380), channel_id=1, source_target_pairs={{0,1},{1,0},{2,3},{3,2},{4,5},{5,4},{6,7},{7,6},{8,9},{9,8},{10,11... | collective-permute-start | bytes 1277960 | tf_op jit(solution)/shard_map/ppermute | solution.py:13
  26.8 11.5 %collective-permute-start.11 = (bf16[64,3328]{1,0:T(8,128)(2,1)S(1)}, bf16[64,3328]{1,0:T(8,128)(2,1)S(1)}, u32[]{:S(2)}, u32[]{:S(2)}) collective-permute-start(bf16[64,3328]{1,0:T(8,128)(2,1)S(1)} %get-tuple-element.378), channel_id=1, source_target_pairs={{0,1},{1,0},{2,3},{3,2},{4,5},{5,4},{6,7},{7,6},{8,9},{9,8},{10,11... | collective-permute-start | bytes 1277960 | tf_op jit(solution)/shard_map/ppermute | solution.py:13
  36.7 10.4 %collective-permute-start.8 = (bf16[64,3328]{1,0:T(8,128)(2,1)S(1)}, bf16[64,3328]{1,0:T(8,128)(2,1)S(1)}, u32[]{:S(2)}, u32[]{:S(2)}) collective-permute-start(bf16[64,3328]{1,0:T(8,128)(2,1)S(1)} %get-tuple-element.384), channel_id=1, source_target_pairs={{0,1},{1,0},{2,3},{3,2},{4,5},{5,4},{6,7},{7,6},{8,9},{9,8},{10,11... | collective-permute-start | bytes 1277960 | tf_op jit(solution)/shard_map/ppermute | solution.py:13
  37.1 11.9 %collective-permute-start.6 = (bf16[64,3328]{1,0:T(8,128)(2,1)S(1)}, bf16[64,3328]{1,0:T(8,128)(2,1)S(1)}, u32[]{:S(2)}, u32[]{:S(2)}) collective-permute-start(bf16[64,3328]{1,0:T(8,128)(2,1)S(1)} %get-tuple-element.388), channel_id=1, source_target_pairs={{0,1},{1,0},{2,3},{3,2},{4,5},{5,4},{6,7},{7,6},{8,9},{9,8},{10,11... | collective-permute-start | bytes 1277960 | tf_op jit(solution)/shard_map/ppermute | solution.py:13
  37.5 11.4 %collective-permute-start.7 = (bf16[64,3328]{1,0:T(8,128)(2,1)S(1)}, bf16[64,3328]{1,0:T(8,128)(2,1)S(1)}, u32[]{:S(2)}, u32[]{:S(2)}) collective-permute-start(bf16[64,3328]{1,0:T(8,128)(2,1)S(1)} %get-tuple-element.386), channel_id=1, source_target_pairs={{0,1},{1,0},{2,3},{3,2},{4,5},{5,4},{6,7},{7,6},{8,9},{9,8},{10,11... | collective-permute-start | bytes 1277960 | tf_op jit(solution)/shard_map/ppermute | solution.py:13
  37.9 10.8 %collective-permute-start.9 = (bf16[64,3328]{1,0:T(8,128)(2,1)S(1)}, bf16[64,3328]{1,0:T(8,128)(2,1)S(1)}, u32[]{:S(2)}, u32[]{:S(2)}) collective-permute-start(bf16[64,3328]{1,0:T(8,128)(2,1)S(1)} %get-tuple-element.382), channel_id=1, source_target_pairs={{0,1},{1,0},{2,3},{3,2},{4,5},{5,4},{6,7},{7,6},{8,9},{9,8},{10,11... | collective-permute-start | bytes 1277960 | tf_op jit(solution)/shard_map/ppermute | solution.py:13
  38.6 20.6 %collective-permute-start.15 = (bf16[2,32,3328]{2,1,0:T(8,128)(2,1)S(1)}, bf16[2,32,3328]{2,1,0:T(8,128)(2,1)S(1)}, u32[]{:S(2)}, u32[]{:S(2)}) collective-permute-start(bf16[2,32,3328]{2,1,0:T(8,128)(2,1)S(1)} %pad_maximum_fusion.2), channel_id=1, source_target_pairs={{0,16},{8,24},{16,0},{24,8},{1,17},{9,25},{17,1},{25,9},{2,18},{10... | collective-permute-start | bytes 1277960 | tf_op jit(solution)/shard_map/ppermute | solution.py:13
  47.1 12.0 %collective-permute-start.5 = (bf16[2,32,3328]{2,1,0:T(8,128)(2,1)S(1)}, bf16[2,32,3328]{2,1,0:T(8,128)(2,1)S(1)}, u32[]{:S(2)}, u32[]{:S(2)}) collective-permute-start(bf16[2,32,3328]{2,1,0:T(8,128)(2,1)S(1)} %pad_maximum_fusion.1), channel_id=1, source_target_pairs={{0,8},{8,0},{16,24},{24,16},{1,9},{9,1},{17,25},{25,17},{2,10},{10... | collective-permute-start | bytes 1277960 | tf_op jit(solution)/shard_map/ppermute | solution.py:13
  55.9 13.6 %collective-permute-start.13 = (bf16[2,32,3328]{2,1,0:T(8,128)(2,1)S(1)}, bf16[2,32,3328]{2,1,0:T(8,128)(2,1)S(1)}, u32[]{:S(2)}, u32[]{:S(2)}) collective-permute-start(bf16[2,32,3328]{2,1,0:T(8,128)(2,1)S(1)} %pad_maximum_fusion.4), channel_id=1, source_target_pairs={{0,16},{8,24},{16,0},{24,8},{1,17},{9,25},{17,1},{25,9},{2,18},{10... | collective-permute-start | bytes 1277960 | tf_op jit(solution)/shard_map/ppermute | solution.py:13
  56.5 11.4 %collective-permute-start.14 = (bf16[2,32,3328]{2,1,0:T(8,128)(2,1)S(1)}, bf16[2,32,3328]{2,1,0:T(8,128)(2,1)S(1)}, u32[]{:S(2)}, u32[]{:S(2)}) collective-permute-start(bf16[2,32,3328]{2,1,0:T(8,128)(2,1)S(1)} %pad_maximum_fusion.3), channel_id=1, source_target_pairs={{0,8},{8,0},{16,24},{24,16},{1,9},{9,1},{17,25},{25,17},{2,10},{10... | collective-permute-start | bytes 1277960 | tf_op jit(solution)/shard_map/ppermute | solution.py:13
  57.0 19.5 %collective-permute-start.19 = (bf16[64,3328]{1,0:T(8,128)(2,1)S(1)}, bf16[64,3328]{1,0:T(8,128)(2,1)S(1)}, u32[]{:S(2)}, u32[]{:S(2)}) collective-permute-start(bf16[64,3328]{1,0:T(8,128)(2,1)S(1)} %get-tuple-element.356), channel_id=1, source_target_pairs={{0,1},{1,0},{2,3},{3,2},{4,5},{5,4},{6,7},{7,6},{8,9},{9,8},{10,11... | collective-permute-start | bytes 1277960 | tf_op jit(solution)/shard_map/ppermute | solution.py:13
  59.0 18.8 %collective-permute-start.20 = (bf16[64,3328]{1,0:T(8,128)(2,1)S(1)}, bf16[64,3328]{1,0:T(8,128)(2,1)S(1)}, u32[]{:S(2)}, u32[]{:S(2)}) collective-permute-start(bf16[64,3328]{1,0:T(8,128)(2,1)S(1)} %get-tuple-element.354), channel_id=1, source_target_pairs={{0,1},{1,0},{2,3},{3,2},{4,5},{5,4},{6,7},{7,6},{8,9},{9,8},{10,11... | collective-permute-start | bytes 1277960 | tf_op jit(solution)/shard_map/ppermute | solution.py:13
  59.2 16.4 %collective-permute-start.21 = (bf16[64,3328]{1,0:T(8,128)(2,1)S(1)}, bf16[64,3328]{1,0:T(8,128)(2,1)S(1)}, u32[]{:S(2)}, u32[]{:S(2)}) collective-permute-start(bf16[64,3328]{1,0:T(8,128)(2,1)S(1)} %get-tuple-element.352), channel_id=1, source_target_pairs={{0,1},{1,0},{2,3},{3,2},{4,5},{5,4},{6,7},{7,6},{8,9},{9,8},{10,11... | collective-permute-start | bytes 1277960 | tf_op jit(solution)/shard_map/ppermute | solution.py:13
  67.9 5.9 %collective-permute-start.16 = (bf16[2,16,3328]{2,1,0:T(8,128)(2,1)S(1)}, bf16[2,16,3328]{2,1,0:T(8,128)(2,1)S(1)}, u32[]{:S(2)}, u32[]{:S(2)}) collective-permute-start(bf16[2,16,3328]{2,1,0:T(8,128)(2,1)S(1)} %get-tuple-element.362), channel_id=1, source_target_pairs={{0,8},{8,0},{16,24},{24,16},{1,9},{9,1},{17,25},{25,17},{2,10},{10... | collective-permute-start | bytes 638984 | tf_op jit(solution)/shard_map/ppermute | solution.py:13
  69.5 5.9 %collective-permute-start.12 = (bf16[2,16,3328]{2,1,0:T(8,128)(2,1)S(1)}, bf16[2,16,3328]{2,1,0:T(8,128)(2,1)S(1)}, u32[]{:S(2)}, u32[]{:S(2)}) collective-permute-start(bf16[2,16,3328]{2,1,0:T(8,128)(2,1)S(1)} %get-tuple-element.375), channel_id=1, source_target_pairs={{0,16},{8,24},{16,0},{24,8},{1,17},{9,25},{17,1},{25,9},{2,18},{10... | collective-permute-start | bytes 638984 | tf_op jit(solution)/shard_map/ppermute | solution.py:13
  75.4 18.9 %collective-permute-start.28 = (bf16[64,3328]{1,0:T(8,128)(2,1)S(1)}, bf16[64,3328]{1,0:T(8,128)(2,1)S(1)}, u32[]{:S(2)}, u32[]{:S(2)}) collective-permute-start(bf16[64,3328]{1,0:T(8,128)(2,1)S(1)} %get-tuple-element.336), channel_id=1, source_target_pairs={{0,1},{1,0},{2,3},{3,2},{4,5},{5,4},{6,7},{7,6},{8,9},{9,8},{10,11... | collective-permute-start | bytes 1277960 | tf_op jit(solution)/shard_map/ppermute | solution.py:13
  75.6 22.3 %collective-permute-start.29 = (bf16[64,3328]{1,0:T(8,128)(2,1)S(1)}, bf16[64,3328]{1,0:T(8,128)(2,1)S(1)}, u32[]{:S(2)}, u32[]{:S(2)}) collective-permute-start(bf16[64,3328]{1,0:T(8,128)(2,1)S(1)} %get-tuple-element.334), channel_id=1, source_target_pairs={{0,1},{1,0},{2,3},{3,2},{4,5},{5,4},{6,7},{7,6},{8,9},{9,8},{10,11... | collective-permute-start | bytes 1277960 | tf_op jit(solution)/shard_map/ppermute | solution.py:13
  76.1 16.4 %collective-permute-start.30 = (bf16[64,3328]{1,0:T(8,128)(2,1)S(1)}, bf16[64,3328]{1,0:T(8,128)(2,1)S(1)}, u32[]{:S(2)}, u32[]{:S(2)}) collective-permute-start(bf16[64,3328]{1,0:T(8,128)(2,1)S(1)} %get-tuple-element.332), channel_id=1, source_target_pairs={{0,1},{1,0},{2,3},{3,2},{4,5},{5,4},{6,7},{7,6},{8,9},{9,8},{10,11... | collective-permute-start | bytes 1277960 | tf_op jit(solution)/shard_map/ppermute | solution.py:13
  76.5 7.7 %collective-permute-start.23 = (bf16[2,16,3328]{2,1,0:T(8,128)(2,1)S(1)}, bf16[2,16,3328]{2,1,0:T(8,128)(2,1)S(1)}, u32[]{:S(2)}, u32[]{:S(2)}) collective-permute-start(bf16[2,16,3328]{2,1,0:T(8,128)(2,1)S(1)} %get-tuple-element.348), channel_id=1, source_target_pairs={{0,8},{8,0},{16,24},{24,16},{1,9},{9,1},{17,25},{25,17},{2,10},{10... | collective-permute-start | bytes 638984 | tf_op jit(solution)/shard_map/ppermute | solution.py:13
  77.8 7.2 %collective-permute-start.18 = (bf16[2,16,3328]{2,1,0:T(8,128)(2,1)S(1)}, bf16[2,16,3328]{2,1,0:T(8,128)(2,1)S(1)}, u32[]{:S(2)}, u32[]{:S(2)}) collective-permute-start(bf16[2,16,3328]{2,1,0:T(8,128)(2,1)S(1)} %get-tuple-element.358), channel_id=1, source_target_pairs={{0,16},{8,24},{16,0},{24,8},{1,17},{9,25},{17,1},{25,9},{2,18},{10... | collective-permute-start | bytes 638984 | tf_op jit(solution)/shard_map/ppermute | solution.py:13
  84.2 9.6 %collective-permute-start.31 = (bf16[64,3328]{1,0:T(8,128)(2,1)S(1)}, bf16[64,3328]{1,0:T(8,128)(2,1)S(1)}, u32[]{:S(2)}, u32[]{:S(2)}) collective-permute-start(bf16[64,3328]{1,0:T(8,128)(2,1)S(1)} %get-tuple-element.330), channel_id=1, source_target_pairs={{0,1},{1,0},{2,3},{3,2},{4,5},{5,4},{6,7},{7,6},{8,9},{9,8},{10,11... | collective-permute-start | bytes 1277960 | tf_op jit(solution)/shard_map/ppermute | solution.py:13
  85.0 6.8 %collective-permute-start.17 = (bf16[2,2,8,3328]{3,2,1,0:T(8,128)(2,1)S(1)}, bf16[2,2,8,3328]{3,2,1,0:T(8,128)(2,1)S(1)}, u32[]{:S(2)}, u32[]{:S(2)}) collective-permute-start(bf16[2,2,8,3328]{3,2,1,0:T(8,128)(2,1)S(1)} %get-tuple-element.359), channel_id=1, source_target_pairs={{0,2},{1,3},{2,0},{3,1},{4,6},{5,7},{6,4},{7,5},{8,10},{9,11},{10,... | collective-permute-start | bytes 638984 | tf_op jit(solution)/shard_map/ppermute | solution.py:13
  91.8 15.6 %collective-permute-start.25 = (bf16[2,32,3328]{2,1,0:T(8,128)(2,1)S(1)}, bf16[2,32,3328]{2,1,0:T(8,128)(2,1)S(1)}, u32[]{:S(2)}, u32[]{:S(2)}) collective-permute-start(bf16[2,32,3328]{2,1,0:T(8,128)(2,1)S(1)} %pad_maximum_fusion.9), channel_id=1, source_target_pairs={{0,16},{8,24},{16,0},{24,8},{1,17},{9,25},{17,1},{25,9},{2,18},{10... | collective-permute-start | bytes 1277960 | tf_op jit(solution)/shard_map/ppermute | solution.py:13
  92.5 12.8 %collective-permute-start.26 = (bf16[2,32,3328]{2,1,0:T(8,128)(2,1)S(1)}, bf16[2,32,3328]{2,1,0:T(8,128)(2,1)S(1)}, u32[]{:S(2)}, u32[]{:S(2)}) collective-permute-start(bf16[2,32,3328]{2,1,0:T(8,128)(2,1)S(1)} %pad_maximum_fusion.8), channel_id=1, source_target_pairs={{0,8},{8,0},{16,24},{24,16},{1,9},{9,1},{17,25},{25,17},{2,10},{10... | collective-permute-start | bytes 1277960 | tf_op jit(solution)/shard_map/ppermute | solution.py:13
  93.7 7.9 %collective-permute-start.27 = (bf16[2,2,8,3328]{3,2,0,1:T(8,128)(2,1)S(1)}, bf16[2,2,8,3328]{3,2,0,1:T(8,128)(2,1)S(1)}, u32[]{:S(2)}, u32[]{:S(2)}) collective-permute-start(bf16[2,2,8,3328]{3,2,0,1:T(8,128)(2,1)S(1)} %get-tuple-element.338), channel_id=1, source_target_pairs={{0,2},{1,3},{2,0},{3,1},{4,6},{5,7},{6,4},{7,5},{8,10},{9,11},{10,... | collective-permute-start | bytes 638984 | tf_op jit(solution)/shard_map/ppermute | solution.py:13
  94.4 14.8 %collective-permute-start.24 = (bf16[2,2,4,3328]{3,2,1,0:T(4,128)(2,1)S(1)}, bf16[2,2,4,3328]{3,2,1,0:T(4,128)(2,1)S(1)}, u32[]{:S(2)}, u32[]{:S(2)}) collective-permute-start(bf16[2,2,4,3328]{3,2,1,0:T(4,128)(2,1)S(1)} %get-tuple-element.403), channel_id=1, source_target_pairs={{0,4},{1,5},{2,6},{3,7},{4,0},{5,1},{6,2},{7,3},{8,12},{9,13},{10,... | collective-permute-start | bytes 319496 | tf_op jit(solution)/shard_map/ppermute | solution.py:13
  97.8 16.3 %collective-permute-start.34 = (bf16[2,32,3328]{2,1,0:T(8,128)(2,1)S(1)}, bf16[2,32,3328]{2,1,0:T(8,128)(2,1)S(1)}, u32[]{:S(2)}, u32[]{:S(2)}) collective-permute-start(bf16[2,32,3328]{2,1,0:T(8,128)(2,1)S(1)} %pad_maximum_fusion.12), channel_id=1, source_target_pairs={{0,8},{8,0},{16,24},{24,16},{1,9},{9,1},{17,25},{25,17},{2,10},{10... | collective-permute-start | bytes 1277960 | tf_op jit(solution)/shard_map/ppermute | solution.py:13
  101.7 14.9 %collective-permute-start.33 = (bf16[2,32,3328]{2,1,0:T(8,128)(2,1)S(1)}, bf16[2,32,3328]{2,1,0:T(8,128)(2,1)S(1)}, u32[]{:S(2)}, u32[]{:S(2)}) collective-permute-start(bf16[2,32,3328]{2,1,0:T(8,128)(2,1)S(1)} %pad_maximum_fusion.13), channel_id=1, source_target_pairs={{0,16},{8,24},{16,0},{24,8},{1,17},{9,25},{17,1},{25,9},{2,18},{10... | collective-permute-start | bytes 1277960 | tf_op jit(solution)/shard_map/ppermute | solution.py:13
  105.3 7.5 %collective-permute-start.35 = (bf16[2,2,4,3328]{3,2,0,1:T(4,128)(2,1)S(1)}, bf16[2,2,4,3328]{3,2,0,1:T(4,128)(2,1)S(1)}, u32[]{:S(2)}, u32[]{:S(2)}) collective-permute-start(bf16[2,2,4,3328]{3,2,0,1:T(4,128)(2,1)S(1)} %get-tuple-element.402), channel_id=1, source_target_pairs={{0,4},{1,5},{2,6},{3,7},{4,0},{5,1},{6,2},{7,3},{8,12},{9,13},{10,... | collective-permute-start | bytes 319496 | tf_op jit(solution)/shard_map/ppermute | solution.py:13
  107.5 13.9 %collective-permute-start.39 = (bf16[2,16,3328]{2,1,0:T(8,128)(2,1)S(1)}, bf16[2,16,3328]{2,1,0:T(8,128)(2,1)S(1)}, u32[]{:S(2)}, u32[]{:S(2)}) collective-permute-start(bf16[2,16,3328]{2,1,0:T(8,128)(2,1)S(1)} %get-tuple-element.318), channel_id=1, source_target_pairs={{0,16},{8,24},{16,0},{24,8},{1,17},{9,25},{17,1},{25,9},{2,18},{10... | collective-permute-start | bytes 638984 | tf_op jit(solution)/shard_map/ppermute | solution.py:13
  109.2 10.8 %collective-permute-start.40 = (bf16[2,16,3328]{2,1,0:T(8,128)(2,1)S(1)}, bf16[2,16,3328]{2,1,0:T(8,128)(2,1)S(1)}, u32[]{:S(2)}, u32[]{:S(2)}) collective-permute-start(bf16[2,16,3328]{2,1,0:T(8,128)(2,1)S(1)} %get-tuple-element.316), channel_id=1, source_target_pairs={{0,8},{8,0},{16,24},{24,16},{1,9},{9,1},{17,25},{25,17},{2,10},{10... | collective-permute-start | bytes 638984 | tf_op jit(solution)/shard_map/ppermute | solution.py:13
  114.2 8.1 %collective-permute-start.38 = (bf16[2,4,3328]{2,1,0:T(4,128)(2,1)S(1)}, bf16[2,4,3328]{2,1,0:T(4,128)(2,1)S(1)}, u32[]{:S(2)}, u32[]{:S(2)}) collective-permute-start(bf16[2,4,3328]{2,1,0:T(4,128)(2,1)S(1)} %fusion.123), channel_id=1, source_target_pairs={{0,4},{1,5},{2,6},{3,7},{4,0},{5,1},{6,2},{7,3},{8,12},{9,13},{10,... | collective-permute-start | bytes 159752 | tf_op jit(solution)/shard_map/ppermute | solution.py:13
  116.6 8.8 %collective-permute-start.37 = (bf16[2,16,3328]{2,1,0:T(8,128)(2,1)S(1)}, bf16[2,16,3328]{2,1,0:T(8,128)(2,1)S(1)}, u32[]{:S(2)}, u32[]{:S(2)}) collective-permute-start(bf16[2,16,3328]{2,1,0:T(8,128)(2,1)S(1)} %get-tuple-element.320), channel_id=1, source_target_pairs={{0,16},{8,24},{16,0},{24,8},{1,17},{9,25},{17,1},{25,9},{2,18},{10... | collective-permute-start | bytes 638984 | tf_op jit(solution)/shard_map/ppermute | solution.py:13
  118.3 7.0 %collective-permute-start.41 = (bf16[2,16,3328]{2,1,0:T(8,128)(2,1)S(1)}, bf16[2,16,3328]{2,1,0:T(8,128)(2,1)S(1)}, u32[]{:S(2)}, u32[]{:S(2)}) collective-permute-start(bf16[2,16,3328]{2,1,0:T(8,128)(2,1)S(1)} %get-tuple-element.314), channel_id=1, source_target_pairs={{0,8},{8,0},{16,24},{24,16},{1,9},{9,1},{17,25},{25,17},{2,10},{10... | collective-permute-start | bytes 638984 | tf_op jit(solution)/shard_map/ppermute | solution.py:13
  119.9 7.0 %collective-permute-start.36 = (bf16[2,8,3328]{2,1,0:T(8,128)(2,1)S(1)}, bf16[2,8,3328]{2,1,0:T(8,128)(2,1)S(1)}, u32[]{:S(2)}, u32[]{:S(2)}) collective-permute-start(bf16[2,8,3328]{2,1,0:T(8,128)(2,1)S(1)} %pad_maximum_fusion.25), channel_id=1, source_target_pairs={{0,2},{1,3},{2,0},{3,1},{4,6},{5,7},{6,4},{7,5},{8,10},{9,11},{10,... | collective-permute-start | bytes 319496 | tf_op jit(solution)/shard_map/ppermute | solution.py:13
  121.5 8.6 %collective-permute-start.43 = (bf16[2,2,8,3328]{3,2,0,1:T(8,128)(2,1)S(1)}, bf16[2,2,8,3328]{3,2,0,1:T(8,128)(2,1)S(1)}, u32[]{:S(2)}, u32[]{:S(2)}) collective-permute-start(bf16[2,2,8,3328]{3,2,0,1:T(8,128)(2,1)S(1)} %get-tuple-element.312), channel_id=1, source_target_pairs={{0,2},{1,3},{2,0},{3,1},{4,6},{5,7},{6,4},{7,5},{8,10},{9,11},{10,... | collective-permute-start | bytes 638984 | tf_op jit(solution)/shard_map/ppermute | solution.py:13
  122.3 9.1 %collective-permute-start.46 = (bf16[2,8,3328]{2,1,0:T(8,128)(2,1)S(1)}, bf16[2,8,3328]{2,1,0:T(8,128)(2,1)S(1)}, u32[]{:S(2)}, u32[]{:S(2)}) collective-permute-start(bf16[2,8,3328]{2,1,0:T(8,128)(2,1)S(1)} %pad_maximum_fusion.26), channel_id=1, source_target_pairs={{0,2},{1,3},{2,0},{3,1},{4,6},{5,7},{6,4},{7,5},{8,10},{9,11},{10,... | collective-permute-start | bytes 319496 | tf_op jit(solution)/shard_map/ppermute | solution.py:13
  125.5 9.7 %collective-permute-start.45 = (bf16[2,2,8,3328]{3,2,0,1:T(8,128)(2,1)S(1)}, bf16[2,2,8,3328]{3,2,0,1:T(8,128)(2,1)S(1)}, u32[]{:S(2)}, u32[]{:S(2)}) collective-permute-start(bf16[2,2,8,3328]{3,2,0,1:T(8,128)(2,1)S(1)} %get-tuple-element.310), channel_id=1, source_target_pairs={{0,2},{1,3},{2,0},{3,1},{4,6},{5,7},{6,4},{7,5},{8,10},{9,11},{10,... | collective-permute-start | bytes 638984 | tf_op jit(solution)/shard_map/ppermute | solution.py:13
  127.0 11.3 %collective-permute-start.50 = (bf16[16,3328]{1,0:T(8,128)(2,1)S(1)}, bf16[16,3328]{1,0:T(8,128)(2,1)S(1)}, u32[]{:S(2)}, u32[]{:S(2)}) collective-permute-start(bf16[16,3328]{1,0:T(8,128)(2,1)S(1)} %get-tuple-element.253), channel_id=1, source_target_pairs={{0,8},{8,0},{16,24},{24,16},{1,9},{9,1},{17,25},{25,17},{2,10},{10... | collective-permute-start | bytes 319496 | tf_op jit(solution)/shard_map/ppermute | solution.py:13
  130.3 7.9 %collective-permute-start.44 = (bf16[2,2,4,3328]{3,2,0,1:T(4,128)(2,1)S(1)}, bf16[2,2,4,3328]{3,2,0,1:T(4,128)(2,1)S(1)}, u32[]{:S(2)}, u32[]{:S(2)}) collective-permute-start(bf16[2,2,4,3328]{3,2,0,1:T(4,128)(2,1)S(1)} %get-tuple-element.399), channel_id=1, source_target_pairs={{0,4},{1,5},{2,6},{3,7},{4,0},{5,1},{6,2},{7,3},{8,12},{9,13},{10,... | collective-permute-start | bytes 319496 | tf_op jit(solution)/shard_map/ppermute | solution.py:13
  131.5 16.2 %collective-permute-start.53 = (bf16[16,3328]{1,0:T(8,128)(2,1)S(1)}, bf16[16,3328]{1,0:T(8,128)(2,1)S(1)}, u32[]{:S(2)}, u32[]{:S(2)}) collective-permute-start(bf16[16,3328]{1,0:T(8,128)(2,1)S(1)} %get-tuple-element.259), channel_id=1, source_target_pairs={{0,8},{8,0},{16,24},{24,16},{1,9},{9,1},{17,25},{25,17},{2,10},{10... | collective-permute-start | bytes 319496 | tf_op jit(solution)/shard_map/ppermute | solution.py:13
  133.0 8.3 %collective-permute-start.42 = (bf16[16,3328]{1,0:T(8,128)(2,1)S(1)}, bf16[16,3328]{1,0:T(8,128)(2,1)S(1)}, u32[]{:S(2)}, u32[]{:S(2)}) collective-permute-start(bf16[16,3328]{1,0:T(8,128)(2,1)S(1)} %get-tuple-element.251), channel_id=1, source_target_pairs={{0,16},{8,24},{16,0},{24,8},{1,17},{9,25},{17,1},{25,9},{2,18},{10... | collective-permute-start | bytes 319496 | tf_op jit(solution)/shard_map/ppermute | solution.py:13
  135.1 14.6 %collective-permute-start.60 = (bf16[16,3328]{1,0:T(8,128)(2,1)S(1)}, bf16[16,3328]{1,0:T(8,128)(2,1)S(1)}, u32[]{:S(2)}, u32[]{:S(2)}) collective-permute-start(bf16[16,3328]{1,0:T(8,128)(2,1)S(1)} %get-tuple-element.279), channel_id=1, source_target_pairs={{0,16},{8,24},{16,0},{24,8},{1,17},{9,25},{17,1},{25,9},{2,18},{10... | collective-permute-start | bytes 319496 | tf_op jit(solution)/shard_map/ppermute | solution.py:13
  138.2 8.5 %collective-permute-start.49 = (bf16[2,2,4,3328]{3,2,0,1:T(4,128)(2,1)S(1)}, bf16[2,2,4,3328]{3,2,0,1:T(4,128)(2,1)S(1)}, u32[]{:S(2)}, u32[]{:S(2)}) collective-permute-start(bf16[2,2,4,3328]{3,2,0,1:T(4,128)(2,1)S(1)} %get-tuple-element.398), channel_id=1, source_target_pairs={{0,4},{1,5},{2,6},{3,7},{4,0},{5,1},{6,2},{7,3},{8,12},{9,13},{10,... | collective-permute-start | bytes 319496 | tf_op jit(solution)/shard_map/ppermute | solution.py:13
  138.3 9.2 %collective-permute-start.48 = (bf16[2,4,3328]{2,1,0:T(4,128)(2,1)S(1)}, bf16[2,4,3328]{2,1,0:T(4,128)(2,1)S(1)}, u32[]{:S(2)}, u32[]{:S(2)}) collective-permute-start(bf16[2,4,3328]{2,1,0:T(4,128)(2,1)S(1)} %fusion.122), channel_id=1, source_target_pairs={{0,4},{1,5},{2,6},{3,7},{4,0},{5,1},{6,2},{7,3},{8,12},{9,13},{10,... | collective-permute-start | bytes 159752 | tf_op jit(solution)/shard_map/ppermute | solution.py:13
  141.4 13.1 %collective-permute-start.56 = (bf16[32,3328]{1,0:T(8,128)(2,1)S(1)}, bf16[32,3328]{1,0:T(8,128)(2,1)S(1)}, u32[]{:S(2)}, u32[]{:S(2)}) collective-permute-start(bf16[32,3328]{1,0:T(8,128)(2,1)S(1)} %constant_dynamic-update-slice_fusion.6), channel_id=1, source_target_pairs={{0,16},{8,24},{16,0},{24,8},{1,17},{9,25},{17,1},{25,9},{2,18},{10... | collective-permute-start | bytes 638984 | tf_op jit(solution)/shard_map/ppermute | solution.py:13
  146.7 8.8 %collective-permute-start.47 = (bf16[32,3328]{1,0:T(8,128)(2,1)S(1)}, bf16[32,3328]{1,0:T(8,128)(2,1)S(1)}, u32[]{:S(2)}, u32[]{:S(2)}) collective-permute-start(bf16[32,3328]{1,0:T(8,128)(2,1)S(1)} %constant_dynamic-update-slice_fusion.4), channel_id=1, source_target_pairs={{0,8},{8,0},{16,24},{24,16},{1,9},{9,1},{17,25},{25,17},{2,10},{10... | collective-permute-start | bytes 638984 | tf_op jit(solution)/shard_map/ppermute | solution.py:13
  147.7 6.4 %collective-permute-start.51 = (bf16[2,8,3328]{2,1,0:T(8,128)(2,1)S(1)}, bf16[2,8,3328]{2,1,0:T(8,128)(2,1)S(1)}, u32[]{:S(2)}, u32[]{:S(2)}) collective-permute-start(bf16[2,8,3328]{2,1,0:T(8,128)(2,1)S(1)} %pad_maximum_fusion.27), channel_id=1, source_target_pairs={{0,2},{1,3},{2,0},{3,1},{4,6},{5,7},{6,4},{7,5},{8,10},{9,11},{10,... | collective-permute-start | bytes 319496 | tf_op jit(solution)/shard_map/ppermute | solution.py:13
  149.7 10.6 %collective-permute-start.58 = (bf16[32,3328]{1,0:T(8,128)(2,1)S(1)}, bf16[32,3328]{1,0:T(8,128)(2,1)S(1)}, u32[]{:S(2)}, u32[]{:S(2)}) collective-permute-start(bf16[32,3328]{1,0:T(8,128)(2,1)S(1)} %constant_dynamic-update-slice_fusion.8), channel_id=1, source_target_pairs={{0,16},{8,24},{16,0},{24,8},{1,17},{9,25},{17,1},{25,9},{2,18},{10... | collective-permute-start | bytes 638984 | tf_op jit(solution)/shard_map/ppermute | solution.py:13
  152.7 8.9 %collective-permute-start.61 = (bf16[32,3328]{1,0:T(8,128)(2,1)S(1)}, bf16[32,3328]{1,0:T(8,128)(2,1)S(1)}, u32[]{:S(2)}, u32[]{:S(2)}) collective-permute-start(bf16[32,3328]{1,0:T(8,128)(2,1)S(1)} %constant_dynamic-update-slice_fusion.24), channel_id=1, source_target_pairs={{0,8},{8,0},{16,24},{24,16},{1,9},{9,1},{17,25},{25,17},{2,10},{10... | collective-permute-start | bytes 638984 | tf_op jit(solution)/shard_map/ppermute | solution.py:13
  155.5 14.8 %collective-permute-start.64 = (bf16[64,3328]{1,0:T(8,128)(2,1)S(1)}, bf16[64,3328]{1,0:T(8,128)(2,1)S(1)}, u32[]{:S(2)}, u32[]{:S(2)}) collective-permute-start(bf16[64,3328]{1,0:T(8,128)(2,1)S(1)} %constant_dynamic-update-slice_fusion.14), channel_id=1, source_target_pairs={{0,1},{1,0},{2,3},{3,2},{4,5},{5,4},{6,7},{7,6},{8,9},{9,8},{10,11... | collective-permute-start | bytes 1277960 | tf_op jit(solution)/shard_map/ppermute | solution.py:13
  158.9 8.8 %collective-permute-start.54 = (bf16[64,3328]{1,0:T(8,128)(2,1)S(1)}, bf16[64,3328]{1,0:T(8,128)(2,1)S(1)}, u32[]{:S(2)}, u32[]{:S(2)}) collective-permute-start(bf16[64,3328]{1,0:T(8,128)(2,1)S(1)} %constant_dynamic-update-slice_fusion.12), channel_id=1, source_target_pairs={{0,1},{1,0},{2,3},{3,2},{4,5},{5,4},{6,7},{7,6},{8,9},{9,8},{10,11... | collective-permute-start | bytes 1277960 | tf_op jit(solution)/shard_map/ppermute | solution.py:13
  159.7 5.8 %collective-permute-start.65 = (bf16[16,3328]{1,0:T(8,128)(2,1)S(1)}, bf16[16,3328]{1,0:T(8,128)(2,1)S(1)}, u32[]{:S(2)}, u32[]{:S(2)}) collective-permute-start(bf16[16,3328]{1,0:T(8,128)(2,1)S(1)} %get-tuple-element.289), channel_id=1, source_target_pairs={{0,16},{8,24},{16,0},{24,8},{1,17},{9,25},{17,1},{25,9},{2,18},{10... | collective-permute-start | bytes 319496 | tf_op jit(solution)/shard_map/ppermute | solution.py:13
  161.6 6.0 %collective-permute-start.70 = (bf16[16,3328]{1,0:T(8,128)(2,1)S(1)}, bf16[16,3328]{1,0:T(8,128)(2,1)S(1)}, u32[]{:S(2)}, u32[]{:S(2)}) collective-permute-start(bf16[16,3328]{1,0:T(8,128)(2,1)S(1)} %get-tuple-element.299), channel_id=1, source_target_pairs={{0,16},{8,24},{16,0},{24,8},{1,17},{9,25},{17,1},{25,9},{2,18},{10... | collective-permute-start | bytes 319496 | tf_op jit(solution)/shard_map/ppermute | solution.py:13
  165.5 7.2 %collective-permute-start.63 = (bf16[32,3328]{1,0:T(8,128)(2,1)S(1)}, bf16[32,3328]{1,0:T(8,128)(2,1)S(1)}, u32[]{:S(2)}, u32[]{:S(2)}) collective-permute-start(bf16[32,3328]{1,0:T(8,128)(2,1)S(1)} %constant_dynamic-update-slice_fusion.18), channel_id=1, source_target_pairs={{0,16},{8,24},{16,0},{24,8},{1,17},{9,25},{17,1},{25,9},{2,18},{10... | collective-permute-start | bytes 638984 | tf_op jit(solution)/shard_map/ppermute | solution.py:13
  165.7 11.8 %collective-permute-start.69 = (bf16[64,3328]{1,0:T(8,128)(2,1)S(1)}, bf16[64,3328]{1,0:T(8,128)(2,1)S(1)}, u32[]{:S(2)}, u32[]{:S(2)}) collective-permute-start(bf16[64,3328]{1,0:T(8,128)(2,1)S(1)} %constant_dynamic-update-slice_fusion.20), channel_id=1, source_target_pairs={{0,1},{1,0},{2,3},{3,2},{4,5},{5,4},{6,7},{7,6},{8,9},{9,8},{10,11... | collective-permute-start | bytes 1277960 | tf_op jit(solution)/shard_map/ppermute | solution.py:13
  167.6 7.9 %collective-permute-start.62 = (bf16[64,3328]{1,0:T(8,128)(2,1)S(1)}, bf16[64,3328]{1,0:T(8,128)(2,1)S(1)}, u32[]{:S(2)}, u32[]{:S(2)}) collective-permute-start(bf16[64,3328]{1,0:T(8,128)(2,1)S(1)} %constant_dynamic-update-slice_fusion.26), channel_id=1, source_target_pairs={{0,1},{1,0},{2,3},{3,2},{4,5},{5,4},{6,7},{7,6},{8,9},{9,8},{10,11... | collective-permute-start | bytes 1277960 | tf_op jit(solution)/shard_map/ppermute | solution.py:13
  167.6 7.8 %collective-permute-start.66 = (bf16[32,3328]{1,0:T(8,128)(2,1)S(1)}, bf16[32,3328]{1,0:T(8,128)(2,1)S(1)}, u32[]{:S(2)}, u32[]{:S(2)}) collective-permute-start(bf16[32,3328]{1,0:T(8,128)(2,1)S(1)} %constant_dynamic-update-slice_fusion.30), channel_id=1, source_target_pairs={{0,8},{8,0},{16,24},{24,16},{1,9},{9,1},{17,25},{25,17},{2,10},{10... | collective-permute-start | bytes 638984 | tf_op jit(solution)/shard_map/ppermute | solution.py:13
  170.3 8.5 %collective-permute-start.68 = (bf16[32,3328]{1,0:T(8,128)(2,1)S(1)}, bf16[32,3328]{1,0:T(8,128)(2,1)S(1)}, u32[]{:S(2)}, u32[]{:S(2)}) collective-permute-start(bf16[32,3328]{1,0:T(8,128)(2,1)S(1)} %constant_dynamic-update-slice_fusion.22), channel_id=1, source_target_pairs={{0,16},{8,24},{16,0},{24,8},{1,17},{9,25},{17,1},{25,9},{2,18},{10... | collective-permute-start | bytes 638984 | tf_op jit(solution)/shard_map/ppermute | solution.py:13
  172.7 7.3 %collective-permute-start.71 = (bf16[32,3328]{1,0:T(8,128)(2,1)S(1)}, bf16[32,3328]{1,0:T(8,128)(2,1)S(1)}, u32[]{:S(2)}, u32[]{:S(2)}) collective-permute-start(bf16[32,3328]{1,0:T(8,128)(2,1)S(1)} %constant_dynamic-update-slice_fusion.36), channel_id=1, source_target_pairs={{0,8},{8,0},{16,24},{24,16},{1,9},{9,1},{17,25},{25,17},{2,10},{10... | collective-permute-start | bytes 638984 | tf_op jit(solution)/shard_map/ppermute | solution.py:13
  175.4 5.9 %collective-permute-start.73 = (bf16[64,3328]{1,0:T(8,128)(2,1)S(1)}, bf16[64,3328]{1,0:T(8,128)(2,1)S(1)}, u32[]{:S(2)}, u32[]{:S(2)}) collective-permute-start(bf16[64,3328]{1,0:T(8,128)(2,1)S(1)} %constant_dynamic-update-slice_fusion.28), channel_id=1, source_target_pairs={{0,1},{1,0},{2,3},{3,2},{4,5},{5,4},{6,7},{7,6},{8,9},{9,8},{10,11... | collective-permute-start | bytes 1277960 | tf_op jit(solution)/shard_map/ppermute | solution.py:13
  (22 other events, 584.4 us)

commit v2 on v1

v2 whole, which is shorter than its diff:
```python
import functools

import jax
import jax.numpy as jnp
import numpy as np
from jax import lax
from jax.sharding import PartitionSpec as P

SHARES = (4, 4, 4, 4)
ORDER = (1, 3, 1, 0, 3, 1, 2, 3, 0, 1, 2, 3, 1, 3, 1, 0, 3, 1, 2, 3, 0, 1, 2, 3, 0, 1, 2, 0, 3, 2, 0, 1, 2, 0, 3, 2, 0, 2, 1, 0, 3, 2, 0, 2)


def step_order(chunks, steps):
    if len(ORDER) == chunks * steps:
        return ORDER
    return [c for t in range(steps + 2 * chunks) for c in range(chunks) if 0 <= t - 2 * c < steps]


def gate_up(x, gate_weight, up_weight, start, width):
    half = x.shape[0] // 2
    parts = [
        jnp.dot(
            x, lax.slice_in_dim(weight, start, start + width, axis=1),
            preferred_element_type=jnp.float32,
        ).astype(jnp.bfloat16)
        for weight in (gate_weight, up_weight)
    ]
    return [p[:half] for p in parts], [p[half:] for p in parts]


def down(own, other, down_weight, before, start):
    hidden = jnp.concatenate([own, other], 0)
    weight = lax.slice_in_dim(down_weight, start, start + own.shape[1], axis=1)
    return before + lax.dot_general(
        hidden, weight, (((1,), (1,)), ((), ())), preferred_element_type=jnp.float32
    )


def add_halves(keep, received, axis):
    half = keep.shape[axis] // 2
    sides = []
    for k in range(2):
        kept = lax.slice_in_dim(keep, k * half, (k + 1) * half, axis=axis).astype(jnp.float32)
        came = lax.slice_in_dim(received, k * half, (k + 1) * half, axis=axis).astype(jnp.float32)
        sides.append((kept + came).astype(jnp.bfloat16))
    return sides


def on_device(n_row, n_col, tokens, gate_weight, up_weight, down_weight):
    batches, local_tokens, local_features = tokens.shape
    own_tokens = batches * local_tokens
    all_tokens = own_tokens * n_col
    features, units = gate_weight.shape
    per_device = own_tokens // n_row
    row, col = lax.axis_index("row"), lax.axis_index("col")
    core = 1
    col_bits = [1 << k for k in range(1, n_col.bit_length() - 1)]
    row_bits = [n_col << k for k in range(n_row.bit_length() - 1)]
    orders = (row_bits + col_bits, row_bits[::-1] + col_bits[::-1])
    stages = list(zip(*orders))

    def swap(value, bits):
        pairs = [(d, d ^ bits[d & core]) for d in range(n_row * n_col)]
        return lax.ppermute(value, ("row", "col"), pairs)

    x = tokens.reshape(own_tokens, local_features)
    for bit in col_bits[::-1] + [core]:
        half = x.shape[1] // 2
        low, high = x[:, :half], x[:, half:]
        mine = (col & bit) != 0
        keep, send = jnp.where(mine, high, low), jnp.where(mine, low, high)
        x = jnp.concatenate([keep, swap(send, (bit, bit))], 0)

    weight = {bit: all_tokens >> (k + 1) for k, bit in enumerate([core] + col_bits)}
    weight.update({bit: bit // n_col * per_device for bit in row_bits})

    def half_source(order):
        rows = np.zeros(1, np.int32)
        for bit in order:
            rows = (rows[:, None] + np.array([0, weight[bit]])).reshape(-1)
        return (rows[:, None] + np.arange(per_device)).reshape(-1)

    own_first = [
        np.concatenate([half_source(orders[k]), weight[core] + half_source(orders[1 - k])])
        for k in range(2)
    ]
    source = jnp.where((col & core) == 0, *(jnp.asarray(s, jnp.int32) for s in own_first))
    source = source ^ (row * per_device)
    pick = source[:, None] == lax.broadcasted_iota(jnp.int32, (all_tokens, all_tokens), 1)
    x = jnp.dot(pick.astype(jnp.bfloat16), x, preferred_element_type=jnp.float32).astype(jnp.bfloat16)

    total = [jnp.zeros((all_tokens, features), jnp.float32)]
    last = [x]

    def after(*values):
        return lax.optimization_barrier((values, last[0]))[0]

    def steps(start, width):
        (x_now,) = after(x)
        keep, send = gate_up(x_now, gate_weight, up_weight, start, width)
        last[0] = send
        received = [swap(part, (core, core)) for part in send]
        yield
        keep, received = after(keep, received)
        halves = [add_halves(k, r, 0) for k, r in zip(keep, received)]
        keep, send = (jnp.stack(side) for side in zip(*halves))
        for n, bits in enumerate(stages):
            if n > 0:
                keep, send = add_halves(*after(keep, received), 1)
            last[0] = send
            received = swap(send, bits)
            yield
        keep, received = after(keep, received)
        both = keep.astype(jnp.float32) + received.astype(jnp.float32)
        hidden = (jax.nn.silu(both[0]) * both[1]).astype(jnp.bfloat16)
        for bits in stages[::-1]:
            last[0] = hidden
            received = swap(hidden, bits)
            yield
            hidden = jnp.concatenate(after(hidden, received), 0)
        last[0] = hidden
        other = swap(hidden, (core, core))
        yield
        own, other = after(hidden, other)
        total[0] = last[0] = down(own, other, down_weight, total[0], start)

    share = units // sum(SHARES)
    ends = np.cumsum(SHARES) * share
    running = [steps(int(end) - n * share, n * share) for n, end in zip(SHARES, ends)]
    for chunk in step_order(len(SHARES), 3 + 2 * len(stages)):
        next(running[chunk], None)

    out = lax.dot_general(
        pick.astype(jnp.float32), total[0], (((0,), (0,)), ((), ())),
        precision=lax.Precision.HIGHEST, preferred_element_type=jnp.float32,
    ).astype(jnp.bfloat16)

    for bit in [core] + col_bits:
        half = out.shape[0] // 2
        keep, came = out[:half], swap(out[half:], (bit, bit))
        mine = (col & bit) != 0
        out = jnp.concatenate([jnp.where(mine, came, keep), jnp.where(mine, keep, came)], 1)
    return out.reshape(batches, local_tokens, local_features)


def solution(mesh):
    in_specs = (
        P(None, "col", "row"),
        P(("row", "col"), None),
        P(("row", "col"), None),
        P(("row", "col"), None),
    )
    out_specs = P(None, "col", "row")
    body = functools.partial(on_device, mesh.shape["row"], mesh.shape["col"])
    return jax.shard_map(body, mesh=mesh, in_specs=in_specs, out_specs=out_specs, check_vma=False)
```

time: 198 us -> 171 us (0.86)
  starting transfers between devices: 69 us -> 37.9 us
  waiting for transfers between devices: 74.2 us -> 79.6 us
    ppermute x78 -> x50, starting transfers between devices: 69 us -> 37.9 us  [swap(): return lax.ppermute(value, ('row', 'col'), pairs)]
    ppermute x78 -> x50, waiting for transfers between devices: 74.2 us -> 79.6 us  [swap(): return lax.ppermute(value, ('row', 'col'), pairs)]
    dot_general x16 -> x8, matrix products: 33.4 us -> 32.5 us  [gate_up(): jnp.dot(x, lax.slice_in_dim(weight, start, start + width, axis=1), prefer...]
    dot_general x8 -> x4, matrix products: 10.3 us -> 10.7 us  [down(): lax.dot_general(hidden, weight, (((1,), (1,)), ((), ())), preferred_eleme...]
  transfers between devices with their start and end apart: 78 -> 50, of which waited for: 29 -> 27; matrix products, arithmetic and copies ran while one was open for 19% -> 23% of each run, Pallas kernels for 0% -> 0%
where the time goes in v2:
time: 171 us
  waiting for transfers between devices  79.6 us (47%)
  matrix products  43.9 us (26%)
  starting transfers between devices  37.9 us (22%)
  other arithmetic  7.09 us (4%)
    ppermute x50, waiting for transfers between devices, swap(): return lax.ppermute(value, ('row', 'col'), pairs)  79.6 us
    ppermute x50, starting transfers between devices, swap(): return lax.ppermute(value, ('row', 'col'), pairs)  37.9 us
    dot_general x8, matrix products, gate_up(): jnp.dot(x, lax.slice_in_dim(weight, start, start + width, axis=1), prefer...  32.5 us
    dot_general x4, matrix products, down(): lax.dot_general(hidden, weight, (((1,), (1,)), ((), ())), preferred_eleme...  10.7 us
  transfers between devices with their start and end apart: 50, of which 27 were waited for; matrix products, arithmetic and copies ran while one was open for 23% of the time, Pallas kernels for 0%

profile of v2, /device:TPU:0, one launch (start us, length us, event | category | flops | bytes accessed | tf_op | source)
XLA Modules:
  0.0 170.7 jit_solution(16178415267028062288)
XLA Ops:
  0.0 0.9 broadcast_select_fusion.11
  0.9 4.1 %collective-permute-start = (bf16[16,2048]{1,0:T(8,128)(2,1)S(1)}, bf16[16,2048]{1,0:T(8,128)(2,1)S(1)}, u32[]{:S(2)}, u32[]{:S(2)}) collective-permute-start(bf16[16,2048]{1,0:T(8,128)(2,1)S(1)} %get-tuple-element.256), channel_id=1, source_target_pairs={{0,4},{1,5},{2,6},{3,7},{4,0},{5,1},{6,2},{7,3},{8,12},{9,13},{10,... | collective-permute-start | bytes 196616 | tf_op jit(solution)/shard_map/ppermute | solution.py:64
  5.0 3.6 %collective-permute-done = bf16[16,2048]{1,0:T(8,128)(2,1)S(1)} collective-permute-done((bf16[16,2048]{1,0:T(8,128)(2,1)S(1)}, bf16[16,2048]{1,0:T(8,128)(2,1)S(1)}, u32[]{:S(2)}, u32[]{:S(2)}) %collective-permute-start) | collective-permute-done | bytes 65568 | tf_op jit(solution)/shard_map/ppermute | solution.py:64
  8.7 0.6 collective-permute-start.1
  9.3 3.7 %collective-permute-done.1 = bf16[32,1024]{1,0:T(8,128)(2,1)S(1)} collective-permute-done((bf16[32,1024]{1,0:T(8,128)(2,1)S(1)}, bf16[32,1024]{1,0:T(8,128)(2,1)S(1)}, u32[]{:S(2)}, u32[]{:S(2)}) %collective-permute-start.1) | collective-permute-done | bytes 65568 | tf_op jit(solution)/shard_map/ppermute | solution.py:64
  13.1 0.7 fusion.76
  13.8 0.6 collective-permute-done.2
  14.6 4.0 %convolution_convert_fusion.7 = bf16[128,6656]{1,0:T(8,128)(2,1)S(1)} fusion(bf16[128,512]{1,0:T(8,128)(2,1)S(1)} %convolution_convert_fusion.9, bf16[512,26624]{1,0:T(8,128)(2,1)} %param.7), kind=kOutput, calls=%fused_computation.7 | convolution fusion | flops 873267200 | bytes 8650752 | tf_op jit(solution)/shard_map/dot_general | solution.py:22
  18.7 4.0 %convolution_convert_fusion.6 = bf16[128,6656]{1,0:T(8,128)(2,1)S(1)} fusion(bf16[128,512]{1,0:T(8,128)(2,1)S(1)} %convolution_convert_fusion.9, bf16[512,26624]{1,0:T(8,128)(2,1)} %param.8), kind=kOutput, calls=%fused_computation.6 | convolution fusion | flops 873267200 | bytes 8650752 | tf_op jit(solution)/shard_map/dot_general | solution.py:22
  23.5 4.0 %convolution_convert_fusion.5 = bf16[128,6656]{1,0:T(8,128)(2,1)S(1)} fusion(bf16[128,512]{1,0:T(8,128)(2,1)S(1)} %convolution_convert_fusion.9, bf16[512,26624]{1,0:T(8,128)(2,1)} %param.7), kind=kOutput, calls=%fused_computation.5 | convolution fusion | flops 873267200 | bytes 8650752 | tf_op jit(solution)/shard_map/dot_general | solution.py:22
  27.5 4.0 %convolution_convert_fusion.4 = bf16[128,6656]{1,0:T(8,128)(2,1)S(1)} fusion(bf16[128,512]{1,0:T(8,128)(2,1)S(1)} %convolution_convert_fusion.9, bf16[512,26624]{1,0:T(8,128)(2,1)} %param.8), kind=kOutput, calls=%fused_computation.4 | convolution fusion | flops 873267200 | bytes 8650752 | tf_op jit(solution)/shard_map/dot_general | solution.py:22
  33.0 1.8 %collective-permute-start.5 = (bf16[2,32,6656]{2,1,0:T(8,128)(2,1)S(1)}, bf16[2,32,6656]{2,1,0:T(8,128)(2,1)S(1)}, u32[]{:S(2)}, u32[]{:S(2)}) collective-permute-start(bf16[2,32,6656]{2,1,0:T(8,128)(2,1)S(1)} %pad_maximum_fusion.1), channel_id=1, source_target_pairs={{0,8},{1,17},{2,10},{3,19},{4,12},{5,21},{6,14},{7,23},{8,0},{9,25... | collective-permute-start | bytes 2555912 | tf_op jit(solution)/shard_map/ppermute | solution.py:64
  34.7 4.0 %convolution_convert_fusion.3 = bf16[128,6656]{1,0:T(8,128)(2,1)S(1)} fusion(bf16[128,512]{1,0:T(8,128)(2,1)S(1)} %convolution_convert_fusion.9, bf16[512,26624]{1,0:T(8,128)(2,1)} %param.7), kind=kOutput, calls=%fused_computation.3 | convolution fusion | flops 873267200 | bytes 8650752 | tf_op jit(solution)/shard_map/dot_general | solution.py:22
  38.8 4.0 %convolution_convert_fusion.2 = bf16[128,6656]{1,0:T(8,128)(2,1)S(1)} fusion(bf16[128,512]{1,0:T(8,128)(2,1)S(1)} %convolution_convert_fusion.9, bf16[512,26624]{1,0:T(8,128)(2,1)} %param.8), kind=kOutput, calls=%fused_computation.2 | convolution fusion | flops 873267200 | bytes 8650752 | tf_op jit(solution)/shard_map/dot_general | solution.py:22
  43.1 0.6 collective-permute-start.10
  44.2 1.0 collective-permute-start.11
  45.9 1.8 %collective-permute-start.8 = (bf16[2,16,6656]{2,1,0:T(8,128)(2,1)S(1)}, bf16[2,16,6656]{2,1,0:T(8,128)(2,1)S(1)}, u32[]{:S(2)}, u32[]{:S(2)}) collective-permute-start(bf16[2,16,6656]{2,1,0:T(8,128)(2,1)S(1)} %get-tuple-element.215), channel_id=1, source_target_pairs={{0,16},{1,9},{2,18},{3,11},{4,20},{5,13},{6,22},{7,15},{8,24},{9,1... | collective-permute-start | bytes 1277960 | tf_op jit(solution)/shard_map/ppermute | solution.py:64
  47.7 4.1 %convolution_convert_fusion.1 = bf16[128,6656]{1,0:T(8,128)(2,1)S(1)} fusion(bf16[128,512]{1,0:T(8,128)(2,1)S(1)} %convolution_convert_fusion.9, bf16[512,26624]{1,0:T(8,128)(2,1)} %param.7), kind=kOutput, calls=%fused_computation.1 | convolution fusion | flops 873267200 | bytes 8650752 | tf_op jit(solution)/shard_map/dot_general | solution.py:22
  51.8 4.2 %convolution_convert_fusion = bf16[128,6656]{1,0:T(8,128)(2,1)S(1)} fusion(bf16[128,512]{1,0:T(8,128)(2,1)S(1)} %convolution_convert_fusion.9, bf16[512,26624]{1,0:T(8,128)(2,1)} %param.8), kind=kOutput, calls=%fused_computation | convolution fusion | flops 873267200 | bytes 8650752 | tf_op jit(solution)/shard_map/dot_general | solution.py:22
  56.3 5.2 %collective-permute-done.11 = bf16[2,32,6656]{2,1,0:T(8,128)(2,1)S(1)} collective-permute-done((bf16[2,32,6656]{2,1,0:T(8,128)(2,1)S(1)}, bf16[2,32,6656]{2,1,0:T(8,128)(2,1)S(1)}, u32[]{:S(2)}, u32[]{:S(2)}) %collective-permute-start.11) | collective-permute-done | bytes 852000 | tf_op jit(solution)/shard_map/ppermute | solution.py:64
  61.7 1.6 collective-permute-start.13
  64.0 0.6 collective-permute-start.20
  64.8 0.4 collective-permute-start.12
  65.7 1.6 collective-permute-start.24
  67.3 6.3 %collective-permute-done.13 = bf16[2,16,6656]{2,1,0:T(8,128)(2,1)S(1)} collective-permute-done((bf16[2,16,6656]{2,1,0:T(8,128)(2,1)S(1)}, bf16[2,16,6656]{2,1,0:T(8,128)(2,1)S(1)}, u32[]{:S(2)}, u32[]{:S(2)}) %collective-permute-start.13) | collective-permute-done | bytes 426016 | tf_op jit(solution)/shard_map/ppermute | solution.py:64
  73.7 0.4 collective-permute-start.17
  74.2 3.4 %collective-permute-start.16 = (bf16[2,4,6656]{2,1,0:T(4,128)(2,1)S(1)}, bf16[2,4,6656]{2,1,0:T(4,128)(2,1)S(1)}, u32[]{:S(2)}, u32[]{:S(2)}) collective-permute-start(bf16[2,4,6656]{2,1,0:T(4,128)(2,1)S(1)} %get-tuple-element.243), channel_id=1, source_target_pairs={{0,4},{1,3},{2,6},{3,1},{4,0},{5,7},{6,2},{7,5},{8,12},{9,11},{10,... | collective-permute-start | bytes 319496 | tf_op jit(solution)/shard_map/ppermute | solution.py:64
  77.8 4.6 %collective-permute-done.17 = bf16[2,8,6656]{2,1,0:T(8,128)(2,1)S(1)} collective-permute-done((bf16[2,8,6656]{2,1,0:T(8,128)(2,1)S(1)}, bf16[2,8,6656]{2,1,0:T(8,128)(2,1)S(1)}, u32[]{:S(2)}, u32[]{:S(2)}) %collective-permute-start.17) | collective-permute-done | bytes 213024 | tf_op jit(solution)/shard_map/ppermute | solution.py:64
  82.5 1.4 collective-permute-start.19
  84.0 1.7 collective-permute-start.18
  85.9 2.5 %collective-permute-start.22 = (bf16[2,16,6656]{2,1,0:T(8,128)(2,1)S(1)}, bf16[2,16,6656]{2,1,0:T(8,128)(2,1)S(1)}, u32[]{:S(2)}, u32[]{:S(2)}) collective-permute-start(bf16[2,16,6656]{2,1,0:T(8,128)(2,1)S(1)} %get-tuple-element.196), channel_id=1, source_target_pairs={{0,16},{1,9},{2,18},{3,11},{4,20},{5,13},{6,22},{7,15},{8,24},{9,1... | collective-permute-start | bytes 1277960 | tf_op jit(solution)/shard_map/ppermute | solution.py:64
  88.4 3.2 %collective-permute-done.19 = bf16[2,4,6656]{2,1,0:T(4,128)(2,1)S(1)} collective-permute-done((bf16[2,4,6656]{2,1,0:T(4,128)(2,1)S(1)}, bf16[2,4,6656]{2,1,0:T(4,128)(2,1)S(1)}, u32[]{:S(2)}, u32[]{:S(2)}) %collective-permute-start.19) | collective-permute-done | bytes 106528 | tf_op jit(solution)/shard_map/ppermute | solution.py:64
  91.7 0.9 collective-permute-done.18
  92.7 2.4 %collective-permute-start.21 = (bf16[8,6656]{1,0:T(8,128)(2,1)S(1)}, bf16[8,6656]{1,0:T(8,128)(2,1)S(1)}, u32[]{:S(2)}, u32[]{:S(2)}) collective-permute-start(bf16[8,6656]{1,0:T(8,128)(2,1)S(1)} %pad_maximum_fusion.8), channel_id=1, source_target_pairs={{0,2},{1,5},{2,0},{3,7},{4,6},{5,1},{6,4},{7,3},{8,10},{9,13},{10,... | collective-permute-start | bytes 319496 | tf_op jit(solution)/shard_map/ppermute | solution.py:64
  95.5 4.5 %collective-permute-done.23 = bf16[4,6656]{1,0:T(4,128)(2,1)S(1)} collective-permute-done((bf16[4,6656]{1,0:T(4,128)(2,1)S(1)}, bf16[4,6656]{1,0:T(4,128)(2,1)S(1)}, u32[]{:S(2)}, u32[]{:S(2)}) %collective-permute-start.23) | collective-permute-done | bytes 53280 | tf_op jit(solution)/shard_map/ppermute | solution.py:64
  100.3 2.1 %collective-permute-start.26 = (bf16[2,8,6656]{2,1,0:T(8,128)(2,1)S(1)}, bf16[2,8,6656]{2,1,0:T(8,128)(2,1)S(1)}, u32[]{:S(2)}, u32[]{:S(2)}) collective-permute-start(bf16[2,8,6656]{2,1,0:T(8,128)(2,1)S(1)} %get-tuple-element.232), channel_id=1, source_target_pairs={{0,2},{1,5},{2,0},{3,7},{4,6},{5,1},{6,4},{7,3},{8,10},{9,13},{10,... | collective-permute-start | bytes 638984 | tf_op jit(solution)/shard_map/ppermute | solution.py:64
  102.5 1.1 collective-permute-done.28
  103.8 4.4 %collective-permute-done.27 = bf16[8,6656]{1,0:T(8,128)(2,1)S(1)} collective-permute-done((bf16[8,6656]{1,0:T(8,128)(2,1)S(1)}, bf16[8,6656]{1,0:T(8,128)(2,1)S(1)}, u32[]{:S(2)}, u32[]{:S(2)}) %collective-permute-start.27) | collective-permute-done | bytes 106528 | tf_op jit(solution)/shard_map/ppermute | solution.py:64
  108.2 3.8 %collective-permute-done.26 = bf16[2,8,6656]{2,1,0:T(8,128)(2,1)S(1)} collective-permute-done((bf16[2,8,6656]{2,1,0:T(8,128)(2,1)S(1)}, bf16[2,8,6656]{2,1,0:T(8,128)(2,1)S(1)}, u32[]{:S(2)}, u32[]{:S(2)}) %collective-permute-start.26) | collective-permute-done | bytes 213024 | tf_op jit(solution)/shard_map/ppermute | solution.py:64
  112.4 0.6 collective-permute-start.29
  113.0 2.4 %collective-permute-done.31 = bf16[2,8,6656]{2,1,0:T(8,128)(2,1)S(1)} collective-permute-done((bf16[2,8,6656]{2,1,0:T(8,128)(2,1)S(1)}, bf16[2,8,6656]{2,1,0:T(8,128)(2,1)S(1)}, u32[]{:S(2)}, u32[]{:S(2)}) %collective-permute-start.31) | collective-permute-done | bytes 213024 | tf_op jit(solution)/shard_map/ppermute | solution.py:64
  115.8 5.8 %collective-permute-done.30 = bf16[2,4,6656]{2,1,0:T(4,128)(2,1)S(1)} collective-permute-done((bf16[2,4,6656]{2,1,0:T(4,128)(2,1)S(1)}, bf16[2,4,6656]{2,1,0:T(4,128)(2,1)S(1)}, u32[]{:S(2)}, u32[]{:S(2)}) %collective-permute-start.30) | collective-permute-done | bytes 106528 | tf_op jit(solution)/shard_map/ppermute | solution.py:64
  121.9 0.8 collective-permute-done.33
  122.8 2.1 %collective-permute-start.36 = (bf16[4,6656]{1,0:T(4,128)(2,1)S(1)}, bf16[4,6656]{1,0:T(4,128)(2,1)S(1)}, u32[]{:S(2)}, u32[]{:S(2)}) collective-permute-start(bf16[4,6656]{1,0:T(4,128)(2,1)S(1)} %fusion.66), channel_id=1, source_target_pairs={{0,4},{1,3},{2,6},{3,1},{4,0},{5,7},{6,2},{7,5},{8,12},{9,11},{10,... | collective-permute-start | bytes 159752 | tf_op jit(solution)/shard_map/ppermute | solution.py:64
  125.0 1.8 %collective-permute-done.32 = bf16[4,6656]{1,0:T(4,128)(2,1)S(1)} collective-permute-done((bf16[4,6656]{1,0:T(4,128)(2,1)S(1)}, bf16[4,6656]{1,0:T(4,128)(2,1)S(1)}, u32[]{:S(2)}, u32[]{:S(2)}) %collective-permute-start.32) | collective-permute-done | bytes 53280 | tf_op jit(solution)/shard_map/ppermute | solution.py:64
  127.1 0.8 collective-permute-done.36
  128.0 1.7 collective-permute-start.37
  129.6 3.1 %collective-permute-done.39 = bf16[8,6656]{1,0:T(8,128)(2,1)S(1)} collective-permute-done((bf16[8,6656]{1,0:T(8,128)(2,1)S(1)}, bf16[8,6656]{1,0:T(8,128)(2,1)S(1)}, u32[]{:S(2)}, u32[]{:S(2)}) %collective-permute-start.39) | collective-permute-done | bytes 106528 | tf_op jit(solution)/shard_map/ppermute | solution.py:64
  133.0 0.9 collective-permute-done.37
  133.9 1.2 collective-permute-start.40
  135.1 4.9 %collective-permute-done.41 = bf16[16,6656]{1,0:T(8,128)(2,1)S(1)} collective-permute-done((bf16[16,6656]{1,0:T(8,128)(2,1)S(1)}, bf16[16,6656]{1,0:T(8,128)(2,1)S(1)}, u32[]{:S(2)}, u32[]{:S(2)}) %collective-permute-start.41) | collective-permute-done | bytes 213024 | tf_op jit(solution)/shard_map/ppermute | solution.py:64
  140.2 4.4 %collective-permute-done.40 = bf16[16,6656]{1,0:T(8,128)(2,1)S(1)} collective-permute-done((bf16[16,6656]{1,0:T(8,128)(2,1)S(1)}, bf16[16,6656]{1,0:T(8,128)(2,1)S(1)}, u32[]{:S(2)}, u32[]{:S(2)}) %collective-permute-start.40) | collective-permute-done | bytes 213024 | tf_op jit(solution)/shard_map/ppermute | solution.py:64
  144.8 2.4 %fusion.6 = f32[128,512]{1,0:T(8,128)S(1)} fusion(bf16[512,26624]{1,0:T(8,128)(2,1)S(1)} %bitcast.118, bf16[64,6656]{1,0:T(8,128)(2,1)S(1)} %collective-permute-done.35, bf16[64,6656]{1,0:T(8,128)(2,1)S(1)} %constant_dynamic-update-slice_fusion.8), kind=kOutput, calls=%fused_computation.14 | convolution fusion | flops 875823104 | bytes 8781824 | tf_op jit(solution)/shard_map/dot_general | solution.py:34
  147.2 1.1 collective-permute-done.43
  148.4 3.6 %fusion.28 = f32[128,512]{1,0:T(8,128)S(1)} fusion(f32[128,512]{1,0:T(8,128)S(1)} %fusion.6, bf16[512,26624]{1,0:T(8,128)(2,1)S(1)} %bitcast.118, bf16[64,6656]{1,0:T(8,128)(2,1)} %collective-permute-done.42, bf16[64,6656]{1,0:T(8,128)(2,1)S(1)} %constant_dynamic-update-slice_fusion.12), kind=kOutput, calls=%fused_computation.36 | convolution fusion | flops 875888640 | bytes 9043968 | tf_op jit(solution)/shard_map/dot_general | solution.py:34
  152.0 0.8 collective-permute-done.45
  153.0 2.4 %fusion.33 = f32[128,512]{1,0:T(8,128)S(1)} fusion(f32[128,512]{1,0:T(8,128)S(1)} %fusion.28, bf16[512,26624]{1,0:T(8,128)(2,1)S(1)} %bitcast.118, bf16[64,6656]{1,0:T(8,128)(2,1)S(1)} %collective-permute-done.44, bf16[64,6656]{1,0:T(8,128)(2,1)S(1)} %constant_dynamic-update-slice_fusion.20), kind=kOutput, calls=%fused_computation.37 | convolution fusion | flops 875888640 | bytes 9043968 | tf_op jit(solution)/shard_map/dot_general | solution.py:34
  155.4 2.4 %fusion.38 = f32[128,512]{1,0:T(8,128)S(1)} fusion(f32[128,512]{1,0:T(8,128)S(1)} %fusion.33, bf16[512,26624]{1,0:T(8,128)(2,1)S(1)} %bitcast.118, bf16[64,6656]{1,0:T(8,128)(2,1)S(1)} %collective-permute-done.46, bf16[64,6656]{1,0:T(8,128)(2,1)S(1)} %constant_dynamic-update-slice_fusion.22), kind=kOutput, calls=%fused_computation.38 | convolution fusion | flops 875888640 | bytes 9043968 | tf_op jit(solution)/shard_map/dot_general | solution.py:34
  158.2 0.6 collective-permute-start.47
  158.8 0.9 collective-permute-done.47
  159.8 4.3 %collective-permute-done.48 = bf16[32,1024]{1,0:T(8,128)(2,1)S(1)} collective-permute-done((bf16[32,1024]{1,0:T(8,128)(2,1)S(1)}, bf16[32,1024]{1,0:T(8,128)(2,1)S(1)}, u32[]{:S(2)}, u32[]{:S(2)}) %collective-permute-start.48) | collective-permute-done | bytes 65568 | tf_op jit(solution)/shard_map/ppermute | solution.py:64
  164.2 0.7 collective-permute-start.49
  164.8 5.2 %collective-permute-done.49 = bf16[16,2048]{1,0:T(8,128)(2,1)S(1)} collective-permute-done((bf16[16,2048]{1,0:T(8,128)(2,1)S(1)}, bf16[16,2048]{1,0:T(8,128)(2,1)S(1)}, u32[]{:S(2)}, u32[]{:S(2)}) %collective-permute-start.49) | collective-permute-done | bytes 65568 | tf_op jit(solution)/shard_map/ppermute | solution.py:64
  170.1 0.7 maximum_bitcast_fusion
  (147 shorter events, 10.4 us)
Async XLA Ops:
  0.9 7.8 %collective-permute-start = (bf16[16,2048]{1,0:T(8,128)(2,1)S(1)}, bf16[16,2048]{1,0:T(8,128)(2,1)S(1)}, u32[]{:S(2)}, u32[]{:S(2)}) collective-permute-start(bf16[16,2048]{1,0:T(8,128)(2,1)S(1)} %get-tuple-element.256), channel_id=1, source_target_pairs={{0,4},{1,5},{2,6},{3,7},{4,0},{5,1},{6,2},{7,3},{8,12},{9,13},{10,... | collective-permute-start | bytes 196616 | tf_op jit(solution)/shard_map/ppermute | solution.py:64
  8.7 4.3 %collective-permute-start.1 = (bf16[32,1024]{1,0:T(8,128)(2,1)S(1)}, bf16[32,1024]{1,0:T(8,128)(2,1)S(1)}, u32[]{:S(2)}, u32[]{:S(2)}) collective-permute-start(bf16[32,1024]{1,0:T(8,128)(2,1)S(1)} %get-tuple-element.254), channel_id=1, source_target_pairs={{0,2},{1,3},{2,0},{3,1},{4,6},{5,7},{6,4},{7,5},{8,10},{9,11},{10,... | collective-permute-start | bytes 196616 | tf_op jit(solution)/shard_map/ppermute | solution.py:64
  13.0 1.3 collective-permute-start.2
  22.9 9.5 %collective-permute-start.3 = (bf16[64,6656]{1,0:T(8,128)(2,1)S(1)}, bf16[64,6656]{1,0:T(8,128)(2,1)S(1)}, u32[]{:S(2)}, u32[]{:S(2)}) collective-permute-start(bf16[64,6656]{1,0:T(8,128)(2,1)S(1)} %get-tuple-element.227), channel_id=1, source_target_pairs={{0,1},{1,0},{2,3},{3,2},{4,5},{5,4},{6,7},{7,6},{8,9},{9,8},{10,11... | collective-permute-start | bytes 2555912 | tf_op jit(solution)/shard_map/ppermute | solution.py:64
  23.1 9.3 %collective-permute-start.4 = (bf16[64,6656]{1,0:T(8,128)(2,1)S(1)}, bf16[64,6656]{1,0:T(8,128)(2,1)S(1)}, u32[]{:S(2)}, u32[]{:S(2)}) collective-permute-start(bf16[64,6656]{1,0:T(8,128)(2,1)S(1)} %get-tuple-element.225), channel_id=1, source_target_pairs={{0,1},{1,0},{2,3},{3,2},{4,5},{5,4},{6,7},{7,6},{8,9},{9,8},{10,11... | collective-permute-start | bytes 2555912 | tf_op jit(solution)/shard_map/ppermute | solution.py:64
  31.7 12.0 %collective-permute-start.6 = (bf16[64,6656]{1,0:T(8,128)(2,1)S(1)}, bf16[64,6656]{1,0:T(8,128)(2,1)S(1)}, u32[]{:S(2)}, u32[]{:S(2)}) collective-permute-start(bf16[64,6656]{1,0:T(8,128)(2,1)S(1)} %get-tuple-element.220), channel_id=1, source_target_pairs={{0,1},{1,0},{2,3},{3,2},{4,5},{5,4},{6,7},{7,6},{8,9},{9,8},{10,11... | collective-permute-start | bytes 2555912 | tf_op jit(solution)/shard_map/ppermute | solution.py:64
  32.0 11.6 %collective-permute-start.7 = (bf16[64,6656]{1,0:T(8,128)(2,1)S(1)}, bf16[64,6656]{1,0:T(8,128)(2,1)S(1)}, u32[]{:S(2)}, u32[]{:S(2)}) collective-permute-start(bf16[64,6656]{1,0:T(8,128)(2,1)S(1)} %get-tuple-element.218), channel_id=1, source_target_pairs={{0,1},{1,0},{2,3},{3,2},{4,5},{5,4},{6,7},{7,6},{8,9},{9,8},{10,11... | collective-permute-start | bytes 2555912 | tf_op jit(solution)/shard_map/ppermute | solution.py:64
  33.0 12.8 %collective-permute-start.5 = (bf16[2,32,6656]{2,1,0:T(8,128)(2,1)S(1)}, bf16[2,32,6656]{2,1,0:T(8,128)(2,1)S(1)}, u32[]{:S(2)}, u32[]{:S(2)}) collective-permute-start(bf16[2,32,6656]{2,1,0:T(8,128)(2,1)S(1)} %pad_maximum_fusion.1), channel_id=1, source_target_pairs={{0,8},{1,17},{2,10},{3,19},{4,12},{5,21},{6,14},{7,23},{8,0},{9,25... | collective-permute-start | bytes 2555912 | tf_op jit(solution)/shard_map/ppermute | solution.py:64
  42.9 18.8 %collective-permute-start.9 = (bf16[64,6656]{1,0:T(8,128)(2,1)S(1)}, bf16[64,6656]{1,0:T(8,128)(2,1)S(1)}, u32[]{:S(2)}, u32[]{:S(2)}) collective-permute-start(bf16[64,6656]{1,0:T(8,128)(2,1)S(1)} %get-tuple-element.214), channel_id=1, source_target_pairs={{0,1},{1,0},{2,3},{3,2},{4,5},{5,4},{6,7},{7,6},{8,9},{9,8},{10,11... | collective-permute-start | bytes 2555912 | tf_op jit(solution)/shard_map/ppermute | solution.py:64
  43.1 20.2 %collective-permute-start.10 = (bf16[64,6656]{1,0:T(8,128)(2,1)S(1)}, bf16[64,6656]{1,0:T(8,128)(2,1)S(1)}, u32[]{:S(2)}, u32[]{:S(2)}) collective-permute-start(bf16[64,6656]{1,0:T(8,128)(2,1)S(1)} %get-tuple-element.212), channel_id=1, source_target_pairs={{0,1},{1,0},{2,3},{3,2},{4,5},{5,4},{6,7},{7,6},{8,9},{9,8},{10,11... | collective-permute-start | bytes 2555912 | tf_op jit(solution)/shard_map/ppermute | solution.py:64
  44.2 17.3 %collective-permute-start.11 = (bf16[2,32,6656]{2,1,0:T(8,128)(2,1)S(1)}, bf16[2,32,6656]{2,1,0:T(8,128)(2,1)S(1)}, u32[]{:S(2)}, u32[]{:S(2)}) collective-permute-start(bf16[2,32,6656]{2,1,0:T(8,128)(2,1)S(1)} %pad_maximum_fusion.2), channel_id=1, source_target_pairs={{0,8},{1,17},{2,10},{3,19},{4,12},{5,21},{6,14},{7,23},{8,0},{9,25... | collective-permute-start | bytes 2555912 | tf_op jit(solution)/shard_map/ppermute | solution.py:64
  45.9 18.8 %collective-permute-start.8 = (bf16[2,16,6656]{2,1,0:T(8,128)(2,1)S(1)}, bf16[2,16,6656]{2,1,0:T(8,128)(2,1)S(1)}, u32[]{:S(2)}, u32[]{:S(2)}) collective-permute-start(bf16[2,16,6656]{2,1,0:T(8,128)(2,1)S(1)} %get-tuple-element.215), channel_id=1, source_target_pairs={{0,16},{1,9},{2,18},{3,11},{4,20},{5,13},{6,22},{7,15},{8,24},{9,1... | collective-permute-start | bytes 1277960 | tf_op jit(solution)/shard_map/ppermute | solution.py:64
  51.8 93.0 %slice-start = ((s8[27262976]{0:T(1024)(128)(4,1)}), s8[2097152]{0:T(1024)(128)(4,1)S(1)}, s32[]{:S(2)}) async-start(s8[27262976]{0:T(1024)(128)(4,1)} %bitcast.117), calls=%async_computation | async-start | bytes 4194304
  51.8 93.0 %slice-start.1 = ((s8[27262976]{0:T(1024)(128)(4,1)}), s8[4194304]{0:T(1024)(128)(4,1)S(1)}, s32[]{:S(2)}) async-start(s8[27262976]{0:T(1024)(128)(4,1)} %bitcast.117), calls=%async_computation.1 | async-start | bytes 8388608
  56.1 9.1 %collective-permute-start.14 = (bf16[64,6656]{1,0:T(8,128)(2,1)S(1)}, bf16[64,6656]{1,0:T(8,128)(2,1)S(1)}, u32[]{:S(2)}, u32[]{:S(2)}) collective-permute-start(bf16[64,6656]{1,0:T(8,128)(2,1)S(1)} %get-tuple-element.204), channel_id=1, source_target_pairs={{0,1},{1,0},{2,3},{3,2},{4,5},{5,4},{6,7},{7,6},{8,9},{9,8},{10,11... | collective-permute-start | bytes 2555912 | tf_op jit(solution)/shard_map/ppermute | solution.py:64
  61.5 83.2 %slice-start.2 = ((s8[27262976]{0:T(1024)(128)(4,1)}), s8[4194304]{0:T(1024)(128)(4,1)S(1)}, s32[]{:S(2)}) async-start(s8[27262976]{0:T(1024)(128)(4,1)} %bitcast.117), calls=%async_computation.2 | async-start | bytes 8388608
  61.5 3.7 %collective-permute-start.15 = (bf16[64,6656]{1,0:T(8,128)(2,1)S(1)}, bf16[64,6656]{1,0:T(8,128)(2,1)S(1)}, u32[]{:S(2)}, u32[]{:S(2)}) collective-permute-start(bf16[64,6656]{1,0:T(8,128)(2,1)S(1)} %get-tuple-element.202), channel_id=1, source_target_pairs={{0,1},{1,0},{2,3},{3,2},{4,5},{5,4},{6,7},{7,6},{8,9},{9,8},{10,11... | collective-permute-start | bytes 2555912 | tf_op jit(solution)/shard_map/ppermute | solution.py:64
  61.7 11.8 %collective-permute-start.13 = (bf16[2,16,6656]{2,1,0:T(8,128)(2,1)S(1)}, bf16[2,16,6656]{2,1,0:T(8,128)(2,1)S(1)}, u32[]{:S(2)}, u32[]{:S(2)}) collective-permute-start(bf16[2,16,6656]{2,1,0:T(8,128)(2,1)S(1)} %get-tuple-element.206), channel_id=1, source_target_pairs={{0,16},{1,9},{2,18},{3,11},{4,20},{5,13},{6,22},{7,15},{8,24},{9,1... | collective-permute-start | bytes 1277960 | tf_op jit(solution)/shard_map/ppermute | solution.py:64
  64.0 21.7 %collective-permute-start.20 = (bf16[2,32,6656]{2,1,0:T(8,128)(2,1)S(1)}, bf16[2,32,6656]{2,1,0:T(8,128)(2,1)S(1)}, u32[]{:S(2)}, u32[]{:S(2)}) collective-permute-start(bf16[2,32,6656]{2,1,0:T(8,128)(2,1)S(1)} %pad_maximum_fusion.4), channel_id=1, source_target_pairs={{0,8},{1,17},{2,10},{3,19},{4,12},{5,21},{6,14},{7,23},{8,0},{9,25... | collective-permute-start | bytes 2555912 | tf_op jit(solution)/shard_map/ppermute | solution.py:64
  64.6 80.2 %slice-start.3 = ((s8[27262976]{0:T(1024)(128)(4,1)}), s8[4194304]{0:T(1024)(128)(4,1)S(1)}, s32[]{:S(2)}) async-start(s8[27262976]{0:T(1024)(128)(4,1)} %bitcast.117), calls=%async_computation.3 | async-start | bytes 8388608
  64.8 9.3 %collective-permute-start.12 = (bf16[2,8,6656]{2,1,0:T(8,128)(2,1)S(1)}, bf16[2,8,6656]{2,1,0:T(8,128)(2,1)S(1)}, u32[]{:S(2)}, u32[]{:S(2)}) collective-permute-start(bf16[2,8,6656]{2,1,0:T(8,128)(2,1)S(1)} %get-tuple-element.235), channel_id=1, source_target_pairs={{0,2},{1,5},{2,0},{3,7},{4,6},{5,1},{6,4},{7,3},{8,10},{9,13},{10,... | collective-permute-start | bytes 638984 | tf_op jit(solution)/shard_map/ppermute | solution.py:64
  65.6 79.1 %slice-start.4 = ((s8[27262976]{0:T(1024)(128)(4,1)}), s8[4194304]{0:T(1024)(128)(4,1)S(1)}, s32[]{:S(2)}) async-start(s8[27262976]{0:T(1024)(128)(4,1)} %bitcast.117), calls=%async_computation.4 | async-start | bytes 8388608
  65.7 29.5 %collective-permute-start.24 = (bf16[2,32,6656]{2,1,0:T(8,128)(2,1)S(1)}, bf16[2,32,6656]{2,1,0:T(8,128)(2,1)S(1)}, u32[]{:S(2)}, u32[]{:S(2)}) collective-permute-start(bf16[2,32,6656]{2,1,0:T(8,128)(2,1)S(1)} %pad_maximum_fusion.5), channel_id=1, source_target_pairs={{0,8},{1,17},{2,10},{3,19},{4,12},{5,21},{6,14},{7,23},{8,0},{9,25... | collective-permute-start | bytes 2555912 | tf_op jit(solution)/shard_map/ppermute | solution.py:64
  73.7 8.7 %collective-permute-start.17 = (bf16[2,8,6656]{2,1,0:T(8,128)(2,1)S(1)}, bf16[2,8,6656]{2,1,0:T(8,128)(2,1)S(1)}, u32[]{:S(2)}, u32[]{:S(2)}) collective-permute-start(bf16[2,8,6656]{2,1,0:T(8,128)(2,1)S(1)} %get-tuple-element.234), channel_id=1, source_target_pairs={{0,2},{1,5},{2,0},{3,7},{4,6},{5,1},{6,4},{7,3},{8,10},{9,13},{10,... | collective-permute-start | bytes 638984 | tf_op jit(solution)/shard_map/ppermute | solution.py:64
  74.2 9.7 %collective-permute-start.16 = (bf16[2,4,6656]{2,1,0:T(4,128)(2,1)S(1)}, bf16[2,4,6656]{2,1,0:T(4,128)(2,1)S(1)}, u32[]{:S(2)}, u32[]{:S(2)}) collective-permute-start(bf16[2,4,6656]{2,1,0:T(4,128)(2,1)S(1)} %get-tuple-element.243), channel_id=1, source_target_pairs={{0,4},{1,3},{2,6},{3,1},{4,0},{5,7},{6,2},{7,5},{8,12},{9,11},{10,... | collective-permute-start | bytes 319496 | tf_op jit(solution)/shard_map/ppermute | solution.py:64
  82.5 9.0 %collective-permute-start.19 = (bf16[2,4,6656]{2,1,0:T(4,128)(2,1)S(1)}, bf16[2,4,6656]{2,1,0:T(4,128)(2,1)S(1)}, u32[]{:S(2)}, u32[]{:S(2)}) collective-permute-start(bf16[2,4,6656]{2,1,0:T(4,128)(2,1)S(1)} %get-tuple-element.242), channel_id=1, source_target_pairs={{0,4},{1,3},{2,6},{3,1},{4,0},{5,7},{6,2},{7,5},{8,12},{9,11},{10,... | collective-permute-start | bytes 319496 | tf_op jit(solution)/shard_map/ppermute | solution.py:64
  84.0 8.7 %collective-permute-start.18 = (bf16[4,6656]{1,0:T(4,128)(2,1)S(1)}, bf16[4,6656]{1,0:T(4,128)(2,1)S(1)}, u32[]{:S(2)}, u32[]{:S(2)}) collective-permute-start(bf16[4,6656]{1,0:T(4,128)(2,1)S(1)} %fusion.69), channel_id=1, source_target_pairs={{0,4},{1,3},{2,6},{3,1},{4,0},{5,7},{6,2},{7,5},{8,12},{9,11},{10,... | collective-permute-start | bytes 159752 | tf_op jit(solution)/shard_map/ppermute | solution.py:64
  85.9 14.3 %collective-permute-start.22 = (bf16[2,16,6656]{2,1,0:T(8,128)(2,1)S(1)}, bf16[2,16,6656]{2,1,0:T(8,128)(2,1)S(1)}, u32[]{:S(2)}, u32[]{:S(2)}) collective-permute-start(bf16[2,16,6656]{2,1,0:T(8,128)(2,1)S(1)} %get-tuple-element.196), channel_id=1, source_target_pairs={{0,16},{1,9},{2,18},{3,11},{4,20},{5,13},{6,22},{7,15},{8,24},{9,1... | collective-permute-start | bytes 1277960 | tf_op jit(solution)/shard_map/ppermute | solution.py:64
  91.6 53.2 %slice-start.5 = ((s8[27262976]{0:T(1024)(128)(4,1)}), s8[4194304]{0:T(1024)(128)(4,1)S(1)}, s32[]{:S(2)}) async-start(s8[27262976]{0:T(1024)(128)(4,1)} %bitcast.117), calls=%async_computation.5 | async-start | bytes 8388608
  91.7 8.4 %collective-permute-start.23 = (bf16[4,6656]{1,0:T(4,128)(2,1)S(1)}, bf16[4,6656]{1,0:T(4,128)(2,1)S(1)}, u32[]{:S(2)}, u32[]{:S(2)}) collective-permute-start(bf16[4,6656]{1,0:T(4,128)(2,1)S(1)} %fusion.68), channel_id=1, source_target_pairs={{0,4},{1,3},{2,6},{3,1},{4,0},{5,7},{6,2},{7,5},{8,12},{9,11},{10,... | collective-permute-start | bytes 159752 | tf_op jit(solution)/shard_map/ppermute | solution.py:64
  92.7 9.6 %collective-permute-start.21 = (bf16[8,6656]{1,0:T(8,128)(2,1)S(1)}, bf16[8,6656]{1,0:T(8,128)(2,1)S(1)}, u32[]{:S(2)}, u32[]{:S(2)}) collective-permute-start(bf16[8,6656]{1,0:T(8,128)(2,1)S(1)} %pad_maximum_fusion.8), channel_id=1, source_target_pairs={{0,2},{1,5},{2,0},{3,7},{4,6},{5,1},{6,4},{7,3},{8,10},{9,13},{10,... | collective-permute-start | bytes 319496 | tf_op jit(solution)/shard_map/ppermute | solution.py:64
  95.4 8.2 %collective-permute-start.28 = (bf16[2,16,6656]{2,1,0:T(8,128)(2,1)S(1)}, bf16[2,16,6656]{2,1,0:T(8,128)(2,1)S(1)}, u32[]{:S(2)}, u32[]{:S(2)}) collective-permute-start(bf16[2,16,6656]{2,1,0:T(8,128)(2,1)S(1)} %get-tuple-element.190), channel_id=1, source_target_pairs={{0,16},{1,9},{2,18},{3,11},{4,20},{5,13},{6,22},{7,15},{8,24},{9,1... | collective-permute-start | bytes 1277960 | tf_op jit(solution)/shard_map/ppermute | solution.py:64
  100.1 8.0 %collective-permute-start.27 = (bf16[8,6656]{1,0:T(8,128)(2,1)S(1)}, bf16[8,6656]{1,0:T(8,128)(2,1)S(1)}, u32[]{:S(2)}, u32[]{:S(2)}) collective-permute-start(bf16[8,6656]{1,0:T(8,128)(2,1)S(1)} %pad_maximum_fusion.9), channel_id=1, source_target_pairs={{0,2},{1,5},{2,0},{3,7},{4,6},{5,1},{6,4},{7,3},{8,10},{9,13},{10,... | collective-permute-start | bytes 319496 | tf_op jit(solution)/shard_map/ppermute | solution.py:64
  100.3 11.8 %collective-permute-start.26 = (bf16[2,8,6656]{2,1,0:T(8,128)(2,1)S(1)}, bf16[2,8,6656]{2,1,0:T(8,128)(2,1)S(1)}, u32[]{:S(2)}, u32[]{:S(2)}) collective-permute-start(bf16[2,8,6656]{2,1,0:T(8,128)(2,1)S(1)} %get-tuple-element.232), channel_id=1, source_target_pairs={{0,2},{1,5},{2,0},{3,7},{4,6},{5,1},{6,4},{7,3},{8,10},{9,13},{10,... | collective-permute-start | bytes 638984 | tf_op jit(solution)/shard_map/ppermute | solution.py:64
  102.4 10.0 %collective-permute-start.25 = (bf16[16,6656]{1,0:T(8,128)(2,1)S(1)}, bf16[16,6656]{1,0:T(8,128)(2,1)S(1)}, u32[]{:S(2)}, u32[]{:S(2)}) collective-permute-start(bf16[16,6656]{1,0:T(8,128)(2,1)S(1)} %constant_dynamic-update-slice_fusion), channel_id=1, source_target_pairs={{0,16},{1,9},{2,18},{3,11},{4,20},{5,13},{6,22},{7,15},{8,24},{9,1... | collective-permute-start | bytes 638984 | tf_op jit(solution)/shard_map/ppermute | solution.py:64
  103.7 11.7 %collective-permute-start.31 = (bf16[2,8,6656]{2,1,0:T(8,128)(2,1)S(1)}, bf16[2,8,6656]{2,1,0:T(8,128)(2,1)S(1)}, u32[]{:S(2)}, u32[]{:S(2)}) collective-permute-start(bf16[2,8,6656]{2,1,0:T(8,128)(2,1)S(1)} %get-tuple-element.230), channel_id=1, source_target_pairs={{0,2},{1,5},{2,0},{3,7},{4,6},{5,1},{6,4},{7,3},{8,10},{9,13},{10,... | collective-permute-start | bytes 638984 | tf_op jit(solution)/shard_map/ppermute | solution.py:64
  108.2 13.6 %collective-permute-start.34 = (bf16[16,6656]{1,0:T(8,128)(2,1)S(1)}, bf16[16,6656]{1,0:T(8,128)(2,1)S(1)}, u32[]{:S(2)}, u32[]{:S(2)}) collective-permute-start(bf16[16,6656]{1,0:T(8,128)(2,1)S(1)} %constant_dynamic-update-slice_fusion.2), channel_id=1, source_target_pairs={{0,16},{1,9},{2,18},{3,11},{4,20},{5,13},{6,22},{7,15},{8,24},{9,1... | collective-permute-start | bytes 638984 | tf_op jit(solution)/shard_map/ppermute | solution.py:64
  112.2 9.4 %collective-permute-start.30 = (bf16[2,4,6656]{2,1,0:T(4,128)(2,1)S(1)}, bf16[2,4,6656]{2,1,0:T(4,128)(2,1)S(1)}, u32[]{:S(2)}, u32[]{:S(2)}) collective-permute-start(bf16[2,4,6656]{2,1,0:T(4,128)(2,1)S(1)} %get-tuple-element.240), channel_id=1, source_target_pairs={{0,4},{1,3},{2,6},{3,1},{4,0},{5,7},{6,2},{7,5},{8,12},{9,11},{10,... | collective-permute-start | bytes 319496 | tf_op jit(solution)/shard_map/ppermute | solution.py:64
  112.4 14.5 %collective-permute-start.29 = (bf16[32,6656]{1,0:T(8,128)(2,1)S(1)}, bf16[32,6656]{1,0:T(8,128)(2,1)S(1)}, u32[]{:S(2)}, u32[]{:S(2)}) collective-permute-start(bf16[32,6656]{1,0:T(8,128)(2,1)S(1)} %constant_dynamic-update-slice_fusion.4), channel_id=1, source_target_pairs={{0,8},{1,17},{2,10},{3,19},{4,12},{5,21},{6,14},{7,23},{8,0},{9,25... | collective-permute-start | bytes 1277960 | tf_op jit(solution)/shard_map/ppermute | solution.py:64
  115.4 29.4 %slice-start.6 = ((s8[27262976]{0:T(1024)(128)(4,1)}), s8[4194304]{0:T(1024)(128)(4,1)S(1)}, s32[]{:S(2)}) async-start(s8[27262976]{0:T(1024)(128)(4,1)} %bitcast.117), calls=%async_computation.6 | async-start | bytes 8388608
  115.5 7.2 %collective-permute-start.33 = (bf16[2,4,6656]{2,1,0:T(4,128)(2,1)S(1)}, bf16[2,4,6656]{2,1,0:T(4,128)(2,1)S(1)}, u32[]{:S(2)}, u32[]{:S(2)}) collective-permute-start(bf16[2,4,6656]{2,1,0:T(4,128)(2,1)S(1)} %get-tuple-element.238), channel_id=1, source_target_pairs={{0,4},{1,3},{2,6},{3,1},{4,0},{5,7},{6,2},{7,5},{8,12},{9,11},{10,... | collective-permute-start | bytes 319496 | tf_op jit(solution)/shard_map/ppermute | solution.py:64
  121.7 5.1 %collective-permute-start.32 = (bf16[4,6656]{1,0:T(4,128)(2,1)S(1)}, bf16[4,6656]{1,0:T(4,128)(2,1)S(1)}, u32[]{:S(2)}, u32[]{:S(2)}) collective-permute-start(bf16[4,6656]{1,0:T(4,128)(2,1)S(1)} %fusion.67), channel_id=1, source_target_pairs={{0,4},{1,3},{2,6},{3,1},{4,0},{5,7},{6,2},{7,5},{8,12},{9,11},{10,... | collective-permute-start | bytes 159752 | tf_op jit(solution)/shard_map/ppermute | solution.py:64
  121.8 11.0 %collective-permute-start.38 = (bf16[32,6656]{1,0:T(8,128)(2,1)S(1)}, bf16[32,6656]{1,0:T(8,128)(2,1)S(1)}, u32[]{:S(2)}, u32[]{:S(2)}) collective-permute-start(bf16[32,6656]{1,0:T(8,128)(2,1)S(1)} %constant_dynamic-update-slice_fusion.6), channel_id=1, source_target_pairs={{0,8},{1,17},{2,10},{3,19},{4,12},{5,21},{6,14},{7,23},{8,0},{9,25... | collective-permute-start | bytes 1277960 | tf_op jit(solution)/shard_map/ppermute | solution.py:64
  122.8 5.1 %collective-permute-start.36 = (bf16[4,6656]{1,0:T(4,128)(2,1)S(1)}, bf16[4,6656]{1,0:T(4,128)(2,1)S(1)}, u32[]{:S(2)}, u32[]{:S(2)}) collective-permute-start(bf16[4,6656]{1,0:T(4,128)(2,1)S(1)} %fusion.66), channel_id=1, source_target_pairs={{0,4},{1,3},{2,6},{3,1},{4,0},{5,7},{6,2},{7,5},{8,12},{9,11},{10,... | collective-permute-start | bytes 159752 | tf_op jit(solution)/shard_map/ppermute | solution.py:64
  126.8 5.9 %collective-permute-start.39 = (bf16[8,6656]{1,0:T(8,128)(2,1)S(1)}, bf16[8,6656]{1,0:T(8,128)(2,1)S(1)}, u32[]{:S(2)}, u32[]{:S(2)}) collective-permute-start(bf16[8,6656]{1,0:T(8,128)(2,1)S(1)} %pad_maximum_fusion.10), channel_id=1, source_target_pairs={{0,2},{1,5},{2,0},{3,7},{4,6},{5,1},{6,4},{7,3},{8,10},{9,13},{10,... | collective-permute-start | bytes 319496 | tf_op jit(solution)/shard_map/ppermute | solution.py:64
  127.0 17.7 %collective-permute-start.35 = (bf16[64,6656]{1,0:T(8,128)(2,1)S(1)}, bf16[64,6656]{1,0:T(8,128)(2,1)S(1)}, u32[]{:S(2)}, u32[]{:S(2)}) collective-permute-start(bf16[64,6656]{1,0:T(8,128)(2,1)S(1)} %constant_dynamic-update-slice_fusion.8), channel_id=1, source_target_pairs={{0,1},{1,0},{2,3},{3,2},{4,5},{5,4},{6,7},{7,6},{8,9},{9,8},{10,11... | collective-permute-start | bytes 2555912 | tf_op jit(solution)/shard_map/ppermute | solution.py:64
  128.0 5.9 %collective-permute-start.37 = (bf16[8,6656]{1,0:T(8,128)(2,1)S(1)}, bf16[8,6656]{1,0:T(8,128)(2,1)S(1)}, u32[]{:S(2)}, u32[]{:S(2)}) collective-permute-start(bf16[8,6656]{1,0:T(8,128)(2,1)S(1)} %pad_maximum_fusion.11), channel_id=1, source_target_pairs={{0,2},{1,5},{2,0},{3,7},{4,6},{5,1},{6,4},{7,3},{8,10},{9,13},{10,... | collective-permute-start | bytes 319496 | tf_op jit(solution)/shard_map/ppermute | solution.py:64
  132.8 7.3 %collective-permute-start.41 = (bf16[16,6656]{1,0:T(8,128)(2,1)S(1)}, bf16[16,6656]{1,0:T(8,128)(2,1)S(1)}, u32[]{:S(2)}, u32[]{:S(2)}) collective-permute-start(bf16[16,6656]{1,0:T(8,128)(2,1)S(1)} %constant_dynamic-update-slice_fusion.10), channel_id=1, source_target_pairs={{0,16},{1,9},{2,18},{3,11},{4,20},{5,13},{6,22},{7,15},{8,24},{9,1... | collective-permute-start | bytes 638984 | tf_op jit(solution)/shard_map/ppermute | solution.py:64
  132.9 15.5 %collective-permute-start.42 = (bf16[64,6656]{1,0:T(8,128)(2,1)S(1)}, bf16[64,6656]{1,0:T(8,128)(2,1)}, u32[]{:S(2)}, u32[]{:S(2)}) collective-permute-start(bf16[64,6656]{1,0:T(8,128)(2,1)S(1)} %constant_dynamic-update-slice_fusion.12), channel_id=1, source_target_pairs={{0,1},{1,0},{2,3},{3,2},{4,5},{5,4},{6,7},{7,6},{8,9},{9,8},{10,11... | collective-permute-start | bytes 2555912 | tf_op jit(solution)/shard_map/ppermute | solution.py:64
  133.9 10.7 %collective-permute-start.40 = (bf16[16,6656]{1,0:T(8,128)(2,1)S(1)}, bf16[16,6656]{1,0:T(8,128)(2,1)S(1)}, u32[]{:S(2)}, u32[]{:S(2)}) collective-permute-start(bf16[16,6656]{1,0:T(8,128)(2,1)S(1)} %constant_dynamic-update-slice_fusion.14), channel_id=1, source_target_pairs={{0,16},{1,9},{2,18},{3,11},{4,20},{5,13},{6,22},{7,15},{8,24},{9,1... | collective-permute-start | bytes 638984 | tf_op jit(solution)/shard_map/ppermute | solution.py:64
  140.1 8.2 %collective-permute-start.43 = (bf16[32,6656]{1,0:T(8,128)(2,1)S(1)}, bf16[32,6656]{1,0:T(8,128)(2,1)S(1)}, u32[]{:S(2)}, u32[]{:S(2)}) collective-permute-start(bf16[32,6656]{1,0:T(8,128)(2,1)S(1)} %constant_dynamic-update-slice_fusion.16), channel_id=1, source_target_pairs={{0,8},{1,17},{2,10},{3,19},{4,12},{5,21},{6,14},{7,23},{8,0},{9,25... | collective-permute-start | bytes 1277960 | tf_op jit(solution)/shard_map/ppermute | solution.py:64
  144.6 8.2 %collective-permute-start.45 = (bf16[32,6656]{1,0:T(8,128)(2,1)S(1)}, bf16[32,6656]{1,0:T(8,128)(2,1)S(1)}, u32[]{:S(2)}, u32[]{:S(2)}) collective-permute-start(bf16[32,6656]{1,0:T(8,128)(2,1)S(1)} %constant_dynamic-update-slice_fusion.18), channel_id=1, source_target_pairs={{0,8},{1,17},{2,10},{3,19},{4,12},{5,21},{6,14},{7,23},{8,0},{9,25... | collective-permute-start | bytes 1277960 | tf_op jit(solution)/shard_map/ppermute | solution.py:64
  148.3 4.6 %collective-permute-start.44 = (bf16[64,6656]{1,0:T(8,128)(2,1)S(1)}, bf16[64,6656]{1,0:T(8,128)(2,1)S(1)}, u32[]{:S(2)}, u32[]{:S(2)}) collective-permute-start(bf16[64,6656]{1,0:T(8,128)(2,1)S(1)} %constant_dynamic-update-slice_fusion.20), channel_id=1, source_target_pairs={{0,1},{1,0},{2,3},{3,2},{4,5},{5,4},{6,7},{7,6},{8,9},{9,8},{10,11... | collective-permute-start | bytes 2555912 | tf_op jit(solution)/shard_map/ppermute | solution.py:64
  152.9 2.5 %collective-permute-start.46 = (bf16[64,6656]{1,0:T(8,128)(2,1)S(1)}, bf16[64,6656]{1,0:T(8,128)(2,1)S(1)}, u32[]{:S(2)}, u32[]{:S(2)}) collective-permute-start(bf16[64,6656]{1,0:T(8,128)(2,1)S(1)} %constant_dynamic-update-slice_fusion.22), channel_id=1, source_target_pairs={{0,1},{1,0},{2,3},{3,2},{4,5},{5,4},{6,7},{7,6},{8,9},{9,8},{10,11... | collective-permute-start | bytes 2555912 | tf_op jit(solution)/shard_map/ppermute | solution.py:64
  158.2 1.5 collective-permute-start.47
  159.7 4.4 %collective-permute-start.48 = (bf16[32,1024]{1,0:T(8,128)(2,1)S(1)}, bf16[32,1024]{1,0:T(8,128)(2,1)S(1)}, u32[]{:S(2)}, u32[]{:S(2)}) collective-permute-start(bf16[32,1024]{1,0:T(8,128)(2,1)S(1)} %fusion.71), channel_id=1, source_target_pairs={{0,2},{1,3},{2,0},{3,1},{4,6},{5,7},{6,4},{7,5},{8,10},{9,11},{10,... | collective-permute-start | bytes 196616 | tf_op jit(solution)/shard_map/ppermute | solution.py:64
  164.2 5.9 %collective-permute-start.49 = (bf16[16,2048]{1,0:T(8,128)(2,1)S(1)}, bf16[16,2048]{1,0:T(8,128)(2,1)S(1)}, u32[]{:S(2)}, u32[]{:S(2)}) collective-permute-start(bf16[16,2048]{1,0:T(8,128)(2,1)S(1)} %fusion.70), channel_id=1, source_target_pairs={{0,4},{1,5},{2,6},{3,7},{4,0},{5,1},{6,2},{7,3},{8,12},{9,13},{10,... | collective-permute-start | bytes 196616 | tf_op jit(solution)/shard_map/ppermute | solution.py:64

commit v3 on v2

v3 whole, which is shorter than its diff:
```python
import functools

import jax
import jax.numpy as jnp
import numpy as np
from jax import lax
from jax.experimental import pallas as pl
from jax.experimental.pallas import tpu as pltpu
from jax.sharding import PartitionSpec as P

VMEM_BYTES = 40 * 2**20
SHARES = (3, 4, 4, 3, 2)
ORDER = (1, 3, 1, 3, 2, 1, 4, 2, 3, 1, 0, 2, 1, 4, 3, 0, 2, 1, 3, 4, 2, 0, 1, 4, 3, 0, 2, 1, 4, 3, 0, 2, 4, 1, 3, 0, 4, 2, 3, 0, 1, 4, 2, 0, 3, 4, 2, 0, 4, 0)


def step_order(chunks, steps):
    if len(ORDER) == chunks * steps:
        return ORDER
    return [c for t in range(steps + 2 * chunks) for c in range(chunks) if 0 <= t - 2 * c < steps]


def cut(weight, start, width):
    return lax.slice_in_dim(weight, start, start + width, axis=1)


def block_width(width, most):
    for blocks in range(1, width // 128 + 1):
        if width % (128 * blocks) == 0 and width // blocks <= most:
            return width // blocks
    return width


def gate_up_kernel(start, x_ref, gate_ref, up_ref, keep_ref, send_ref, held, arrived):
    step = pl.program_id(0)
    block = keep_ref.shape[2]
    half = keep_ref.shape[1]

    def copy(n, k):
        columns = pl.ds(pl.multiple_of(start + n * block, 128), block)
        return pltpu.make_async_copy((gate_ref, up_ref)[k].at[:, columns], held.at[n, k], arrived.at[n, k])

    @pl.when(step == 0)
    def _():
        for n in range(held.shape[0]):
            for k in range(2):
                copy(n, k).start()

    for k in range(2):
        copy(step, k).wait()
        part = jnp.dot(x_ref[...], held[step, k], preferred_element_type=jnp.float32).astype(jnp.bfloat16)
        keep_ref[k] = part[:half]
        send_ref[k] = part[half:]


def gate_up(x, gate_weight, up_weight, start, width):
    tokens, depth = x.shape
    block = block_width(width, 1664)
    blocks = width // block
    out_spec = pl.BlockSpec((2, tokens // 2, block), lambda n: (0, 0, n))
    out_shape = jax.ShapeDtypeStruct((2, tokens // 2, width), jnp.bfloat16)
    return pl.pallas_call(
        functools.partial(gate_up_kernel, start),
        grid=(blocks,),
        in_specs=[
            pl.BlockSpec((tokens, depth), lambda n: (0, 0)),
            pl.BlockSpec(memory_space=pl.ANY),
            pl.BlockSpec(memory_space=pl.ANY),
        ],
        out_specs=[out_spec, out_spec],
        out_shape=[out_shape, out_shape],
        scratch_shapes=[
            pltpu.VMEM((blocks, 2, depth, block), jnp.bfloat16),
            pltpu.SemaphoreType.DMA((blocks, 2)),
        ],
        compiler_params=pltpu.CompilerParams(vmem_limit_bytes=VMEM_BYTES),
        cost_estimate=pl.CostEstimate(flops=0, bytes_accessed=0, transcendentals=0),
    )(x, gate_weight, up_weight)


def down(own, other, down_weight, before, start):
    hidden = jnp.concatenate([own, other], 0)
    weight = cut(down_weight, start, own.shape[1])
    return before + lax.dot_general(
        hidden, weight, (((1,), (1,)), ((), ())), preferred_element_type=jnp.float32
    )


def add_halves(keep, received, axis):
    half = keep.shape[axis] // 2
    sides = []
    for k in range(2):
        kept = lax.slice_in_dim(keep, k * half, (k + 1) * half, axis=axis).astype(jnp.float32)
        came = lax.slice_in_dim(received, k * half, (k + 1) * half, axis=axis).astype(jnp.float32)
        sides.append((kept + came).astype(jnp.bfloat16))
    return sides


def on_device(n_row, n_col, tokens, gate_weight, up_weight, down_weight):
    batches, local_tokens, local_features = tokens.shape
    own_tokens = batches * local_tokens
    all_tokens = own_tokens * n_col
    features, units = gate_weight.shape
    per_device = own_tokens // n_row
    row, col = lax.axis_index("row"), lax.axis_index("col")
    device = row * n_col + col
    core = 1
    col_bits = [1 << k for k in range(1, n_col.bit_length() - 1)]
    row_bits = [n_col << k for k in range(n_row.bit_length() - 1)]
    orders = (row_bits + col_bits, row_bits[::-1] + col_bits[::-1])
    stages = list(zip(*orders))

    def swap(value, bits):
        pairs = [(d, d ^ bits[d & core]) for d in range(n_row * n_col)]
        return lax.ppermute(value, ("row", "col"), pairs)

    on_upper = (col & core) != 0
    others = n_col // 2

    def turn(blocks):
        for k in range(others.bit_length() - 1):
            turned = jnp.stack([blocks[i ^ (1 << k)] for i in range(others)])
            blocks = jnp.where((col & (2 << k)) != 0, turned, blocks)
        return blocks

    def exchange(blocks):
        return [blocks[0]] + [swap(blocks[s], (2 * s, 2 * s)) for s in range(1, others)]

    x = tokens.reshape(own_tokens, local_features)
    lower, upper = (
        jnp.stack([cut(x, (2 * i + k) * features, features) for i in range(others)]) for k in range(2)
    )
    keep, send = jnp.where(on_upper, upper, lower), jnp.where(on_upper, lower, upper)
    x = jnp.concatenate([keep, swap(send, (core, core))], 1)
    x = jnp.concatenate(exchange(turn(x)), 0)

    weight = {core: own_tokens}
    weight.update({bit: bit * own_tokens for bit in col_bits})
    weight.update({bit: bit // n_col * per_device for bit in row_bits})

    def half_source(order):
        rows = np.zeros(1, np.int32)
        for bit in order:
            rows = (rows[:, None] + np.array([0, weight[bit]])).reshape(-1)
        return (rows[:, None] + np.arange(per_device)).reshape(-1)

    own_first = [
        np.concatenate([half_source(orders[k]), weight[core] + half_source(orders[1 - k])])
        for k in range(2)
    ]
    source = jnp.where(on_upper, *(jnp.asarray(own_first[k], jnp.int32) for k in (1, 0)))
    lasts = [jnp.where((device & o[-1]) != 0, weight[o[-1]], 0) for o in orders]
    own_last, other_last = jnp.where(on_upper, lasts[1], lasts[0]), jnp.where(on_upper, *lasts)
    is_own = np.arange(all_tokens) < all_tokens // 2
    source = source ^ (row * per_device) ^ jnp.where(is_own, own_last, other_last)
    pick = source[:, None] == lax.broadcasted_iota(jnp.int32, (all_tokens, all_tokens), 1)
    x = jnp.dot(pick.astype(jnp.bfloat16), x, preferred_element_type=jnp.float32).astype(jnp.bfloat16)

    total = [jnp.zeros((all_tokens, features), jnp.float32)]
    last = [x]

    def after(*values):
        return lax.optimization_barrier((values, last[0]))[0]

    def steps(start, width):
        (x_now,) = after(x)
        keep, send = gate_up(x_now, gate_weight, up_weight, start, width)
        last[0] = send
        received = swap(send, (core, core))
        yield
        for n, bits in enumerate(stages[:-1]):
            keep, send = add_halves(*after(keep, received), 1)
            last[0] = send
            received = swap(send, bits)
            yield
        keep, received = after(keep, received)
        whole = (keep.astype(jnp.float32) + received.astype(jnp.float32)).astype(jnp.bfloat16)
        last[0] = whole
        received = swap(whole, stages[-1])
        yield
        whole, received = after(whole, received)
        both = whole.astype(jnp.float32) + received.astype(jnp.float32)
        hidden = (jax.nn.silu(both[0]) * both[1]).astype(jnp.bfloat16)
        for bits in stages[-2::-1]:
            last[0] = hidden
            received = swap(hidden, bits)
            yield
            hidden = jnp.concatenate(after(hidden, received), 0)
        last[0] = hidden
        other = swap(hidden, (core, core))
        yield
        own, other = after(hidden, other)
        total[0] = last[0] = down(own, other, down_weight, total[0], start)

    share = units // sum(SHARES)
    ends = np.cumsum(SHARES) * share
    running = [steps(int(end) - n * share, n * share) for n, end in zip(SHARES, ends)]
    for chunk in step_order(len(SHARES), 2 + 2 * len(stages)):
        next(running[chunk], None)

    out = lax.dot_general(
        pick.astype(jnp.float32), total[0], (((0,), (0,)), ((), ())),
        precision=lax.Precision.HIGHEST, preferred_element_type=jnp.float32,
    ).astype(jnp.bfloat16)

    out = jnp.stack(exchange(out.reshape(others, 2 * own_tokens, features)))
    keep, came = out[:, :own_tokens], swap(out[:, own_tokens:], (core, core))
    lower, upper = turn(jnp.where(on_upper, came, keep)), turn(jnp.where(on_upper, keep, came))
    out = jnp.concatenate([side[i] for i in range(others) for side in (lower, upper)], 1)
    return out.reshape(batches, local_tokens, local_features)


def solution(mesh):
    in_specs = (
        P(None, "col", "row"),
        P(("row", "col"), None),
        P(("row", "col"), None),
        P(("row", "col"), None),
    )
    out_specs = P(None, "col", "row")
    body = functools.partial(on_device, mesh.shape["row"], mesh.shape["col"])
    return jax.shard_map(body, mesh=mesh, in_specs=in_specs, out_specs=out_specs, check_vma=False)
```

time: 171 us -> 152 us (0.89)
  waiting for transfers between devices: 79.6 us -> 49.9 us
  matrix products: 43.9 us -> 15.9 us
  Pallas kernels: 0 us -> 23.8 us
  starting transfers between devices: 37.9 us -> 54.8 us
  other arithmetic: 7.09 us -> 3.72 us
    dot_general x8 -> x0, matrix products: 32.5 us -> none  [gate_up(): jnp.dot(x, lax.slice_in_dim(weight, start, start + width, axis=1), prefer...]
    ppermute x50 -> x53, waiting for transfers between devices: 79.6 us -> 49.9 us  [swap(): return lax.ppermute(value, ('row', 'col'), pairs)]
    pallas_call x0 -> x5, Pallas kernels: none -> 23.8 us  [gate_up(): pl.pallas_call(functools.partial(gate_up_kernel, start), grid=(blocks,),...]
    ppermute x50 -> x53, starting transfers between devices: 37.9 us -> 54.8 us  [swap(): return lax.ppermute(value, ('row', 'col'), pairs)]
    dot_general x4 -> x5, matrix products: 10.7 us -> 15.3 us  [down(): lax.dot_general(hidden, weight, (((1,), (1,)), ((), ())), preferred_eleme...]
    another operation x15 -> x1, other arithmetic: 2.39 us -> 0.02 us  [on_device(): out = jnp.stack(exchange(out.reshape(others, 2 * own_tokens, features)))]
  transfers between devices with their start and end apart: 50 -> 53, of which waited for: 27 -> 22; matrix products, arithmetic and copies ran while one was open for 23% -> 12% of each run, Pallas kernels for 0% -> 12%
where the time goes in v3:
time: 152 us
  starting transfers between devices  54.8 us (36%)
  waiting for transfers between devices  49.9 us (33%)
  Pallas kernels  23.8 us (16%)
  matrix products  15.9 us (10%)
  other arithmetic  3.72 us (2%)
  local copies, waits for them, and re-layouts  2.75 us (2%)
    ppermute x53, starting transfers between devices, swap(): return lax.ppermute(value, ('row', 'col'), pairs)  54.8 us
    ppermute x53, waiting for transfers between devices, swap(): return lax.ppermute(value, ('row', 'col'), pairs)  49.9 us
    pallas_call x5, Pallas kernels, gate_up(): pl.pallas_call(functools.partial(gate_up_kernel, start), grid=(blocks,),...  23.8 us
    dot_general x5, matrix products, down(): lax.dot_general(hidden, weight, (((1,), (1,)), ((), ())), preferred_eleme...  15.3 us
  transfers between devices with their start and end apart: 53, of which 22 were waited for; matrix products, arithmetic and copies ran while one was open for 12% of the time, Pallas kernels for 12%

profile of v3, /device:TPU:0, one launch (start us, length us, event | category | flops | bytes accessed | tf_op | source)
XLA Modules:
  0.0 151.7 jit_solution(6112903514162418040)
XLA Ops:
  0.0 0.9 slice_bitcast_fusion.30
  1.4 0.9 collective-permute-done
  2.5 5.0 %collective-permute-start.3 = (bf16[32,512]{1,0:T(8,128)(2,1)S(1)}, bf16[32,512]{1,0:T(8,128)(2,1)S(1)}, u32[]{:S(2)}, u32[]{:S(2)}) collective-permute-start(bf16[32,512]{1,0:T(8,128)(2,1)S(1)} %get-tuple-element.252), channel_id=1, source_target_pairs={{0,6},{1,7},{2,4},{3,5},{4,2},{5,3},{6,0},{7,1},{8,14},{9,15},{10,... | collective-permute-start | bytes 98312 | tf_op jit(solution)/shard_map/ppermute | solution.py:114
  7.5 0.6 collective-permute-start.1
  8.1 1.3 collective-permute-done.3
  9.4 2.9 %collective-permute-done.2 = bf16[32,512]{1,0:T(8,128)(2,1)S(1)} collective-permute-done((bf16[32,512]{1,0:T(8,128)(2,1)S(1)}, bf16[32,512]{1,0:T(8,128)(2,1)S(1)}, u32[]{:S(2)}, u32[]{:S(2)}) %collective-permute-start.2) | collective-permute-done | bytes 32800 | tf_op jit(solution)/shard_map/ppermute | solution.py:114
  12.5 5.5 %shard_map.73 = (bf16[2,64,6656]{2,1,0:T(8,128)(2,1)S(1)}, bf16[2,64,6656]{2,1,0:T(8,128)(2,1)S(1)}) custom-call(bf16[128,512]{1,0:T(8,128)(2,1)S(1)} %convolution_convert_fusion.1.x_ref, bf16[512,26624]{1,0:T(8,128)(2,1)} %gate_ref.9, bf16[512,26624]{1,0:T(8,128)(2,1)} %up_ref.9), custom_call_target="tpu_custom_call" | custom-call | tf_op jit(solution)/shard_map/pallas_call | solution.py:61
  18.1 4.5 %shard_map.74 = (bf16[2,64,4992]{2,1,0:T(8,128)(2,1)S(1)}, bf16[2,64,4992]{2,1,0:T(8,128)(2,1)S(1)}) custom-call(bf16[128,512]{1,0:T(8,128)(2,1)S(1)} %convolution_convert_fusion.1.x_ref, bf16[512,26624]{1,0:T(8,128)(2,1)} %gate_ref.9, bf16[512,26624]{1,0:T(8,128)(2,1)} %up_ref.9), custom_call_target="tpu_custom_call" | custom-call | tf_op jit(solution)/shard_map/pallas_call | solution.py:61
  22.7 0.5 collective-permute-start.6
  23.6 1.6 %collective-permute-start.5 = (bf16[2,32,6656]{2,1,0:T(8,128)(2,1)S(1)}, bf16[2,32,6656]{2,1,0:T(8,128)(2,1)S(1)}, u32[]{:S(2)}, u32[]{:S(2)}) collective-permute-start(bf16[2,32,6656]{2,1,0:T(8,128)(2,1)S(1)} %get-tuple-element.217), channel_id=1, source_target_pairs={{0,8},{1,17},{2,10},{3,19},{4,12},{5,21},{6,14},{7,23},{8,0},{9,25... | collective-permute-start | bytes 2555912 | tf_op jit(solution)/shard_map/ppermute | solution.py:114
  25.2 0.7 collective-permute-done.6
  26.2 5.5 %shard_map.75 = (bf16[2,64,6656]{2,1,0:T(8,128)(2,1)S(1)}, bf16[2,64,6656]{2,1,0:T(8,128)(2,1)S(1)}) custom-call(bf16[128,512]{1,0:T(8,128)(2,1)S(1)} %convolution_convert_fusion.1.x_ref, bf16[512,26624]{1,0:T(8,128)(2,1)} %gate_ref.9, bf16[512,26624]{1,0:T(8,128)(2,1)} %up_ref.9), custom_call_target="tpu_custom_call" | custom-call | tf_op jit(solution)/shard_map/pallas_call | solution.py:61
  32.2 1.5 collective-permute-start.8
  33.7 2.7 %collective-permute-done.5 = bf16[2,32,6656]{2,1,0:T(8,128)(2,1)S(1)} collective-permute-done((bf16[2,32,6656]{2,1,0:T(8,128)(2,1)S(1)}, bf16[2,32,6656]{2,1,0:T(8,128)(2,1)S(1)}, u32[]{:S(2)}, u32[]{:S(2)}) %collective-permute-start.5) | collective-permute-done | bytes 852000 | tf_op jit(solution)/shard_map/ppermute | solution.py:114
  36.6 1.6 %collective-permute-start.7 = (bf16[2,16,6656]{2,1,0:T(8,128)(2,1)S(1)}, bf16[2,16,6656]{2,1,0:T(8,128)(2,1)S(1)}, u32[]{:S(2)}, u32[]{:S(2)}) collective-permute-start(bf16[2,16,6656]{2,1,0:T(8,128)(2,1)S(1)} %get-tuple-element.227), channel_id=1, source_target_pairs={{0,16},{1,9},{2,18},{3,11},{4,20},{5,13},{6,22},{7,15},{8,24},{9,1... | collective-permute-start | bytes 1277960 | tf_op jit(solution)/shard_map/ppermute | solution.py:114
  38.2 3.5 %shard_map.76 = (bf16[2,64,3328]{2,1,0:T(8,128)(2,1)S(1)}, bf16[2,64,3328]{2,1,0:T(8,128)(2,1)S(1)}) custom-call(bf16[128,512]{1,0:T(8,128)(2,1)S(1)} %convolution_convert_fusion.1.x_ref, bf16[512,26624]{1,0:T(8,128)(2,1)} %gate_ref.9, bf16[512,26624]{1,0:T(8,128)(2,1)} %up_ref.9), custom_call_target="tpu_custom_call" | custom-call | tf_op jit(solution)/shard_map/pallas_call | solution.py:61
  42.2 1.6 %collective-permute-start.11 = (bf16[2,32,6656]{2,1,0:T(8,128)(2,1)S(1)}, bf16[2,32,6656]{2,1,0:T(8,128)(2,1)S(1)}, u32[]{:S(2)}, u32[]{:S(2)}) collective-permute-start(bf16[2,32,6656]{2,1,0:T(8,128)(2,1)S(1)} %get-tuple-element.216), channel_id=1, source_target_pairs={{0,8},{1,17},{2,10},{3,19},{4,12},{5,21},{6,14},{7,23},{8,0},{9,25... | collective-permute-start | bytes 2555912 | tf_op jit(solution)/shard_map/ppermute | solution.py:114
  43.7 4.1 %collective-permute-done.8 = bf16[2,32,4992]{2,1,0:T(8,128)(2,1)S(1)} collective-permute-done((bf16[2,32,4992]{2,1,0:T(8,128)(2,1)S(1)}, bf16[2,32,4992]{2,1,0:T(8,128)(2,1)S(1)}, u32[]{:S(2)}, u32[]{:S(2)}) %collective-permute-start.8) | collective-permute-done | bytes 639008 | tf_op jit(solution)/shard_map/ppermute | solution.py:114
  48.6 2.5 %collective-permute-start.15 = (bf16[2,16,4992]{2,1,0:T(8,128)(2,1)S(1)}, bf16[2,16,4992]{2,1,0:T(8,128)(2,1)S(1)}, u32[]{:S(2)}, u32[]{:S(2)}) collective-permute-start(bf16[2,16,4992]{2,1,0:T(8,128)(2,1)S(1)} %get-tuple-element.232), channel_id=1, source_target_pairs={{0,16},{1,9},{2,18},{3,11},{4,20},{5,13},{6,22},{7,15},{8,24},{9,1... | collective-permute-start | bytes 958472 | tf_op jit(solution)/shard_map/ppermute | solution.py:114
  51.2 4.7 %shard_map.77 = (bf16[2,64,4992]{2,1,0:T(8,128)(2,1)S(1)}, bf16[2,64,4992]{2,1,0:T(8,128)(2,1)S(1)}) custom-call(bf16[128,512]{1,0:T(8,128)(2,1)S(1)} %convolution_convert_fusion.1.x_ref, bf16[512,26624]{1,0:T(8,128)(2,1)} %gate_ref.9, bf16[512,26624]{1,0:T(8,128)(2,1)} %up_ref.9), custom_call_target="tpu_custom_call" | custom-call | tf_op jit(solution)/shard_map/pallas_call | solution.py:61
  55.9 4.4 %collective-permute-done.11 = bf16[2,32,6656]{2,1,0:T(8,128)(2,1)S(1)} collective-permute-done((bf16[2,32,6656]{2,1,0:T(8,128)(2,1)S(1)}, bf16[2,32,6656]{2,1,0:T(8,128)(2,1)S(1)}, u32[]{:S(2)}, u32[]{:S(2)}) %collective-permute-start.11) | collective-permute-done | bytes 852000 | tf_op jit(solution)/shard_map/ppermute | solution.py:114
  60.5 1.6 %collective-permute-start.13 = (bf16[2,16,6656]{2,1,0:T(8,128)(2,1)S(1)}, bf16[2,16,6656]{2,1,0:T(8,128)(2,1)S(1)}, u32[]{:S(2)}, u32[]{:S(2)}) collective-permute-start(bf16[2,16,6656]{2,1,0:T(8,128)(2,1)S(1)} %get-tuple-element.226), channel_id=1, source_target_pairs={{0,16},{1,9},{2,18},{3,11},{4,20},{5,13},{6,22},{7,15},{8,24},{9,1... | collective-permute-start | bytes 1277960 | tf_op jit(solution)/shard_map/ppermute | solution.py:114
  62.2 2.1 %collective-permute-start.12 = (bf16[2,8,6656]{2,1,0:T(8,128)(2,1)S(1)}, bf16[2,8,6656]{2,1,0:T(8,128)(2,1)S(1)}, u32[]{:S(2)}, u32[]{:S(2)}) collective-permute-start(bf16[2,8,6656]{2,1,0:T(8,128)(2,1)S(1)} %add_convert_fusion.23), channel_id=1, source_target_pairs={{0,4},{1,3},{2,6},{3,1},{4,0},{5,7},{6,2},{7,5},{8,12},{9,11},{10,... | collective-permute-start | bytes 638984 | tf_op jit(solution)/shard_map/ppermute | solution.py:114
  64.5 1.6 %collective-permute-start.20 = (bf16[2,32,3328]{2,1,0:T(8,128)(2,1)S(1)}, bf16[2,32,3328]{2,1,0:T(8,128)(2,1)S(1)}, u32[]{:S(2)}, u32[]{:S(2)}) collective-permute-start(bf16[2,32,3328]{2,1,0:T(8,128)(2,1)S(1)} %get-tuple-element.224), channel_id=1, source_target_pairs={{0,8},{1,17},{2,10},{3,19},{4,12},{5,21},{6,14},{7,23},{8,0},{9,25... | collective-permute-start | bytes 1277960 | tf_op jit(solution)/shard_map/ppermute | solution.py:114
  66.1 0.6 collective-permute-start.21
  67.0 0.6 collective-permute-start.18
  67.6 5.6 %collective-permute-done.13 = bf16[2,16,6656]{2,1,0:T(8,128)(2,1)S(1)} collective-permute-done((bf16[2,16,6656]{2,1,0:T(8,128)(2,1)S(1)}, bf16[2,16,6656]{2,1,0:T(8,128)(2,1)S(1)}, u32[]{:S(2)}, u32[]{:S(2)}) %collective-permute-start.13) | collective-permute-done | bytes 426016 | tf_op jit(solution)/shard_map/ppermute | solution.py:114
  73.4 5.4 %collective-permute-done.12 = bf16[2,8,6656]{2,1,0:T(8,128)(2,1)S(1)} collective-permute-done((bf16[2,8,6656]{2,1,0:T(8,128)(2,1)S(1)}, bf16[2,8,6656]{2,1,0:T(8,128)(2,1)S(1)}, u32[]{:S(2)}, u32[]{:S(2)}) %collective-permute-start.12) | collective-permute-done | bytes 213024 | tf_op jit(solution)/shard_map/ppermute | solution.py:114
  79.1 2.4 %collective-permute-start.25 = (bf16[2,8,4992]{2,1,0:T(8,128)(2,1)S(1)}, bf16[2,8,4992]{2,1,0:T(8,128)(2,1)S(1)}, u32[]{:S(2)}, u32[]{:S(2)}) collective-permute-start(bf16[2,8,4992]{2,1,0:T(8,128)(2,1)S(1)} %add_convert_fusion.29), channel_id=1, source_target_pairs={{0,4},{1,3},{2,6},{3,1},{4,0},{5,7},{6,2},{7,5},{8,12},{9,11},{10,... | collective-permute-start | bytes 479240 | tf_op jit(solution)/shard_map/ppermute | solution.py:114
  81.6 5.5 %collective-permute-done.19 = bf16[2,8,6656]{2,1,0:T(8,128)(2,1)S(1)} collective-permute-done((bf16[2,8,6656]{2,1,0:T(8,128)(2,1)S(1)}, bf16[2,8,6656]{2,1,0:T(8,128)(2,1)S(1)}, u32[]{:S(2)}, u32[]{:S(2)}) %collective-permute-start.19) | collective-permute-done | bytes 213024 | tf_op jit(solution)/shard_map/ppermute | solution.py:114
  87.8 1.4 collective-permute-start.24
  89.2 1.3 collective-permute-done.17
  90.5 0.8 collective-permute-start.22
  91.3 1.4 collective-permute-start.28
  92.9 0.7 collective-permute-start.32
  93.6 1.3 collective-permute-done.24
  94.9 2.7 %collective-permute-start.31 = (bf16[2,8,4992]{2,1,0:T(8,128)(2,1)S(1)}, bf16[2,8,4992]{2,1,0:T(8,128)(2,1)S(1)}, u32[]{:S(2)}, u32[]{:S(2)}) collective-permute-start(bf16[2,8,4992]{2,1,0:T(8,128)(2,1)S(1)} %get-tuple-element.240), channel_id=1, source_target_pairs={{0,2},{1,5},{2,0},{3,7},{4,6},{5,1},{6,4},{7,3},{8,10},{9,13},{10,... | collective-permute-start | bytes 479240 | tf_op jit(solution)/shard_map/ppermute | solution.py:114
  97.7 3.5 %collective-permute-done.23 = bf16[2,8,6656]{2,1,0:T(8,128)(2,1)S(1)} collective-permute-done((bf16[2,8,6656]{2,1,0:T(8,128)(2,1)S(1)}, bf16[2,8,6656]{2,1,0:T(8,128)(2,1)S(1)}, u32[]{:S(2)}, u32[]{:S(2)}) %collective-permute-start.23) | collective-permute-done | bytes 213024 | tf_op jit(solution)/shard_map/ppermute | solution.py:114
  101.5 0.7 collective-permute-start.27
  102.2 2.3 %collective-permute-start.29 = (bf16[2,8,3328]{2,1,0:T(8,128)(2,1)S(1)}, bf16[2,8,3328]{2,1,0:T(8,128)(2,1)S(1)}, u32[]{:S(2)}, u32[]{:S(2)}) collective-permute-start(bf16[2,8,3328]{2,1,0:T(8,128)(2,1)S(1)} %add_convert_fusion.32), channel_id=1, source_target_pairs={{0,4},{1,3},{2,6},{3,1},{4,0},{5,7},{6,2},{7,5},{8,12},{9,11},{10,... | collective-permute-start | bytes 319496 | tf_op jit(solution)/shard_map/ppermute | solution.py:114
  104.5 2.1 %collective-permute-start.35 = (bf16[16,4992]{1,0:T(8,128)(2,1)S(1)}, bf16[16,4992]{1,0:T(8,128)(2,1)S(1)}, u32[]{:S(2)}, u32[]{:S(2)}) collective-permute-start(bf16[16,4992]{1,0:T(8,128)(2,1)S(1)} %constant_dynamic-update-slice_fusion.4), channel_id=1, source_target_pairs={{0,16},{1,9},{2,18},{3,11},{4,20},{5,13},{6,22},{7,15},{8,24},{9,1... | collective-permute-start | bytes 479240 | tf_op jit(solution)/shard_map/ppermute | solution.py:114
  106.6 1.8 %collective-permute-start.34 = (bf16[2,8,4992]{2,1,0:T(8,128)(2,1)S(1)}, bf16[2,8,4992]{2,1,0:T(8,128)(2,1)S(1)}, u32[]{:S(2)}, u32[]{:S(2)}) collective-permute-start(bf16[2,8,4992]{2,1,0:T(8,128)(2,1)S(1)} %add_convert_fusion.26), channel_id=1, source_target_pairs={{0,4},{1,3},{2,6},{3,1},{4,0},{5,7},{6,2},{7,5},{8,12},{9,11},{10,... | collective-permute-start | bytes 479240 | tf_op jit(solution)/shard_map/ppermute | solution.py:114
  108.4 0.6 collective-permute-done.30
  109.0 1.1 collective-permute-start.38
  110.2 2.9 %collective-permute-start.39 = (bf16[8,3328]{1,0:T(8,128)(2,1)S(1)}, bf16[8,3328]{1,0:T(8,128)(2,1)S(1)}, u32[]{:S(2)}, u32[]{:S(2)}) collective-permute-start(bf16[8,3328]{1,0:T(8,128)(2,1)S(1)} %fusion.60), channel_id=1, source_target_pairs={{0,2},{1,5},{2,0},{3,7},{4,6},{5,1},{6,4},{7,3},{8,10},{9,13},{10,... | collective-permute-start | bytes 159752 | tf_op jit(solution)/shard_map/ppermute | solution.py:114
  113.6 1.0 collective-permute-done.34
  115.2 1.1 collective-permute-start.43
  116.4 1.4 collective-permute-start.42
  117.7 3.7 %collective-permute-done.37 = bf16[32,4992]{1,0:T(8,128)(2,1)S(1)} collective-permute-done((bf16[32,4992]{1,0:T(8,128)(2,1)S(1)}, bf16[32,4992]{1,0:T(8,128)(2,1)S(1)}, u32[]{:S(2)}, u32[]{:S(2)}) %collective-permute-start.37) | collective-permute-done | bytes 319520 | tf_op jit(solution)/shard_map/ppermute | solution.py:114
  121.8 5.4 %fusion.2 = f32[128,512]{1,0:T(8,128)S(1)} fusion(bf16[512,26624]{1,0:T(8,128)(2,1)} %param.10, bf16[64,6656]{1,0:T(8,128)(2,1)S(1)} %collective-permute-done.33, bf16[64,6656]{1,0:T(8,128)(2,1)S(1)} %constant_dynamic-update-slice_fusion.8), kind=kOutput, calls=%fused_computation.2 | convolution fusion | flops 875823104 | bytes 8781824 | tf_op jit(solution)/shard_map/dot_general | solution.py:83
  127.3 1.7 %collective-permute-start.45 = (bf16[32,3328]{1,0:T(8,128)(2,1)S(1)}, bf16[32,3328]{1,0:T(8,128)(2,1)S(1)}, u32[]{:S(2)}, u32[]{:S(2)}) collective-permute-start(bf16[32,3328]{1,0:T(8,128)(2,1)S(1)} %constant_dynamic-update-slice_fusion.20), channel_id=1, source_target_pairs={{0,8},{1,17},{2,10},{3,19},{4,12},{5,21},{6,14},{7,23},{8,0},{9,25... | collective-permute-start | bytes 638984 | tf_op jit(solution)/shard_map/ppermute | solution.py:114
  129.2 1.1 collective-permute-start.47
  130.3 4.4 %fusion.30 = f32[128,512]{1,0:T(8,128)S(1)} fusion(f32[128,512]{1,0:T(8,128)S(1)} %fusion.2, bf16[512,26624]{1,0:T(8,128)(2,1)} %param.10, bf16[64,4992]{1,0:T(8,128)(2,1)S(1)} %collective-permute-done.40, bf16[64,4992]{1,0:T(8,128)(2,1)S(1)} %constant_dynamic-update-slice_fusion.16), kind=kOutput, calls=%fused_computation.32 | convolution fusion | flops 656932864 | bytes 6914048 | tf_op jit(solution)/shard_map/dot_general | solution.py:83
  135.1 2.4 %fusion.22 = f32[128,512]{1,0:T(8,128)S(1)} fusion(f32[128,512]{1,0:T(8,128)S(1)} %fusion.30, bf16[512,26624]{1,0:T(8,128)(2,1)S(1)} %bitcast.118, bf16[64,6656]{1,0:T(8,128)(2,1)S(1)} %collective-permute-done.44, bf16[64,6656]{1,0:T(8,128)(2,1)S(1)} %constant_dynamic-update-slice_fusion.22), kind=kOutput, calls=%fused_computation.30 | convolution fusion | flops 875888640 | bytes 9043968 | tf_op jit(solution)/shard_map/dot_general | solution.py:83
  137.9 1.3 fusion.27
  139.7 1.8 %fusion.35 = f32[128,512]{1,0:T(8,128)S(1)} fusion(f32[128,512]{1,0:T(8,128)S(1)} %fusion.27, bf16[512,26624]{1,0:T(8,128)(2,1)S(1)} %bitcast.118, bf16[64,4992]{1,0:T(8,128)(2,1)S(1)} %collective-permute-done.48, bf16[64,4992]{1,0:T(8,128)(2,1)S(1)} %constant_dynamic-update-slice_fusion.28), kind=kOutput, calls=%fused_computation.33 | convolution fusion | flops 656932864 | bytes 6914048 | tf_op jit(solution)/shard_map/dot_general | solution.py:83
  142.0 1.3 collective-permute-start.51
  143.3 1.5 collective-permute-start.50
  144.8 1.7 %collective-permute-start.49 = (bf16[32,512]{1,0:T(8,128)(2,1)S(1)}, bf16[32,512]{1,0:T(8,128)(2,1)S(1)}, u32[]{:S(2)}, u32[]{:S(2)}) collective-permute-start(bf16[32,512]{1,0:T(8,128)(2,1)S(1)} %get-tuple-element.250), channel_id=1, source_target_pairs={{0,2},{1,3},{2,0},{3,1},{4,6},{5,7},{6,4},{7,5},{8,10},{9,11},{10,... | collective-permute-start | bytes 98312 | tf_op jit(solution)/shard_map/ppermute | solution.py:114
  146.4 1.7 %collective-permute-done.51 = bf16[32,512]{1,0:T(8,128)(2,1)S(1)} collective-permute-done((bf16[32,512]{1,0:T(8,128)(2,1)S(1)}, bf16[32,512]{1,0:T(8,128)(2,1)S(1)}, u32[]{:S(2)}, u32[]{:S(2)}) %collective-permute-start.51) | collective-permute-done | bytes 32800 | tf_op jit(solution)/shard_map/ppermute | solution.py:114
  148.1 0.7 collective-permute-done.50
  149.0 1.2 collective-permute-done.52
  150.5 0.6 copy-done
  151.1 0.6 constant_dynamic-update-slice_fusion.30
  (164 shorter events, 9.9 us)
Async XLA Ops:
  0.0 8.1 %copy-start.1 = (s32[128]{0:T(128)S(1)}, s32[128]{0:T(128)}, u32[]{:S(2)}) copy-start(s32[128]{0:T(128)} %constant.37.clone) | copy-start | bytes 1540
  0.0 8.1 %copy-start.2 = (s32[128]{0:T(128)S(1)}, s32[128]{0:T(128)}, u32[]{:S(2)}) copy-start(s32[128]{0:T(128)} %constant.38.clone) | copy-start | bytes 1540
  0.0 8.1 %copy-start.3 = (pred[128]{0:T(512)(128)(4,1)S(1)}, pred[128]{0:T(512)(128)(4,1)}, u32[]{:S(2)}) copy-start(pred[128]{0:T(512)(128)(4,1)} %constant.39.clone) | copy-start | bytes 388
  0.9 1.4 collective-permute-start
  2.5 6.9 %collective-permute-start.3 = (bf16[32,512]{1,0:T(8,128)(2,1)S(1)}, bf16[32,512]{1,0:T(8,128)(2,1)S(1)}, u32[]{:S(2)}, u32[]{:S(2)}) collective-permute-start(bf16[32,512]{1,0:T(8,128)(2,1)S(1)} %get-tuple-element.252), channel_id=1, source_target_pairs={{0,6},{1,7},{2,4},{3,5},{4,2},{5,3},{6,0},{7,1},{8,14},{9,15},{10,... | collective-permute-start | bytes 98312 | tf_op jit(solution)/shard_map/ppermute | solution.py:114
  7.5 4.8 %collective-permute-start.2 = (bf16[32,512]{1,0:T(8,128)(2,1)S(1)}, bf16[32,512]{1,0:T(8,128)(2,1)S(1)}, u32[]{:S(2)}, u32[]{:S(2)}) collective-permute-start(bf16[32,512]{1,0:T(8,128)(2,1)S(1)} %get-tuple-element.253), channel_id=1, source_target_pairs={{0,4},{1,5},{2,6},{3,7},{4,0},{5,1},{6,2},{7,3},{8,12},{9,13},{10,... | collective-permute-start | bytes 98312 | tf_op jit(solution)/shard_map/ppermute | solution.py:114
  7.5 4.8 %collective-permute-start.1 = (bf16[32,512]{1,0:T(8,128)(2,1)S(1)}, bf16[32,512]{1,0:T(8,128)(2,1)S(1)}, u32[]{:S(2)}, u32[]{:S(2)}) collective-permute-start(bf16[32,512]{1,0:T(8,128)(2,1)S(1)} %get-tuple-element.254), channel_id=1, source_target_pairs={{0,2},{1,3},{2,0},{3,1},{4,6},{5,7},{6,4},{7,5},{8,10},{9,11},{10,... | collective-permute-start | bytes 98312 | tf_op jit(solution)/shard_map/ppermute | solution.py:114
  18.1 5.2 %collective-permute-start.4 = (bf16[2,64,6656]{2,1,0:T(8,128)(2,1)S(1)}, bf16[2,64,6656]{2,1,0:T(8,128)(2,1)S(1)}, u32[]{:S(2)}, u32[]{:S(2)}) collective-permute-start(bf16[2,64,6656]{2,1,0:T(8,128)(2,1)S(1)} %get-tuple-element.112), channel_id=1, source_target_pairs={{0,1},{1,0},{2,3},{3,2},{4,5},{5,4},{6,7},{7,6},{8,9},{9,8},{10,11... | collective-permute-start | bytes 5111816 | tf_op jit(solution)/shard_map/ppermute | solution.py:114
  22.7 3.2 %collective-permute-start.6 = (bf16[2,64,4992]{2,1,0:T(8,128)(2,1)S(1)}, bf16[2,64,4992]{2,1,0:T(8,128)(2,1)S(1)}, u32[]{:S(2)}, u32[]{:S(2)}) collective-permute-start(bf16[2,64,4992]{2,1,0:T(8,128)(2,1)S(1)} %get-tuple-element.114), channel_id=1, source_target_pairs={{0,1},{1,0},{2,3},{3,2},{4,5},{5,4},{6,7},{7,6},{8,9},{9,8},{10,11... | collective-permute-start | bytes 3833864 | tf_op jit(solution)/shard_map/ppermute | solution.py:114
  23.6 12.8 %collective-permute-start.5 = (bf16[2,32,6656]{2,1,0:T(8,128)(2,1)S(1)}, bf16[2,32,6656]{2,1,0:T(8,128)(2,1)S(1)}, u32[]{:S(2)}, u32[]{:S(2)}) collective-permute-start(bf16[2,32,6656]{2,1,0:T(8,128)(2,1)S(1)} %get-tuple-element.217), channel_id=1, source_target_pairs={{0,8},{1,17},{2,10},{3,19},{4,12},{5,21},{6,14},{7,23},{8,0},{9,25... | collective-permute-start | bytes 2555912 | tf_op jit(solution)/shard_map/ppermute | solution.py:114
  31.8 10.0 %collective-permute-start.9 = (bf16[2,64,6656]{2,1,0:T(8,128)(2,1)S(1)}, bf16[2,64,6656]{2,1,0:T(8,128)(2,1)S(1)}, u32[]{:S(2)}, u32[]{:S(2)}) collective-permute-start(bf16[2,64,6656]{2,1,0:T(8,128)(2,1)S(1)} %get-tuple-element.121), channel_id=1, source_target_pairs={{0,1},{1,0},{2,3},{3,2},{4,5},{5,4},{6,7},{7,6},{8,9},{9,8},{10,11... | collective-permute-start | bytes 5111816 | tf_op jit(solution)/shard_map/ppermute | solution.py:114
  32.2 15.6 %collective-permute-start.8 = (bf16[2,32,4992]{2,1,0:T(8,128)(2,1)S(1)}, bf16[2,32,4992]{2,1,0:T(8,128)(2,1)S(1)}, u32[]{:S(2)}, u32[]{:S(2)}) collective-permute-start(bf16[2,32,4992]{2,1,0:T(8,128)(2,1)S(1)} %get-tuple-element.222), channel_id=1, source_target_pairs={{0,8},{1,17},{2,10},{3,19},{4,12},{5,21},{6,14},{7,23},{8,0},{9,25... | collective-permute-start | bytes 1916936 | tf_op jit(solution)/shard_map/ppermute | solution.py:114
  36.6 11.9 %collective-permute-start.7 = (bf16[2,16,6656]{2,1,0:T(8,128)(2,1)S(1)}, bf16[2,16,6656]{2,1,0:T(8,128)(2,1)S(1)}, u32[]{:S(2)}, u32[]{:S(2)}) collective-permute-start(bf16[2,16,6656]{2,1,0:T(8,128)(2,1)S(1)} %get-tuple-element.227), channel_id=1, source_target_pairs={{0,16},{1,9},{2,18},{3,11},{4,20},{5,13},{6,22},{7,15},{8,24},{9,1... | collective-permute-start | bytes 1277960 | tf_op jit(solution)/shard_map/ppermute | solution.py:114
  41.7 22.6 %collective-permute-start.16 = (bf16[2,64,3328]{2,1,0:T(8,128)(2,1)S(1)}, bf16[2,64,3328]{2,1,0:T(8,128)(2,1)S(1)}, u32[]{:S(2)}, u32[]{:S(2)}) collective-permute-start(bf16[2,64,3328]{2,1,0:T(8,128)(2,1)S(1)} %get-tuple-element.126), channel_id=1, source_target_pairs={{0,1},{1,0},{2,3},{3,2},{4,5},{5,4},{6,7},{7,6},{8,9},{9,8},{10,11... | collective-permute-start | bytes 2555912 | tf_op jit(solution)/shard_map/ppermute | solution.py:114
  42.2 18.2 %collective-permute-start.11 = (bf16[2,32,6656]{2,1,0:T(8,128)(2,1)S(1)}, bf16[2,32,6656]{2,1,0:T(8,128)(2,1)S(1)}, u32[]{:S(2)}, u32[]{:S(2)}) collective-permute-start(bf16[2,32,6656]{2,1,0:T(8,128)(2,1)S(1)} %get-tuple-element.216), channel_id=1, source_target_pairs={{0,8},{1,17},{2,10},{3,19},{4,12},{5,21},{6,14},{7,23},{8,0},{9,25... | collective-permute-start | bytes 2555912 | tf_op jit(solution)/shard_map/ppermute | solution.py:114
  48.5 13.6 %collective-permute-start.10 = (bf16[2,8,6656]{2,1,0:T(8,128)(2,1)S(1)}, bf16[2,8,6656]{2,1,0:T(8,128)(2,1)S(1)}, u32[]{:S(2)}, u32[]{:S(2)}) collective-permute-start(bf16[2,8,6656]{2,1,0:T(8,128)(2,1)S(1)} %get-tuple-element.237), channel_id=1, source_target_pairs={{0,2},{1,5},{2,0},{3,7},{4,6},{5,1},{6,4},{7,3},{8,10},{9,13},{10,... | collective-permute-start | bytes 638984 | tf_op jit(solution)/shard_map/ppermute | solution.py:114
  48.6 17.4 %collective-permute-start.15 = (bf16[2,16,4992]{2,1,0:T(8,128)(2,1)S(1)}, bf16[2,16,4992]{2,1,0:T(8,128)(2,1)S(1)}, u32[]{:S(2)}, u32[]{:S(2)}) collective-permute-start(bf16[2,16,4992]{2,1,0:T(8,128)(2,1)S(1)} %get-tuple-element.232), channel_id=1, source_target_pairs={{0,16},{1,9},{2,18},{3,11},{4,20},{5,13},{6,22},{7,15},{8,24},{9,1... | collective-permute-start | bytes 958472 | tf_op jit(solution)/shard_map/ppermute | solution.py:114
  55.8 10.9 %collective-permute-start.14 = (bf16[2,64,4992]{2,1,0:T(8,128)(2,1)S(1)}, bf16[2,64,4992]{2,1,0:T(8,128)(2,1)S(1)}, u32[]{:S(2)}, u32[]{:S(2)}) collective-permute-start(bf16[2,64,4992]{2,1,0:T(8,128)(2,1)S(1)} %get-tuple-element.134), channel_id=1, source_target_pairs={{0,1},{1,0},{2,3},{3,2},{4,5},{5,4},{6,7},{7,6},{8,9},{9,8},{10,11... | collective-permute-start | bytes 3833864 | tf_op jit(solution)/shard_map/ppermute | solution.py:114
  60.5 12.7 %collective-permute-start.13 = (bf16[2,16,6656]{2,1,0:T(8,128)(2,1)S(1)}, bf16[2,16,6656]{2,1,0:T(8,128)(2,1)S(1)}, u32[]{:S(2)}, u32[]{:S(2)}) collective-permute-start(bf16[2,16,6656]{2,1,0:T(8,128)(2,1)S(1)} %get-tuple-element.226), channel_id=1, source_target_pairs={{0,16},{1,9},{2,18},{3,11},{4,20},{5,13},{6,22},{7,15},{8,24},{9,1... | collective-permute-start | bytes 1277960 | tf_op jit(solution)/shard_map/ppermute | solution.py:114
  62.1 72.9 %slice-start = ((s8[27262976]{0:T(1024)(128)(4,1)}), s8[2097152]{0:T(1024)(128)(4,1)S(1)}, s32[]{:S(2)}) async-start(s8[27262976]{0:T(1024)(128)(4,1)} %bitcast.117), calls=%async_computation | async-start | bytes 4194304
  62.2 16.6 %collective-permute-start.12 = (bf16[2,8,6656]{2,1,0:T(8,128)(2,1)S(1)}, bf16[2,8,6656]{2,1,0:T(8,128)(2,1)S(1)}, u32[]{:S(2)}, u32[]{:S(2)}) collective-permute-start(bf16[2,8,6656]{2,1,0:T(8,128)(2,1)S(1)} %add_convert_fusion.23), channel_id=1, source_target_pairs={{0,4},{1,3},{2,6},{3,1},{4,0},{5,7},{6,2},{7,5},{8,12},{9,11},{10,... | collective-permute-start | bytes 638984 | tf_op jit(solution)/shard_map/ppermute | solution.py:114
  64.5 17.0 %collective-permute-start.20 = (bf16[2,32,3328]{2,1,0:T(8,128)(2,1)S(1)}, bf16[2,32,3328]{2,1,0:T(8,128)(2,1)S(1)}, u32[]{:S(2)}, u32[]{:S(2)}) collective-permute-start(bf16[2,32,3328]{2,1,0:T(8,128)(2,1)S(1)} %get-tuple-element.224), channel_id=1, source_target_pairs={{0,8},{1,17},{2,10},{3,19},{4,12},{5,21},{6,14},{7,23},{8,0},{9,25... | collective-permute-start | bytes 1277960 | tf_op jit(solution)/shard_map/ppermute | solution.py:114
  66.1 12.9 %collective-permute-start.21 = (bf16[2,8,4992]{2,1,0:T(8,128)(2,1)S(1)}, bf16[2,8,4992]{2,1,0:T(8,128)(2,1)S(1)}, u32[]{:S(2)}, u32[]{:S(2)}) collective-permute-start(bf16[2,8,4992]{2,1,0:T(8,128)(2,1)S(1)} %get-tuple-element.242), channel_id=1, source_target_pairs={{0,2},{1,5},{2,0},{3,7},{4,6},{5,1},{6,4},{7,3},{8,10},{9,13},{10,... | collective-permute-start | bytes 479240 | tf_op jit(solution)/shard_map/ppermute | solution.py:114
  66.7 68.3 %slice-start.1 = ((s8[27262976]{0:T(1024)(128)(4,1)}), s8[4194304]{0:T(1024)(128)(4,1)S(1)}, s32[]{:S(2)}) async-start(s8[27262976]{0:T(1024)(128)(4,1)} %bitcast.117), calls=%async_computation.1 | async-start | bytes 8388608
  67.0 20.6 %collective-permute-start.18 = (bf16[2,32,4992]{2,1,0:T(8,128)(2,1)S(1)}, bf16[2,32,4992]{2,1,0:T(8,128)(2,1)S(1)}, u32[]{:S(2)}, u32[]{:S(2)}) collective-permute-start(bf16[2,32,4992]{2,1,0:T(8,128)(2,1)S(1)} %get-tuple-element.220), channel_id=1, source_target_pairs={{0,8},{1,17},{2,10},{3,19},{4,12},{5,21},{6,14},{7,23},{8,0},{9,25... | collective-permute-start | bytes 1916936 | tf_op jit(solution)/shard_map/ppermute | solution.py:114
  73.3 13.9 %collective-permute-start.19 = (bf16[2,8,6656]{2,1,0:T(8,128)(2,1)S(1)}, bf16[2,8,6656]{2,1,0:T(8,128)(2,1)S(1)}, u32[]{:S(2)}, u32[]{:S(2)}) collective-permute-start(bf16[2,8,6656]{2,1,0:T(8,128)(2,1)S(1)} %get-tuple-element.236), channel_id=1, source_target_pairs={{0,2},{1,5},{2,0},{3,7},{4,6},{5,1},{6,4},{7,3},{8,10},{9,13},{10,... | collective-permute-start | bytes 638984 | tf_op jit(solution)/shard_map/ppermute | solution.py:114
  78.9 11.6 %collective-permute-start.17 = (bf16[8,6656]{1,0:T(8,128)(2,1)S(1)}, bf16[8,6656]{1,0:T(8,128)(2,1)S(1)}, u32[]{:S(2)}, u32[]{:S(2)}) collective-permute-start(bf16[8,6656]{1,0:T(8,128)(2,1)S(1)} %fusion.46), channel_id=1, source_target_pairs={{0,2},{1,5},{2,0},{3,7},{4,6},{5,1},{6,4},{7,3},{8,10},{9,13},{10,... | collective-permute-start | bytes 319496 | tf_op jit(solution)/shard_map/ppermute | solution.py:114
  79.1 13.7 %collective-permute-start.25 = (bf16[2,8,4992]{2,1,0:T(8,128)(2,1)S(1)}, bf16[2,8,4992]{2,1,0:T(8,128)(2,1)S(1)}, u32[]{:S(2)}, u32[]{:S(2)}) collective-permute-start(bf16[2,8,4992]{2,1,0:T(8,128)(2,1)S(1)} %add_convert_fusion.29), channel_id=1, source_target_pairs={{0,4},{1,3},{2,6},{3,1},{4,0},{5,7},{6,2},{7,5},{8,12},{9,11},{10,... | collective-permute-start | bytes 479240 | tf_op jit(solution)/shard_map/ppermute | solution.py:114
  81.5 9.7 %collective-permute-start.26 = (bf16[2,16,3328]{2,1,0:T(8,128)(2,1)S(1)}, bf16[2,16,3328]{2,1,0:T(8,128)(2,1)S(1)}, u32[]{:S(2)}, u32[]{:S(2)}) collective-permute-start(bf16[2,16,3328]{2,1,0:T(8,128)(2,1)S(1)} %get-tuple-element.234), channel_id=1, source_target_pairs={{0,16},{1,9},{2,18},{3,11},{4,20},{5,13},{6,22},{7,15},{8,24},{9,1... | collective-permute-start | bytes 638984 | tf_op jit(solution)/shard_map/ppermute | solution.py:114
  87.2 14.0 %collective-permute-start.23 = (bf16[2,8,6656]{2,1,0:T(8,128)(2,1)S(1)}, bf16[2,8,6656]{2,1,0:T(8,128)(2,1)S(1)}, u32[]{:S(2)}, u32[]{:S(2)}) collective-permute-start(bf16[2,8,6656]{2,1,0:T(8,128)(2,1)S(1)} %add_convert_fusion.19), channel_id=1, source_target_pairs={{0,4},{1,3},{2,6},{3,1},{4,0},{5,7},{6,2},{7,5},{8,12},{9,11},{10,... | collective-permute-start | bytes 638984 | tf_op jit(solution)/shard_map/ppermute | solution.py:114
  87.8 7.1 %collective-permute-start.24 = (bf16[2,16,4992]{2,1,0:T(8,128)(2,1)S(1)}, bf16[2,16,4992]{2,1,0:T(8,128)(2,1)S(1)}, u32[]{:S(2)}, u32[]{:S(2)}) collective-permute-start(bf16[2,16,4992]{2,1,0:T(8,128)(2,1)S(1)} %get-tuple-element.230), channel_id=1, source_target_pairs={{0,16},{1,9},{2,18},{3,11},{4,20},{5,13},{6,22},{7,15},{8,24},{9,1... | collective-permute-start | bytes 958472 | tf_op jit(solution)/shard_map/ppermute | solution.py:114
  90.5 10.9 %collective-permute-start.22 = (bf16[16,6656]{1,0:T(8,128)(2,1)S(1)}, bf16[16,6656]{1,0:T(8,128)(2,1)S(1)}, u32[]{:S(2)}, u32[]{:S(2)}) collective-permute-start(bf16[16,6656]{1,0:T(8,128)(2,1)S(1)} %constant_dynamic-update-slice_fusion), channel_id=1, source_target_pairs={{0,16},{1,9},{2,18},{3,11},{4,20},{5,13},{6,22},{7,15},{8,24},{9,1... | collective-permute-start | bytes 638984 | tf_op jit(solution)/shard_map/ppermute | solution.py:114
  91.3 43.8 %slice-start.2 = ((s8[27262976]{0:T(1024)(128)(4,1)}), s8[4194304]{0:T(1024)(128)(4,1)S(1)}, s32[]{:S(2)}) async-start(s8[27262976]{0:T(1024)(128)(4,1)} %bitcast.117), calls=%async_computation.2 | async-start | bytes 8388608
  91.3 10.8 %collective-permute-start.28 = (bf16[2,8,3328]{2,1,0:T(8,128)(2,1)S(1)}, bf16[2,8,3328]{2,1,0:T(8,128)(2,1)S(1)}, u32[]{:S(2)}, u32[]{:S(2)}) collective-permute-start(bf16[2,8,3328]{2,1,0:T(8,128)(2,1)S(1)} %get-tuple-element.244), channel_id=1, source_target_pairs={{0,2},{1,5},{2,0},{3,7},{4,6},{5,1},{6,4},{7,3},{8,10},{9,13},{10,... | collective-permute-start | bytes 319496 | tf_op jit(solution)/shard_map/ppermute | solution.py:114
  92.9 11.6 %collective-permute-start.32 = (bf16[8,4992]{1,0:T(8,128)(2,1)S(1)}, bf16[8,4992]{1,0:T(8,128)(2,1)S(1)}, u32[]{:S(2)}, u32[]{:S(2)}) collective-permute-start(bf16[8,4992]{1,0:T(8,128)(2,1)S(1)} %fusion.50), channel_id=1, source_target_pairs={{0,2},{1,5},{2,0},{3,7},{4,6},{5,1},{6,4},{7,3},{8,10},{9,13},{10,... | collective-permute-start | bytes 239624 | tf_op jit(solution)/shard_map/ppermute | solution.py:114
  94.9 11.7 %collective-permute-start.31 = (bf16[2,8,4992]{2,1,0:T(8,128)(2,1)S(1)}, bf16[2,8,4992]{2,1,0:T(8,128)(2,1)S(1)}, u32[]{:S(2)}, u32[]{:S(2)}) collective-permute-start(bf16[2,8,4992]{2,1,0:T(8,128)(2,1)S(1)} %get-tuple-element.240), channel_id=1, source_target_pairs={{0,2},{1,5},{2,0},{3,7},{4,6},{5,1},{6,4},{7,3},{8,10},{9,13},{10,... | collective-permute-start | bytes 479240 | tf_op jit(solution)/shard_map/ppermute | solution.py:114
  101.3 7.7 %collective-permute-start.30 = (bf16[8,6656]{1,0:T(8,128)(2,1)S(1)}, bf16[8,6656]{1,0:T(8,128)(2,1)S(1)}, u32[]{:S(2)}, u32[]{:S(2)}) collective-permute-start(bf16[8,6656]{1,0:T(8,128)(2,1)S(1)} %fusion.44), channel_id=1, source_target_pairs={{0,2},{1,5},{2,0},{3,7},{4,6},{5,1},{6,4},{7,3},{8,10},{9,13},{10,... | collective-permute-start | bytes 319496 | tf_op jit(solution)/shard_map/ppermute | solution.py:114
  101.5 11.6 %collective-permute-start.27 = (bf16[32,6656]{1,0:T(8,128)(2,1)S(1)}, bf16[32,6656]{1,0:T(8,128)(2,1)S(1)}, u32[]{:S(2)}, u32[]{:S(2)}) collective-permute-start(bf16[32,6656]{1,0:T(8,128)(2,1)S(1)} %constant_dynamic-update-slice_fusion.2), channel_id=1, source_target_pairs={{0,8},{1,17},{2,10},{3,19},{4,12},{5,21},{6,14},{7,23},{8,0},{9,25... | collective-permute-start | bytes 1277960 | tf_op jit(solution)/shard_map/ppermute | solution.py:114
  102.2 7.9 %collective-permute-start.29 = (bf16[2,8,3328]{2,1,0:T(8,128)(2,1)S(1)}, bf16[2,8,3328]{2,1,0:T(8,128)(2,1)S(1)}, u32[]{:S(2)}, u32[]{:S(2)}) collective-permute-start(bf16[2,8,3328]{2,1,0:T(8,128)(2,1)S(1)} %add_convert_fusion.32), channel_id=1, source_target_pairs={{0,4},{1,3},{2,6},{3,1},{4,0},{5,7},{6,2},{7,5},{8,12},{9,11},{10,... | collective-permute-start | bytes 319496 | tf_op jit(solution)/shard_map/ppermute | solution.py:114
  104.5 8.7 %collective-permute-start.35 = (bf16[16,4992]{1,0:T(8,128)(2,1)S(1)}, bf16[16,4992]{1,0:T(8,128)(2,1)S(1)}, u32[]{:S(2)}, u32[]{:S(2)}) collective-permute-start(bf16[16,4992]{1,0:T(8,128)(2,1)S(1)} %constant_dynamic-update-slice_fusion.4), channel_id=1, source_target_pairs={{0,16},{1,9},{2,18},{3,11},{4,20},{5,13},{6,22},{7,15},{8,24},{9,1... | collective-permute-start | bytes 479240 | tf_op jit(solution)/shard_map/ppermute | solution.py:114
  106.6 8.0 %collective-permute-start.34 = (bf16[2,8,4992]{2,1,0:T(8,128)(2,1)S(1)}, bf16[2,8,4992]{2,1,0:T(8,128)(2,1)S(1)}, u32[]{:S(2)}, u32[]{:S(2)}) collective-permute-start(bf16[2,8,4992]{2,1,0:T(8,128)(2,1)S(1)} %add_convert_fusion.26), channel_id=1, source_target_pairs={{0,4},{1,3},{2,6},{3,1},{4,0},{5,7},{6,2},{7,5},{8,12},{9,11},{10,... | collective-permute-start | bytes 479240 | tf_op jit(solution)/shard_map/ppermute | solution.py:114
  109.0 7.3 %collective-permute-start.38 = (bf16[16,6656]{1,0:T(8,128)(2,1)S(1)}, bf16[16,6656]{1,0:T(8,128)(2,1)S(1)}, u32[]{:S(2)}, u32[]{:S(2)}) collective-permute-start(bf16[16,6656]{1,0:T(8,128)(2,1)S(1)} %constant_dynamic-update-slice_fusion.6), channel_id=1, source_target_pairs={{0,16},{1,9},{2,18},{3,11},{4,20},{5,13},{6,22},{7,15},{8,24},{9,1... | collective-permute-start | bytes 638984 | tf_op jit(solution)/shard_map/ppermute | solution.py:114
  110.1 24.9 %slice-start.3 = ((s8[27262976]{0:T(1024)(128)(4,1)}), s8[4194304]{0:T(1024)(128)(4,1)S(1)}, s32[]{:S(2)}) async-start(s8[27262976]{0:T(1024)(128)(4,1)} %bitcast.117), calls=%async_computation.3 | async-start | bytes 8388608
  110.2 5.0 %collective-permute-start.39 = (bf16[8,3328]{1,0:T(8,128)(2,1)S(1)}, bf16[8,3328]{1,0:T(8,128)(2,1)S(1)}, u32[]{:S(2)}, u32[]{:S(2)}) collective-permute-start(bf16[8,3328]{1,0:T(8,128)(2,1)S(1)} %fusion.60), channel_id=1, source_target_pairs={{0,2},{1,5},{2,0},{3,7},{4,6},{5,1},{6,4},{7,3},{8,10},{9,13},{10,... | collective-permute-start | bytes 159752 | tf_op jit(solution)/shard_map/ppermute | solution.py:114
  113.1 8.7 %collective-permute-start.33 = (bf16[64,6656]{1,0:T(8,128)(2,1)S(1)}, bf16[64,6656]{1,0:T(8,128)(2,1)S(1)}, u32[]{:S(2)}, u32[]{:S(2)}) collective-permute-start(bf16[64,6656]{1,0:T(8,128)(2,1)S(1)} %constant_dynamic-update-slice_fusion.8), channel_id=1, source_target_pairs={{0,1},{1,0},{2,3},{3,2},{4,5},{5,4},{6,7},{7,6},{8,9},{9,8},{10,11... | collective-permute-start | bytes 2555912 | tf_op jit(solution)/shard_map/ppermute | solution.py:114
  113.3 8.2 %collective-permute-start.37 = (bf16[32,4992]{1,0:T(8,128)(2,1)S(1)}, bf16[32,4992]{1,0:T(8,128)(2,1)S(1)}, u32[]{:S(2)}, u32[]{:S(2)}) collective-permute-start(bf16[32,4992]{1,0:T(8,128)(2,1)S(1)} %constant_dynamic-update-slice_fusion.10), channel_id=1, source_target_pairs={{0,8},{1,17},{2,10},{3,19},{4,12},{5,21},{6,14},{7,23},{8,0},{9,25... | collective-permute-start | bytes 958472 | tf_op jit(solution)/shard_map/ppermute | solution.py:114
  114.7 6.9 %collective-permute-start.36 = (bf16[8,4992]{1,0:T(8,128)(2,1)S(1)}, bf16[8,4992]{1,0:T(8,128)(2,1)S(1)}, u32[]{:S(2)}, u32[]{:S(2)}) collective-permute-start(bf16[8,4992]{1,0:T(8,128)(2,1)S(1)} %fusion.48), channel_id=1, source_target_pairs={{0,2},{1,5},{2,0},{3,7},{4,6},{5,1},{6,4},{7,3},{8,10},{9,13},{10,... | collective-permute-start | bytes 239624 | tf_op jit(solution)/shard_map/ppermute | solution.py:114
  115.2 12.0 %collective-permute-start.43 = (bf16[16,3328]{1,0:T(8,128)(2,1)S(1)}, bf16[16,3328]{1,0:T(8,128)(2,1)S(1)}, u32[]{:S(2)}, u32[]{:S(2)}) collective-permute-start(bf16[16,3328]{1,0:T(8,128)(2,1)S(1)} %constant_dynamic-update-slice_fusion.12), channel_id=1, source_target_pairs={{0,16},{1,9},{2,18},{3,11},{4,20},{5,13},{6,22},{7,15},{8,24},{9,1... | collective-permute-start | bytes 319496 | tf_op jit(solution)/shard_map/ppermute | solution.py:114
  116.4 12.6 %collective-permute-start.42 = (bf16[32,6656]{1,0:T(8,128)(2,1)S(1)}, bf16[32,6656]{1,0:T(8,128)(2,1)S(1)}, u32[]{:S(2)}, u32[]{:S(2)}) collective-permute-start(bf16[32,6656]{1,0:T(8,128)(2,1)S(1)} %constant_dynamic-update-slice_fusion.14), channel_id=1, source_target_pairs={{0,8},{1,17},{2,10},{3,19},{4,12},{5,21},{6,14},{7,23},{8,0},{9,25... | collective-permute-start | bytes 1277960 | tf_op jit(solution)/shard_map/ppermute | solution.py:114
  121.5 8.8 %collective-permute-start.40 = (bf16[64,4992]{1,0:T(8,128)(2,1)S(1)}, bf16[64,4992]{1,0:T(8,128)(2,1)S(1)}, u32[]{:S(2)}, u32[]{:S(2)}) collective-permute-start(bf16[64,4992]{1,0:T(8,128)(2,1)S(1)} %constant_dynamic-update-slice_fusion.16), channel_id=1, source_target_pairs={{0,1},{1,0},{2,3},{3,2},{4,5},{5,4},{6,7},{7,6},{8,9},{9,8},{10,11... | collective-permute-start | bytes 1916936 | tf_op jit(solution)/shard_map/ppermute | solution.py:114
  121.6 13.4 %slice-start.4 = ((s8[27262976]{0:T(1024)(128)(4,1)}), s8[4194304]{0:T(1024)(128)(4,1)S(1)}, s32[]{:S(2)}) async-start(s8[27262976]{0:T(1024)(128)(4,1)} %bitcast.117), calls=%async_computation.4 | async-start | bytes 8388608
  121.7 13.4 %slice-start.5 = ((s8[27262976]{0:T(1024)(128)(4,1)}), s8[4194304]{0:T(1024)(128)(4,1)S(1)}, s32[]{:S(2)}) async-start(s8[27262976]{0:T(1024)(128)(4,1)} %bitcast.117), calls=%async_computation.5 | async-start | bytes 8388608
  121.7 7.5 %collective-permute-start.41 = (bf16[16,4992]{1,0:T(8,128)(2,1)S(1)}, bf16[16,4992]{1,0:T(8,128)(2,1)S(1)}, u32[]{:S(2)}, u32[]{:S(2)}) collective-permute-start(bf16[16,4992]{1,0:T(8,128)(2,1)S(1)} %constant_dynamic-update-slice_fusion.18), channel_id=1, source_target_pairs={{0,16},{1,9},{2,18},{3,11},{4,20},{5,13},{6,22},{7,15},{8,24},{9,1... | collective-permute-start | bytes 479240 | tf_op jit(solution)/shard_map/ppermute | solution.py:114
  127.3 7.4 %collective-permute-start.45 = (bf16[32,3328]{1,0:T(8,128)(2,1)S(1)}, bf16[32,3328]{1,0:T(8,128)(2,1)S(1)}, u32[]{:S(2)}, u32[]{:S(2)}) collective-permute-start(bf16[32,3328]{1,0:T(8,128)(2,1)S(1)} %constant_dynamic-update-slice_fusion.20), channel_id=1, source_target_pairs={{0,8},{1,17},{2,10},{3,19},{4,12},{5,21},{6,14},{7,23},{8,0},{9,25... | collective-permute-start | bytes 638984 | tf_op jit(solution)/shard_map/ppermute | solution.py:114
  129.0 6.0 %collective-permute-start.44 = (bf16[64,6656]{1,0:T(8,128)(2,1)S(1)}, bf16[64,6656]{1,0:T(8,128)(2,1)S(1)}, u32[]{:S(2)}, u32[]{:S(2)}) collective-permute-start(bf16[64,6656]{1,0:T(8,128)(2,1)S(1)} %constant_dynamic-update-slice_fusion.22), channel_id=1, source_target_pairs={{0,1},{1,0},{2,3},{3,2},{4,5},{5,4},{6,7},{7,6},{8,9},{9,8},{10,11... | collective-permute-start | bytes 2555912 | tf_op jit(solution)/shard_map/ppermute | solution.py:114
  129.2 5.9 %slice-start.6 = ((s8[27262976]{0:T(1024)(128)(4,1)}), s8[4194304]{0:T(1024)(128)(4,1)S(1)}, s32[]{:S(2)}) async-start(s8[27262976]{0:T(1024)(128)(4,1)} %bitcast.117), calls=%async_computation.6 | async-start | bytes 8388608
  129.2 8.3 %collective-permute-start.47 = (bf16[32,4992]{1,0:T(8,128)(2,1)S(1)}, bf16[32,4992]{1,0:T(8,128)(2,1)S(1)}, u32[]{:S(2)}, u32[]{:S(2)}) collective-permute-start(bf16[32,4992]{1,0:T(8,128)(2,1)S(1)} %constant_dynamic-update-slice_fusion.24), channel_id=1, source_target_pairs={{0,8},{1,17},{2,10},{3,19},{4,12},{5,21},{6,14},{7,23},{8,0},{9,25... | collective-permute-start | bytes 958472 | tf_op jit(solution)/shard_map/ppermute | solution.py:114
  134.8 3.2 %collective-permute-start.46 = (bf16[64,3328]{1,0:T(8,128)(2,1)S(1)}, bf16[64,3328]{1,0:T(8,128)(2,1)S(1)}, u32[]{:S(2)}, u32[]{:S(2)}) collective-permute-start(bf16[64,3328]{1,0:T(8,128)(2,1)S(1)} %constant_dynamic-update-slice_fusion.26), channel_id=1, source_target_pairs={{0,1},{1,0},{2,3},{3,2},{4,5},{5,4},{6,7},{7,6},{8,9},{9,8},{10,11... | collective-permute-start | bytes 1277960 | tf_op jit(solution)/shard_map/ppermute | solution.py:114
  137.6 2.1 %collective-permute-start.48 = (bf16[64,4992]{1,0:T(8,128)(2,1)S(1)}, bf16[64,4992]{1,0:T(8,128)(2,1)S(1)}, u32[]{:S(2)}, u32[]{:S(2)}) collective-permute-start(bf16[64,4992]{1,0:T(8,128)(2,1)S(1)} %constant_dynamic-update-slice_fusion.28), channel_id=1, source_target_pairs={{0,1},{1,0},{2,3},{3,2},{4,5},{5,4},{6,7},{7,6},{8,9},{9,8},{10,11... | collective-permute-start | bytes 1916936 | tf_op jit(solution)/shard_map/ppermute | solution.py:114
  142.0 6.1 %collective-permute-start.51 = (bf16[32,512]{1,0:T(8,128)(2,1)S(1)}, bf16[32,512]{1,0:T(8,128)(2,1)S(1)}, u32[]{:S(2)}, u32[]{:S(2)}) collective-permute-start(bf16[32,512]{1,0:T(8,128)(2,1)S(1)} %get-tuple-element.248), channel_id=1, source_target_pairs={{0,6},{1,7},{2,4},{3,5},{4,2},{5,3},{6,0},{7,1},{8,14},{9,15},{10,... | collective-permute-start | bytes 98312 | tf_op jit(solution)/shard_map/ppermute | solution.py:114
  143.3 5.6 %collective-permute-start.50 = (bf16[32,512]{1,0:T(8,128)(2,1)S(1)}, bf16[32,512]{1,0:T(8,128)(2,1)S(1)}, u32[]{:S(2)}, u32[]{:S(2)}) collective-permute-start(bf16[32,512]{1,0:T(8,128)(2,1)S(1)} %get-tuple-element.249), channel_id=1, source_target_pairs={{0,4},{1,5},{2,6},{3,7},{4,0},{5,1},{6,2},{7,3},{8,12},{9,13},{10,... | collective-permute-start | bytes 98312 | tf_op jit(solution)/shard_map/ppermute | solution.py:114
  144.8 4.1 %collective-permute-start.49 = (bf16[32,512]{1,0:T(8,128)(2,1)S(1)}, bf16[32,512]{1,0:T(8,128)(2,1)S(1)}, u32[]{:S(2)}, u32[]{:S(2)}) collective-permute-start(bf16[32,512]{1,0:T(8,128)(2,1)S(1)} %get-tuple-element.250), channel_id=1, source_target_pairs={{0,2},{1,3},{2,0},{3,1},{4,6},{5,7},{6,4},{7,5},{8,10},{9,11},{10,... | collective-permute-start | bytes 98312 | tf_op jit(solution)/shard_map/ppermute | solution.py:114
  148.9 1.3 collective-permute-start.52
  150.4 0.7 copy-start

commit v4 on v3

--- a/solution.py
+++ b/solution.py
@@ -8,9 +8,9 @@
 from jax.experimental.pallas import tpu as pltpu
 from jax.sharding import PartitionSpec as P
 
-VMEM_BYTES = 40 * 2**20
-SHARES = (3, 4, 4, 3, 2)
-ORDER = (1, 3, 1, 3, 2, 1, 4, 2, 3, 1, 0, 2, 1, 4, 3, 0, 2, 1, 3, 4, 2, 0, 1, 4, 3, 0, 2, 1, 4, 3, 0, 2, 4, 1, 3, 0, 4, 2, 3, 0, 1, 4, 2, 0, 3, 4, 2, 0, 4, 0)
+VMEM_BYTES = 28 * 2**20
+SHARES = (3,4,4,3,2)
+ORDER = (2, 4, 2, 1, 4, 2, 1, 0, 4, 2, 3, 1, 2, 0, 4, 3, 1, 2, 4, 0, 1, 2, 4, 3, 0, 1, 4, 3, 2, 0, 1, 3, 4, 0, 2, 1, 3, 0, 2, 3, 0, 4, 1, 3, 1, 0, 4, 3, 0, 3)
 
 
 def step_order(chunks, steps):
@@ -77,6 +77,57 @@
     )(x, gate_weight, up_weight)
 
 
+def fetch_kernel(start, gate_ref, up_ref, held_ref, arrived):
+    columns = pl.ds(start, held_ref.shape[2])
+    copies = [
+        pltpu.make_async_copy(ref.at[:, columns], held_ref.at[k], arrived.at[k])
+        for k, ref in enumerate((gate_ref, up_ref))
+    ]
+    for copy in copies:
+        copy.start()
+    for copy in copies:
+        copy.wait()
+
+
+def fetch(gate_weight, up_weight, start, width):
+    held = (2, gate_weight.shape[0], width)
+    return pl.pallas_call(
+        functools.partial(fetch_kernel, start),
+        in_specs=[pl.BlockSpec(memory_space=pl.ANY)] * 2,
+        out_specs=pl.BlockSpec(memory_space=pltpu.VMEM),
+        out_shape=pltpu.VMEM(held, jnp.bfloat16),
+        scratch_shapes=[pltpu.SemaphoreType.DMA((2,))],
+        compiler_params=pltpu.CompilerParams(vmem_limit_bytes=VMEM_BYTES),
+        cost_estimate=pl.CostEstimate(flops=0, bytes_accessed=0, transcendentals=0),
+    )(gate_weight, up_weight)
+
+
+def gate_up_held_kernel(x_ref, held_ref, keep_ref, send_ref):
+    half, width = keep_ref.shape[1:]
+    block = block_width(width, 1664)
+    for n in range(0, width, block):
+        for k in range(2):
+            part = jnp.dot(
+                x_ref[...], held_ref[k, :, n : n + block], preferred_element_type=jnp.float32
+            ).astype(jnp.bfloat16)
+            keep_ref[k, :, n : n + block] = part[:half]
+            send_ref[k, :, n : n + block] = part[half:]
+
+
+def gate_up_held(x, held):
+    tokens, width = x.shape[0], held.shape[2]
+    out_shape = jax.ShapeDtypeStruct((2, tokens // 2, width), jnp.bfloat16)
+    in_vmem = pl.BlockSpec(memory_space=pltpu.VMEM)
+    return pl.pallas_call(
+        gate_up_held_kernel,
+        in_specs=[in_vmem, in_vmem],
+        out_specs=[in_vmem, in_vmem],
+        out_shape=[out_shape, out_shape],
+        compiler_params=pltpu.CompilerParams(vmem_limit_bytes=VMEM_BYTES),
+        cost_estimate=pl.CostEstimate(flops=0, bytes_accessed=0, transcendentals=0),
+    )(x, held)
+
+
 def down(own, other, down_weight, before, start):
     hidden = jnp.concatenate([own, other], 0)
     weight = cut(down_weight, start, own.shape[1])
@@ -161,9 +212,12 @@
     def after(*values):
         return lax.optimization_barrier((values, last[0]))[0]
 
-    def steps(start, width):
+    def steps(start, width, held):
         (x_now,) = after(x)
-        keep, send = gate_up(x_now, gate_weight, up_weight, start, width)
+        if held is None:
+            keep, send = gate_up(x_now, gate_weight, up_weight, start, width)
+        else:
+            keep, send = gate_up_held(x_now, held)
         last[0] = send
         received = swap(send, (core, core))
         yield
@@ -193,8 +247,13 @@
 
     share = units // sum(SHARES)
     ends = np.cumsum(SHARES) * share
-    running = [steps(int(end) - n * share, n * share) for n, end in zip(SHARES, ends)]
-    for chunk in step_order(len(SHARES), 2 + 2 * len(stages)):
+    turns = step_order(len(SHARES), 2 + 2 * len(stages))
+    running = []
+    for chunk, (n, end) in enumerate(zip(SHARES, ends)):
+        start, width = int(end) - n * share, n * share
+        held = fetch(gate_weight, up_weight, start, width) if chunk == turns[0] else None
+        running.append(steps(start, width, held))
+    for chunk in turns:
         next(running[chunk], None)
 
     out = lax.dot_general(

time: 152 us -> 145 us (0.954)
  waiting for transfers between devices: 49.9 us -> 41.7 us
  matrix products: 15.9 us -> 10.3 us
  starting transfers between devices: 54.8 us -> 59.8 us
  Pallas kernels: 23.8 us -> 25.4 us
    ppermute x53, waiting for transfers between devices: 49.9 us -> 41.7 us  [swap(): return lax.ppermute(value, ('row', 'col'), pairs)]
    pallas_call x0 -> x2, Pallas kernels: none -> 6.97 us  [the longest x1 4.89 us: fetch(): pl.pallas_call(functools.partial(fetch_kernel, start), in_specs=[pl.Block...]
    dot_general x5, matrix products: 15.3 us -> 9.74 us  [down(): lax.dot_general(hidden, weight, (((1,), (1,)), ((), ())), preferred_eleme...]
    pallas_call x5 -> x4, Pallas kernels: 23.8 us -> 18.4 us  [gate_up(): pl.pallas_call(functools.partial(gate_up_kernel, start), grid=(blocks,),...]
    ppermute x53, starting transfers between devices: 54.8 us -> 59.8 us  [swap(): return lax.ppermute(value, ('row', 'col'), pairs)]
  transfers between devices with their start and end apart: 53 -> 53, of which waited for: 22 -> 18; matrix products, arithmetic and copies ran while one was open for 12% -> 8% of each run, Pallas kernels for 12% -> 16%
where the time goes in v4:
time: 145 us
  starting transfers between devices  59.8 us (41%)
  waiting for transfers between devices  41.7 us (29%)
  Pallas kernels  25.4 us (18%)
  matrix products  10.3 us (7%)
  other arithmetic  3.74 us (3%)
  local copies, waits for them, and re-layouts  2.74 us (2%)
    ppermute x53, starting transfers between devices, swap(): return lax.ppermute(value, ('row', 'col'), pairs)  59.8 us
    ppermute x53, waiting for transfers between devices, swap(): return lax.ppermute(value, ('row', 'col'), pairs)  41.7 us
    pallas_call x4, Pallas kernels, gate_up(): pl.pallas_call(functools.partial(gate_up_kernel, start), grid=(blocks,),...  18.4 us
    dot_general x5, matrix products, down(): lax.dot_general(hidden, weight, (((1,), (1,)), ((), ())), preferred_eleme...  9.74 us
    pallas_call x1, Pallas kernels, fetch(): pl.pallas_call(functools.partial(fetch_kernel, start), in_specs=[pl.Block...  4.89 us
  transfers between devices with their start and end apart: 53, of which 18 were waited for; matrix products, arithmetic and copies ran while one was open for 8% of the time, Pallas kernels for 16%

profile of v4, /device:TPU:0, one launch (start us, length us, event | category | flops | bytes accessed | tf_op | source)
XLA Modules:
  0.0 144.6 jit_solution(4051571799610945394)
XLA Ops:
  0.0 0.9 slice_bitcast_fusion.30
  0.9 0.5 collective-permute-start
  1.4 0.9 collective-permute-done
  2.5 5.0 %collective-permute-start.3 = (bf16[32,512]{1,0:T(8,128)(2,1)S(1)}, bf16[32,512]{1,0:T(8,128)(2,1)S(1)}, u32[]{:S(2)}, u32[]{:S(2)}) collective-permute-start(bf16[32,512]{1,0:T(8,128)(2,1)S(1)} %get-tuple-element.252), channel_id=1, source_target_pairs={{0,6},{1,7},{2,4},{3,5},{4,2},{5,3},{6,0},{7,1},{8,14},{9,15},{10,... | collective-permute-start | bytes 98312 | tf_op jit(solution)/shard_map/ppermute | solution.py:165
  7.5 0.6 collective-permute-start.1
  8.1 4.9 %shard_map.73.held_ref = bf16[2,512,6656]{2,1,0:T(8,128)(2,1)S(1)} custom-call(bf16[512,26624]{1,0:T(8,128)(2,1)} %gate_ref.9, bf16[512,26624]{1,0:T(8,128)(2,1)} %up_ref.9), custom_call_target="tpu_custom_call" | custom-call | tf_op jit(solution)/shard_map/pallas_call | solution.py:94
  13.3 2.1 %shard_map.74 = (bf16[2,64,6656]{2,1,0:T(8,128)(2,1)S(1)}, bf16[2,64,6656]{2,1,0:T(8,128)(2,1)S(1)}) custom-call(bf16[128,512]{1,0:T(8,128)(2,1)S(1)} %convolution_convert_fusion.1.x_ref, bf16[2,512,6656]{2,1,0:T(8,128)(2,1)S(1)} %shard_map.73.held_ref), custom_call_target="tpu_custom_call" | custom-call | tf_op jit(solution)/shard_map/pallas_call | solution.py:121
  15.5 3.5 %shard_map.75 = (bf16[2,64,3328]{2,1,0:T(8,128)(2,1)S(1)}, bf16[2,64,3328]{2,1,0:T(8,128)(2,1)S(1)}) custom-call(bf16[128,512]{1,0:T(8,128)(2,1)S(1)} %convolution_convert_fusion.1.x_ref, bf16[512,26624]{1,0:T(8,128)(2,1)} %gate_ref.9, bf16[512,26624]{1,0:T(8,128)(2,1)} %up_ref.9), custom_call_target="tpu_custom_call" | custom-call | tf_op jit(solution)/shard_map/pallas_call | solution.py:61
  19.0 0.5 collective-permute-start.6
  19.9 1.7 %collective-permute-start.5 = (bf16[2,32,6656]{2,1,0:T(8,128)(2,1)S(1)}, bf16[2,32,6656]{2,1,0:T(8,128)(2,1)S(1)}, u32[]{:S(2)}, u32[]{:S(2)}) collective-permute-start(bf16[2,32,6656]{2,1,0:T(8,128)(2,1)S(1)} %get-tuple-element.217), channel_id=1, source_target_pairs={{0,8},{1,17},{2,10},{3,19},{4,12},{5,21},{6,14},{7,23},{8,0},{9,25... | collective-permute-start | bytes 2555912 | tf_op jit(solution)/shard_map/ppermute | solution.py:165
  21.7 5.5 %shard_map.76 = (bf16[2,64,6656]{2,1,0:T(8,128)(2,1)S(1)}, bf16[2,64,6656]{2,1,0:T(8,128)(2,1)S(1)}) custom-call(bf16[128,512]{1,0:T(8,128)(2,1)S(1)} %convolution_convert_fusion.1.x_ref, bf16[512,26624]{1,0:T(8,128)(2,1)} %gate_ref.9, bf16[512,26624]{1,0:T(8,128)(2,1)} %up_ref.9), custom_call_target="tpu_custom_call" | custom-call | tf_op jit(solution)/shard_map/pallas_call | solution.py:61
  27.5 1.3 collective-permute-start.8
  28.8 3.9 %collective-permute-done.5 = bf16[2,32,6656]{2,1,0:T(8,128)(2,1)S(1)} collective-permute-done((bf16[2,32,6656]{2,1,0:T(8,128)(2,1)S(1)}, bf16[2,32,6656]{2,1,0:T(8,128)(2,1)S(1)}, u32[]{:S(2)}, u32[]{:S(2)}) %collective-permute-start.5) | collective-permute-done | bytes 852000 | tf_op jit(solution)/shard_map/ppermute | solution.py:165
  32.9 1.7 %collective-permute-start.7 = (bf16[2,16,6656]{2,1,0:T(8,128)(2,1)S(1)}, bf16[2,16,6656]{2,1,0:T(8,128)(2,1)S(1)}, u32[]{:S(2)}, u32[]{:S(2)}) collective-permute-start(bf16[2,16,6656]{2,1,0:T(8,128)(2,1)S(1)} %get-tuple-element.227), channel_id=1, source_target_pairs={{0,16},{1,9},{2,18},{3,11},{4,20},{5,13},{6,22},{7,15},{8,24},{9,1... | collective-permute-start | bytes 1277960 | tf_op jit(solution)/shard_map/ppermute | solution.py:165
  34.6 0.5 add_convert_fusion
  35.1 1.6 %collective-permute-start.11 = (bf16[2,32,6656]{2,1,0:T(8,128)(2,1)S(1)}, bf16[2,32,6656]{2,1,0:T(8,128)(2,1)S(1)}, u32[]{:S(2)}, u32[]{:S(2)}) collective-permute-start(bf16[2,32,6656]{2,1,0:T(8,128)(2,1)S(1)} %get-tuple-element.216), channel_id=1, source_target_pairs={{0,8},{1,17},{2,10},{3,19},{4,12},{5,21},{6,14},{7,23},{8,0},{9,25... | collective-permute-start | bytes 2555912 | tf_op jit(solution)/shard_map/ppermute | solution.py:165
  36.7 4.5 %shard_map.77 = (bf16[2,64,4992]{2,1,0:T(8,128)(2,1)S(1)}, bf16[2,64,4992]{2,1,0:T(8,128)(2,1)S(1)}) custom-call(bf16[128,512]{1,0:T(8,128)(2,1)S(1)} %convolution_convert_fusion.1.x_ref, bf16[512,26624]{1,0:T(8,128)(2,1)} %gate_ref.9, bf16[512,26624]{1,0:T(8,128)(2,1)} %up_ref.9), custom_call_target="tpu_custom_call" | custom-call | tf_op jit(solution)/shard_map/pallas_call | solution.py:61
  41.3 4.2 %collective-permute-done.7 = bf16[2,16,6656]{2,1,0:T(8,128)(2,1)S(1)} collective-permute-done((bf16[2,16,6656]{2,1,0:T(8,128)(2,1)S(1)}, bf16[2,16,6656]{2,1,0:T(8,128)(2,1)S(1)}, u32[]{:S(2)}, u32[]{:S(2)}) %collective-permute-start.7) | collective-permute-done | bytes 426016 | tf_op jit(solution)/shard_map/ppermute | solution.py:165
  45.7 1.6 %collective-permute-start.10 = (bf16[2,8,6656]{2,1,0:T(8,128)(2,1)S(1)}, bf16[2,8,6656]{2,1,0:T(8,128)(2,1)S(1)}, u32[]{:S(2)}, u32[]{:S(2)}) collective-permute-start(bf16[2,8,6656]{2,1,0:T(8,128)(2,1)S(1)} %get-tuple-element.237), channel_id=1, source_target_pairs={{0,2},{1,5},{2,0},{3,7},{4,6},{5,1},{6,4},{7,3},{8,10},{9,13},{10,... | collective-permute-start | bytes 638984 | tf_op jit(solution)/shard_map/ppermute | solution.py:165
  47.2 1.5 %collective-permute-start.15 = (bf16[2,16,3328]{2,1,0:T(8,128)(2,1)S(1)}, bf16[2,16,3328]{2,1,0:T(8,128)(2,1)S(1)}, u32[]{:S(2)}, u32[]{:S(2)}) collective-permute-start(bf16[2,16,3328]{2,1,0:T(8,128)(2,1)S(1)} %get-tuple-element.236), channel_id=1, source_target_pairs={{0,16},{1,9},{2,18},{3,11},{4,20},{5,13},{6,22},{7,15},{8,24},{9,1... | collective-permute-start | bytes 638984 | tf_op jit(solution)/shard_map/ppermute | solution.py:165
  48.8 4.9 %shard_map.78 = (bf16[2,64,4992]{2,1,0:T(8,128)(2,1)S(1)}, bf16[2,64,4992]{2,1,0:T(8,128)(2,1)S(1)}) custom-call(bf16[128,512]{1,0:T(8,128)(2,1)S(1)} %convolution_convert_fusion.1.x_ref, bf16[512,26624]{1,0:T(8,128)(2,1)} %gate_ref.9, bf16[512,26624]{1,0:T(8,128)(2,1)} %up_ref.9), custom_call_target="tpu_custom_call" | custom-call | tf_op jit(solution)/shard_map/pallas_call | solution.py:61
  53.7 0.6 collective-permute-start.14
  54.4 0.7 collective-permute-start.13
  55.1 2.9 %collective-permute-start.12 = (bf16[2,8,6656]{2,1,0:T(8,128)(2,1)S(1)}, bf16[2,8,6656]{2,1,0:T(8,128)(2,1)S(1)}, u32[]{:S(2)}, u32[]{:S(2)}) collective-permute-start(bf16[2,8,6656]{2,1,0:T(8,128)(2,1)S(1)} %add_convert_fusion.22), channel_id=1, source_target_pairs={{0,4},{1,3},{2,6},{3,1},{4,0},{5,7},{6,2},{7,5},{8,12},{9,11},{10,... | collective-permute-start | bytes 638984 | tf_op jit(solution)/shard_map/ppermute | solution.py:165
  58.3 1.6 %collective-permute-start.19 = (bf16[2,32,4992]{2,1,0:T(8,128)(2,1)S(1)}, bf16[2,32,4992]{2,1,0:T(8,128)(2,1)S(1)}, u32[]{:S(2)}, u32[]{:S(2)}) collective-permute-start(bf16[2,32,4992]{2,1,0:T(8,128)(2,1)S(1)} %get-tuple-element.222), channel_id=1, source_target_pairs={{0,8},{1,17},{2,10},{3,19},{4,12},{5,21},{6,14},{7,23},{8,0},{9,25... | collective-permute-start | bytes 1916936 | tf_op jit(solution)/shard_map/ppermute | solution.py:165
  60.0 1.4 collective-permute-start.20
  61.7 0.6 collective-permute-start.22
  62.3 3.4 %collective-permute-done.13 = bf16[2,16,6656]{2,1,0:T(8,128)(2,1)S(1)} collective-permute-done((bf16[2,16,6656]{2,1,0:T(8,128)(2,1)S(1)}, bf16[2,16,6656]{2,1,0:T(8,128)(2,1)S(1)}, u32[]{:S(2)}, u32[]{:S(2)}) %collective-permute-start.13) | collective-permute-done | bytes 426016 | tf_op jit(solution)/shard_map/ppermute | solution.py:165
  66.4 2.2 %collective-permute-start.17 = (bf16[8,6656]{1,0:T(8,128)(2,1)S(1)}, bf16[8,6656]{1,0:T(8,128)(2,1)S(1)}, u32[]{:S(2)}, u32[]{:S(2)}) collective-permute-start(bf16[8,6656]{1,0:T(8,128)(2,1)S(1)} %fusion.46), channel_id=1, source_target_pairs={{0,2},{1,5},{2,0},{3,7},{4,6},{5,1},{6,4},{7,3},{8,10},{9,13},{10,... | collective-permute-start | bytes 319496 | tf_op jit(solution)/shard_map/ppermute | solution.py:165
  68.6 3.4 %collective-permute-start.23 = (bf16[2,8,3328]{2,1,0:T(8,128)(2,1)S(1)}, bf16[2,8,3328]{2,1,0:T(8,128)(2,1)S(1)}, u32[]{:S(2)}, u32[]{:S(2)}) collective-permute-start(bf16[2,8,3328]{2,1,0:T(8,128)(2,1)S(1)} %add_convert_fusion.32), channel_id=1, source_target_pairs={{0,4},{1,3},{2,6},{3,1},{4,0},{5,7},{6,2},{7,5},{8,12},{9,11},{10,... | collective-permute-start | bytes 319496 | tf_op jit(solution)/shard_map/ppermute | solution.py:165
  72.5 5.7 %collective-permute-done.18 = bf16[2,8,6656]{2,1,0:T(8,128)(2,1)S(1)} collective-permute-done((bf16[2,8,6656]{2,1,0:T(8,128)(2,1)S(1)}, bf16[2,8,6656]{2,1,0:T(8,128)(2,1)S(1)}, u32[]{:S(2)}, u32[]{:S(2)}) %collective-permute-start.18) | collective-permute-done | bytes 213024 | tf_op jit(solution)/shard_map/ppermute | solution.py:165
  78.3 2.7 %collective-permute-done.17 = bf16[8,6656]{1,0:T(8,128)(2,1)S(1)} collective-permute-done((bf16[8,6656]{1,0:T(8,128)(2,1)S(1)}, bf16[8,6656]{1,0:T(8,128)(2,1)S(1)}, u32[]{:S(2)}, u32[]{:S(2)}) %collective-permute-start.17) | collective-permute-done | bytes 106528 | tf_op jit(solution)/shard_map/ppermute | solution.py:165
  81.3 1.8 %collective-permute-start.25 = (bf16[8,3328]{1,0:T(8,128)(2,1)S(1)}, bf16[8,3328]{1,0:T(8,128)(2,1)S(1)}, u32[]{:S(2)}, u32[]{:S(2)}) collective-permute-start(bf16[8,3328]{1,0:T(8,128)(2,1)S(1)} %fusion.60), channel_id=1, source_target_pairs={{0,2},{1,5},{2,0},{3,7},{4,6},{5,1},{6,4},{7,3},{8,10},{9,13},{10,... | collective-permute-start | bytes 159752 | tf_op jit(solution)/shard_map/ppermute | solution.py:165
  83.7 2.1 %collective-permute-start.29 = (bf16[2,8,4992]{2,1,0:T(8,128)(2,1)S(1)}, bf16[2,8,4992]{2,1,0:T(8,128)(2,1)S(1)}, u32[]{:S(2)}, u32[]{:S(2)}) collective-permute-start(bf16[2,8,4992]{2,1,0:T(8,128)(2,1)S(1)} %get-tuple-element.242), channel_id=1, source_target_pairs={{0,2},{1,5},{2,0},{3,7},{4,6},{5,1},{6,4},{7,3},{8,10},{9,13},{10,... | collective-permute-start | bytes 479240 | tf_op jit(solution)/shard_map/ppermute | solution.py:165
  85.7 7.9 %collective-permute-done.26 = bf16[2,8,6656]{2,1,0:T(8,128)(2,1)S(1)} collective-permute-done((bf16[2,8,6656]{2,1,0:T(8,128)(2,1)S(1)}, bf16[2,8,6656]{2,1,0:T(8,128)(2,1)S(1)}, u32[]{:S(2)}, u32[]{:S(2)}) %collective-permute-start.26) | collective-permute-done | bytes 213024 | tf_op jit(solution)/shard_map/ppermute | solution.py:165
  93.9 0.6 collective-permute-start.31
  94.6 1.6 %collective-permute-start.32 = (bf16[2,8,4992]{2,1,0:T(8,128)(2,1)S(1)}, bf16[2,8,4992]{2,1,0:T(8,128)(2,1)S(1)}, u32[]{:S(2)}, u32[]{:S(2)}) collective-permute-start(bf16[2,8,4992]{2,1,0:T(8,128)(2,1)S(1)} %get-tuple-element.240), channel_id=1, source_target_pairs={{0,2},{1,5},{2,0},{3,7},{4,6},{5,1},{6,4},{7,3},{8,10},{9,13},{10,... | collective-permute-start | bytes 479240 | tf_op jit(solution)/shard_map/ppermute | solution.py:165
  96.2 2.1 %collective-permute-start.28 = (bf16[32,6656]{1,0:T(8,128)(2,1)S(1)}, bf16[32,6656]{1,0:T(8,128)(2,1)S(1)}, u32[]{:S(2)}, u32[]{:S(2)}) collective-permute-start(bf16[32,6656]{1,0:T(8,128)(2,1)S(1)} %constant_dynamic-update-slice_fusion.4), channel_id=1, source_target_pairs={{0,8},{1,17},{2,10},{3,19},{4,12},{5,21},{6,14},{7,23},{8,0},{9,25... | collective-permute-start | bytes 1277960 | tf_op jit(solution)/shard_map/ppermute | solution.py:165
  98.5 0.6 collective-permute-done.33
  99.1 1.5 %collective-permute-start.37 = (bf16[16,6656]{1,0:T(8,128)(2,1)S(1)}, bf16[16,6656]{1,0:T(8,128)(2,1)S(1)}, u32[]{:S(2)}, u32[]{:S(2)}) collective-permute-start(bf16[16,6656]{1,0:T(8,128)(2,1)S(1)} %constant_dynamic-update-slice_fusion.6), channel_id=1, source_target_pairs={{0,16},{1,9},{2,18},{3,11},{4,20},{5,13},{6,22},{7,15},{8,24},{9,1... | collective-permute-start | bytes 638984 | tf_op jit(solution)/shard_map/ppermute | solution.py:165
  100.6 2.2 %collective-permute-done.32 = bf16[2,8,4992]{2,1,0:T(8,128)(2,1)S(1)} collective-permute-done((bf16[2,8,4992]{2,1,0:T(8,128)(2,1)S(1)}, bf16[2,8,4992]{2,1,0:T(8,128)(2,1)S(1)}, u32[]{:S(2)}, u32[]{:S(2)}) %collective-permute-start.32) | collective-permute-done | bytes 159776 | tf_op jit(solution)/shard_map/ppermute | solution.py:165
  102.9 1.4 collective-permute-start.36
  104.3 0.7 collective-permute-start.39
  105.0 1.7 %collective-permute-done.30 = bf16[2,8,4992]{2,1,0:T(8,128)(2,1)S(1)} collective-permute-done((bf16[2,8,4992]{2,1,0:T(8,128)(2,1)S(1)}, bf16[2,8,4992]{2,1,0:T(8,128)(2,1)S(1)}, u32[]{:S(2)}, u32[]{:S(2)}) %collective-permute-start.30) | collective-permute-done | bytes 159776 | tf_op jit(solution)/shard_map/ppermute | solution.py:165
  107.1 3.1 %collective-permute-start.38 = (bf16[32,6656]{1,0:T(8,128)(2,1)S(1)}, bf16[32,6656]{1,0:T(8,128)(2,1)S(1)}, u32[]{:S(2)}, u32[]{:S(2)}) collective-permute-start(bf16[32,6656]{1,0:T(8,128)(2,1)S(1)} %constant_dynamic-update-slice_fusion.12), channel_id=1, source_target_pairs={{0,8},{1,17},{2,10},{3,19},{4,12},{5,21},{6,14},{7,23},{8,0},{9,25... | collective-permute-start | bytes 1277960 | tf_op jit(solution)/shard_map/ppermute | solution.py:165
  110.7 0.5 collective-permute-done.35
  111.3 1.5 %collective-permute-start.40 = (bf16[16,4992]{1,0:T(8,128)(2,1)S(1)}, bf16[16,4992]{1,0:T(8,128)(2,1)S(1)}, u32[]{:S(2)}, u32[]{:S(2)}) collective-permute-start(bf16[16,4992]{1,0:T(8,128)(2,1)S(1)} %constant_dynamic-update-slice_fusion.14), channel_id=1, source_target_pairs={{0,16},{1,9},{2,18},{3,11},{4,20},{5,13},{6,22},{7,15},{8,24},{9,1... | collective-permute-start | bytes 479240 | tf_op jit(solution)/shard_map/ppermute | solution.py:165
  112.9 2.4 %fusion.2 = f32[128,512]{1,0:T(8,128)S(1)} fusion(bf16[512,26624]{1,0:T(8,128)(2,1)S(1)} %bitcast.118, bf16[64,6656]{1,0:T(8,128)(2,1)S(1)} %collective-permute-done.34, bf16[64,6656]{1,0:T(8,128)(2,1)S(1)} %constant_dynamic-update-slice_fusion.10), kind=kOutput, calls=%fused_computation.2 | convolution fusion | flops 875823104 | bytes 8781824 | tf_op jit(solution)/shard_map/dot_general | solution.py:134
  115.3 0.9 collective-permute-start.43
  116.7 3.0 %collective-permute-start.45 = (bf16[32,4992]{1,0:T(8,128)(2,1)S(1)}, bf16[32,4992]{1,0:T(8,128)(2,1)S(1)}, u32[]{:S(2)}, u32[]{:S(2)}) collective-permute-start(bf16[32,4992]{1,0:T(8,128)(2,1)S(1)} %constant_dynamic-update-slice_fusion.18), channel_id=1, source_target_pairs={{0,8},{1,17},{2,10},{3,19},{4,12},{5,21},{6,14},{7,23},{8,0},{9,25... | collective-permute-start | bytes 958472 | tf_op jit(solution)/shard_map/ppermute | solution.py:165
  119.9 0.6 collective-permute-start.42
  120.7 2.3 %collective-permute-start.47 = (bf16[32,4992]{1,0:T(8,128)(2,1)S(1)}, bf16[32,4992]{1,0:T(8,128)(2,1)S(1)}, u32[]{:S(2)}, u32[]{:S(2)}) collective-permute-start(bf16[32,4992]{1,0:T(8,128)(2,1)S(1)} %constant_dynamic-update-slice_fusion.24), channel_id=1, source_target_pairs={{0,8},{1,17},{2,10},{3,19},{4,12},{5,21},{6,14},{7,23},{8,0},{9,25... | collective-permute-start | bytes 958472 | tf_op jit(solution)/shard_map/ppermute | solution.py:165
  122.9 2.4 %fusion.22 = f32[128,512]{1,0:T(8,128)S(1)} fusion(f32[128,512]{1,0:T(8,128)S(1)} %fusion.2, bf16[512,26624]{1,0:T(8,128)(2,1)S(1)} %bitcast.118, bf16[64,6656]{1,0:T(8,128)(2,1)S(1)} %collective-permute-done.42, bf16[64,6656]{1,0:T(8,128)(2,1)S(1)} %constant_dynamic-update-slice_fusion.22), kind=kOutput, calls=%fused_computation.30 | convolution fusion | flops 875888640 | bytes 9043968 | tf_op jit(solution)/shard_map/dot_general | solution.py:134
  125.6 1.3 fusion.27
  126.9 1.2 collective-permute-done.47
  128.3 1.8 %fusion.30 = f32[128,512]{1,0:T(8,128)S(1)} fusion(f32[128,512]{1,0:T(8,128)S(1)} %fusion.27, bf16[512,26624]{1,0:T(8,128)(2,1)S(1)} %bitcast.118, bf16[64,4992]{1,0:T(8,128)(2,1)S(1)} %collective-permute-done.46, bf16[64,4992]{1,0:T(8,128)(2,1)S(1)} %constant_dynamic-update-slice_fusion.26), kind=kOutput, calls=%fused_computation.32 | convolution fusion | flops 656932864 | bytes 6914048 | tf_op jit(solution)/shard_map/dot_general | solution.py:134
  130.3 1.8 %fusion.35 = f32[128,512]{1,0:T(8,128)S(1)} fusion(f32[128,512]{1,0:T(8,128)S(1)} %fusion.30, bf16[512,26624]{1,0:T(8,128)(2,1)S(1)} %bitcast.118, bf16[64,4992]{1,0:T(8,128)(2,1)S(1)} %collective-permute-done.48, bf16[64,4992]{1,0:T(8,128)(2,1)S(1)} %constant_dynamic-update-slice_fusion.28), kind=kOutput, calls=%fused_computation.33 | convolution fusion | flops 656932864 | bytes 6914048 | tf_op jit(solution)/shard_map/dot_general | solution.py:134
  132.6 4.1 %collective-permute-start.51 = (bf16[32,512]{1,0:T(8,128)(2,1)S(1)}, bf16[32,512]{1,0:T(8,128)(2,1)S(1)}, u32[]{:S(2)}, u32[]{:S(2)}) collective-permute-start(bf16[32,512]{1,0:T(8,128)(2,1)S(1)} %get-tuple-element.248), channel_id=1, source_target_pairs={{0,6},{1,7},{2,4},{3,5},{4,2},{5,3},{6,0},{7,1},{8,14},{9,15},{10,... | collective-permute-start | bytes 98312 | tf_op jit(solution)/shard_map/ppermute | solution.py:165
  136.9 0.5 collective-permute-start.49
  137.4 1.2 collective-permute-done.51
  138.6 3.1 %collective-permute-done.50 = bf16[32,512]{1,0:T(8,128)(2,1)S(1)} collective-permute-done((bf16[32,512]{1,0:T(8,128)(2,1)S(1)}, bf16[32,512]{1,0:T(8,128)(2,1)S(1)}, u32[]{:S(2)}, u32[]{:S(2)}) %collective-permute-start.50) | collective-permute-done | bytes 32800 | tf_op jit(solution)/shard_map/ppermute | solution.py:165
  141.9 1.2 collective-permute-done.52
  143.4 0.6 copy-done
  144.0 0.6 constant_dynamic-update-slice_fusion.30
  (165 shorter events, 8.0 us)
Async XLA Ops:
  0.0 8.1 %copy-start.1 = (pred[128]{0:T(512)(128)(4,1)S(1)}, pred[128]{0:T(512)(128)(4,1)}, u32[]{:S(2)}) copy-start(pred[128]{0:T(512)(128)(4,1)} %constant.39.clone) | copy-start | bytes 388
  0.0 8.1 %copy-start.2 = (s32[128]{0:T(128)S(1)}, s32[128]{0:T(128)}, u32[]{:S(2)}) copy-start(s32[128]{0:T(128)} %constant.38.clone) | copy-start | bytes 1540
  0.0 8.1 %copy-start.3 = (s32[128]{0:T(128)S(1)}, s32[128]{0:T(128)}, u32[]{:S(2)}) copy-start(s32[128]{0:T(128)} %constant.37.clone) | copy-start | bytes 1540
  0.9 1.4 collective-permute-start
  2.5 10.6 %collective-permute-start.3 = (bf16[32,512]{1,0:T(8,128)(2,1)S(1)}, bf16[32,512]{1,0:T(8,128)(2,1)S(1)}, u32[]{:S(2)}, u32[]{:S(2)}) collective-permute-start(bf16[32,512]{1,0:T(8,128)(2,1)S(1)} %get-tuple-element.252), channel_id=1, source_target_pairs={{0,6},{1,7},{2,4},{3,5},{4,2},{5,3},{6,0},{7,1},{8,14},{9,15},{10,... | collective-permute-start | bytes 98312 | tf_op jit(solution)/shard_map/ppermute | solution.py:165
  7.5 5.6 %collective-permute-start.2 = (bf16[32,512]{1,0:T(8,128)(2,1)S(1)}, bf16[32,512]{1,0:T(8,128)(2,1)S(1)}, u32[]{:S(2)}, u32[]{:S(2)}) collective-permute-start(bf16[32,512]{1,0:T(8,128)(2,1)S(1)} %get-tuple-element.253), channel_id=1, source_target_pairs={{0,4},{1,5},{2,6},{3,7},{4,0},{5,1},{6,2},{7,3},{8,12},{9,13},{10,... | collective-permute-start | bytes 98312 | tf_op jit(solution)/shard_map/ppermute | solution.py:165
  7.5 5.6 %collective-permute-start.1 = (bf16[32,512]{1,0:T(8,128)(2,1)S(1)}, bf16[32,512]{1,0:T(8,128)(2,1)S(1)}, u32[]{:S(2)}, u32[]{:S(2)}) collective-permute-start(bf16[32,512]{1,0:T(8,128)(2,1)S(1)} %get-tuple-element.254), channel_id=1, source_target_pairs={{0,2},{1,3},{2,0},{3,1},{4,6},{5,7},{6,4},{7,5},{8,10},{9,11},{10,... | collective-permute-start | bytes 98312 | tf_op jit(solution)/shard_map/ppermute | solution.py:165
  15.4 4.2 %collective-permute-start.4 = (bf16[2,64,6656]{2,1,0:T(8,128)(2,1)S(1)}, bf16[2,64,6656]{2,1,0:T(8,128)(2,1)S(1)}, u32[]{:S(2)}, u32[]{:S(2)}) collective-permute-start(bf16[2,64,6656]{2,1,0:T(8,128)(2,1)S(1)} %get-tuple-element.112), channel_id=1, source_target_pairs={{0,1},{1,0},{2,3},{3,2},{4,5},{5,4},{6,7},{7,6},{8,9},{9,8},{10,11... | collective-permute-start | bytes 5111816 | tf_op jit(solution)/shard_map/ppermute | solution.py:165
  19.0 8.2 %collective-permute-start.6 = (bf16[2,64,3328]{2,1,0:T(8,128)(2,1)S(1)}, bf16[2,64,3328]{2,1,0:T(8,128)(2,1)S(1)}, u32[]{:S(2)}, u32[]{:S(2)}) collective-permute-start(bf16[2,64,3328]{2,1,0:T(8,128)(2,1)S(1)} %get-tuple-element.114), channel_id=1, source_target_pairs={{0,1},{1,0},{2,3},{3,2},{4,5},{5,4},{6,7},{7,6},{8,9},{9,8},{10,11... | collective-permute-start | bytes 2555912 | tf_op jit(solution)/shard_map/ppermute | solution.py:165
  19.9 12.8 %collective-permute-start.5 = (bf16[2,32,6656]{2,1,0:T(8,128)(2,1)S(1)}, bf16[2,32,6656]{2,1,0:T(8,128)(2,1)S(1)}, u32[]{:S(2)}, u32[]{:S(2)}) collective-permute-start(bf16[2,32,6656]{2,1,0:T(8,128)(2,1)S(1)} %get-tuple-element.217), channel_id=1, source_target_pairs={{0,8},{1,17},{2,10},{3,19},{4,12},{5,21},{6,14},{7,23},{8,0},{9,25... | collective-permute-start | bytes 2555912 | tf_op jit(solution)/shard_map/ppermute | solution.py:165
  27.2 7.5 %collective-permute-start.9 = (bf16[2,64,6656]{2,1,0:T(8,128)(2,1)S(1)}, bf16[2,64,6656]{2,1,0:T(8,128)(2,1)S(1)}, u32[]{:S(2)}, u32[]{:S(2)}) collective-permute-start(bf16[2,64,6656]{2,1,0:T(8,128)(2,1)S(1)} %get-tuple-element.119), channel_id=1, source_target_pairs={{0,1},{1,0},{2,3},{3,2},{4,5},{5,4},{6,7},{7,6},{8,9},{9,8},{10,11... | collective-permute-start | bytes 5111816 | tf_op jit(solution)/shard_map/ppermute | solution.py:165
  27.5 13.7 %collective-permute-start.8 = (bf16[2,32,3328]{2,1,0:T(8,128)(2,1)S(1)}, bf16[2,32,3328]{2,1,0:T(8,128)(2,1)S(1)}, u32[]{:S(2)}, u32[]{:S(2)}) collective-permute-start(bf16[2,32,3328]{2,1,0:T(8,128)(2,1)S(1)} %get-tuple-element.226), channel_id=1, source_target_pairs={{0,8},{1,17},{2,10},{3,19},{4,12},{5,21},{6,14},{7,23},{8,0},{9,25... | collective-permute-start | bytes 1277960 | tf_op jit(solution)/shard_map/ppermute | solution.py:165
  32.9 12.6 %collective-permute-start.7 = (bf16[2,16,6656]{2,1,0:T(8,128)(2,1)S(1)}, bf16[2,16,6656]{2,1,0:T(8,128)(2,1)S(1)}, u32[]{:S(2)}, u32[]{:S(2)}) collective-permute-start(bf16[2,16,6656]{2,1,0:T(8,128)(2,1)S(1)} %get-tuple-element.227), channel_id=1, source_target_pairs={{0,16},{1,9},{2,18},{3,11},{4,20},{5,13},{6,22},{7,15},{8,24},{9,1... | collective-permute-start | bytes 1277960 | tf_op jit(solution)/shard_map/ppermute | solution.py:165
  35.1 19.1 %collective-permute-start.11 = (bf16[2,32,6656]{2,1,0:T(8,128)(2,1)S(1)}, bf16[2,32,6656]{2,1,0:T(8,128)(2,1)S(1)}, u32[]{:S(2)}, u32[]{:S(2)}) collective-permute-start(bf16[2,32,6656]{2,1,0:T(8,128)(2,1)S(1)} %get-tuple-element.216), channel_id=1, source_target_pairs={{0,8},{1,17},{2,10},{3,19},{4,12},{5,21},{6,14},{7,23},{8,0},{9,25... | collective-permute-start | bytes 2555912 | tf_op jit(solution)/shard_map/ppermute | solution.py:165
  45.7 9.4 %collective-permute-start.10 = (bf16[2,8,6656]{2,1,0:T(8,128)(2,1)S(1)}, bf16[2,8,6656]{2,1,0:T(8,128)(2,1)S(1)}, u32[]{:S(2)}, u32[]{:S(2)}) collective-permute-start(bf16[2,8,6656]{2,1,0:T(8,128)(2,1)S(1)} %get-tuple-element.237), channel_id=1, source_target_pairs={{0,2},{1,5},{2,0},{3,7},{4,6},{5,1},{6,4},{7,3},{8,10},{9,13},{10,... | collective-permute-start | bytes 638984 | tf_op jit(solution)/shard_map/ppermute | solution.py:165
  47.2 12.7 %collective-permute-start.15 = (bf16[2,16,3328]{2,1,0:T(8,128)(2,1)S(1)}, bf16[2,16,3328]{2,1,0:T(8,128)(2,1)S(1)}, u32[]{:S(2)}, u32[]{:S(2)}) collective-permute-start(bf16[2,16,3328]{2,1,0:T(8,128)(2,1)S(1)} %get-tuple-element.236), channel_id=1, source_target_pairs={{0,16},{1,9},{2,18},{3,11},{4,20},{5,13},{6,22},{7,15},{8,24},{9,1... | collective-permute-start | bytes 638984 | tf_op jit(solution)/shard_map/ppermute | solution.py:165
  48.8 9.3 %collective-permute-start.16 = (bf16[2,64,4992]{2,1,0:T(8,128)(2,1)S(1)}, bf16[2,64,4992]{2,1,0:T(8,128)(2,1)S(1)}, u32[]{:S(2)}, u32[]{:S(2)}) collective-permute-start(bf16[2,64,4992]{2,1,0:T(8,128)(2,1)S(1)} %get-tuple-element.128), channel_id=1, source_target_pairs={{0,1},{1,0},{2,3},{3,2},{4,5},{5,4},{6,7},{7,6},{8,9},{9,8},{10,11... | collective-permute-start | bytes 3833864 | tf_op jit(solution)/shard_map/ppermute | solution.py:165
  48.8 64.0 %slice-start = ((s8[27262976]{0:T(1024)(128)(4,1)}), s8[4194304]{0:T(1024)(128)(4,1)S(1)}, s32[]{:S(2)}) async-start(s8[27262976]{0:T(1024)(128)(4,1)} %bitcast.117), calls=%async_computation | async-start | bytes 8388608
  48.8 64.0 %slice-start.1 = ((s8[27262976]{0:T(1024)(128)(4,1)}), s8[4194304]{0:T(1024)(128)(4,1)S(1)}, s32[]{:S(2)}) async-start(s8[27262976]{0:T(1024)(128)(4,1)} %bitcast.117), calls=%async_computation.1 | async-start | bytes 8388608
  48.8 64.0 %slice-start.2 = ((s8[27262976]{0:T(1024)(128)(4,1)}), s8[4194304]{0:T(1024)(128)(4,1)S(1)}, s32[]{:S(2)}) async-start(s8[27262976]{0:T(1024)(128)(4,1)} %bitcast.117), calls=%async_computation.2 | async-start | bytes 8388608
  48.8 64.0 %slice-start.3 = ((s8[27262976]{0:T(1024)(128)(4,1)}), s8[4194304]{0:T(1024)(128)(4,1)S(1)}, s32[]{:S(2)}) async-start(s8[27262976]{0:T(1024)(128)(4,1)} %bitcast.117), calls=%async_computation.3 | async-start | bytes 8388608
  48.8 64.0 %slice-start.4 = ((s8[27262976]{0:T(1024)(128)(4,1)}), s8[2097152]{0:T(1024)(128)(4,1)S(1)}, s32[]{:S(2)}) async-start(s8[27262976]{0:T(1024)(128)(4,1)} %bitcast.117), calls=%async_computation.4 | async-start | bytes 4194304
  53.7 7.8 %collective-permute-start.14 = (bf16[2,64,4992]{2,1,0:T(8,128)(2,1)S(1)}, bf16[2,64,4992]{2,1,0:T(8,128)(2,1)S(1)}, u32[]{:S(2)}, u32[]{:S(2)}) collective-permute-start(bf16[2,64,4992]{2,1,0:T(8,128)(2,1)S(1)} %get-tuple-element.134), channel_id=1, source_target_pairs={{0,1},{1,0},{2,3},{3,2},{4,5},{5,4},{6,7},{7,6},{8,9},{9,8},{10,11... | collective-permute-start | bytes 3833864 | tf_op jit(solution)/shard_map/ppermute | solution.py:165
  54.4 11.4 %collective-permute-start.13 = (bf16[2,16,6656]{2,1,0:T(8,128)(2,1)S(1)}, bf16[2,16,6656]{2,1,0:T(8,128)(2,1)S(1)}, u32[]{:S(2)}, u32[]{:S(2)}) collective-permute-start(bf16[2,16,6656]{2,1,0:T(8,128)(2,1)S(1)} %get-tuple-element.224), channel_id=1, source_target_pairs={{0,16},{1,9},{2,18},{3,11},{4,20},{5,13},{6,22},{7,15},{8,24},{9,1... | collective-permute-start | bytes 1277960 | tf_op jit(solution)/shard_map/ppermute | solution.py:165
  55.1 11.1 %collective-permute-start.12 = (bf16[2,8,6656]{2,1,0:T(8,128)(2,1)S(1)}, bf16[2,8,6656]{2,1,0:T(8,128)(2,1)S(1)}, u32[]{:S(2)}, u32[]{:S(2)}) collective-permute-start(bf16[2,8,6656]{2,1,0:T(8,128)(2,1)S(1)} %add_convert_fusion.22), channel_id=1, source_target_pairs={{0,4},{1,3},{2,6},{3,1},{4,0},{5,7},{6,2},{7,5},{8,12},{9,11},{10,... | collective-permute-start | bytes 638984 | tf_op jit(solution)/shard_map/ppermute | solution.py:165
  58.0 54.8 %slice-start.5 = ((s8[27262976]{0:T(1024)(128)(4,1)}), s8[4194304]{0:T(1024)(128)(4,1)S(1)}, s32[]{:S(2)}) async-start(s8[27262976]{0:T(1024)(128)(4,1)} %bitcast.117), calls=%async_computation.5 | async-start | bytes 8388608
  58.3 13.7 %collective-permute-start.19 = (bf16[2,32,4992]{2,1,0:T(8,128)(2,1)S(1)}, bf16[2,32,4992]{2,1,0:T(8,128)(2,1)S(1)}, u32[]{:S(2)}, u32[]{:S(2)}) collective-permute-start(bf16[2,32,4992]{2,1,0:T(8,128)(2,1)S(1)} %get-tuple-element.222), channel_id=1, source_target_pairs={{0,8},{1,17},{2,10},{3,19},{4,12},{5,21},{6,14},{7,23},{8,0},{9,25... | collective-permute-start | bytes 1916936 | tf_op jit(solution)/shard_map/ppermute | solution.py:165
  60.0 8.6 %collective-permute-start.20 = (bf16[2,8,3328]{2,1,0:T(8,128)(2,1)S(1)}, bf16[2,8,3328]{2,1,0:T(8,128)(2,1)S(1)}, u32[]{:S(2)}, u32[]{:S(2)}) collective-permute-start(bf16[2,8,3328]{2,1,0:T(8,128)(2,1)S(1)} %get-tuple-element.244), channel_id=1, source_target_pairs={{0,2},{1,5},{2,0},{3,7},{4,6},{5,1},{6,4},{7,3},{8,10},{9,13},{10,... | collective-permute-start | bytes 319496 | tf_op jit(solution)/shard_map/ppermute | solution.py:165
  61.7 21.3 %collective-permute-start.22 = (bf16[2,32,4992]{2,1,0:T(8,128)(2,1)S(1)}, bf16[2,32,4992]{2,1,0:T(8,128)(2,1)S(1)}, u32[]{:S(2)}, u32[]{:S(2)}) collective-permute-start(bf16[2,32,4992]{2,1,0:T(8,128)(2,1)S(1)} %get-tuple-element.220), channel_id=1, source_target_pairs={{0,8},{1,17},{2,10},{3,19},{4,12},{5,21},{6,14},{7,23},{8,0},{9,25... | collective-permute-start | bytes 1916936 | tf_op jit(solution)/shard_map/ppermute | solution.py:165
  65.9 12.3 %collective-permute-start.18 = (bf16[2,8,6656]{2,1,0:T(8,128)(2,1)S(1)}, bf16[2,8,6656]{2,1,0:T(8,128)(2,1)S(1)}, u32[]{:S(2)}, u32[]{:S(2)}) collective-permute-start(bf16[2,8,6656]{2,1,0:T(8,128)(2,1)S(1)} %get-tuple-element.234), channel_id=1, source_target_pairs={{0,2},{1,5},{2,0},{3,7},{4,6},{5,1},{6,4},{7,3},{8,10},{9,13},{10,... | collective-permute-start | bytes 638984 | tf_op jit(solution)/shard_map/ppermute | solution.py:165
  66.4 14.7 %collective-permute-start.17 = (bf16[8,6656]{1,0:T(8,128)(2,1)S(1)}, bf16[8,6656]{1,0:T(8,128)(2,1)S(1)}, u32[]{:S(2)}, u32[]{:S(2)}) collective-permute-start(bf16[8,6656]{1,0:T(8,128)(2,1)S(1)} %fusion.46), channel_id=1, source_target_pairs={{0,2},{1,5},{2,0},{3,7},{4,6},{5,1},{6,4},{7,3},{8,10},{9,13},{10,... | collective-permute-start | bytes 319496 | tf_op jit(solution)/shard_map/ppermute | solution.py:165
  68.6 12.6 %collective-permute-start.23 = (bf16[2,8,3328]{2,1,0:T(8,128)(2,1)S(1)}, bf16[2,8,3328]{2,1,0:T(8,128)(2,1)S(1)}, u32[]{:S(2)}, u32[]{:S(2)}) collective-permute-start(bf16[2,8,3328]{2,1,0:T(8,128)(2,1)S(1)} %add_convert_fusion.32), channel_id=1, source_target_pairs={{0,4},{1,3},{2,6},{3,1},{4,0},{5,7},{6,2},{7,5},{8,12},{9,11},{10,... | collective-permute-start | bytes 319496 | tf_op jit(solution)/shard_map/ppermute | solution.py:165
  72.2 11.4 %collective-permute-start.27 = (bf16[2,16,4992]{2,1,0:T(8,128)(2,1)S(1)}, bf16[2,16,4992]{2,1,0:T(8,128)(2,1)S(1)}, u32[]{:S(2)}, u32[]{:S(2)}) collective-permute-start(bf16[2,16,4992]{2,1,0:T(8,128)(2,1)S(1)} %get-tuple-element.230), channel_id=1, source_target_pairs={{0,16},{1,9},{2,18},{3,11},{4,20},{5,13},{6,22},{7,15},{8,24},{9,1... | collective-permute-start | bytes 958472 | tf_op jit(solution)/shard_map/ppermute | solution.py:165
  78.3 15.4 %collective-permute-start.26 = (bf16[2,8,6656]{2,1,0:T(8,128)(2,1)S(1)}, bf16[2,8,6656]{2,1,0:T(8,128)(2,1)S(1)}, u32[]{:S(2)}, u32[]{:S(2)}) collective-permute-start(bf16[2,8,6656]{2,1,0:T(8,128)(2,1)S(1)} %add_convert_fusion.18), channel_id=1, source_target_pairs={{0,4},{1,3},{2,6},{3,1},{4,0},{5,7},{6,2},{7,5},{8,12},{9,11},{10,... | collective-permute-start | bytes 638984 | tf_op jit(solution)/shard_map/ppermute | solution.py:165
  81.1 15.1 %collective-permute-start.21 = (bf16[16,6656]{1,0:T(8,128)(2,1)S(1)}, bf16[16,6656]{1,0:T(8,128)(2,1)S(1)}, u32[]{:S(2)}, u32[]{:S(2)}) collective-permute-start(bf16[16,6656]{1,0:T(8,128)(2,1)S(1)} %constant_dynamic-update-slice_fusion), channel_id=1, source_target_pairs={{0,16},{1,9},{2,18},{3,11},{4,20},{5,13},{6,22},{7,15},{8,24},{9,1... | collective-permute-start | bytes 638984 | tf_op jit(solution)/shard_map/ppermute | solution.py:165
  81.3 12.6 %collective-permute-start.25 = (bf16[8,3328]{1,0:T(8,128)(2,1)S(1)}, bf16[8,3328]{1,0:T(8,128)(2,1)S(1)}, u32[]{:S(2)}, u32[]{:S(2)}) collective-permute-start(bf16[8,3328]{1,0:T(8,128)(2,1)S(1)} %fusion.60), channel_id=1, source_target_pairs={{0,2},{1,5},{2,0},{3,7},{4,6},{5,1},{6,4},{7,3},{8,10},{9,13},{10,... | collective-permute-start | bytes 159752 | tf_op jit(solution)/shard_map/ppermute | solution.py:165
  83.1 29.8 %slice-start.6 = ((s8[27262976]{0:T(1024)(128)(4,1)}), s8[4194304]{0:T(1024)(128)(4,1)S(1)}, s32[]{:S(2)}) async-start(s8[27262976]{0:T(1024)(128)(4,1)} %bitcast.117), calls=%async_computation.6 | async-start | bytes 8388608
  83.2 11.3 %collective-permute-start.24 = (bf16[2,16,4992]{2,1,0:T(8,128)(2,1)S(1)}, bf16[2,16,4992]{2,1,0:T(8,128)(2,1)S(1)}, u32[]{:S(2)}, u32[]{:S(2)}) collective-permute-start(bf16[2,16,4992]{2,1,0:T(8,128)(2,1)S(1)} %get-tuple-element.231), channel_id=1, source_target_pairs={{0,16},{1,9},{2,18},{3,11},{4,20},{5,13},{6,22},{7,15},{8,24},{9,1... | collective-permute-start | bytes 958472 | tf_op jit(solution)/shard_map/ppermute | solution.py:165
  83.7 14.7 %collective-permute-start.29 = (bf16[2,8,4992]{2,1,0:T(8,128)(2,1)S(1)}, bf16[2,8,4992]{2,1,0:T(8,128)(2,1)S(1)}, u32[]{:S(2)}, u32[]{:S(2)}) collective-permute-start(bf16[2,8,4992]{2,1,0:T(8,128)(2,1)S(1)} %get-tuple-element.242), channel_id=1, source_target_pairs={{0,2},{1,5},{2,0},{3,7},{4,6},{5,1},{6,4},{7,3},{8,10},{9,13},{10,... | collective-permute-start | bytes 479240 | tf_op jit(solution)/shard_map/ppermute | solution.py:165
  93.8 5.3 %collective-permute-start.33 = (bf16[8,6656]{1,0:T(8,128)(2,1)S(1)}, bf16[8,6656]{1,0:T(8,128)(2,1)S(1)}, u32[]{:S(2)}, u32[]{:S(2)}) collective-permute-start(bf16[8,6656]{1,0:T(8,128)(2,1)S(1)} %fusion.44), channel_id=1, source_target_pairs={{0,2},{1,5},{2,0},{3,7},{4,6},{5,1},{6,4},{7,3},{8,10},{9,13},{10,... | collective-permute-start | bytes 319496 | tf_op jit(solution)/shard_map/ppermute | solution.py:165
  93.9 10.4 %collective-permute-start.31 = (bf16[16,3328]{1,0:T(8,128)(2,1)S(1)}, bf16[16,3328]{1,0:T(8,128)(2,1)S(1)}, u32[]{:S(2)}, u32[]{:S(2)}) collective-permute-start(bf16[16,3328]{1,0:T(8,128)(2,1)S(1)} %constant_dynamic-update-slice_fusion.2), channel_id=1, source_target_pairs={{0,16},{1,9},{2,18},{3,11},{4,20},{5,13},{6,22},{7,15},{8,24},{9,1... | collective-permute-start | bytes 319496 | tf_op jit(solution)/shard_map/ppermute | solution.py:165
  94.6 8.2 %collective-permute-start.32 = (bf16[2,8,4992]{2,1,0:T(8,128)(2,1)S(1)}, bf16[2,8,4992]{2,1,0:T(8,128)(2,1)S(1)}, u32[]{:S(2)}, u32[]{:S(2)}) collective-permute-start(bf16[2,8,4992]{2,1,0:T(8,128)(2,1)S(1)} %get-tuple-element.240), channel_id=1, source_target_pairs={{0,2},{1,5},{2,0},{3,7},{4,6},{5,1},{6,4},{7,3},{8,10},{9,13},{10,... | collective-permute-start | bytes 479240 | tf_op jit(solution)/shard_map/ppermute | solution.py:165
  96.2 10.6 %collective-permute-start.28 = (bf16[32,6656]{1,0:T(8,128)(2,1)S(1)}, bf16[32,6656]{1,0:T(8,128)(2,1)S(1)}, u32[]{:S(2)}, u32[]{:S(2)}) collective-permute-start(bf16[32,6656]{1,0:T(8,128)(2,1)S(1)} %constant_dynamic-update-slice_fusion.4), channel_id=1, source_target_pairs={{0,8},{1,17},{2,10},{3,19},{4,12},{5,21},{6,14},{7,23},{8,0},{9,25... | collective-permute-start | bytes 1277960 | tf_op jit(solution)/shard_map/ppermute | solution.py:165
  98.4 8.3 %collective-permute-start.30 = (bf16[2,8,4992]{2,1,0:T(8,128)(2,1)S(1)}, bf16[2,8,4992]{2,1,0:T(8,128)(2,1)S(1)}, u32[]{:S(2)}, u32[]{:S(2)}) collective-permute-start(bf16[2,8,4992]{2,1,0:T(8,128)(2,1)S(1)} %add_convert_fusion.28), channel_id=1, source_target_pairs={{0,4},{1,3},{2,6},{3,1},{4,0},{5,7},{6,2},{7,5},{8,12},{9,11},{10,... | collective-permute-start | bytes 479240 | tf_op jit(solution)/shard_map/ppermute | solution.py:165
  99.1 7.9 %collective-permute-start.37 = (bf16[16,6656]{1,0:T(8,128)(2,1)S(1)}, bf16[16,6656]{1,0:T(8,128)(2,1)S(1)}, u32[]{:S(2)}, u32[]{:S(2)}) collective-permute-start(bf16[16,6656]{1,0:T(8,128)(2,1)S(1)} %constant_dynamic-update-slice_fusion.6), channel_id=1, source_target_pairs={{0,16},{1,9},{2,18},{3,11},{4,20},{5,13},{6,22},{7,15},{8,24},{9,1... | collective-permute-start | bytes 638984 | tf_op jit(solution)/shard_map/ppermute | solution.py:165
  102.9 7.4 %collective-permute-start.36 = (bf16[2,8,4992]{2,1,0:T(8,128)(2,1)S(1)}, bf16[2,8,4992]{2,1,0:T(8,128)(2,1)S(1)}, u32[]{:S(2)}, u32[]{:S(2)}) collective-permute-start(bf16[2,8,4992]{2,1,0:T(8,128)(2,1)S(1)} %add_convert_fusion.26), channel_id=1, source_target_pairs={{0,4},{1,3},{2,6},{3,1},{4,0},{5,7},{6,2},{7,5},{8,12},{9,11},{10,... | collective-permute-start | bytes 479240 | tf_op jit(solution)/shard_map/ppermute | solution.py:165
  104.3 15.4 %collective-permute-start.39 = (bf16[32,3328]{1,0:T(8,128)(2,1)S(1)}, bf16[32,3328]{1,0:T(8,128)(2,1)S(1)}, u32[]{:S(2)}, u32[]{:S(2)}) collective-permute-start(bf16[32,3328]{1,0:T(8,128)(2,1)S(1)} %constant_dynamic-update-slice_fusion.8), channel_id=1, source_target_pairs={{0,8},{1,17},{2,10},{3,19},{4,12},{5,21},{6,14},{7,23},{8,0},{9,25... | collective-permute-start | bytes 638984 | tf_op jit(solution)/shard_map/ppermute | solution.py:165
  106.8 4.5 %collective-permute-start.35 = (bf16[8,4992]{1,0:T(8,128)(2,1)S(1)}, bf16[8,4992]{1,0:T(8,128)(2,1)S(1)}, u32[]{:S(2)}, u32[]{:S(2)}) collective-permute-start(bf16[8,4992]{1,0:T(8,128)(2,1)S(1)} %fusion.50), channel_id=1, source_target_pairs={{0,2},{1,5},{2,0},{3,7},{4,6},{5,1},{6,4},{7,3},{8,10},{9,13},{10,... | collective-permute-start | bytes 239624 | tf_op jit(solution)/shard_map/ppermute | solution.py:165
  107.0 5.8 %collective-permute-start.34 = (bf16[64,6656]{1,0:T(8,128)(2,1)S(1)}, bf16[64,6656]{1,0:T(8,128)(2,1)S(1)}, u32[]{:S(2)}, u32[]{:S(2)}) collective-permute-start(bf16[64,6656]{1,0:T(8,128)(2,1)S(1)} %constant_dynamic-update-slice_fusion.10), channel_id=1, source_target_pairs={{0,1},{1,0},{2,3},{3,2},{4,5},{5,4},{6,7},{7,6},{8,9},{9,8},{10,11... | collective-permute-start | bytes 2555912 | tf_op jit(solution)/shard_map/ppermute | solution.py:165
  107.1 12.7 %collective-permute-start.38 = (bf16[32,6656]{1,0:T(8,128)(2,1)S(1)}, bf16[32,6656]{1,0:T(8,128)(2,1)S(1)}, u32[]{:S(2)}, u32[]{:S(2)}) collective-permute-start(bf16[32,6656]{1,0:T(8,128)(2,1)S(1)} %constant_dynamic-update-slice_fusion.12), channel_id=1, source_target_pairs={{0,8},{1,17},{2,10},{3,19},{4,12},{5,21},{6,14},{7,23},{8,0},{9,25... | collective-permute-start | bytes 1277960 | tf_op jit(solution)/shard_map/ppermute | solution.py:165
  110.4 4.9 %collective-permute-start.41 = (bf16[8,4992]{1,0:T(8,128)(2,1)S(1)}, bf16[8,4992]{1,0:T(8,128)(2,1)S(1)}, u32[]{:S(2)}, u32[]{:S(2)}) collective-permute-start(bf16[8,4992]{1,0:T(8,128)(2,1)S(1)} %fusion.48), channel_id=1, source_target_pairs={{0,2},{1,5},{2,0},{3,7},{4,6},{5,1},{6,4},{7,3},{8,10},{9,13},{10,... | collective-permute-start | bytes 239624 | tf_op jit(solution)/shard_map/ppermute | solution.py:165
  111.3 5.3 %collective-permute-start.40 = (bf16[16,4992]{1,0:T(8,128)(2,1)S(1)}, bf16[16,4992]{1,0:T(8,128)(2,1)S(1)}, u32[]{:S(2)}, u32[]{:S(2)}) collective-permute-start(bf16[16,4992]{1,0:T(8,128)(2,1)S(1)} %constant_dynamic-update-slice_fusion.14), channel_id=1, source_target_pairs={{0,16},{1,9},{2,18},{3,11},{4,20},{5,13},{6,22},{7,15},{8,24},{9,1... | collective-permute-start | bytes 479240 | tf_op jit(solution)/shard_map/ppermute | solution.py:165
  115.3 5.3 %collective-permute-start.43 = (bf16[16,4992]{1,0:T(8,128)(2,1)S(1)}, bf16[16,4992]{1,0:T(8,128)(2,1)S(1)}, u32[]{:S(2)}, u32[]{:S(2)}) collective-permute-start(bf16[16,4992]{1,0:T(8,128)(2,1)S(1)} %constant_dynamic-update-slice_fusion.16), channel_id=1, source_target_pairs={{0,16},{1,9},{2,18},{3,11},{4,20},{5,13},{6,22},{7,15},{8,24},{9,1... | collective-permute-start | bytes 479240 | tf_op jit(solution)/shard_map/ppermute | solution.py:165
  116.7 8.7 %collective-permute-start.45 = (bf16[32,4992]{1,0:T(8,128)(2,1)S(1)}, bf16[32,4992]{1,0:T(8,128)(2,1)S(1)}, u32[]{:S(2)}, u32[]{:S(2)}) collective-permute-start(bf16[32,4992]{1,0:T(8,128)(2,1)S(1)} %constant_dynamic-update-slice_fusion.18), channel_id=1, source_target_pairs={{0,8},{1,17},{2,10},{3,19},{4,12},{5,21},{6,14},{7,23},{8,0},{9,25... | collective-permute-start | bytes 958472 | tf_op jit(solution)/shard_map/ppermute | solution.py:165
  119.8 5.9 %collective-permute-start.44 = (bf16[64,3328]{1,0:T(8,128)(2,1)S(1)}, bf16[64,3328]{1,0:T(8,128)(2,1)S(1)}, u32[]{:S(2)}, u32[]{:S(2)}) collective-permute-start(bf16[64,3328]{1,0:T(8,128)(2,1)S(1)} %constant_dynamic-update-slice_fusion.20), channel_id=1, source_target_pairs={{0,1},{1,0},{2,3},{3,2},{4,5},{5,4},{6,7},{7,6},{8,9},{9,8},{10,11... | collective-permute-start | bytes 1277960 | tf_op jit(solution)/shard_map/ppermute | solution.py:165
  119.9 3.0 %collective-permute-start.42 = (bf16[64,6656]{1,0:T(8,128)(2,1)S(1)}, bf16[64,6656]{1,0:T(8,128)(2,1)S(1)}, u32[]{:S(2)}, u32[]{:S(2)}) collective-permute-start(bf16[64,6656]{1,0:T(8,128)(2,1)S(1)} %constant_dynamic-update-slice_fusion.22), channel_id=1, source_target_pairs={{0,1},{1,0},{2,3},{3,2},{4,5},{5,4},{6,7},{7,6},{8,9},{9,8},{10,11... | collective-permute-start | bytes 2555912 | tf_op jit(solution)/shard_map/ppermute | solution.py:165
  120.7 7.4 %collective-permute-start.47 = (bf16[32,4992]{1,0:T(8,128)(2,1)S(1)}, bf16[32,4992]{1,0:T(8,128)(2,1)S(1)}, u32[]{:S(2)}, u32[]{:S(2)}) collective-permute-start(bf16[32,4992]{1,0:T(8,128)(2,1)S(1)} %constant_dynamic-update-slice_fusion.24), channel_id=1, source_target_pairs={{0,8},{1,17},{2,10},{3,19},{4,12},{5,21},{6,14},{7,23},{8,0},{9,25... | collective-permute-start | bytes 958472 | tf_op jit(solution)/shard_map/ppermute | solution.py:165
  125.4 2.8 %collective-permute-start.46 = (bf16[64,4992]{1,0:T(8,128)(2,1)S(1)}, bf16[64,4992]{1,0:T(8,128)(2,1)S(1)}, u32[]{:S(2)}, u32[]{:S(2)}) collective-permute-start(bf16[64,4992]{1,0:T(8,128)(2,1)S(1)} %constant_dynamic-update-slice_fusion.26), channel_id=1, source_target_pairs={{0,1},{1,0},{2,3},{3,2},{4,5},{5,4},{6,7},{7,6},{8,9},{9,8},{10,11... | collective-permute-start | bytes 1916936 | tf_op jit(solution)/shard_map/ppermute | solution.py:165
  128.2 2.1 %collective-permute-start.48 = (bf16[64,4992]{1,0:T(8,128)(2,1)S(1)}, bf16[64,4992]{1,0:T(8,128)(2,1)S(1)}, u32[]{:S(2)}, u32[]{:S(2)}) collective-permute-start(bf16[64,4992]{1,0:T(8,128)(2,1)S(1)} %constant_dynamic-update-slice_fusion.28), channel_id=1, source_target_pairs={{0,1},{1,0},{2,3},{3,2},{4,5},{5,4},{6,7},{7,6},{8,9},{9,8},{10,11... | collective-permute-start | bytes 1916936 | tf_op jit(solution)/shard_map/ppermute | solution.py:165
  132.6 6.1 %collective-permute-start.51 = (bf16[32,512]{1,0:T(8,128)(2,1)S(1)}, bf16[32,512]{1,0:T(8,128)(2,1)S(1)}, u32[]{:S(2)}, u32[]{:S(2)}) collective-permute-start(bf16[32,512]{1,0:T(8,128)(2,1)S(1)} %get-tuple-element.248), channel_id=1, source_target_pairs={{0,6},{1,7},{2,4},{3,5},{4,2},{5,3},{6,0},{7,1},{8,14},{9,15},{10,... | collective-permute-start | bytes 98312 | tf_op jit(solution)/shard_map/ppermute | solution.py:165
  136.7 5.1 %collective-permute-start.50 = (bf16[32,512]{1,0:T(8,128)(2,1)S(1)}, bf16[32,512]{1,0:T(8,128)(2,1)S(1)}, u32[]{:S(2)}, u32[]{:S(2)}) collective-permute-start(bf16[32,512]{1,0:T(8,128)(2,1)S(1)} %get-tuple-element.249), channel_id=1, source_target_pairs={{0,4},{1,5},{2,6},{3,7},{4,0},{5,1},{6,2},{7,3},{8,12},{9,13},{10,... | collective-permute-start | bytes 98312 | tf_op jit(solution)/shard_map/ppermute | solution.py:165
  136.9 4.8 %collective-permute-start.49 = (bf16[32,512]{1,0:T(8,128)(2,1)S(1)}, bf16[32,512]{1,0:T(8,128)(2,1)S(1)}, u32[]{:S(2)}, u32[]{:S(2)}) collective-permute-start(bf16[32,512]{1,0:T(8,128)(2,1)S(1)} %get-tuple-element.250), channel_id=1, source_target_pairs={{0,2},{1,3},{2,0},{3,1},{4,6},{5,7},{6,4},{7,5},{8,10},{9,11},{10,... | collective-permute-start | bytes 98312 | tf_op jit(solution)/shard_map/ppermute | solution.py:165
  141.8 1.3 collective-permute-start.52
  143.3 0.7 copy-start

commit v5 on v4

--- a/solution.py
+++ b/solution.py
@@ -9,8 +9,9 @@
 from jax.sharding import PartitionSpec as P
 
 VMEM_BYTES = 28 * 2**20
-SHARES = (3,4,4,3,2)
-ORDER = (2, 4, 2, 1, 4, 2, 1, 0, 4, 2, 3, 1, 2, 0, 4, 3, 1, 2, 4, 0, 1, 2, 4, 3, 0, 1, 4, 3, 2, 0, 1, 3, 4, 0, 2, 1, 3, 0, 2, 3, 0, 4, 1, 3, 1, 0, 4, 3, 0, 3)
+SHARES = (4, 4, 3, 2, 3)
+PLANS = (0, 0, 0, 0, 1)
+ORDER = (0, 3, 0, 4, 3, 2, 4, 0, 2, 1, 3, 0, 1, 4, 2, 0, 3, 1, 4, 2, 0, 3, 1, 4, 2, 0, 3, 4, 1, 0, 2, 4, 3, 1, 2, 3, 0, 4, 1, 2, 0, 1, 3, 4, 2, 3, 4, 1, 2, 1)
 
 
 def step_order(chunks, steps):
@@ -157,8 +158,10 @@
     core = 1
     col_bits = [1 << k for k in range(1, n_col.bit_length() - 1)]
     row_bits = [n_col << k for k in range(n_row.bit_length() - 1)]
-    orders = (row_bits + col_bits, row_bits[::-1] + col_bits[::-1])
-    stages = list(zip(*orders))
+    plans = (
+        (row_bits + col_bits, row_bits[::-1] + col_bits[::-1]),
+        (col_bits + row_bits, col_bits[::-1] + row_bits[::-1]),
+    )
 
     def swap(value, bits):
         pairs = [(d, d ^ bits[d & core]) for d in range(n_row * n_col)]
@@ -194,26 +197,30 @@
             rows = (rows[:, None] + np.array([0, weight[bit]])).reshape(-1)
         return (rows[:, None] + np.arange(per_device)).reshape(-1)
 
-    own_first = [
-        np.concatenate([half_source(orders[k]), weight[core] + half_source(orders[1 - k])])
-        for k in range(2)
-    ]
-    source = jnp.where(on_upper, *(jnp.asarray(own_first[k], jnp.int32) for k in (1, 0)))
-    lasts = [jnp.where((device & o[-1]) != 0, weight[o[-1]], 0) for o in orders]
-    own_last, other_last = jnp.where(on_upper, lasts[1], lasts[0]), jnp.where(on_upper, *lasts)
-    is_own = np.arange(all_tokens) < all_tokens // 2
-    source = source ^ (row * per_device) ^ jnp.where(is_own, own_last, other_last)
-    pick = source[:, None] == lax.broadcasted_iota(jnp.int32, (all_tokens, all_tokens), 1)
-    x = jnp.dot(pick.astype(jnp.bfloat16), x, preferred_element_type=jnp.float32).astype(jnp.bfloat16)
-
-    total = [jnp.zeros((all_tokens, features), jnp.float32)]
-    last = [x]
+    def scattered(orders):
+        own_first = [
+            np.concatenate([half_source(orders[k]), weight[core] + half_source(orders[1 - k])])
+            for k in range(2)
+        ]
+        source = jnp.where(on_upper, *(jnp.asarray(own_first[k], jnp.int32) for k in (1, 0)))
+        lasts = [jnp.where((device & o[-1]) != 0, weight[o[-1]], 0) for o in orders]
+        own_last, other_last = jnp.where(on_upper, lasts[1], lasts[0]), jnp.where(on_upper, *lasts)
+        is_own = np.arange(all_tokens) < all_tokens // 2
+        return source ^ (row * per_device) ^ jnp.where(is_own, own_last, other_last)
+
+    source = jnp.concatenate([scattered(orders) for orders in plans])
+    pick = source[:, None] == lax.broadcasted_iota(jnp.int32, (len(plans) * all_tokens, all_tokens), 1)
+    placed = jnp.dot(pick.astype(jnp.bfloat16), x, preferred_element_type=jnp.float32).astype(jnp.bfloat16)
+
+    totals = [jnp.zeros((all_tokens, features), jnp.float32) for _ in plans]
+    last = [placed]
 
     def after(*values):
         return lax.optimization_barrier((values, last[0]))[0]
 
-    def steps(start, width, held):
-        (x_now,) = after(x)
+    def steps(plan, start, width, held):
+        stages = list(zip(*plans[plan]))
+        (x_now,) = after(placed[plan * all_tokens : (plan + 1) * all_tokens])
         if held is None:
             keep, send = gate_up(x_now, gate_weight, up_weight, start, width)
         else:
@@ -243,21 +250,21 @@
         other = swap(hidden, (core, core))
         yield
         own, other = after(hidden, other)
-        total[0] = last[0] = down(own, other, down_weight, total[0], start)
+        totals[plan] = last[0] = down(own, other, down_weight, totals[plan], start)
 
     share = units // sum(SHARES)
     ends = np.cumsum(SHARES) * share
-    turns = step_order(len(SHARES), 2 + 2 * len(stages))
+    turns = step_order(len(SHARES), 2 + 2 * len(plans[0][0]))
     running = []
     for chunk, (n, end) in enumerate(zip(SHARES, ends)):
         start, width = int(end) - n * share, n * share
         held = fetch(gate_weight, up_weight, start, width) if chunk == turns[0] else None
-        running.append(steps(start, width, held))
+        running.append(steps(PLANS[chunk], start, width, held))
     for chunk in turns:
         next(running[chunk], None)
 
     out = lax.dot_general(
-        pick.astype(jnp.float32), total[0], (((0,), (0,)), ((), ())),
+        pick.astype(jnp.float32), jnp.concatenate(totals, 0), (((0,), (0,)), ((), ())),
         precision=lax.Precision.HIGHEST, preferred_element_type=jnp.float32,
     ).astype(jnp.bfloat16)
 

time: 145 us -> 144 us (level)
  waiting for transfers between devices: 41.7 us -> 31.6 us
  starting transfers between devices: 59.8 us -> 68 us
    ppermute x53, waiting for transfers between devices: 41.7 us -> 31.6 us  [swap(): return lax.ppermute(value, ('row', 'col'), pairs)]
    ppermute x53, starting transfers between devices: 59.8 us -> 68 us  [swap(): return lax.ppermute(value, ('row', 'col'), pairs)]
  transfers between devices with their start and end apart: 53 -> 53, of which waited for: 18 -> 16; matrix products, arithmetic and copies ran while one was open for 8% -> 8% of each run, Pallas kernels for 16% -> 16%
where the time goes in v5:
time: 144 us; the launch traced here: 143 us
  starting transfers between devices  68 us (47%)
  waiting for transfers between devices  31.6 us (22%)
  Pallas kernels  25.4 us (18%)
  matrix products  10.4 us (7%)
  other arithmetic  4.41 us (3%)
  local copies, waits for them, and re-layouts  2.73 us (2%)
    ppermute x53, starting transfers between devices, swap(): return lax.ppermute(value, ('row', 'col'), pairs)  68 us
    ppermute x53, waiting for transfers between devices, swap(): return lax.ppermute(value, ('row', 'col'), pairs)  31.6 us
    pallas_call x4, Pallas kernels, gate_up(): pl.pallas_call(functools.partial(gate_up_kernel, start), grid=(blocks,),...  18.4 us
    dot_general x5, matrix products, down(): lax.dot_general(hidden, weight, (((1,), (1,)), ((), ())), preferred_eleme...  9.72 us
    pallas_call x1, Pallas kernels, fetch(): pl.pallas_call(functools.partial(fetch_kernel, start), in_specs=[pl.Block...  4.89 us
  transfers between devices with their start and end apart: 53, of which 16 were waited for; matrix products, arithmetic and copies ran while one was open for 8% of the time, Pallas kernels for 16%

profile of v5, /device:TPU:0, one launch (start us, length us, event | category | flops | bytes accessed | tf_op | source)
XLA Modules:
  0.0 143.5 jit_solution(3875732498546674636)
XLA Ops:
  0.0 0.8 slice_bitcast_fusion.30
  0.9 0.5 collective-permute-start
  1.4 0.7 fusion.66
  2.4 5.0 %collective-permute-start.3 = (bf16[32,512]{1,0:T(8,128)(2,1)S(1)}, bf16[32,512]{1,0:T(8,128)(2,1)S(1)}, u32[]{:S(2)}, u32[]{:S(2)}) collective-permute-start(bf16[32,512]{1,0:T(8,128)(2,1)S(1)} %get-tuple-element.254), channel_id=1, source_target_pairs={{0,6},{1,7},{2,4},{3,5},{4,2},{5,3},{6,0},{7,1},{8,14},{9,15},{10,... | collective-permute-start | bytes 98312 | tf_op jit(solution)/shard_map/ppermute | solution.py:168
  7.4 0.6 collective-permute-start.1
  8.1 4.9 %shard_map.100.held_ref = bf16[2,512,6656]{2,1,0:T(8,128)(2,1)S(1)} custom-call(bf16[512,26624]{1,0:T(8,128)(2,1)} %gate_ref.9, bf16[512,26624]{1,0:T(8,128)(2,1)} %up_ref.9), custom_call_target="tpu_custom_call" | custom-call | tf_op jit(solution)/shard_map/pallas_call | solution.py:95
  13.3 2.1 %shard_map.101 = (bf16[2,64,6656]{2,1,0:T(8,128)(2,1)S(1)}, bf16[2,64,6656]{2,1,0:T(8,128)(2,1)S(1)}) custom-call(bf16[128,512]{1,0:T(8,128)(2,1)S(1)} %get-tuple-element.132.x_ref, bf16[2,512,6656]{2,1,0:T(8,128)(2,1)S(1)} %shard_map.100.held_ref), custom_call_target="tpu_custom_call" | custom-call | tf_op jit(solution)/shard_map/pallas_call | solution.py:122
  15.5 3.5 %shard_map.102 = (bf16[2,64,3328]{2,1,0:T(8,128)(2,1)S(1)}, bf16[2,64,3328]{2,1,0:T(8,128)(2,1)S(1)}) custom-call(bf16[128,512]{1,0:T(8,128)(2,1)S(1)} %get-tuple-element.132.x_ref, bf16[512,26624]{1,0:T(8,128)(2,1)} %gate_ref.9, bf16[512,26624]{1,0:T(8,128)(2,1)} %up_ref.9), custom_call_target="tpu_custom_call" | custom-call | tf_op jit(solution)/shard_map/pallas_call | solution.py:62
  19.0 0.5 collective-permute-start.7
  20.0 4.5 %shard_map.103 = (bf16[2,64,4992]{2,1,0:T(8,128)(2,1)S(1)}, bf16[2,64,4992]{2,1,0:T(8,128)(2,1)S(1)}) custom-call(bf16[128,512]{1,0:T(8,128)(2,1)S(1)} %get-tuple-element.117.x_ref, bf16[512,26624]{1,0:T(8,128)(2,1)} %gate_ref.9, bf16[512,26624]{1,0:T(8,128)(2,1)} %up_ref.9), custom_call_target="tpu_custom_call" | custom-call | tf_op jit(solution)/shard_map/pallas_call | solution.py:62
  24.6 1.7 %collective-permute-start.5 = (bf16[2,32,6656]{2,1,0:T(8,128)(2,1)S(1)}, bf16[2,32,6656]{2,1,0:T(8,128)(2,1)S(1)}, u32[]{:S(2)}, u32[]{:S(2)}) collective-permute-start(bf16[2,32,6656]{2,1,0:T(8,128)(2,1)S(1)} %get-tuple-element.218), channel_id=1, source_target_pairs={{0,8},{1,17},{2,10},{3,19},{4,12},{5,21},{6,14},{7,23},{8,0},{9,25... | collective-permute-start | bytes 2555912 | tf_op jit(solution)/shard_map/ppermute | solution.py:168
  26.5 0.5 collective-permute-start.9
  26.9 4.5 %shard_map.104 = (bf16[2,64,4992]{2,1,0:T(8,128)(2,1)S(1)}, bf16[2,64,4992]{2,1,0:T(8,128)(2,1)S(1)}) custom-call(bf16[128,512]{1,0:T(8,128)(2,1)S(1)} %get-tuple-element.132.x_ref, bf16[512,26624]{1,0:T(8,128)(2,1)} %gate_ref.9, bf16[512,26624]{1,0:T(8,128)(2,1)} %up_ref.9), custom_call_target="tpu_custom_call" | custom-call | tf_op jit(solution)/shard_map/pallas_call | solution.py:62
  31.8 1.5 %collective-permute-start.13 = (bf16[2,32,4992]{2,1,0:T(8,128)(2,1)S(1)}, bf16[2,32,4992]{2,1,0:T(8,128)(2,1)S(1)}, u32[]{:S(2)}, u32[]{:S(2)}) collective-permute-start(bf16[2,32,4992]{2,1,0:T(8,128)(2,1)S(1)} %get-tuple-element.221), channel_id=1, source_target_pairs={{0,2},{1,5},{2,0},{3,7},{4,6},{5,1},{6,4},{7,3},{8,10},{9,13},{10,... | collective-permute-start | bytes 1916936 | tf_op jit(solution)/shard_map/ppermute | solution.py:168
  33.3 4.0 %collective-permute-done.5 = bf16[2,32,6656]{2,1,0:T(8,128)(2,1)S(1)} collective-permute-done((bf16[2,32,6656]{2,1,0:T(8,128)(2,1)S(1)}, bf16[2,32,6656]{2,1,0:T(8,128)(2,1)S(1)}, u32[]{:S(2)}, u32[]{:S(2)}) %collective-permute-start.5) | collective-permute-done | bytes 852000 | tf_op jit(solution)/shard_map/ppermute | solution.py:168
  37.5 1.7 %collective-permute-start.8 = (bf16[2,16,6656]{2,1,0:T(8,128)(2,1)S(1)}, bf16[2,16,6656]{2,1,0:T(8,128)(2,1)S(1)}, u32[]{:S(2)}, u32[]{:S(2)}) collective-permute-start(bf16[2,16,6656]{2,1,0:T(8,128)(2,1)S(1)} %get-tuple-element.228), channel_id=1, source_target_pairs={{0,16},{1,9},{2,18},{3,11},{4,20},{5,13},{6,22},{7,15},{8,24},{9,1... | collective-permute-start | bytes 1277960 | tf_op jit(solution)/shard_map/ppermute | solution.py:168
  39.6 1.5 %collective-permute-start.12 = (bf16[2,32,4992]{2,1,0:T(8,128)(2,1)S(1)}, bf16[2,32,4992]{2,1,0:T(8,128)(2,1)S(1)}, u32[]{:S(2)}, u32[]{:S(2)}) collective-permute-start(bf16[2,32,4992]{2,1,0:T(8,128)(2,1)S(1)} %get-tuple-element.220), channel_id=1, source_target_pairs={{0,8},{1,17},{2,10},{3,19},{4,12},{5,21},{6,14},{7,23},{8,0},{9,25... | collective-permute-start | bytes 1916936 | tf_op jit(solution)/shard_map/ppermute | solution.py:168
  41.1 5.9 %shard_map.105 = (bf16[2,64,6656]{2,1,0:T(8,128)(2,1)S(1)}, bf16[2,64,6656]{2,1,0:T(8,128)(2,1)S(1)}) custom-call(bf16[128,512]{1,0:T(8,128)(2,1)S(1)} %get-tuple-element.132.x_ref, bf16[512,26624]{1,0:T(8,128)(2,1)} %gate_ref.9, bf16[512,26624]{1,0:T(8,128)(2,1)} %up_ref.9), custom_call_target="tpu_custom_call" | custom-call | tf_op jit(solution)/shard_map/pallas_call | solution.py:62
  47.2 0.6 collective-permute-start.19
  47.8 2.6 %collective-permute-done.8 = bf16[2,16,6656]{2,1,0:T(8,128)(2,1)S(1)} collective-permute-done((bf16[2,16,6656]{2,1,0:T(8,128)(2,1)S(1)}, bf16[2,16,6656]{2,1,0:T(8,128)(2,1)S(1)}, u32[]{:S(2)}, u32[]{:S(2)}) %collective-permute-start.8) | collective-permute-done | bytes 426016 | tf_op jit(solution)/shard_map/ppermute | solution.py:168
  50.5 1.5 %collective-permute-start.11 = (bf16[2,8,6656]{2,1,0:T(8,128)(2,1)S(1)}, bf16[2,8,6656]{2,1,0:T(8,128)(2,1)S(1)}, u32[]{:S(2)}, u32[]{:S(2)}) collective-permute-start(bf16[2,8,6656]{2,1,0:T(8,128)(2,1)S(1)} %get-tuple-element.236), channel_id=1, source_target_pairs={{0,2},{1,5},{2,0},{3,7},{4,6},{5,1},{6,4},{7,3},{8,10},{9,13},{10,... | collective-permute-start | bytes 638984 | tf_op jit(solution)/shard_map/ppermute | solution.py:168
  51.9 0.5 add_convert_fusion
  52.4 1.6 %collective-permute-start.18 = (bf16[2,32,6656]{2,1,0:T(8,128)(2,1)S(1)}, bf16[2,32,6656]{2,1,0:T(8,128)(2,1)S(1)}, u32[]{:S(2)}, u32[]{:S(2)}) collective-permute-start(bf16[2,32,6656]{2,1,0:T(8,128)(2,1)S(1)} %get-tuple-element.216), channel_id=1, source_target_pairs={{0,8},{1,17},{2,10},{3,19},{4,12},{5,21},{6,14},{7,23},{8,0},{9,25... | collective-permute-start | bytes 2555912 | tf_op jit(solution)/shard_map/ppermute | solution.py:168
  54.1 3.0 %collective-permute-start.17 = (bf16[2,16,4992]{2,1,0:T(8,128)(2,1)S(1)}, bf16[2,16,4992]{2,1,0:T(8,128)(2,1)S(1)}, u32[]{:S(2)}, u32[]{:S(2)}) collective-permute-start(bf16[2,16,4992]{2,1,0:T(8,128)(2,1)S(1)} %get-tuple-element.231), channel_id=1, source_target_pairs={{0,4},{1,3},{2,6},{3,1},{4,0},{5,7},{6,2},{7,5},{8,12},{9,11},{10,... | collective-permute-start | bytes 958472 | tf_op jit(solution)/shard_map/ppermute | solution.py:168
  57.2 1.6 %collective-permute-start.16 = (bf16[2,16,4992]{2,1,0:T(8,128)(2,1)S(1)}, bf16[2,16,4992]{2,1,0:T(8,128)(2,1)S(1)}, u32[]{:S(2)}, u32[]{:S(2)}) collective-permute-start(bf16[2,16,4992]{2,1,0:T(8,128)(2,1)S(1)} %get-tuple-element.230), channel_id=1, source_target_pairs={{0,16},{1,9},{2,18},{3,11},{4,20},{5,13},{6,22},{7,15},{8,24},{9,1... | collective-permute-start | bytes 958472 | tf_op jit(solution)/shard_map/ppermute | solution.py:168
  58.9 8.0 %collective-permute-start.15 = (bf16[2,8,6656]{2,1,0:T(8,128)(2,1)S(1)}, bf16[2,8,6656]{2,1,0:T(8,128)(2,1)S(1)}, u32[]{:S(2)}, u32[]{:S(2)}) collective-permute-start(bf16[2,8,6656]{2,1,0:T(8,128)(2,1)S(1)} %add_convert_fusion.22), channel_id=1, source_target_pairs={{0,4},{1,3},{2,6},{3,1},{4,0},{5,7},{6,2},{7,5},{8,12},{9,11},{10,... | collective-permute-start | bytes 638984 | tf_op jit(solution)/shard_map/ppermute | solution.py:168
  67.0 2.8 %collective-permute-start.24 = (bf16[2,8,3328]{2,1,0:T(8,128)(2,1)S(1)}, bf16[2,8,3328]{2,1,0:T(8,128)(2,1)S(1)}, u32[]{:S(2)}, u32[]{:S(2)}) collective-permute-start(bf16[2,8,3328]{2,1,0:T(8,128)(2,1)S(1)} %get-tuple-element.244), channel_id=1, source_target_pairs={{0,2},{1,5},{2,0},{3,7},{4,6},{5,1},{6,4},{7,3},{8,10},{9,13},{10,... | collective-permute-start | bytes 319496 | tf_op jit(solution)/shard_map/ppermute | solution.py:168
  69.9 1.6 %collective-permute-start.23 = (bf16[2,16,6656]{2,1,0:T(8,128)(2,1)S(1)}, bf16[2,16,6656]{2,1,0:T(8,128)(2,1)S(1)}, u32[]{:S(2)}, u32[]{:S(2)}) collective-permute-start(bf16[2,16,6656]{2,1,0:T(8,128)(2,1)S(1)} %get-tuple-element.224), channel_id=1, source_target_pairs={{0,16},{1,9},{2,18},{3,11},{4,20},{5,13},{6,22},{7,15},{8,24},{9,1... | collective-permute-start | bytes 1277960 | tf_op jit(solution)/shard_map/ppermute | solution.py:168
  71.6 1.6 %collective-permute-start.22 = (bf16[2,8,4992]{2,1,0:T(8,128)(2,1)S(1)}, bf16[2,8,4992]{2,1,0:T(8,128)(2,1)S(1)}, u32[]{:S(2)}, u32[]{:S(2)}) collective-permute-start(bf16[2,8,4992]{2,1,0:T(8,128)(2,1)S(1)} %get-tuple-element.241), channel_id=1, source_target_pairs={{0,8},{1,17},{2,10},{3,19},{4,12},{5,21},{6,14},{7,23},{8,0},{9,25... | collective-permute-start | bytes 479240 | tf_op jit(solution)/shard_map/ppermute | solution.py:168
  73.5 2.1 %collective-permute-start.20 = (bf16[8,6656]{1,0:T(8,128)(2,1)S(1)}, bf16[8,6656]{1,0:T(8,128)(2,1)S(1)}, u32[]{:S(2)}, u32[]{:S(2)}) collective-permute-start(bf16[8,6656]{1,0:T(8,128)(2,1)S(1)} %fusion.44), channel_id=1, source_target_pairs={{0,2},{1,5},{2,0},{3,7},{4,6},{5,1},{6,4},{7,3},{8,10},{9,13},{10,... | collective-permute-start | bytes 319496 | tf_op jit(solution)/shard_map/ppermute | solution.py:168
  75.6 2.1 %collective-permute-start.28 = (bf16[2,8,3328]{2,1,0:T(8,128)(2,1)S(1)}, bf16[2,8,3328]{2,1,0:T(8,128)(2,1)S(1)}, u32[]{:S(2)}, u32[]{:S(2)}) collective-permute-start(bf16[2,8,3328]{2,1,0:T(8,128)(2,1)S(1)} %add_convert_fusion.32), channel_id=1, source_target_pairs={{0,4},{1,3},{2,6},{3,1},{4,0},{5,7},{6,2},{7,5},{8,12},{9,11},{10,... | collective-permute-start | bytes 319496 | tf_op jit(solution)/shard_map/ppermute | solution.py:168
  77.7 0.7 collective-permute-done.23
  78.5 1.3 collective-permute-start.26
  79.8 1.7 %collective-permute-start.27 = (bf16[2,8,4992]{2,1,0:T(8,128)(2,1)S(1)}, bf16[2,8,4992]{2,1,0:T(8,128)(2,1)S(1)}, u32[]{:S(2)}, u32[]{:S(2)}) collective-permute-start(bf16[2,8,4992]{2,1,0:T(8,128)(2,1)S(1)} %add_convert_fusion.27), channel_id=1, source_target_pairs={{0,16},{1,9},{2,18},{3,11},{4,20},{5,13},{6,22},{7,15},{8,24},{9,1... | collective-permute-start | bytes 479240 | tf_op jit(solution)/shard_map/ppermute | solution.py:168
  81.6 2.5 %collective-permute-done.21 = bf16[2,8,4992]{2,1,0:T(8,128)(2,1)S(1)} collective-permute-done((bf16[2,8,4992]{2,1,0:T(8,128)(2,1)S(1)}, bf16[2,8,4992]{2,1,0:T(8,128)(2,1)S(1)}, u32[]{:S(2)}, u32[]{:S(2)}) %collective-permute-start.21) | collective-permute-done | bytes 159776 | tf_op jit(solution)/shard_map/ppermute | solution.py:168
  84.5 2.0 %collective-permute-done.20 = bf16[8,6656]{1,0:T(8,128)(2,1)S(1)} collective-permute-done((bf16[8,6656]{1,0:T(8,128)(2,1)S(1)}, bf16[8,6656]{1,0:T(8,128)(2,1)S(1)}, u32[]{:S(2)}, u32[]{:S(2)}) %collective-permute-start.20) | collective-permute-done | bytes 106528 | tf_op jit(solution)/shard_map/ppermute | solution.py:168
  87.1 1.9 %collective-permute-start.31 = (bf16[8,4992]{1,0:T(8,128)(2,1)S(1)}, bf16[8,4992]{1,0:T(8,128)(2,1)S(1)}, u32[]{:S(2)}, u32[]{:S(2)}) collective-permute-start(bf16[8,4992]{1,0:T(8,128)(2,1)S(1)} %fusion.48), channel_id=1, source_target_pairs={{0,8},{1,17},{2,10},{3,19},{4,12},{5,21},{6,14},{7,23},{8,0},{9,25... | collective-permute-start | bytes 239624 | tf_op jit(solution)/shard_map/ppermute | solution.py:168
  89.0 3.8 %collective-permute-done.26 = bf16[2,8,6656]{2,1,0:T(8,128)(2,1)S(1)} collective-permute-done((bf16[2,8,6656]{2,1,0:T(8,128)(2,1)S(1)}, bf16[2,8,6656]{2,1,0:T(8,128)(2,1)S(1)}, u32[]{:S(2)}, u32[]{:S(2)}) %collective-permute-start.26) | collective-permute-done | bytes 213024 | tf_op jit(solution)/shard_map/ppermute | solution.py:168
  92.8 2.8 %collective-permute-start.35 = (bf16[2,8,6656]{2,1,0:T(8,128)(2,1)S(1)}, bf16[2,8,6656]{2,1,0:T(8,128)(2,1)S(1)}, u32[]{:S(2)}, u32[]{:S(2)}) collective-permute-start(bf16[2,8,6656]{2,1,0:T(8,128)(2,1)S(1)} %add_convert_fusion.18), channel_id=1, source_target_pairs={{0,4},{1,3},{2,6},{3,1},{4,0},{5,7},{6,2},{7,5},{8,12},{9,11},{10,... | collective-permute-start | bytes 638984 | tf_op jit(solution)/shard_map/ppermute | solution.py:168
  95.9 2.5 %collective-permute-start.34 = (bf16[8,4992]{1,0:T(8,128)(2,1)S(1)}, bf16[8,4992]{1,0:T(8,128)(2,1)S(1)}, u32[]{:S(2)}, u32[]{:S(2)}) collective-permute-start(bf16[8,4992]{1,0:T(8,128)(2,1)S(1)} %fusion.46), channel_id=1, source_target_pairs={{0,2},{1,5},{2,0},{3,7},{4,6},{5,1},{6,4},{7,3},{8,10},{9,13},{10,... | collective-permute-start | bytes 239624 | tf_op jit(solution)/shard_map/ppermute | solution.py:168
  98.5 2.6 %collective-permute-start.39 = (bf16[16,4992]{1,0:T(8,128)(2,1)S(1)}, bf16[16,4992]{1,0:T(8,128)(2,1)S(1)}, u32[]{:S(2)}, u32[]{:S(2)}) collective-permute-start(bf16[16,4992]{1,0:T(8,128)(2,1)S(1)} %constant_dynamic-update-slice_fusion.4), channel_id=1, source_target_pairs={{0,4},{1,3},{2,6},{3,1},{4,0},{5,7},{6,2},{7,5},{8,12},{9,11},{10,... | collective-permute-start | bytes 479240 | tf_op jit(solution)/shard_map/ppermute | solution.py:168
  101.1 5.1 %collective-permute-done.35 = bf16[2,8,6656]{2,1,0:T(8,128)(2,1)S(1)} collective-permute-done((bf16[2,8,6656]{2,1,0:T(8,128)(2,1)S(1)}, bf16[2,8,6656]{2,1,0:T(8,128)(2,1)S(1)}, u32[]{:S(2)}, u32[]{:S(2)}) %collective-permute-start.35) | collective-permute-done | bytes 213024 | tf_op jit(solution)/shard_map/ppermute | solution.py:168
  106.3 1.1 collective-permute-start.38
  107.6 1.4 collective-permute-start.40
  109.3 1.8 %collective-permute-done.38 = bf16[8,6656]{1,0:T(8,128)(2,1)S(1)} collective-permute-done((bf16[8,6656]{1,0:T(8,128)(2,1)S(1)}, bf16[8,6656]{1,0:T(8,128)(2,1)S(1)}, u32[]{:S(2)}, u32[]{:S(2)}) %collective-permute-start.38) | collective-permute-done | bytes 106528 | tf_op jit(solution)/shard_map/ppermute | solution.py:168
  111.2 1.6 %collective-permute-done.37 = bf16[16,4992]{1,0:T(8,128)(2,1)S(1)} collective-permute-done((bf16[16,4992]{1,0:T(8,128)(2,1)S(1)}, bf16[16,4992]{1,0:T(8,128)(2,1)S(1)}, u32[]{:S(2)}, u32[]{:S(2)}) %collective-permute-start.37) | collective-permute-done | bytes 159776 | tf_op jit(solution)/shard_map/ppermute | solution.py:168
  112.8 1.0 collective-permute-start.43
  113.9 2.4 %fusion.2 = f32[128,512]{1,0:T(8,128)S(1)} fusion(bf16[512,26624]{1,0:T(8,128)(2,1)S(1)} %bitcast.117, bf16[64,6656]{1,0:T(8,128)(2,1)S(1)} %collective-permute-done.36, bf16[64,6656]{1,0:T(8,128)(2,1)S(1)} %constant_dynamic-update-slice_fusion.12), kind=kOutput, calls=%fused_computation.2 | convolution fusion | flops 875823104 | bytes 8781824 | tf_op jit(solution)/shard_map/dot_general | solution.py:135
  116.3 1.3 collective-permute-done.41
  117.8 3.9 %collective-permute-start.42 = (bf16[64,3328]{1,0:T(8,128)(2,1)S(1)}, bf16[64,3328]{1,0:T(8,128)(2,1)S(1)}, u32[]{:S(2)}, u32[]{:S(2)}) collective-permute-start(bf16[64,3328]{1,0:T(8,128)(2,1)S(1)} %constant_dynamic-update-slice_fusion.22), channel_id=1, source_target_pairs={{0,1},{1,0},{2,3},{3,2},{4,5},{5,4},{6,7},{7,6},{8,9},{9,8},{10,11... | collective-permute-start | bytes 1277960 | tf_op jit(solution)/shard_map/ppermute | solution.py:168
  122.0 0.6 collective-permute-start.45
  122.5 0.6 collective-permute-done.42
  123.2 1.3 fusion.27
  124.4 1.8 %fusion.6 = f32[128,512]{1,0:T(8,128)S(1)} fusion(bf16[512,26624]{1,0:T(8,128)(2,1)S(1)} %bitcast.117, bf16[64,4992]{1,0:T(8,128)(2,1)S(1)} %collective-permute-done.47, bf16[64,4992]{1,0:T(8,128)(2,1)S(1)} %constant_dynamic-update-slice_fusion.24), kind=kOutput, calls=%fused_computation.6 | convolution fusion | flops 656867328 | bytes 6651904 | tf_op jit(solution)/shard_map/dot_general | solution.py:135
  126.4 0.9 collective-permute-start.48
  127.3 1.8 %fusion.30 = f32[128,512]{1,0:T(8,128)S(1)} fusion(f32[128,512]{1,0:T(8,128)S(1)} %fusion.27, bf16[512,26624]{1,0:T(8,128)(2,1)S(1)} %bitcast.117, bf16[64,4992]{1,0:T(8,128)(2,1)S(1)} %collective-permute-done.45, bf16[64,4992]{1,0:T(8,128)(2,1)S(1)} %constant_dynamic-update-slice_fusion.26), kind=kOutput, calls=%fused_computation.33 | convolution fusion | flops 656932864 | bytes 6914048 | tf_op jit(solution)/shard_map/dot_general | solution.py:135
  129.3 2.4 %fusion.22 = f32[128,512]{1,0:T(8,128)S(1)} fusion(f32[128,512]{1,0:T(8,128)S(1)} %fusion.30, bf16[512,26624]{1,0:T(8,128)(2,1)S(1)} %bitcast.117, bf16[64,6656]{1,0:T(8,128)(2,1)S(1)} %collective-permute-done.48, bf16[64,6656]{1,0:T(8,128)(2,1)S(1)} %constant_dynamic-update-slice_fusion.28), kind=kOutput, calls=%fused_computation.31 | convolution fusion | flops 875888640 | bytes 9043968 | tf_op jit(solution)/shard_map/dot_general | solution.py:135
  132.1 3.7 %collective-permute-start.51 = (bf16[32,512]{1,0:T(8,128)(2,1)S(1)}, bf16[32,512]{1,0:T(8,128)(2,1)S(1)}, u32[]{:S(2)}, u32[]{:S(2)}) collective-permute-start(bf16[32,512]{1,0:T(8,128)(2,1)S(1)} %get-tuple-element.250), channel_id=1, source_target_pairs={{0,6},{1,7},{2,4},{3,5},{4,2},{5,3},{6,0},{7,1},{8,14},{9,15},{10,... | collective-permute-start | bytes 98312 | tf_op jit(solution)/shard_map/ppermute | solution.py:168
  135.8 0.8 collective-permute-start.49
  136.6 1.3 collective-permute-done.51
  137.9 2.7 %collective-permute-done.50 = bf16[32,512]{1,0:T(8,128)(2,1)S(1)} collective-permute-done((bf16[32,512]{1,0:T(8,128)(2,1)S(1)}, bf16[32,512]{1,0:T(8,128)(2,1)S(1)}, u32[]{:S(2)}, u32[]{:S(2)}) %collective-permute-start.50) | collective-permute-done | bytes 32800 | tf_op jit(solution)/shard_map/ppermute | solution.py:168
  140.7 1.2 collective-permute-done.52
  142.2 0.6 copy-done
  142.9 0.6 constant_dynamic-update-slice_fusion.30
  (161 shorter events, 6.9 us)
Async XLA Ops:
  0.9 1.4 collective-permute-start
  2.4 10.6 %collective-permute-start.3 = (bf16[32,512]{1,0:T(8,128)(2,1)S(1)}, bf16[32,512]{1,0:T(8,128)(2,1)S(1)}, u32[]{:S(2)}, u32[]{:S(2)}) collective-permute-start(bf16[32,512]{1,0:T(8,128)(2,1)S(1)} %get-tuple-element.254), channel_id=1, source_target_pairs={{0,6},{1,7},{2,4},{3,5},{4,2},{5,3},{6,0},{7,1},{8,14},{9,15},{10,... | collective-permute-start | bytes 98312 | tf_op jit(solution)/shard_map/ppermute | solution.py:168
  7.4 5.6 %collective-permute-start.2 = (bf16[32,512]{1,0:T(8,128)(2,1)S(1)}, bf16[32,512]{1,0:T(8,128)(2,1)S(1)}, u32[]{:S(2)}, u32[]{:S(2)}) collective-permute-start(bf16[32,512]{1,0:T(8,128)(2,1)S(1)} %get-tuple-element.255), channel_id=1, source_target_pairs={{0,4},{1,5},{2,6},{3,7},{4,0},{5,1},{6,2},{7,3},{8,12},{9,13},{10,... | collective-permute-start | bytes 98312 | tf_op jit(solution)/shard_map/ppermute | solution.py:168
  7.4 5.6 %collective-permute-start.1 = (bf16[32,512]{1,0:T(8,128)(2,1)S(1)}, bf16[32,512]{1,0:T(8,128)(2,1)S(1)}, u32[]{:S(2)}, u32[]{:S(2)}) collective-permute-start(bf16[32,512]{1,0:T(8,128)(2,1)S(1)} %get-tuple-element.256), channel_id=1, source_target_pairs={{0,2},{1,3},{2,0},{3,1},{4,6},{5,7},{6,4},{7,5},{8,10},{9,11},{10,... | collective-permute-start | bytes 98312 | tf_op jit(solution)/shard_map/ppermute | solution.py:168
  15.4 4.2 %collective-permute-start.4 = (bf16[2,64,6656]{2,1,0:T(8,128)(2,1)S(1)}, bf16[2,64,6656]{2,1,0:T(8,128)(2,1)S(1)}, u32[]{:S(2)}, u32[]{:S(2)}) collective-permute-start(bf16[2,64,6656]{2,1,0:T(8,128)(2,1)S(1)} %get-tuple-element.112), channel_id=1, source_target_pairs={{0,1},{1,0},{2,3},{3,2},{4,5},{5,4},{6,7},{7,6},{8,9},{9,8},{10,11... | collective-permute-start | bytes 5111816 | tf_op jit(solution)/shard_map/ppermute | solution.py:168
  19.0 7.3 %collective-permute-start.7 = (bf16[2,64,3328]{2,1,0:T(8,128)(2,1)S(1)}, bf16[2,64,3328]{2,1,0:T(8,128)(2,1)S(1)}, u32[]{:S(2)}, u32[]{:S(2)}) collective-permute-start(bf16[2,64,3328]{2,1,0:T(8,128)(2,1)S(1)} %get-tuple-element.114), channel_id=1, source_target_pairs={{0,1},{1,0},{2,3},{3,2},{4,5},{5,4},{6,7},{7,6},{8,9},{9,8},{10,11... | collective-permute-start | bytes 2555912 | tf_op jit(solution)/shard_map/ppermute | solution.py:168
  24.5 7.0 %collective-permute-start.6 = (bf16[2,64,4992]{2,1,0:T(8,128)(2,1)S(1)}, bf16[2,64,4992]{2,1,0:T(8,128)(2,1)S(1)}, u32[]{:S(2)}, u32[]{:S(2)}) collective-permute-start(bf16[2,64,4992]{2,1,0:T(8,128)(2,1)S(1)} %get-tuple-element.119), channel_id=1, source_target_pairs={{0,1},{1,0},{2,3},{3,2},{4,5},{5,4},{6,7},{7,6},{8,9},{9,8},{10,11... | collective-permute-start | bytes 3833864 | tf_op jit(solution)/shard_map/ppermute | solution.py:168
  24.6 12.7 %collective-permute-start.5 = (bf16[2,32,6656]{2,1,0:T(8,128)(2,1)S(1)}, bf16[2,32,6656]{2,1,0:T(8,128)(2,1)S(1)}, u32[]{:S(2)}, u32[]{:S(2)}) collective-permute-start(bf16[2,32,6656]{2,1,0:T(8,128)(2,1)S(1)} %get-tuple-element.218), channel_id=1, source_target_pairs={{0,8},{1,17},{2,10},{3,19},{4,12},{5,21},{6,14},{7,23},{8,0},{9,25... | collective-permute-start | bytes 2555912 | tf_op jit(solution)/shard_map/ppermute | solution.py:168
  26.5 20.6 %collective-permute-start.9 = (bf16[2,32,3328]{2,1,0:T(8,128)(2,1)S(1)}, bf16[2,32,3328]{2,1,0:T(8,128)(2,1)S(1)}, u32[]{:S(2)}, u32[]{:S(2)}) collective-permute-start(bf16[2,32,3328]{2,1,0:T(8,128)(2,1)S(1)} %get-tuple-element.226), channel_id=1, source_target_pairs={{0,8},{1,17},{2,10},{3,19},{4,12},{5,21},{6,14},{7,23},{8,0},{9,25... | collective-permute-start | bytes 1277960 | tf_op jit(solution)/shard_map/ppermute | solution.py:168
  31.5 7.8 %collective-permute-start.10 = (bf16[2,64,4992]{2,1,0:T(8,128)(2,1)S(1)}, bf16[2,64,4992]{2,1,0:T(8,128)(2,1)S(1)}, u32[]{:S(2)}, u32[]{:S(2)}) collective-permute-start(bf16[2,64,4992]{2,1,0:T(8,128)(2,1)S(1)} %get-tuple-element.124), channel_id=1, source_target_pairs={{0,1},{1,0},{2,3},{3,2},{4,5},{5,4},{6,7},{7,6},{8,9},{9,8},{10,11... | collective-permute-start | bytes 3833864 | tf_op jit(solution)/shard_map/ppermute | solution.py:168
  31.8 22.1 %collective-permute-start.13 = (bf16[2,32,4992]{2,1,0:T(8,128)(2,1)S(1)}, bf16[2,32,4992]{2,1,0:T(8,128)(2,1)S(1)}, u32[]{:S(2)}, u32[]{:S(2)}) collective-permute-start(bf16[2,32,4992]{2,1,0:T(8,128)(2,1)S(1)} %get-tuple-element.221), channel_id=1, source_target_pairs={{0,2},{1,5},{2,0},{3,7},{4,6},{5,1},{6,4},{7,3},{8,10},{9,13},{10,... | collective-permute-start | bytes 1916936 | tf_op jit(solution)/shard_map/ppermute | solution.py:168
  37.5 12.8 %collective-permute-start.8 = (bf16[2,16,6656]{2,1,0:T(8,128)(2,1)S(1)}, bf16[2,16,6656]{2,1,0:T(8,128)(2,1)S(1)}, u32[]{:S(2)}, u32[]{:S(2)}) collective-permute-start(bf16[2,16,6656]{2,1,0:T(8,128)(2,1)S(1)} %get-tuple-element.228), channel_id=1, source_target_pairs={{0,16},{1,9},{2,18},{3,11},{4,20},{5,13},{6,22},{7,15},{8,24},{9,1... | collective-permute-start | bytes 1277960 | tf_op jit(solution)/shard_map/ppermute | solution.py:168
  39.6 17.5 %collective-permute-start.12 = (bf16[2,32,4992]{2,1,0:T(8,128)(2,1)S(1)}, bf16[2,32,4992]{2,1,0:T(8,128)(2,1)S(1)}, u32[]{:S(2)}, u32[]{:S(2)}) collective-permute-start(bf16[2,32,4992]{2,1,0:T(8,128)(2,1)S(1)} %get-tuple-element.220), channel_id=1, source_target_pairs={{0,8},{1,17},{2,10},{3,19},{4,12},{5,21},{6,14},{7,23},{8,0},{9,25... | collective-permute-start | bytes 1916936 | tf_op jit(solution)/shard_map/ppermute | solution.py:168
  41.1 72.7 %slice-start = ((s8[27262976]{0:T(1024)(128)(4,1)}), s8[2097152]{0:T(1024)(128)(4,1)S(1)}, s32[]{:S(2)}) async-start(s8[27262976]{0:T(1024)(128)(4,1)} %bitcast.116), calls=%async_computation | async-start | bytes 4194304
  41.1 72.7 %slice-start.1 = ((s8[27262976]{0:T(1024)(128)(4,1)}), s8[4194304]{0:T(1024)(128)(4,1)S(1)}, s32[]{:S(2)}) async-start(s8[27262976]{0:T(1024)(128)(4,1)} %bitcast.116), calls=%async_computation.1 | async-start | bytes 8388608
  41.1 72.7 %slice-start.2 = ((s8[27262976]{0:T(1024)(128)(4,1)}), s8[4194304]{0:T(1024)(128)(4,1)S(1)}, s32[]{:S(2)}) async-start(s8[27262976]{0:T(1024)(128)(4,1)} %bitcast.116), calls=%async_computation.2 | async-start | bytes 8388608
  41.1 72.8 %slice-start.3 = ((s8[27262976]{0:T(1024)(128)(4,1)}), s8[4194304]{0:T(1024)(128)(4,1)S(1)}, s32[]{:S(2)}) async-start(s8[27262976]{0:T(1024)(128)(4,1)} %bitcast.116), calls=%async_computation.3 | async-start | bytes 8388608
  41.1 72.8 %slice-start.4 = ((s8[27262976]{0:T(1024)(128)(4,1)}), s8[4194304]{0:T(1024)(128)(4,1)S(1)}, s32[]{:S(2)}) async-start(s8[27262976]{0:T(1024)(128)(4,1)} %bitcast.116), calls=%async_computation.4 | async-start | bytes 8388608
  47.0 4.9 %collective-permute-start.14 = (bf16[2,64,6656]{2,1,0:T(8,128)(2,1)S(1)}, bf16[2,64,6656]{2,1,0:T(8,128)(2,1)S(1)}, u32[]{:S(2)}, u32[]{:S(2)}) collective-permute-start(bf16[2,64,6656]{2,1,0:T(8,128)(2,1)S(1)} %get-tuple-element.133), channel_id=1, source_target_pairs={{0,1},{1,0},{2,3},{3,2},{4,5},{5,4},{6,7},{7,6},{8,9},{9,8},{10,11... | collective-permute-start | bytes 5111816 | tf_op jit(solution)/shard_map/ppermute | solution.py:168
  47.2 19.7 %collective-permute-start.19 = (bf16[2,16,3328]{2,1,0:T(8,128)(2,1)S(1)}, bf16[2,16,3328]{2,1,0:T(8,128)(2,1)S(1)}, u32[]{:S(2)}, u32[]{:S(2)}) collective-permute-start(bf16[2,16,3328]{2,1,0:T(8,128)(2,1)S(1)} %get-tuple-element.238), channel_id=1, source_target_pairs={{0,16},{1,9},{2,18},{3,11},{4,20},{5,13},{6,22},{7,15},{8,24},{9,1... | collective-permute-start | bytes 638984 | tf_op jit(solution)/shard_map/ppermute | solution.py:168
  50.5 8.4 %collective-permute-start.11 = (bf16[2,8,6656]{2,1,0:T(8,128)(2,1)S(1)}, bf16[2,8,6656]{2,1,0:T(8,128)(2,1)S(1)}, u32[]{:S(2)}, u32[]{:S(2)}) collective-permute-start(bf16[2,8,6656]{2,1,0:T(8,128)(2,1)S(1)} %get-tuple-element.236), channel_id=1, source_target_pairs={{0,2},{1,5},{2,0},{3,7},{4,6},{5,1},{6,4},{7,3},{8,10},{9,13},{10,... | collective-permute-start | bytes 638984 | tf_op jit(solution)/shard_map/ppermute | solution.py:168
  51.9 62.0 %slice-start.5 = ((s8[27262976]{0:T(1024)(128)(4,1)}), s8[4194304]{0:T(1024)(128)(4,1)S(1)}, s32[]{:S(2)}) async-start(s8[27262976]{0:T(1024)(128)(4,1)} %bitcast.116), calls=%async_computation.5 | async-start | bytes 8388608
  52.4 17.3 %collective-permute-start.18 = (bf16[2,32,6656]{2,1,0:T(8,128)(2,1)S(1)}, bf16[2,32,6656]{2,1,0:T(8,128)(2,1)S(1)}, u32[]{:S(2)}, u32[]{:S(2)}) collective-permute-start(bf16[2,32,6656]{2,1,0:T(8,128)(2,1)S(1)} %get-tuple-element.216), channel_id=1, source_target_pairs={{0,8},{1,17},{2,10},{3,19},{4,12},{5,21},{6,14},{7,23},{8,0},{9,25... | collective-permute-start | bytes 2555912 | tf_op jit(solution)/shard_map/ppermute | solution.py:168
  54.1 17.4 %collective-permute-start.17 = (bf16[2,16,4992]{2,1,0:T(8,128)(2,1)S(1)}, bf16[2,16,4992]{2,1,0:T(8,128)(2,1)S(1)}, u32[]{:S(2)}, u32[]{:S(2)}) collective-permute-start(bf16[2,16,4992]{2,1,0:T(8,128)(2,1)S(1)} %get-tuple-element.231), channel_id=1, source_target_pairs={{0,4},{1,3},{2,6},{3,1},{4,0},{5,7},{6,2},{7,5},{8,12},{9,11},{10,... | collective-permute-start | bytes 958472 | tf_op jit(solution)/shard_map/ppermute | solution.py:168
  57.2 16.0 %collective-permute-start.16 = (bf16[2,16,4992]{2,1,0:T(8,128)(2,1)S(1)}, bf16[2,16,4992]{2,1,0:T(8,128)(2,1)S(1)}, u32[]{:S(2)}, u32[]{:S(2)}) collective-permute-start(bf16[2,16,4992]{2,1,0:T(8,128)(2,1)S(1)} %get-tuple-element.230), channel_id=1, source_target_pairs={{0,16},{1,9},{2,18},{3,11},{4,20},{5,13},{6,22},{7,15},{8,24},{9,1... | collective-permute-start | bytes 958472 | tf_op jit(solution)/shard_map/ppermute | solution.py:168
  58.9 14.5 %collective-permute-start.15 = (bf16[2,8,6656]{2,1,0:T(8,128)(2,1)S(1)}, bf16[2,8,6656]{2,1,0:T(8,128)(2,1)S(1)}, u32[]{:S(2)}, u32[]{:S(2)}) collective-permute-start(bf16[2,8,6656]{2,1,0:T(8,128)(2,1)S(1)} %add_convert_fusion.22), channel_id=1, source_target_pairs={{0,4},{1,3},{2,6},{3,1},{4,0},{5,7},{6,2},{7,5},{8,12},{9,11},{10,... | collective-permute-start | bytes 638984 | tf_op jit(solution)/shard_map/ppermute | solution.py:168
  67.0 8.6 %collective-permute-start.24 = (bf16[2,8,3328]{2,1,0:T(8,128)(2,1)S(1)}, bf16[2,8,3328]{2,1,0:T(8,128)(2,1)S(1)}, u32[]{:S(2)}, u32[]{:S(2)}) collective-permute-start(bf16[2,8,3328]{2,1,0:T(8,128)(2,1)S(1)} %get-tuple-element.244), channel_id=1, source_target_pairs={{0,2},{1,5},{2,0},{3,7},{4,6},{5,1},{6,4},{7,3},{8,10},{9,13},{10,... | collective-permute-start | bytes 319496 | tf_op jit(solution)/shard_map/ppermute | solution.py:168
  69.9 8.4 %collective-permute-start.23 = (bf16[2,16,6656]{2,1,0:T(8,128)(2,1)S(1)}, bf16[2,16,6656]{2,1,0:T(8,128)(2,1)S(1)}, u32[]{:S(2)}, u32[]{:S(2)}) collective-permute-start(bf16[2,16,6656]{2,1,0:T(8,128)(2,1)S(1)} %get-tuple-element.224), channel_id=1, source_target_pairs={{0,16},{1,9},{2,18},{3,11},{4,20},{5,13},{6,22},{7,15},{8,24},{9,1... | collective-permute-start | bytes 1277960 | tf_op jit(solution)/shard_map/ppermute | solution.py:168
  71.6 8.2 %collective-permute-start.22 = (bf16[2,8,4992]{2,1,0:T(8,128)(2,1)S(1)}, bf16[2,8,4992]{2,1,0:T(8,128)(2,1)S(1)}, u32[]{:S(2)}, u32[]{:S(2)}) collective-permute-start(bf16[2,8,4992]{2,1,0:T(8,128)(2,1)S(1)} %get-tuple-element.241), channel_id=1, source_target_pairs={{0,8},{1,17},{2,10},{3,19},{4,12},{5,21},{6,14},{7,23},{8,0},{9,25... | collective-permute-start | bytes 479240 | tf_op jit(solution)/shard_map/ppermute | solution.py:168
  73.3 10.7 %collective-permute-start.21 = (bf16[2,8,4992]{2,1,0:T(8,128)(2,1)S(1)}, bf16[2,8,4992]{2,1,0:T(8,128)(2,1)S(1)}, u32[]{:S(2)}, u32[]{:S(2)}) collective-permute-start(bf16[2,8,4992]{2,1,0:T(8,128)(2,1)S(1)} %get-tuple-element.240), channel_id=1, source_target_pairs={{0,2},{1,5},{2,0},{3,7},{4,6},{5,1},{6,4},{7,3},{8,10},{9,13},{10,... | collective-permute-start | bytes 479240 | tf_op jit(solution)/shard_map/ppermute | solution.py:168
  73.5 12.9 %collective-permute-start.20 = (bf16[8,6656]{1,0:T(8,128)(2,1)S(1)}, bf16[8,6656]{1,0:T(8,128)(2,1)S(1)}, u32[]{:S(2)}, u32[]{:S(2)}) collective-permute-start(bf16[8,6656]{1,0:T(8,128)(2,1)S(1)} %fusion.44), channel_id=1, source_target_pairs={{0,2},{1,5},{2,0},{3,7},{4,6},{5,1},{6,4},{7,3},{8,10},{9,13},{10,... | collective-permute-start | bytes 319496 | tf_op jit(solution)/shard_map/ppermute | solution.py:168
  75.6 10.9 %collective-permute-start.28 = (bf16[2,8,3328]{2,1,0:T(8,128)(2,1)S(1)}, bf16[2,8,3328]{2,1,0:T(8,128)(2,1)S(1)}, u32[]{:S(2)}, u32[]{:S(2)}) collective-permute-start(bf16[2,8,3328]{2,1,0:T(8,128)(2,1)S(1)} %add_convert_fusion.32), channel_id=1, source_target_pairs={{0,4},{1,3},{2,6},{3,1},{4,0},{5,7},{6,2},{7,5},{8,12},{9,11},{10,... | collective-permute-start | bytes 319496 | tf_op jit(solution)/shard_map/ppermute | solution.py:168
  78.4 35.5 %slice-start.6 = ((s8[27262976]{0:T(1024)(128)(4,1)}), s8[4194304]{0:T(1024)(128)(4,1)S(1)}, s32[]{:S(2)}) async-start(s8[27262976]{0:T(1024)(128)(4,1)} %bitcast.116), calls=%async_computation.6 | async-start | bytes 8388608
  78.5 14.3 %collective-permute-start.26 = (bf16[2,8,6656]{2,1,0:T(8,128)(2,1)S(1)}, bf16[2,8,6656]{2,1,0:T(8,128)(2,1)S(1)}, u32[]{:S(2)}, u32[]{:S(2)}) collective-permute-start(bf16[2,8,6656]{2,1,0:T(8,128)(2,1)S(1)} %get-tuple-element.234), channel_id=1, source_target_pairs={{0,2},{1,5},{2,0},{3,7},{4,6},{5,1},{6,4},{7,3},{8,10},{9,13},{10,... | collective-permute-start | bytes 638984 | tf_op jit(solution)/shard_map/ppermute | solution.py:168
  79.8 7.2 %collective-permute-start.27 = (bf16[2,8,4992]{2,1,0:T(8,128)(2,1)S(1)}, bf16[2,8,4992]{2,1,0:T(8,128)(2,1)S(1)}, u32[]{:S(2)}, u32[]{:S(2)}) collective-permute-start(bf16[2,8,4992]{2,1,0:T(8,128)(2,1)S(1)} %add_convert_fusion.27), channel_id=1, source_target_pairs={{0,16},{1,9},{2,18},{3,11},{4,20},{5,13},{6,22},{7,15},{8,24},{9,1... | collective-permute-start | bytes 479240 | tf_op jit(solution)/shard_map/ppermute | solution.py:168
  84.1 11.7 %collective-permute-start.32 = (bf16[2,8,4992]{2,1,0:T(8,128)(2,1)S(1)}, bf16[2,8,4992]{2,1,0:T(8,128)(2,1)S(1)}, u32[]{:S(2)}, u32[]{:S(2)}) collective-permute-start(bf16[2,8,4992]{2,1,0:T(8,128)(2,1)S(1)} %add_convert_fusion.26), channel_id=1, source_target_pairs={{0,4},{1,3},{2,6},{3,1},{4,0},{5,7},{6,2},{7,5},{8,12},{9,11},{10,... | collective-permute-start | bytes 479240 | tf_op jit(solution)/shard_map/ppermute | solution.py:168
  86.5 9.2 %collective-permute-start.25 = (bf16[16,6656]{1,0:T(8,128)(2,1)S(1)}, bf16[16,6656]{1,0:T(8,128)(2,1)S(1)}, u32[]{:S(2)}, u32[]{:S(2)}) collective-permute-start(bf16[16,6656]{1,0:T(8,128)(2,1)S(1)} %constant_dynamic-update-slice_fusion), channel_id=1, source_target_pairs={{0,16},{1,9},{2,18},{3,11},{4,20},{5,13},{6,22},{7,15},{8,24},{9,1... | collective-permute-start | bytes 638984 | tf_op jit(solution)/shard_map/ppermute | solution.py:168
  86.6 14.4 %collective-permute-start.30 = (bf16[8,3328]{1,0:T(8,128)(2,1)S(1)}, bf16[8,3328]{1,0:T(8,128)(2,1)S(1)}, u32[]{:S(2)}, u32[]{:S(2)}) collective-permute-start(bf16[8,3328]{1,0:T(8,128)(2,1)S(1)} %fusion.58), channel_id=1, source_target_pairs={{0,2},{1,5},{2,0},{3,7},{4,6},{5,1},{6,4},{7,3},{8,10},{9,13},{10,... | collective-permute-start | bytes 159752 | tf_op jit(solution)/shard_map/ppermute | solution.py:168
  87.1 11.3 %collective-permute-start.31 = (bf16[8,4992]{1,0:T(8,128)(2,1)S(1)}, bf16[8,4992]{1,0:T(8,128)(2,1)S(1)}, u32[]{:S(2)}, u32[]{:S(2)}) collective-permute-start(bf16[8,4992]{1,0:T(8,128)(2,1)S(1)} %fusion.48), channel_id=1, source_target_pairs={{0,8},{1,17},{2,10},{3,19},{4,12},{5,21},{6,14},{7,23},{8,0},{9,25... | collective-permute-start | bytes 239624 | tf_op jit(solution)/shard_map/ppermute | solution.py:168
  92.8 13.4 %collective-permute-start.35 = (bf16[2,8,6656]{2,1,0:T(8,128)(2,1)S(1)}, bf16[2,8,6656]{2,1,0:T(8,128)(2,1)S(1)}, u32[]{:S(2)}, u32[]{:S(2)}) collective-permute-start(bf16[2,8,6656]{2,1,0:T(8,128)(2,1)S(1)} %add_convert_fusion.18), channel_id=1, source_target_pairs={{0,4},{1,3},{2,6},{3,1},{4,0},{5,7},{6,2},{7,5},{8,12},{9,11},{10,... | collective-permute-start | bytes 638984 | tf_op jit(solution)/shard_map/ppermute | solution.py:168
  95.7 13.3 %collective-permute-start.29 = (bf16[32,6656]{1,0:T(8,128)(2,1)S(1)}, bf16[32,6656]{1,0:T(8,128)(2,1)S(1)}, u32[]{:S(2)}, u32[]{:S(2)}) collective-permute-start(bf16[32,6656]{1,0:T(8,128)(2,1)S(1)} %constant_dynamic-update-slice_fusion.2), channel_id=1, source_target_pairs={{0,8},{1,17},{2,10},{3,19},{4,12},{5,21},{6,14},{7,23},{8,0},{9,25... | collective-permute-start | bytes 1277960 | tf_op jit(solution)/shard_map/ppermute | solution.py:168
  95.9 11.5 %collective-permute-start.34 = (bf16[8,4992]{1,0:T(8,128)(2,1)S(1)}, bf16[8,4992]{1,0:T(8,128)(2,1)S(1)}, u32[]{:S(2)}, u32[]{:S(2)}) collective-permute-start(bf16[8,4992]{1,0:T(8,128)(2,1)S(1)} %fusion.46), channel_id=1, source_target_pairs={{0,2},{1,5},{2,0},{3,7},{4,6},{5,1},{6,4},{7,3},{8,10},{9,13},{10,... | collective-permute-start | bytes 239624 | tf_op jit(solution)/shard_map/ppermute | solution.py:168
  98.5 10.7 %collective-permute-start.39 = (bf16[16,4992]{1,0:T(8,128)(2,1)S(1)}, bf16[16,4992]{1,0:T(8,128)(2,1)S(1)}, u32[]{:S(2)}, u32[]{:S(2)}) collective-permute-start(bf16[16,4992]{1,0:T(8,128)(2,1)S(1)} %constant_dynamic-update-slice_fusion.4), channel_id=1, source_target_pairs={{0,4},{1,3},{2,6},{3,1},{4,0},{5,7},{6,2},{7,5},{8,12},{9,11},{10,... | collective-permute-start | bytes 479240 | tf_op jit(solution)/shard_map/ppermute | solution.py:168
  101.0 6.5 %collective-permute-start.33 = (bf16[16,3328]{1,0:T(8,128)(2,1)S(1)}, bf16[16,3328]{1,0:T(8,128)(2,1)S(1)}, u32[]{:S(2)}, u32[]{:S(2)}) collective-permute-start(bf16[16,3328]{1,0:T(8,128)(2,1)S(1)} %constant_dynamic-update-slice_fusion.6), channel_id=1, source_target_pairs={{0,16},{1,9},{2,18},{3,11},{4,20},{5,13},{6,22},{7,15},{8,24},{9,1... | collective-permute-start | bytes 319496 | tf_op jit(solution)/shard_map/ppermute | solution.py:168
  106.3 4.8 %collective-permute-start.38 = (bf16[8,6656]{1,0:T(8,128)(2,1)S(1)}, bf16[8,6656]{1,0:T(8,128)(2,1)S(1)}, u32[]{:S(2)}, u32[]{:S(2)}) collective-permute-start(bf16[8,6656]{1,0:T(8,128)(2,1)S(1)} %fusion.42), channel_id=1, source_target_pairs={{0,2},{1,5},{2,0},{3,7},{4,6},{5,1},{6,4},{7,3},{8,10},{9,13},{10,... | collective-permute-start | bytes 319496 | tf_op jit(solution)/shard_map/ppermute | solution.py:168
  107.4 5.3 %collective-permute-start.37 = (bf16[16,4992]{1,0:T(8,128)(2,1)S(1)}, bf16[16,4992]{1,0:T(8,128)(2,1)S(1)}, u32[]{:S(2)}, u32[]{:S(2)}) collective-permute-start(bf16[16,4992]{1,0:T(8,128)(2,1)S(1)} %constant_dynamic-update-slice_fusion.8), channel_id=1, source_target_pairs={{0,16},{1,9},{2,18},{3,11},{4,20},{5,13},{6,22},{7,15},{8,24},{9,1... | collective-permute-start | bytes 479240 | tf_op jit(solution)/shard_map/ppermute | solution.py:168
  107.6 10.2 %collective-permute-start.40 = (bf16[32,3328]{1,0:T(8,128)(2,1)S(1)}, bf16[32,3328]{1,0:T(8,128)(2,1)S(1)}, u32[]{:S(2)}, u32[]{:S(2)}) collective-permute-start(bf16[32,3328]{1,0:T(8,128)(2,1)S(1)} %constant_dynamic-update-slice_fusion.10), channel_id=1, source_target_pairs={{0,8},{1,17},{2,10},{3,19},{4,12},{5,21},{6,14},{7,23},{8,0},{9,25... | collective-permute-start | bytes 638984 | tf_op jit(solution)/shard_map/ppermute | solution.py:168
  109.1 4.8 %collective-permute-start.36 = (bf16[64,6656]{1,0:T(8,128)(2,1)S(1)}, bf16[64,6656]{1,0:T(8,128)(2,1)S(1)}, u32[]{:S(2)}, u32[]{:S(2)}) collective-permute-start(bf16[64,6656]{1,0:T(8,128)(2,1)S(1)} %constant_dynamic-update-slice_fusion.12), channel_id=1, source_target_pairs={{0,1},{1,0},{2,3},{3,2},{4,5},{5,4},{6,7},{7,6},{8,9},{9,8},{10,11... | collective-permute-start | bytes 2555912 | tf_op jit(solution)/shard_map/ppermute | solution.py:168
  109.2 12.6 %collective-permute-start.44 = (bf16[32,4992]{1,0:T(8,128)(2,1)S(1)}, bf16[32,4992]{1,0:T(8,128)(2,1)S(1)}, u32[]{:S(2)}, u32[]{:S(2)}) collective-permute-start(bf16[32,4992]{1,0:T(8,128)(2,1)S(1)} %constant_dynamic-update-slice_fusion.14), channel_id=1, source_target_pairs={{0,2},{1,5},{2,0},{3,7},{4,6},{5,1},{6,4},{7,3},{8,10},{9,13},{10,... | collective-permute-start | bytes 958472 | tf_op jit(solution)/shard_map/ppermute | solution.py:168
  111.1 6.6 %collective-permute-start.41 = (bf16[16,6656]{1,0:T(8,128)(2,1)S(1)}, bf16[16,6656]{1,0:T(8,128)(2,1)S(1)}, u32[]{:S(2)}, u32[]{:S(2)}) collective-permute-start(bf16[16,6656]{1,0:T(8,128)(2,1)S(1)} %constant_dynamic-update-slice_fusion.16), channel_id=1, source_target_pairs={{0,16},{1,9},{2,18},{3,11},{4,20},{5,13},{6,22},{7,15},{8,24},{9,1... | collective-permute-start | bytes 638984 | tf_op jit(solution)/shard_map/ppermute | solution.py:168
  112.8 9.1 %collective-permute-start.43 = (bf16[32,4992]{1,0:T(8,128)(2,1)S(1)}, bf16[32,4992]{1,0:T(8,128)(2,1)S(1)}, u32[]{:S(2)}, u32[]{:S(2)}) collective-permute-start(bf16[32,4992]{1,0:T(8,128)(2,1)S(1)} %constant_dynamic-update-slice_fusion.18), channel_id=1, source_target_pairs={{0,8},{1,17},{2,10},{3,19},{4,12},{5,21},{6,14},{7,23},{8,0},{9,25... | collective-permute-start | bytes 958472 | tf_op jit(solution)/shard_map/ppermute | solution.py:168
  117.7 8.6 %collective-permute-start.46 = (bf16[32,6656]{1,0:T(8,128)(2,1)S(1)}, bf16[32,6656]{1,0:T(8,128)(2,1)S(1)}, u32[]{:S(2)}, u32[]{:S(2)}) collective-permute-start(bf16[32,6656]{1,0:T(8,128)(2,1)S(1)} %constant_dynamic-update-slice_fusion.20), channel_id=1, source_target_pairs={{0,8},{1,17},{2,10},{3,19},{4,12},{5,21},{6,14},{7,23},{8,0},{9,25... | collective-permute-start | bytes 1277960 | tf_op jit(solution)/shard_map/ppermute | solution.py:168
  117.8 5.3 %collective-permute-start.42 = (bf16[64,3328]{1,0:T(8,128)(2,1)S(1)}, bf16[64,3328]{1,0:T(8,128)(2,1)S(1)}, u32[]{:S(2)}, u32[]{:S(2)}) collective-permute-start(bf16[64,3328]{1,0:T(8,128)(2,1)S(1)} %constant_dynamic-update-slice_fusion.22), channel_id=1, source_target_pairs={{0,1},{1,0},{2,3},{3,2},{4,5},{5,4},{6,7},{7,6},{8,9},{9,8},{10,11... | collective-permute-start | bytes 1277960 | tf_op jit(solution)/shard_map/ppermute | solution.py:168
  121.8 2.6 %collective-permute-start.47 = (bf16[64,4992]{1,0:T(8,128)(2,1)S(1)}, bf16[64,4992]{1,0:T(8,128)(2,1)S(1)}, u32[]{:S(2)}, u32[]{:S(2)}) collective-permute-start(bf16[64,4992]{1,0:T(8,128)(2,1)S(1)} %constant_dynamic-update-slice_fusion.24), channel_id=1, source_target_pairs={{0,1},{1,0},{2,3},{3,2},{4,5},{5,4},{6,7},{7,6},{8,9},{9,8},{10,11... | collective-permute-start | bytes 1916936 | tf_op jit(solution)/shard_map/ppermute | solution.py:168
  122.0 5.3 %collective-permute-start.45 = (bf16[64,4992]{1,0:T(8,128)(2,1)S(1)}, bf16[64,4992]{1,0:T(8,128)(2,1)S(1)}, u32[]{:S(2)}, u32[]{:S(2)}) collective-permute-start(bf16[64,4992]{1,0:T(8,128)(2,1)S(1)} %constant_dynamic-update-slice_fusion.26), channel_id=1, source_target_pairs={{0,1},{1,0},{2,3},{3,2},{4,5},{5,4},{6,7},{7,6},{8,9},{9,8},{10,11... | collective-permute-start | bytes 1916936 | tf_op jit(solution)/shard_map/ppermute | solution.py:168
  126.4 2.9 %collective-permute-start.48 = (bf16[64,6656]{1,0:T(8,128)(2,1)S(1)}, bf16[64,6656]{1,0:T(8,128)(2,1)S(1)}, u32[]{:S(2)}, u32[]{:S(2)}) collective-permute-start(bf16[64,6656]{1,0:T(8,128)(2,1)S(1)} %constant_dynamic-update-slice_fusion.28), channel_id=1, source_target_pairs={{0,1},{1,0},{2,3},{3,2},{4,5},{5,4},{6,7},{7,6},{8,9},{9,8},{10,11... | collective-permute-start | bytes 2555912 | tf_op jit(solution)/shard_map/ppermute | solution.py:168
  132.1 5.8 %collective-permute-start.51 = (bf16[32,512]{1,0:T(8,128)(2,1)S(1)}, bf16[32,512]{1,0:T(8,128)(2,1)S(1)}, u32[]{:S(2)}, u32[]{:S(2)}) collective-permute-start(bf16[32,512]{1,0:T(8,128)(2,1)S(1)} %get-tuple-element.250), channel_id=1, source_target_pairs={{0,6},{1,7},{2,4},{3,5},{4,2},{5,3},{6,0},{7,1},{8,14},{9,15},{10,... | collective-permute-start | bytes 98312 | tf_op jit(solution)/shard_map/ppermute | solution.py:168
  135.8 4.8 %collective-permute-start.50 = (bf16[32,512]{1,0:T(8,128)(2,1)S(1)}, bf16[32,512]{1,0:T(8,128)(2,1)S(1)}, u32[]{:S(2)}, u32[]{:S(2)}) collective-permute-start(bf16[32,512]{1,0:T(8,128)(2,1)S(1)} %get-tuple-element.251), channel_id=1, source_target_pairs={{0,4},{1,5},{2,6},{3,7},{4,0},{5,1},{6,2},{7,3},{8,12},{9,13},{10,... | collective-permute-start | bytes 98312 | tf_op jit(solution)/shard_map/ppermute | solution.py:168
  135.8 4.8 %collective-permute-start.49 = (bf16[32,512]{1,0:T(8,128)(2,1)S(1)}, bf16[32,512]{1,0:T(8,128)(2,1)S(1)}, u32[]{:S(2)}, u32[]{:S(2)}) collective-permute-start(bf16[32,512]{1,0:T(8,128)(2,1)S(1)} %get-tuple-element.252), channel_id=1, source_target_pairs={{0,2},{1,3},{2,0},{3,1},{4,6},{5,7},{6,4},{7,5},{8,10},{9,11},{10,... | collective-permute-start | bytes 98312 | tf_op jit(solution)/shard_map/ppermute | solution.py:168
  140.6 1.3 collective-permute-start.52
  142.2 0.7 copy-start

commit v6 on v5

--- a/solution.py
+++ b/solution.py
@@ -11,7 +11,7 @@
 VMEM_BYTES = 28 * 2**20
 SHARES = (4, 4, 3, 2, 3)
 PLANS = (0, 0, 0, 0, 1)
-ORDER = (0, 3, 0, 4, 3, 2, 4, 0, 2, 1, 3, 0, 1, 4, 2, 0, 3, 1, 4, 2, 0, 3, 1, 4, 2, 0, 3, 4, 1, 0, 2, 4, 3, 1, 2, 3, 0, 4, 1, 2, 0, 1, 3, 4, 2, 3, 4, 1, 2, 1)
+ORDER = (0, 4, 0, 3, 4, 3, 1, 0, 3, 1, 4, 2, 0, 3, 2, 1, 0, 4, 3, 2, 0, 1, 4, 3, 2, 0, 1, 3, 4, 2, 0, 1, 4, 3, 2, 1, 0, 4, 3, 2, 1, 0, 2, 4, 3, 1, 4, 2, 1, 2)
 
 
 def step_order(chunks, steps):

time: 144 us -> 136 us (0.944)
  starting transfers between devices: 68 us -> 54.8 us
  waiting for transfers between devices: 31.6 us -> 36.8 us
    ppermute x53, starting transfers between devices: 68 us -> 54.8 us  [swap(): return lax.ppermute(value, ('row', 'col'), pairs)]
    ppermute x53, waiting for transfers between devices: 31.6 us -> 36.8 us  [swap(): return lax.ppermute(value, ('row', 'col'), pairs)]
  transfers between devices with their start and end apart: 53 -> 53, of which waited for: 16 -> 25; matrix products, arithmetic and copies ran while one was open for 8% -> 9% of each run, Pallas kernels for 16% -> 17%
where the time goes in v6:
time: 136 us; the launch traced here: 135 us
  starting transfers between devices  54.8 us (40%)
  waiting for transfers between devices  36.8 us (27%)
  Pallas kernels  25.4 us (19%)
  matrix products  10.4 us (8%)
  other arithmetic  4.39 us (3%)
  local copies, waits for them, and re-layouts  2.72 us (2%)
    ppermute x53, starting transfers between devices, swap(): return lax.ppermute(value, ('row', 'col'), pairs)  54.8 us
    ppermute x53, waiting for transfers between devices, swap(): return lax.ppermute(value, ('row', 'col'), pairs)  36.8 us
    pallas_call x4, Pallas kernels, gate_up(): pl.pallas_call(functools.partial(gate_up_kernel, start), grid=(blocks,),...  18.4 us
    dot_general x5, matrix products, down(): lax.dot_general(hidden, weight, (((1,), (1,)), ((), ())), preferred_eleme...  9.72 us
    pallas_call x1, Pallas kernels, fetch(): pl.pallas_call(functools.partial(fetch_kernel, start), in_specs=[pl.Block...  4.89 us
    convert_element_type x15, other arithmetic, add_halves(): sides.append((kept + came).astype(jnp.bfloat16))  2.84 us
  transfers between devices with their start and end apart: 53, of which 25 were waited for; matrix products, arithmetic and copies ran while one was open for 9% of the time, Pallas kernels for 17%

profile of v6, /device:TPU:0, one launch (start us, length us, event | category | flops | bytes accessed | tf_op | source)
XLA Modules:
  0.0 135.3 jit_solution(15503563798250037765)
XLA Ops:
  0.0 0.8 slice_bitcast_fusion.30
  1.4 0.7 fusion.66
  2.4 5.0 %collective-permute-start.3 = (bf16[32,512]{1,0:T(8,128)(2,1)S(1)}, bf16[32,512]{1,0:T(8,128)(2,1)S(1)}, u32[]{:S(2)}, u32[]{:S(2)}) collective-permute-start(bf16[32,512]{1,0:T(8,128)(2,1)S(1)} %get-tuple-element.254), channel_id=1, source_target_pairs={{0,6},{1,7},{2,4},{3,5},{4,2},{5,3},{6,0},{7,1},{8,14},{9,15},{10,... | collective-permute-start | bytes 98312 | tf_op jit(solution)/shard_map/ppermute | solution.py:168
  7.4 0.6 collective-permute-start.1
  8.1 4.9 %shard_map.100.held_ref = bf16[2,512,6656]{2,1,0:T(8,128)(2,1)S(1)} custom-call(bf16[512,26624]{1,0:T(8,128)(2,1)} %gate_ref.9, bf16[512,26624]{1,0:T(8,128)(2,1)} %up_ref.9), custom_call_target="tpu_custom_call" | custom-call | tf_op jit(solution)/shard_map/pallas_call | solution.py:95
  13.3 2.1 %shard_map.101 = (bf16[2,64,6656]{2,1,0:T(8,128)(2,1)S(1)}, bf16[2,64,6656]{2,1,0:T(8,128)(2,1)S(1)}) custom-call(bf16[128,512]{1,0:T(8,128)(2,1)S(1)} %get-tuple-element.136.x_ref, bf16[2,512,6656]{2,1,0:T(8,128)(2,1)S(1)} %shard_map.100.held_ref), custom_call_target="tpu_custom_call" | custom-call | tf_op jit(solution)/shard_map/pallas_call | solution.py:122
  15.5 4.5 %shard_map.102 = (bf16[2,64,4992]{2,1,0:T(8,128)(2,1)S(1)}, bf16[2,64,4992]{2,1,0:T(8,128)(2,1)S(1)}) custom-call(bf16[128,512]{1,0:T(8,128)(2,1)S(1)} %get-tuple-element.113.x_ref, bf16[512,26624]{1,0:T(8,128)(2,1)} %gate_ref.9, bf16[512,26624]{1,0:T(8,128)(2,1)} %up_ref.9), custom_call_target="tpu_custom_call" | custom-call | tf_op jit(solution)/shard_map/pallas_call | solution.py:62
  21.0 1.7 %collective-permute-start.5 = (bf16[2,32,6656]{2,1,0:T(8,128)(2,1)S(1)}, bf16[2,32,6656]{2,1,0:T(8,128)(2,1)S(1)}, u32[]{:S(2)}, u32[]{:S(2)}) collective-permute-start(bf16[2,32,6656]{2,1,0:T(8,128)(2,1)S(1)} %get-tuple-element.218), channel_id=1, source_target_pairs={{0,8},{1,17},{2,10},{3,19},{4,12},{5,21},{6,14},{7,23},{8,0},{9,25... | collective-permute-start | bytes 2555912 | tf_op jit(solution)/shard_map/ppermute | solution.py:168
  22.7 3.5 %shard_map.103 = (bf16[2,64,3328]{2,1,0:T(8,128)(2,1)S(1)}, bf16[2,64,3328]{2,1,0:T(8,128)(2,1)S(1)}) custom-call(bf16[128,512]{1,0:T(8,128)(2,1)S(1)} %get-tuple-element.136.x_ref, bf16[512,26624]{1,0:T(8,128)(2,1)} %gate_ref.9, bf16[512,26624]{1,0:T(8,128)(2,1)} %up_ref.9), custom_call_target="tpu_custom_call" | custom-call | tf_op jit(solution)/shard_map/pallas_call | solution.py:62
  26.6 1.3 collective-permute-start.9
  27.9 0.8 collective-permute-done.6
  28.9 0.9 collective-permute-start.11
  29.8 5.5 %shard_map.104 = (bf16[2,64,6656]{2,1,0:T(8,128)(2,1)S(1)}, bf16[2,64,6656]{2,1,0:T(8,128)(2,1)S(1)}) custom-call(bf16[128,512]{1,0:T(8,128)(2,1)S(1)} %get-tuple-element.136.x_ref, bf16[512,26624]{1,0:T(8,128)(2,1)} %gate_ref.9, bf16[512,26624]{1,0:T(8,128)(2,1)} %up_ref.9), custom_call_target="tpu_custom_call" | custom-call | tf_op jit(solution)/shard_map/pallas_call | solution.py:62
  35.3 0.8 collective-permute-start.10
  36.9 1.4 %collective-permute-done.11 = bf16[2,32,3328]{2,1,0:T(8,128)(2,1)S(1)} collective-permute-done((bf16[2,32,3328]{2,1,0:T(8,128)(2,1)S(1)}, bf16[2,32,3328]{2,1,0:T(8,128)(2,1)S(1)}, u32[]{:S(2)}, u32[]{:S(2)}) %collective-permute-start.11) | collective-permute-done | bytes 426016 | tf_op jit(solution)/shard_map/ppermute | solution.py:168
  38.4 1.7 %collective-permute-start.15 = (bf16[2,16,3328]{2,1,0:T(8,128)(2,1)S(1)}, bf16[2,16,3328]{2,1,0:T(8,128)(2,1)S(1)}, u32[]{:S(2)}, u32[]{:S(2)}) collective-permute-start(bf16[2,16,3328]{2,1,0:T(8,128)(2,1)S(1)} %get-tuple-element.236), channel_id=1, source_target_pairs={{0,16},{1,9},{2,18},{3,11},{4,20},{5,13},{6,22},{7,15},{8,24},{9,1... | collective-permute-start | bytes 638984 | tf_op jit(solution)/shard_map/ppermute | solution.py:168
  40.5 3.4 %collective-permute-done.9 = bf16[2,32,4992]{2,1,0:T(8,128)(2,1)S(1)} collective-permute-done((bf16[2,32,4992]{2,1,0:T(8,128)(2,1)S(1)}, bf16[2,32,4992]{2,1,0:T(8,128)(2,1)S(1)}, u32[]{:S(2)}, u32[]{:S(2)}) %collective-permute-start.9) | collective-permute-done | bytes 639008 | tf_op jit(solution)/shard_map/ppermute | solution.py:168
  44.1 2.0 %collective-permute-start.19 = (bf16[2,16,4992]{2,1,0:T(8,128)(2,1)S(1)}, bf16[2,16,4992]{2,1,0:T(8,128)(2,1)S(1)}, u32[]{:S(2)}, u32[]{:S(2)}) collective-permute-start(bf16[2,16,4992]{2,1,0:T(8,128)(2,1)S(1)} %get-tuple-element.231), channel_id=1, source_target_pairs={{0,4},{1,3},{2,6},{3,1},{4,0},{5,7},{6,2},{7,5},{8,12},{9,11},{10,... | collective-permute-start | bytes 958472 | tf_op jit(solution)/shard_map/ppermute | solution.py:168
  46.0 1.0 collective-permute-start.13
  47.1 4.9 %shard_map.105 = (bf16[2,64,4992]{2,1,0:T(8,128)(2,1)S(1)}, bf16[2,64,4992]{2,1,0:T(8,128)(2,1)S(1)}) custom-call(bf16[128,512]{1,0:T(8,128)(2,1)S(1)} %get-tuple-element.136.x_ref, bf16[512,26624]{1,0:T(8,128)(2,1)} %gate_ref.9, bf16[512,26624]{1,0:T(8,128)(2,1)} %up_ref.9), custom_call_target="tpu_custom_call" | custom-call | tf_op jit(solution)/shard_map/pallas_call | solution.py:62
  52.1 2.5 %collective-permute-start.12 = (bf16[2,8,6656]{2,1,0:T(8,128)(2,1)S(1)}, bf16[2,8,6656]{2,1,0:T(8,128)(2,1)S(1)}, u32[]{:S(2)}, u32[]{:S(2)}) collective-permute-start(bf16[2,8,6656]{2,1,0:T(8,128)(2,1)S(1)} %get-tuple-element.237), channel_id=1, source_target_pairs={{0,2},{1,5},{2,0},{3,7},{4,6},{5,1},{6,4},{7,3},{8,10},{9,13},{10,... | collective-permute-start | bytes 638984 | tf_op jit(solution)/shard_map/ppermute | solution.py:168
  55.3 1.1 collective-permute-start.17
  56.4 2.3 %collective-permute-done.13 = bf16[2,32,6656]{2,1,0:T(8,128)(2,1)S(1)} collective-permute-done((bf16[2,32,6656]{2,1,0:T(8,128)(2,1)S(1)}, bf16[2,32,6656]{2,1,0:T(8,128)(2,1)S(1)}, u32[]{:S(2)}, u32[]{:S(2)}) %collective-permute-start.13) | collective-permute-done | bytes 852000 | tf_op jit(solution)/shard_map/ppermute | solution.py:168
  58.9 1.6 %collective-permute-start.24 = (bf16[2,16,6656]{2,1,0:T(8,128)(2,1)S(1)}, bf16[2,16,6656]{2,1,0:T(8,128)(2,1)S(1)}, u32[]{:S(2)}, u32[]{:S(2)}) collective-permute-start(bf16[2,16,6656]{2,1,0:T(8,128)(2,1)S(1)} %get-tuple-element.224), channel_id=1, source_target_pairs={{0,16},{1,9},{2,18},{3,11},{4,20},{5,13},{6,22},{7,15},{8,24},{9,1... | collective-permute-start | bytes 1277960 | tf_op jit(solution)/shard_map/ppermute | solution.py:168
  60.5 1.4 %collective-permute-done.12 = bf16[2,8,6656]{2,1,0:T(8,128)(2,1)S(1)} collective-permute-done((bf16[2,8,6656]{2,1,0:T(8,128)(2,1)S(1)}, bf16[2,8,6656]{2,1,0:T(8,128)(2,1)S(1)}, u32[]{:S(2)}, u32[]{:S(2)}) %collective-permute-start.12) | collective-permute-done | bytes 213024 | tf_op jit(solution)/shard_map/ppermute | solution.py:168
  62.1 0.7 collective-permute-start.23
  63.1 2.2 %collective-permute-start.22 = (bf16[2,8,3328]{2,1,0:T(8,128)(2,1)S(1)}, bf16[2,8,3328]{2,1,0:T(8,128)(2,1)S(1)}, u32[]{:S(2)}, u32[]{:S(2)}) collective-permute-start(bf16[2,8,3328]{2,1,0:T(8,128)(2,1)S(1)} %add_convert_fusion.32), channel_id=1, source_target_pairs={{0,4},{1,3},{2,6},{3,1},{4,0},{5,7},{6,2},{7,5},{8,12},{9,11},{10,... | collective-permute-start | bytes 319496 | tf_op jit(solution)/shard_map/ppermute | solution.py:168
  65.2 5.1 %collective-permute-done.17 = bf16[2,32,4992]{2,1,0:T(8,128)(2,1)S(1)} collective-permute-done((bf16[2,32,4992]{2,1,0:T(8,128)(2,1)S(1)}, bf16[2,32,4992]{2,1,0:T(8,128)(2,1)S(1)}, u32[]{:S(2)}, u32[]{:S(2)}) %collective-permute-start.17) | collective-permute-done | bytes 639008 | tf_op jit(solution)/shard_map/ppermute | solution.py:168
  70.5 1.4 %collective-permute-start.21 = (bf16[2,16,4992]{2,1,0:T(8,128)(2,1)S(1)}, bf16[2,16,4992]{2,1,0:T(8,128)(2,1)S(1)}, u32[]{:S(2)}, u32[]{:S(2)}) collective-permute-start(bf16[2,16,4992]{2,1,0:T(8,128)(2,1)S(1)} %get-tuple-element.230), channel_id=1, source_target_pairs={{0,16},{1,9},{2,18},{3,11},{4,20},{5,13},{6,22},{7,15},{8,24},{9,1... | collective-permute-start | bytes 958472 | tf_op jit(solution)/shard_map/ppermute | solution.py:168
  72.3 1.5 %collective-permute-start.20 = (bf16[8,6656]{1,0:T(8,128)(2,1)S(1)}, bf16[8,6656]{1,0:T(8,128)(2,1)S(1)}, u32[]{:S(2)}, u32[]{:S(2)}) collective-permute-start(bf16[8,6656]{1,0:T(8,128)(2,1)S(1)} %fusion.44), channel_id=1, source_target_pairs={{0,2},{1,5},{2,0},{3,7},{4,6},{5,1},{6,4},{7,3},{8,10},{9,13},{10,... | collective-permute-start | bytes 319496 | tf_op jit(solution)/shard_map/ppermute | solution.py:168
  73.9 0.7 collective-permute-start.29
  75.2 0.9 collective-permute-done.22
  76.1 1.1 collective-permute-start.28
  77.7 2.0 %collective-permute-start.26 = (bf16[2,8,4992]{2,1,0:T(8,128)(2,1)S(1)}, bf16[2,8,4992]{2,1,0:T(8,128)(2,1)S(1)}, u32[]{:S(2)}, u32[]{:S(2)}) collective-permute-start(bf16[2,8,4992]{2,1,0:T(8,128)(2,1)S(1)} %get-tuple-element.240), channel_id=1, source_target_pairs={{0,2},{1,5},{2,0},{3,7},{4,6},{5,1},{6,4},{7,3},{8,10},{9,13},{10,... | collective-permute-start | bytes 479240 | tf_op jit(solution)/shard_map/ppermute | solution.py:168
  79.7 1.1 collective-permute-start.25
  80.8 2.0 %collective-permute-done.29 = bf16[2,8,6656]{2,1,0:T(8,128)(2,1)S(1)} collective-permute-done((bf16[2,8,6656]{2,1,0:T(8,128)(2,1)S(1)}, bf16[2,8,6656]{2,1,0:T(8,128)(2,1)S(1)}, u32[]{:S(2)}, u32[]{:S(2)}) %collective-permute-start.29) | collective-permute-done | bytes 213024 | tf_op jit(solution)/shard_map/ppermute | solution.py:168
  83.1 1.7 %collective-permute-done.28 = bf16[8,3328]{1,0:T(8,128)(2,1)S(1)} collective-permute-done((bf16[8,3328]{1,0:T(8,128)(2,1)S(1)}, bf16[8,3328]{1,0:T(8,128)(2,1)S(1)}, u32[]{:S(2)}, u32[]{:S(2)}) %collective-permute-start.28) | collective-permute-done | bytes 53280 | tf_op jit(solution)/shard_map/ppermute | solution.py:168
  84.9 0.9 collective-permute-start.34
  85.9 2.0 %collective-permute-start.35 = (bf16[8,4992]{1,0:T(8,128)(2,1)S(1)}, bf16[8,4992]{1,0:T(8,128)(2,1)S(1)}, u32[]{:S(2)}, u32[]{:S(2)}) collective-permute-start(bf16[8,4992]{1,0:T(8,128)(2,1)S(1)} %fusion.48), channel_id=1, source_target_pairs={{0,8},{1,17},{2,10},{3,19},{4,12},{5,21},{6,14},{7,23},{8,0},{9,25... | collective-permute-start | bytes 239624 | tf_op jit(solution)/shard_map/ppermute | solution.py:168
  87.9 1.3 collective-permute-done.26
  89.2 0.7 collective-permute-start.33
  90.0 0.9 collective-permute-start.30
  90.9 0.9 collective-permute-done.31
  92.0 1.6 %collective-permute-start.32 = (bf16[8,6656]{1,0:T(8,128)(2,1)S(1)}, bf16[8,6656]{1,0:T(8,128)(2,1)S(1)}, u32[]{:S(2)}, u32[]{:S(2)}) collective-permute-start(bf16[8,6656]{1,0:T(8,128)(2,1)S(1)} %fusion.42), channel_id=1, source_target_pairs={{0,2},{1,5},{2,0},{3,7},{4,6},{5,1},{6,4},{7,3},{8,10},{9,13},{10,... | collective-permute-start | bytes 319496 | tf_op jit(solution)/shard_map/ppermute | solution.py:168
  94.0 0.7 collective-permute-start.39
  94.8 6.7 %collective-permute-done.33 = bf16[2,8,4992]{2,1,0:T(8,128)(2,1)S(1)} collective-permute-done((bf16[2,8,4992]{2,1,0:T(8,128)(2,1)S(1)}, bf16[2,8,4992]{2,1,0:T(8,128)(2,1)S(1)}, u32[]{:S(2)}, u32[]{:S(2)}) %collective-permute-start.33) | collective-permute-done | bytes 159776 | tf_op jit(solution)/shard_map/ppermute | solution.py:168
  101.7 1.4 %collective-permute-start.37 = (bf16[16,6656]{1,0:T(8,128)(2,1)S(1)}, bf16[16,6656]{1,0:T(8,128)(2,1)S(1)}, u32[]{:S(2)}, u32[]{:S(2)}) collective-permute-start(bf16[16,6656]{1,0:T(8,128)(2,1)S(1)} %constant_dynamic-update-slice_fusion.10), channel_id=1, source_target_pairs={{0,16},{1,9},{2,18},{3,11},{4,20},{5,13},{6,22},{7,15},{8,24},{9,1... | collective-permute-start | bytes 638984 | tf_op jit(solution)/shard_map/ppermute | solution.py:168
  103.5 1.9 %collective-permute-start.42 = (bf16[32,4992]{1,0:T(8,128)(2,1)S(1)}, bf16[32,4992]{1,0:T(8,128)(2,1)S(1)}, u32[]{:S(2)}, u32[]{:S(2)}) collective-permute-start(bf16[32,4992]{1,0:T(8,128)(2,1)S(1)} %constant_dynamic-update-slice_fusion.14), channel_id=1, source_target_pairs={{0,2},{1,5},{2,0},{3,7},{4,6},{5,1},{6,4},{7,3},{8,10},{9,13},{10,... | collective-permute-start | bytes 958472 | tf_op jit(solution)/shard_map/ppermute | solution.py:168
  106.1 1.5 %collective-permute-start.43 = (bf16[16,4992]{1,0:T(8,128)(2,1)S(1)}, bf16[16,4992]{1,0:T(8,128)(2,1)S(1)}, u32[]{:S(2)}, u32[]{:S(2)}) collective-permute-start(bf16[16,4992]{1,0:T(8,128)(2,1)S(1)} %constant_dynamic-update-slice_fusion.18), channel_id=1, source_target_pairs={{0,16},{1,9},{2,18},{3,11},{4,20},{5,13},{6,22},{7,15},{8,24},{9,1... | collective-permute-start | bytes 479240 | tf_op jit(solution)/shard_map/ppermute | solution.py:168
  107.7 1.7 %collective-permute-start.44 = (bf16[32,6656]{1,0:T(8,128)(2,1)S(1)}, bf16[32,6656]{1,0:T(8,128)(2,1)S(1)}, u32[]{:S(2)}, u32[]{:S(2)}) collective-permute-start(bf16[32,6656]{1,0:T(8,128)(2,1)S(1)} %constant_dynamic-update-slice_fusion.20), channel_id=1, source_target_pairs={{0,8},{1,17},{2,10},{3,19},{4,12},{5,21},{6,14},{7,23},{8,0},{9,25... | collective-permute-start | bytes 1277960 | tf_op jit(solution)/shard_map/ppermute | solution.py:168
  109.4 2.4 %fusion.2 = f32[128,512]{1,0:T(8,128)S(1)} fusion(bf16[512,26624]{1,0:T(8,128)(2,1)S(1)} %bitcast.117, bf16[64,6656]{1,0:T(8,128)(2,1)S(1)} %collective-permute-done.36, bf16[64,6656]{1,0:T(8,128)(2,1)S(1)} %constant_dynamic-update-slice_fusion.12), kind=kOutput, calls=%fused_computation.2 | convolution fusion | flops 875823104 | bytes 8781824 | tf_op jit(solution)/shard_map/dot_general | solution.py:135
  111.8 1.2 collective-permute-done.43
  113.1 1.7 %collective-permute-start.46 = (bf16[32,4992]{1,0:T(8,128)(2,1)S(1)}, bf16[32,4992]{1,0:T(8,128)(2,1)S(1)}, u32[]{:S(2)}, u32[]{:S(2)}) collective-permute-start(bf16[32,4992]{1,0:T(8,128)(2,1)S(1)} %constant_dynamic-update-slice_fusion.22), channel_id=1, source_target_pairs={{0,8},{1,17},{2,10},{3,19},{4,12},{5,21},{6,14},{7,23},{8,0},{9,25... | collective-permute-start | bytes 958472 | tf_op jit(solution)/shard_map/ppermute | solution.py:168
  115.0 1.3 fusion.27
  117.0 1.8 %fusion.6 = f32[128,512]{1,0:T(8,128)S(1)} fusion(bf16[512,26624]{1,0:T(8,128)(2,1)S(1)} %bitcast.117, bf16[64,4992]{1,0:T(8,128)(2,1)S(1)} %collective-permute-done.47, bf16[64,4992]{1,0:T(8,128)(2,1)S(1)} %constant_dynamic-update-slice_fusion.24), kind=kOutput, calls=%fused_computation.6 | convolution fusion | flops 656867328 | bytes 6651904 | tf_op jit(solution)/shard_map/dot_general | solution.py:135
  118.9 1.3 collective-permute-done.46
  120.3 2.4 %fusion.22 = f32[128,512]{1,0:T(8,128)S(1)} fusion(f32[128,512]{1,0:T(8,128)S(1)} %fusion.27, bf16[512,26624]{1,0:T(8,128)(2,1)S(1)} %bitcast.117, bf16[64,6656]{1,0:T(8,128)(2,1)S(1)} %collective-permute-done.45, bf16[64,6656]{1,0:T(8,128)(2,1)S(1)} %constant_dynamic-update-slice_fusion.26), kind=kOutput, calls=%fused_computation.31 | convolution fusion | flops 875888640 | bytes 9043968 | tf_op jit(solution)/shard_map/dot_general | solution.py:135
  122.7 1.8 %fusion.30 = f32[128,512]{1,0:T(8,128)S(1)} fusion(f32[128,512]{1,0:T(8,128)S(1)} %fusion.22, bf16[512,26624]{1,0:T(8,128)(2,1)S(1)} %bitcast.117, bf16[64,4992]{1,0:T(8,128)(2,1)S(1)} %collective-permute-done.48, bf16[64,4992]{1,0:T(8,128)(2,1)S(1)} %constant_dynamic-update-slice_fusion.28), kind=kOutput, calls=%fused_computation.33 | convolution fusion | flops 656932864 | bytes 6914048 | tf_op jit(solution)/shard_map/dot_general | solution.py:135
  125.0 2.7 %collective-permute-start.51 = (bf16[32,512]{1,0:T(8,128)(2,1)S(1)}, bf16[32,512]{1,0:T(8,128)(2,1)S(1)}, u32[]{:S(2)}, u32[]{:S(2)}) collective-permute-start(bf16[32,512]{1,0:T(8,128)(2,1)S(1)} %get-tuple-element.250), channel_id=1, source_target_pairs={{0,6},{1,7},{2,4},{3,5},{4,2},{5,3},{6,0},{7,1},{8,14},{9,15},{10,... | collective-permute-start | bytes 98312 | tf_op jit(solution)/shard_map/ppermute | solution.py:168
  127.7 1.8 %collective-permute-start.49 = (bf16[32,512]{1,0:T(8,128)(2,1)S(1)}, bf16[32,512]{1,0:T(8,128)(2,1)S(1)}, u32[]{:S(2)}, u32[]{:S(2)}) collective-permute-start(bf16[32,512]{1,0:T(8,128)(2,1)S(1)} %get-tuple-element.252), channel_id=1, source_target_pairs={{0,2},{1,3},{2,0},{3,1},{4,6},{5,7},{6,4},{7,5},{8,10},{9,11},{10,... | collective-permute-start | bytes 98312 | tf_op jit(solution)/shard_map/ppermute | solution.py:168
  129.4 1.4 collective-permute-done.51
  130.8 1.7 %collective-permute-done.50 = bf16[32,512]{1,0:T(8,128)(2,1)S(1)} collective-permute-done((bf16[32,512]{1,0:T(8,128)(2,1)S(1)}, bf16[32,512]{1,0:T(8,128)(2,1)S(1)}, u32[]{:S(2)}, u32[]{:S(2)}) %collective-permute-start.50) | collective-permute-done | bytes 32800 | tf_op jit(solution)/shard_map/ppermute | solution.py:168
  132.6 1.2 collective-permute-done.52
  134.1 0.6 copy-done
  (161 shorter events, 12.1 us)
Async XLA Ops:
  0.9 1.4 %collective-permute-start = (bf16[4,16,512]{2,1,0:T(8,128)(2,1)S(1)}, bf16[4,16,512]{2,1,0:T(8,128)(2,1)S(1)}, u32[]{:S(2)}, u32[]{:S(2)}) collective-permute-start(bf16[4,16,512]{2,1,0:T(8,128)(2,1)S(1)} %get-tuple-element.264), channel_id=1, source_target_pairs={{0,1},{1,0},{2,3},{3,2},{4,5},{5,4},{6,7},{7,6},{8,9},{9,8},{10,11... | collective-permute-start | bytes 196616 | tf_op jit(solution)/shard_map/ppermute | solution.py:168
  2.4 10.6 %collective-permute-start.3 = (bf16[32,512]{1,0:T(8,128)(2,1)S(1)}, bf16[32,512]{1,0:T(8,128)(2,1)S(1)}, u32[]{:S(2)}, u32[]{:S(2)}) collective-permute-start(bf16[32,512]{1,0:T(8,128)(2,1)S(1)} %get-tuple-element.254), channel_id=1, source_target_pairs={{0,6},{1,7},{2,4},{3,5},{4,2},{5,3},{6,0},{7,1},{8,14},{9,15},{10,... | collective-permute-start | bytes 98312 | tf_op jit(solution)/shard_map/ppermute | solution.py:168
  7.4 5.6 %collective-permute-start.2 = (bf16[32,512]{1,0:T(8,128)(2,1)S(1)}, bf16[32,512]{1,0:T(8,128)(2,1)S(1)}, u32[]{:S(2)}, u32[]{:S(2)}) collective-permute-start(bf16[32,512]{1,0:T(8,128)(2,1)S(1)} %get-tuple-element.255), channel_id=1, source_target_pairs={{0,4},{1,5},{2,6},{3,7},{4,0},{5,1},{6,2},{7,3},{8,12},{9,13},{10,... | collective-permute-start | bytes 98312 | tf_op jit(solution)/shard_map/ppermute | solution.py:168
  7.4 5.6 %collective-permute-start.1 = (bf16[32,512]{1,0:T(8,128)(2,1)S(1)}, bf16[32,512]{1,0:T(8,128)(2,1)S(1)}, u32[]{:S(2)}, u32[]{:S(2)}) collective-permute-start(bf16[32,512]{1,0:T(8,128)(2,1)S(1)} %get-tuple-element.256), channel_id=1, source_target_pairs={{0,2},{1,3},{2,0},{3,1},{4,6},{5,7},{6,4},{7,5},{8,10},{9,11},{10,... | collective-permute-start | bytes 98312 | tf_op jit(solution)/shard_map/ppermute | solution.py:168
  15.4 5.2 %collective-permute-start.4 = (bf16[2,64,6656]{2,1,0:T(8,128)(2,1)S(1)}, bf16[2,64,6656]{2,1,0:T(8,128)(2,1)S(1)}, u32[]{:S(2)}, u32[]{:S(2)}) collective-permute-start(bf16[2,64,6656]{2,1,0:T(8,128)(2,1)S(1)} %get-tuple-element.112), channel_id=1, source_target_pairs={{0,1},{1,0},{2,3},{3,2},{4,5},{5,4},{6,7},{7,6},{8,9},{9,8},{10,11... | collective-permute-start | bytes 5111816 | tf_op jit(solution)/shard_map/ppermute | solution.py:168
  20.0 6.2 %collective-permute-start.7 = (bf16[2,64,4992]{2,1,0:T(8,128)(2,1)S(1)}, bf16[2,64,4992]{2,1,0:T(8,128)(2,1)S(1)}, u32[]{:S(2)}, u32[]{:S(2)}) collective-permute-start(bf16[2,64,4992]{2,1,0:T(8,128)(2,1)S(1)} %get-tuple-element.114), channel_id=1, source_target_pairs={{0,1},{1,0},{2,3},{3,2},{4,5},{5,4},{6,7},{7,6},{8,9},{9,8},{10,11... | collective-permute-start | bytes 3833864 | tf_op jit(solution)/shard_map/ppermute | solution.py:168
  21.0 15.2 %collective-permute-start.5 = (bf16[2,32,6656]{2,1,0:T(8,128)(2,1)S(1)}, bf16[2,32,6656]{2,1,0:T(8,128)(2,1)S(1)}, u32[]{:S(2)}, u32[]{:S(2)}) collective-permute-start(bf16[2,32,6656]{2,1,0:T(8,128)(2,1)S(1)} %get-tuple-element.218), channel_id=1, source_target_pairs={{0,8},{1,17},{2,10},{3,19},{4,12},{5,21},{6,14},{7,23},{8,0},{9,25... | collective-permute-start | bytes 2555912 | tf_op jit(solution)/shard_map/ppermute | solution.py:168
  26.2 2.4 %collective-permute-start.6 = (bf16[2,64,3328]{2,1,0:T(8,128)(2,1)S(1)}, bf16[2,64,3328]{2,1,0:T(8,128)(2,1)S(1)}, u32[]{:S(2)}, u32[]{:S(2)}) collective-permute-start(bf16[2,64,3328]{2,1,0:T(8,128)(2,1)S(1)} %get-tuple-element.119), channel_id=1, source_target_pairs={{0,1},{1,0},{2,3},{3,2},{4,5},{5,4},{6,7},{7,6},{8,9},{9,8},{10,11... | collective-permute-start | bytes 2555912 | tf_op jit(solution)/shard_map/ppermute | solution.py:168
  26.6 17.3 %collective-permute-start.9 = (bf16[2,32,4992]{2,1,0:T(8,128)(2,1)S(1)}, bf16[2,32,4992]{2,1,0:T(8,128)(2,1)S(1)}, u32[]{:S(2)}, u32[]{:S(2)}) collective-permute-start(bf16[2,32,4992]{2,1,0:T(8,128)(2,1)S(1)} %get-tuple-element.221), channel_id=1, source_target_pairs={{0,2},{1,5},{2,0},{3,7},{4,6},{5,1},{6,4},{7,3},{8,10},{9,13},{10,... | collective-permute-start | bytes 1916936 | tf_op jit(solution)/shard_map/ppermute | solution.py:168
  28.9 9.4 %collective-permute-start.11 = (bf16[2,32,3328]{2,1,0:T(8,128)(2,1)S(1)}, bf16[2,32,3328]{2,1,0:T(8,128)(2,1)S(1)}, u32[]{:S(2)}, u32[]{:S(2)}) collective-permute-start(bf16[2,32,3328]{2,1,0:T(8,128)(2,1)S(1)} %get-tuple-element.228), channel_id=1, source_target_pairs={{0,8},{1,17},{2,10},{3,19},{4,12},{5,21},{6,14},{7,23},{8,0},{9,25... | collective-permute-start | bytes 1277960 | tf_op jit(solution)/shard_map/ppermute | solution.py:168
  35.3 4.8 %collective-permute-start.10 = (bf16[2,64,6656]{2,1,0:T(8,128)(2,1)S(1)}, bf16[2,64,6656]{2,1,0:T(8,128)(2,1)S(1)}, u32[]{:S(2)}, u32[]{:S(2)}) collective-permute-start(bf16[2,64,6656]{2,1,0:T(8,128)(2,1)S(1)} %get-tuple-element.126), channel_id=1, source_target_pairs={{0,1},{1,0},{2,3},{3,2},{4,5},{5,4},{6,7},{7,6},{8,9},{9,8},{10,11... | collective-permute-start | bytes 5111816 | tf_op jit(solution)/shard_map/ppermute | solution.py:168
  36.3 15.7 %collective-permute-start.8 = (bf16[2,16,6656]{2,1,0:T(8,128)(2,1)S(1)}, bf16[2,16,6656]{2,1,0:T(8,128)(2,1)S(1)}, u32[]{:S(2)}, u32[]{:S(2)}) collective-permute-start(bf16[2,16,6656]{2,1,0:T(8,128)(2,1)S(1)} %get-tuple-element.226), channel_id=1, source_target_pairs={{0,16},{1,9},{2,18},{3,11},{4,20},{5,13},{6,22},{7,15},{8,24},{9,1... | collective-permute-start | bytes 1277960 | tf_op jit(solution)/shard_map/ppermute | solution.py:168
  38.4 16.3 %collective-permute-start.15 = (bf16[2,16,3328]{2,1,0:T(8,128)(2,1)S(1)}, bf16[2,16,3328]{2,1,0:T(8,128)(2,1)S(1)}, u32[]{:S(2)}, u32[]{:S(2)}) collective-permute-start(bf16[2,16,3328]{2,1,0:T(8,128)(2,1)S(1)} %get-tuple-element.236), channel_id=1, source_target_pairs={{0,16},{1,9},{2,18},{3,11},{4,20},{5,13},{6,22},{7,15},{8,24},{9,1... | collective-permute-start | bytes 638984 | tf_op jit(solution)/shard_map/ppermute | solution.py:168
  44.1 18.0 %collective-permute-start.19 = (bf16[2,16,4992]{2,1,0:T(8,128)(2,1)S(1)}, bf16[2,16,4992]{2,1,0:T(8,128)(2,1)S(1)}, u32[]{:S(2)}, u32[]{:S(2)}) collective-permute-start(bf16[2,16,4992]{2,1,0:T(8,128)(2,1)S(1)} %get-tuple-element.231), channel_id=1, source_target_pairs={{0,4},{1,3},{2,6},{3,1},{4,0},{5,7},{6,2},{7,5},{8,12},{9,11},{10,... | collective-permute-start | bytes 958472 | tf_op jit(solution)/shard_map/ppermute | solution.py:168
  46.0 12.7 %collective-permute-start.13 = (bf16[2,32,6656]{2,1,0:T(8,128)(2,1)S(1)}, bf16[2,32,6656]{2,1,0:T(8,128)(2,1)S(1)}, u32[]{:S(2)}, u32[]{:S(2)}) collective-permute-start(bf16[2,32,6656]{2,1,0:T(8,128)(2,1)S(1)} %get-tuple-element.216), channel_id=1, source_target_pairs={{0,8},{1,17},{2,10},{3,19},{4,12},{5,21},{6,14},{7,23},{8,0},{9,25... | collective-permute-start | bytes 2555912 | tf_op jit(solution)/shard_map/ppermute | solution.py:168
  47.1 62.3 %slice-start = ((s8[27262976]{0:T(1024)(128)(4,1)}), s8[2097152]{0:T(1024)(128)(4,1)S(1)}, s32[]{:S(2)}) async-start(s8[27262976]{0:T(1024)(128)(4,1)} %bitcast.116), calls=%async_computation | async-start | bytes 4194304
  47.1 62.3 %slice-start.1 = ((s8[27262976]{0:T(1024)(128)(4,1)}), s8[4194304]{0:T(1024)(128)(4,1)S(1)}, s32[]{:S(2)}) async-start(s8[27262976]{0:T(1024)(128)(4,1)} %bitcast.116), calls=%async_computation.1 | async-start | bytes 8388608
  47.1 62.3 %slice-start.2 = ((s8[27262976]{0:T(1024)(128)(4,1)}), s8[4194304]{0:T(1024)(128)(4,1)S(1)}, s32[]{:S(2)}) async-start(s8[27262976]{0:T(1024)(128)(4,1)} %bitcast.116), calls=%async_computation.2 | async-start | bytes 8388608
  47.1 62.3 %slice-start.3 = ((s8[27262976]{0:T(1024)(128)(4,1)}), s8[4194304]{0:T(1024)(128)(4,1)S(1)}, s32[]{:S(2)}) async-start(s8[27262976]{0:T(1024)(128)(4,1)} %bitcast.116), calls=%async_computation.3 | async-start | bytes 8388608
  47.1 62.3 %slice-start.4 = ((s8[27262976]{0:T(1024)(128)(4,1)}), s8[4194304]{0:T(1024)(128)(4,1)S(1)}, s32[]{:S(2)}) async-start(s8[27262976]{0:T(1024)(128)(4,1)} %bitcast.116), calls=%async_computation.4 | async-start | bytes 8388608
  51.9 3.1 %collective-permute-start.14 = (bf16[2,64,4992]{2,1,0:T(8,128)(2,1)S(1)}, bf16[2,64,4992]{2,1,0:T(8,128)(2,1)S(1)}, u32[]{:S(2)}, u32[]{:S(2)}) collective-permute-start(bf16[2,64,4992]{2,1,0:T(8,128)(2,1)S(1)} %get-tuple-element.137), channel_id=1, source_target_pairs={{0,1},{1,0},{2,3},{3,2},{4,5},{5,4},{6,7},{7,6},{8,9},{9,8},{10,11... | collective-permute-start | bytes 3833864 | tf_op jit(solution)/shard_map/ppermute | solution.py:168
  52.1 9.7 %collective-permute-start.12 = (bf16[2,8,6656]{2,1,0:T(8,128)(2,1)S(1)}, bf16[2,8,6656]{2,1,0:T(8,128)(2,1)S(1)}, u32[]{:S(2)}, u32[]{:S(2)}) collective-permute-start(bf16[2,8,6656]{2,1,0:T(8,128)(2,1)S(1)} %get-tuple-element.237), channel_id=1, source_target_pairs={{0,2},{1,5},{2,0},{3,7},{4,6},{5,1},{6,4},{7,3},{8,10},{9,13},{10,... | collective-permute-start | bytes 638984 | tf_op jit(solution)/shard_map/ppermute | solution.py:168
  54.7 8.3 %collective-permute-start.18 = (bf16[2,8,3328]{2,1,0:T(8,128)(2,1)S(1)}, bf16[2,8,3328]{2,1,0:T(8,128)(2,1)S(1)}, u32[]{:S(2)}, u32[]{:S(2)}) collective-permute-start(bf16[2,8,3328]{2,1,0:T(8,128)(2,1)S(1)} %get-tuple-element.244), channel_id=1, source_target_pairs={{0,2},{1,5},{2,0},{3,7},{4,6},{5,1},{6,4},{7,3},{8,10},{9,13},{10,... | collective-permute-start | bytes 319496 | tf_op jit(solution)/shard_map/ppermute | solution.py:168
  55.0 54.4 %slice-start.5 = ((s8[27262976]{0:T(1024)(128)(4,1)}), s8[4194304]{0:T(1024)(128)(4,1)S(1)}, s32[]{:S(2)}) async-start(s8[27262976]{0:T(1024)(128)(4,1)} %bitcast.116), calls=%async_computation.5 | async-start | bytes 8388608
  55.3 15.0 %collective-permute-start.17 = (bf16[2,32,4992]{2,1,0:T(8,128)(2,1)S(1)}, bf16[2,32,4992]{2,1,0:T(8,128)(2,1)S(1)}, u32[]{:S(2)}, u32[]{:S(2)}) collective-permute-start(bf16[2,32,4992]{2,1,0:T(8,128)(2,1)S(1)} %get-tuple-element.220), channel_id=1, source_target_pairs={{0,8},{1,17},{2,10},{3,19},{4,12},{5,21},{6,14},{7,23},{8,0},{9,25... | collective-permute-start | bytes 1916936 | tf_op jit(solution)/shard_map/ppermute | solution.py:168
  58.9 14.8 %collective-permute-start.24 = (bf16[2,16,6656]{2,1,0:T(8,128)(2,1)S(1)}, bf16[2,16,6656]{2,1,0:T(8,128)(2,1)S(1)}, u32[]{:S(2)}, u32[]{:S(2)}) collective-permute-start(bf16[2,16,6656]{2,1,0:T(8,128)(2,1)S(1)} %get-tuple-element.224), channel_id=1, source_target_pairs={{0,16},{1,9},{2,18},{3,11},{4,20},{5,13},{6,22},{7,15},{8,24},{9,1... | collective-permute-start | bytes 1277960 | tf_op jit(solution)/shard_map/ppermute | solution.py:168
  61.9 10.2 %collective-permute-start.16 = (bf16[2,8,6656]{2,1,0:T(8,128)(2,1)S(1)}, bf16[2,8,6656]{2,1,0:T(8,128)(2,1)S(1)}, u32[]{:S(2)}, u32[]{:S(2)}) collective-permute-start(bf16[2,8,6656]{2,1,0:T(8,128)(2,1)S(1)} %add_convert_fusion.21), channel_id=1, source_target_pairs={{0,4},{1,3},{2,6},{3,1},{4,0},{5,7},{6,2},{7,5},{8,12},{9,11},{10,... | collective-permute-start | bytes 638984 | tf_op jit(solution)/shard_map/ppermute | solution.py:168
  62.1 12.4 %collective-permute-start.23 = (bf16[2,8,4992]{2,1,0:T(8,128)(2,1)S(1)}, bf16[2,8,4992]{2,1,0:T(8,128)(2,1)S(1)}, u32[]{:S(2)}, u32[]{:S(2)}) collective-permute-start(bf16[2,8,4992]{2,1,0:T(8,128)(2,1)S(1)} %get-tuple-element.241), channel_id=1, source_target_pairs={{0,8},{1,17},{2,10},{3,19},{4,12},{5,21},{6,14},{7,23},{8,0},{9,25... | collective-permute-start | bytes 479240 | tf_op jit(solution)/shard_map/ppermute | solution.py:168
  63.1 13.0 %collective-permute-start.22 = (bf16[2,8,3328]{2,1,0:T(8,128)(2,1)S(1)}, bf16[2,8,3328]{2,1,0:T(8,128)(2,1)S(1)}, u32[]{:S(2)}, u32[]{:S(2)}) collective-permute-start(bf16[2,8,3328]{2,1,0:T(8,128)(2,1)S(1)} %add_convert_fusion.32), channel_id=1, source_target_pairs={{0,4},{1,3},{2,6},{3,1},{4,0},{5,7},{6,2},{7,5},{8,12},{9,11},{10,... | collective-permute-start | bytes 319496 | tf_op jit(solution)/shard_map/ppermute | solution.py:168
  70.5 7.1 %collective-permute-start.21 = (bf16[2,16,4992]{2,1,0:T(8,128)(2,1)S(1)}, bf16[2,16,4992]{2,1,0:T(8,128)(2,1)S(1)}, u32[]{:S(2)}, u32[]{:S(2)}) collective-permute-start(bf16[2,16,4992]{2,1,0:T(8,128)(2,1)S(1)} %get-tuple-element.230), channel_id=1, source_target_pairs={{0,16},{1,9},{2,18},{3,11},{4,20},{5,13},{6,22},{7,15},{8,24},{9,1... | collective-permute-start | bytes 958472 | tf_op jit(solution)/shard_map/ppermute | solution.py:168
  72.3 7.4 %collective-permute-start.20 = (bf16[8,6656]{1,0:T(8,128)(2,1)S(1)}, bf16[8,6656]{1,0:T(8,128)(2,1)S(1)}, u32[]{:S(2)}, u32[]{:S(2)}) collective-permute-start(bf16[8,6656]{1,0:T(8,128)(2,1)S(1)} %fusion.44), channel_id=1, source_target_pairs={{0,2},{1,5},{2,0},{3,7},{4,6},{5,1},{6,4},{7,3},{8,10},{9,13},{10,... | collective-permute-start | bytes 319496 | tf_op jit(solution)/shard_map/ppermute | solution.py:168
  73.9 8.9 %collective-permute-start.29 = (bf16[2,8,6656]{2,1,0:T(8,128)(2,1)S(1)}, bf16[2,8,6656]{2,1,0:T(8,128)(2,1)S(1)}, u32[]{:S(2)}, u32[]{:S(2)}) collective-permute-start(bf16[2,8,6656]{2,1,0:T(8,128)(2,1)S(1)} %get-tuple-element.234), channel_id=1, source_target_pairs={{0,2},{1,5},{2,0},{3,7},{4,6},{5,1},{6,4},{7,3},{8,10},{9,13},{10,... | collective-permute-start | bytes 638984 | tf_op jit(solution)/shard_map/ppermute | solution.py:168
  74.6 11.2 %collective-permute-start.27 = (bf16[2,8,4992]{2,1,0:T(8,128)(2,1)S(1)}, bf16[2,8,4992]{2,1,0:T(8,128)(2,1)S(1)}, u32[]{:S(2)}, u32[]{:S(2)}) collective-permute-start(bf16[2,8,4992]{2,1,0:T(8,128)(2,1)S(1)} %add_convert_fusion.29), channel_id=1, source_target_pairs={{0,16},{1,9},{2,18},{3,11},{4,20},{5,13},{6,22},{7,15},{8,24},{9,1... | collective-permute-start | bytes 479240 | tf_op jit(solution)/shard_map/ppermute | solution.py:168
  76.1 8.7 %collective-permute-start.28 = (bf16[8,3328]{1,0:T(8,128)(2,1)S(1)}, bf16[8,3328]{1,0:T(8,128)(2,1)S(1)}, u32[]{:S(2)}, u32[]{:S(2)}) collective-permute-start(bf16[8,3328]{1,0:T(8,128)(2,1)S(1)} %fusion.58), channel_id=1, source_target_pairs={{0,2},{1,5},{2,0},{3,7},{4,6},{5,1},{6,4},{7,3},{8,10},{9,13},{10,... | collective-permute-start | bytes 159752 | tf_op jit(solution)/shard_map/ppermute | solution.py:168
  77.6 31.8 %slice-start.6 = ((s8[27262976]{0:T(1024)(128)(4,1)}), s8[4194304]{0:T(1024)(128)(4,1)S(1)}, s32[]{:S(2)}) async-start(s8[27262976]{0:T(1024)(128)(4,1)} %bitcast.116), calls=%async_computation.6 | async-start | bytes 8388608
  77.7 11.5 %collective-permute-start.26 = (bf16[2,8,4992]{2,1,0:T(8,128)(2,1)S(1)}, bf16[2,8,4992]{2,1,0:T(8,128)(2,1)S(1)}, u32[]{:S(2)}, u32[]{:S(2)}) collective-permute-start(bf16[2,8,4992]{2,1,0:T(8,128)(2,1)S(1)} %get-tuple-element.240), channel_id=1, source_target_pairs={{0,2},{1,5},{2,0},{3,7},{4,6},{5,1},{6,4},{7,3},{8,10},{9,13},{10,... | collective-permute-start | bytes 479240 | tf_op jit(solution)/shard_map/ppermute | solution.py:168
  79.7 10.2 %collective-permute-start.25 = (bf16[16,6656]{1,0:T(8,128)(2,1)S(1)}, bf16[16,6656]{1,0:T(8,128)(2,1)S(1)}, u32[]{:S(2)}, u32[]{:S(2)}) collective-permute-start(bf16[16,6656]{1,0:T(8,128)(2,1)S(1)} %constant_dynamic-update-slice_fusion), channel_id=1, source_target_pairs={{0,16},{1,9},{2,18},{3,11},{4,20},{5,13},{6,22},{7,15},{8,24},{9,1... | collective-permute-start | bytes 638984 | tf_op jit(solution)/shard_map/ppermute | solution.py:168
  82.8 9.0 %collective-permute-start.31 = (bf16[2,8,6656]{2,1,0:T(8,128)(2,1)S(1)}, bf16[2,8,6656]{2,1,0:T(8,128)(2,1)S(1)}, u32[]{:S(2)}, u32[]{:S(2)}) collective-permute-start(bf16[2,8,6656]{2,1,0:T(8,128)(2,1)S(1)} %add_convert_fusion.18), channel_id=1, source_target_pairs={{0,4},{1,3},{2,6},{3,1},{4,0},{5,7},{6,2},{7,5},{8,12},{9,11},{10,... | collective-permute-start | bytes 638984 | tf_op jit(solution)/shard_map/ppermute | solution.py:168
  84.9 9.1 %collective-permute-start.34 = (bf16[16,3328]{1,0:T(8,128)(2,1)S(1)}, bf16[16,3328]{1,0:T(8,128)(2,1)S(1)}, u32[]{:S(2)}, u32[]{:S(2)}) collective-permute-start(bf16[16,3328]{1,0:T(8,128)(2,1)S(1)} %constant_dynamic-update-slice_fusion.2), channel_id=1, source_target_pairs={{0,16},{1,9},{2,18},{3,11},{4,20},{5,13},{6,22},{7,15},{8,24},{9,1... | collective-permute-start | bytes 319496 | tf_op jit(solution)/shard_map/ppermute | solution.py:168
  85.9 7.7 %collective-permute-start.35 = (bf16[8,4992]{1,0:T(8,128)(2,1)S(1)}, bf16[8,4992]{1,0:T(8,128)(2,1)S(1)}, u32[]{:S(2)}, u32[]{:S(2)}) collective-permute-start(bf16[8,4992]{1,0:T(8,128)(2,1)S(1)} %fusion.48), channel_id=1, source_target_pairs={{0,8},{1,17},{2,10},{3,19},{4,12},{5,21},{6,14},{7,23},{8,0},{9,25... | collective-permute-start | bytes 239624 | tf_op jit(solution)/shard_map/ppermute | solution.py:168
  89.2 12.3 %collective-permute-start.33 = (bf16[2,8,4992]{2,1,0:T(8,128)(2,1)S(1)}, bf16[2,8,4992]{2,1,0:T(8,128)(2,1)S(1)}, u32[]{:S(2)}, u32[]{:S(2)}) collective-permute-start(bf16[2,8,4992]{2,1,0:T(8,128)(2,1)S(1)} %add_convert_fusion.26), channel_id=1, source_target_pairs={{0,4},{1,3},{2,6},{3,1},{4,0},{5,7},{6,2},{7,5},{8,12},{9,11},{10,... | collective-permute-start | bytes 479240 | tf_op jit(solution)/shard_map/ppermute | solution.py:168
  90.0 13.2 %collective-permute-start.30 = (bf16[32,6656]{1,0:T(8,128)(2,1)S(1)}, bf16[32,6656]{1,0:T(8,128)(2,1)S(1)}, u32[]{:S(2)}, u32[]{:S(2)}) collective-permute-start(bf16[32,6656]{1,0:T(8,128)(2,1)S(1)} %constant_dynamic-update-slice_fusion.4), channel_id=1, source_target_pairs={{0,8},{1,17},{2,10},{3,19},{4,12},{5,21},{6,14},{7,23},{8,0},{9,25... | collective-permute-start | bytes 1277960 | tf_op jit(solution)/shard_map/ppermute | solution.py:168
  92.0 9.7 %collective-permute-start.32 = (bf16[8,6656]{1,0:T(8,128)(2,1)S(1)}, bf16[8,6656]{1,0:T(8,128)(2,1)S(1)}, u32[]{:S(2)}, u32[]{:S(2)}) collective-permute-start(bf16[8,6656]{1,0:T(8,128)(2,1)S(1)} %fusion.42), channel_id=1, source_target_pairs={{0,2},{1,5},{2,0},{3,7},{4,6},{5,1},{6,4},{7,3},{8,10},{9,13},{10,... | collective-permute-start | bytes 319496 | tf_op jit(solution)/shard_map/ppermute | solution.py:168
  93.6 9.9 %collective-permute-start.40 = (bf16[16,4992]{1,0:T(8,128)(2,1)S(1)}, bf16[16,4992]{1,0:T(8,128)(2,1)S(1)}, u32[]{:S(2)}, u32[]{:S(2)}) collective-permute-start(bf16[16,4992]{1,0:T(8,128)(2,1)S(1)} %constant_dynamic-update-slice_fusion.6), channel_id=1, source_target_pairs={{0,4},{1,3},{2,6},{3,1},{4,0},{5,7},{6,2},{7,5},{8,12},{9,11},{10,... | collective-permute-start | bytes 479240 | tf_op jit(solution)/shard_map/ppermute | solution.py:168
  94.0 11.4 %collective-permute-start.39 = (bf16[32,3328]{1,0:T(8,128)(2,1)S(1)}, bf16[32,3328]{1,0:T(8,128)(2,1)S(1)}, u32[]{:S(2)}, u32[]{:S(2)}) collective-permute-start(bf16[32,3328]{1,0:T(8,128)(2,1)S(1)} %constant_dynamic-update-slice_fusion.8), channel_id=1, source_target_pairs={{0,8},{1,17},{2,10},{3,19},{4,12},{5,21},{6,14},{7,23},{8,0},{9,25... | collective-permute-start | bytes 638984 | tf_op jit(solution)/shard_map/ppermute | solution.py:168
  101.6 4.5 %collective-permute-start.38 = (bf16[8,4992]{1,0:T(8,128)(2,1)S(1)}, bf16[8,4992]{1,0:T(8,128)(2,1)S(1)}, u32[]{:S(2)}, u32[]{:S(2)}) collective-permute-start(bf16[8,4992]{1,0:T(8,128)(2,1)S(1)} %fusion.46), channel_id=1, source_target_pairs={{0,2},{1,5},{2,0},{3,7},{4,6},{5,1},{6,4},{7,3},{8,10},{9,13},{10,... | collective-permute-start | bytes 239624 | tf_op jit(solution)/shard_map/ppermute | solution.py:168
  101.7 5.9 %collective-permute-start.37 = (bf16[16,6656]{1,0:T(8,128)(2,1)S(1)}, bf16[16,6656]{1,0:T(8,128)(2,1)S(1)}, u32[]{:S(2)}, u32[]{:S(2)}) collective-permute-start(bf16[16,6656]{1,0:T(8,128)(2,1)S(1)} %constant_dynamic-update-slice_fusion.10), channel_id=1, source_target_pairs={{0,16},{1,9},{2,18},{3,11},{4,20},{5,13},{6,22},{7,15},{8,24},{9,1... | collective-permute-start | bytes 638984 | tf_op jit(solution)/shard_map/ppermute | solution.py:168
  103.2 6.1 %collective-permute-start.36 = (bf16[64,6656]{1,0:T(8,128)(2,1)S(1)}, bf16[64,6656]{1,0:T(8,128)(2,1)S(1)}, u32[]{:S(2)}, u32[]{:S(2)}) collective-permute-start(bf16[64,6656]{1,0:T(8,128)(2,1)S(1)} %constant_dynamic-update-slice_fusion.12), channel_id=1, source_target_pairs={{0,1},{1,0},{2,3},{3,2},{4,5},{5,4},{6,7},{7,6},{8,9},{9,8},{10,11... | collective-permute-start | bytes 2555912 | tf_op jit(solution)/shard_map/ppermute | solution.py:168
  103.5 11.3 %collective-permute-start.42 = (bf16[32,4992]{1,0:T(8,128)(2,1)S(1)}, bf16[32,4992]{1,0:T(8,128)(2,1)S(1)}, u32[]{:S(2)}, u32[]{:S(2)}) collective-permute-start(bf16[32,4992]{1,0:T(8,128)(2,1)S(1)} %constant_dynamic-update-slice_fusion.14), channel_id=1, source_target_pairs={{0,2},{1,5},{2,0},{3,7},{4,6},{5,1},{6,4},{7,3},{8,10},{9,13},{10,... | collective-permute-start | bytes 958472 | tf_op jit(solution)/shard_map/ppermute | solution.py:168
  105.5 9.5 %collective-permute-start.41 = (bf16[64,3328]{1,0:T(8,128)(2,1)S(1)}, bf16[64,3328]{1,0:T(8,128)(2,1)S(1)}, u32[]{:S(2)}, u32[]{:S(2)}) collective-permute-start(bf16[64,3328]{1,0:T(8,128)(2,1)S(1)} %constant_dynamic-update-slice_fusion.16), channel_id=1, source_target_pairs={{0,1},{1,0},{2,3},{3,2},{4,5},{5,4},{6,7},{7,6},{8,9},{9,8},{10,11... | collective-permute-start | bytes 1277960 | tf_op jit(solution)/shard_map/ppermute | solution.py:168
  106.1 7.0 %collective-permute-start.43 = (bf16[16,4992]{1,0:T(8,128)(2,1)S(1)}, bf16[16,4992]{1,0:T(8,128)(2,1)S(1)}, u32[]{:S(2)}, u32[]{:S(2)}) collective-permute-start(bf16[16,4992]{1,0:T(8,128)(2,1)S(1)} %constant_dynamic-update-slice_fusion.18), channel_id=1, source_target_pairs={{0,16},{1,9},{2,18},{3,11},{4,20},{5,13},{6,22},{7,15},{8,24},{9,1... | collective-permute-start | bytes 479240 | tf_op jit(solution)/shard_map/ppermute | solution.py:168
  107.7 8.6 %collective-permute-start.44 = (bf16[32,6656]{1,0:T(8,128)(2,1)S(1)}, bf16[32,6656]{1,0:T(8,128)(2,1)S(1)}, u32[]{:S(2)}, u32[]{:S(2)}) collective-permute-start(bf16[32,6656]{1,0:T(8,128)(2,1)S(1)} %constant_dynamic-update-slice_fusion.20), channel_id=1, source_target_pairs={{0,8},{1,17},{2,10},{3,19},{4,12},{5,21},{6,14},{7,23},{8,0},{9,25... | collective-permute-start | bytes 1277960 | tf_op jit(solution)/shard_map/ppermute | solution.py:168
  113.1 7.1 %collective-permute-start.46 = (bf16[32,4992]{1,0:T(8,128)(2,1)S(1)}, bf16[32,4992]{1,0:T(8,128)(2,1)S(1)}, u32[]{:S(2)}, u32[]{:S(2)}) collective-permute-start(bf16[32,4992]{1,0:T(8,128)(2,1)S(1)} %constant_dynamic-update-slice_fusion.22), channel_id=1, source_target_pairs={{0,8},{1,17},{2,10},{3,19},{4,12},{5,21},{6,14},{7,23},{8,0},{9,25... | collective-permute-start | bytes 958472 | tf_op jit(solution)/shard_map/ppermute | solution.py:168
  114.9 2.1 %collective-permute-start.47 = (bf16[64,4992]{1,0:T(8,128)(2,1)S(1)}, bf16[64,4992]{1,0:T(8,128)(2,1)S(1)}, u32[]{:S(2)}, u32[]{:S(2)}) collective-permute-start(bf16[64,4992]{1,0:T(8,128)(2,1)S(1)} %constant_dynamic-update-slice_fusion.24), channel_id=1, source_target_pairs={{0,1},{1,0},{2,3},{3,2},{4,5},{5,4},{6,7},{7,6},{8,9},{9,8},{10,11... | collective-permute-start | bytes 1916936 | tf_op jit(solution)/shard_map/ppermute | solution.py:168
  116.4 4.0 %collective-permute-start.45 = (bf16[64,6656]{1,0:T(8,128)(2,1)S(1)}, bf16[64,6656]{1,0:T(8,128)(2,1)S(1)}, u32[]{:S(2)}, u32[]{:S(2)}) collective-permute-start(bf16[64,6656]{1,0:T(8,128)(2,1)S(1)} %constant_dynamic-update-slice_fusion.26), channel_id=1, source_target_pairs={{0,1},{1,0},{2,3},{3,2},{4,5},{5,4},{6,7},{7,6},{8,9},{9,8},{10,11... | collective-permute-start | bytes 2555912 | tf_op jit(solution)/shard_map/ppermute | solution.py:168
  120.2 2.5 %collective-permute-start.48 = (bf16[64,4992]{1,0:T(8,128)(2,1)S(1)}, bf16[64,4992]{1,0:T(8,128)(2,1)S(1)}, u32[]{:S(2)}, u32[]{:S(2)}) collective-permute-start(bf16[64,4992]{1,0:T(8,128)(2,1)S(1)} %constant_dynamic-update-slice_fusion.28), channel_id=1, source_target_pairs={{0,1},{1,0},{2,3},{3,2},{4,5},{5,4},{6,7},{7,6},{8,9},{9,8},{10,11... | collective-permute-start | bytes 1916936 | tf_op jit(solution)/shard_map/ppermute | solution.py:168
  125.0 5.8 %collective-permute-start.51 = (bf16[32,512]{1,0:T(8,128)(2,1)S(1)}, bf16[32,512]{1,0:T(8,128)(2,1)S(1)}, u32[]{:S(2)}, u32[]{:S(2)}) collective-permute-start(bf16[32,512]{1,0:T(8,128)(2,1)S(1)} %get-tuple-element.250), channel_id=1, source_target_pairs={{0,6},{1,7},{2,4},{3,5},{4,2},{5,3},{6,0},{7,1},{8,14},{9,15},{10,... | collective-permute-start | bytes 98312 | tf_op jit(solution)/shard_map/ppermute | solution.py:168
  127.7 4.8 %collective-permute-start.50 = (bf16[32,512]{1,0:T(8,128)(2,1)S(1)}, bf16[32,512]{1,0:T(8,128)(2,1)S(1)}, u32[]{:S(2)}, u32[]{:S(2)}) collective-permute-start(bf16[32,512]{1,0:T(8,128)(2,1)S(1)} %get-tuple-element.251), channel_id=1, source_target_pairs={{0,4},{1,5},{2,6},{3,7},{4,0},{5,1},{6,2},{7,3},{8,12},{9,13},{10,... | collective-permute-start | bytes 98312 | tf_op jit(solution)/shard_map/ppermute | solution.py:168
  127.7 4.8 %collective-permute-start.49 = (bf16[32,512]{1,0:T(8,128)(2,1)S(1)}, bf16[32,512]{1,0:T(8,128)(2,1)S(1)}, u32[]{:S(2)}, u32[]{:S(2)}) collective-permute-start(bf16[32,512]{1,0:T(8,128)(2,1)S(1)} %get-tuple-element.252), channel_id=1, source_target_pairs={{0,2},{1,3},{2,0},{3,1},{4,6},{5,7},{6,4},{7,5},{8,10},{9,11},{10,... | collective-permute-start | bytes 98312 | tf_op jit(solution)/shard_map/ppermute | solution.py:168
  132.5 1.3 collective-permute-start.52
  134.1 0.7 copy-start
